TPU v7x, 32 devices: a whole 2x2x4 slice. The times are simulated.
32 devices in a mesh: dom: 8 (over z, x), grp: 4 (over y, core).
Axes of the slice: x: 2, y: 2, z: 4, core: 2. Of those that a mesh axis runs over, the one named last changes fastest.
Arguments:
- adjoint_state: float32 [16, 16, 256, 256], P('grp', None, 'dom'), may hold values from -6 to 6
- east_wind: float32 [16, 256, 256], P(None, 'dom'), may hold values from -0.2 to 0.2
- north_wind: float32 [16, 256, 256], P(None, 'dom'), may hold values from -0.2 to 0.2
- east_diff: float32 [16, 256, 256], P(None, 'dom'), may hold values from 0.01 to 0.05
- north_diff: float32 [16, 256, 256], P(None, 'dom'), may hold values from 0.01 to 0.05
- mass_flux: float32 [16, 256, 256], P(None, 'dom'), may hold values from 0.05 to 0.45
- region_map: int32 [256, 256], P('dom'), may hold values from 0 to 15
- cloud_top: int32 [256, 256], P('dom'), may hold values from 1 to 15
Outputs:
- final_adjoint: float32 [16, 16, 256, 256], P('grp', None, 'dom')
- flux_gradient: float32 [256, 256], P('dom')
Inputs may be any that keep to these rules, and one draw needn't show every extreme that they name: `region_map`: tag k of the whole set of 16 tags belongs to region k.
All inputs are finite; a program needn't handle non-finite values.
Results may differ from a plain program's by a relative error of at most 0.00002.
Values sent between devices are 32-bit elements; how exact they have to be, the bound alone decides.
No kernel may reach another device: no remote copies, remote signals or barrier semaphores. Data moves between devices by JAX's collectives and lax.ppermute only.
A program may use at most 64 MiB of HBM per device.

v0:
```python
import jax
import jax.numpy as jnp
from jax import lax
from jax.sharding import PartitionSpec as P

ITERS = 4


def passed_along(value, axis, by):
    size = lax.axis_size(axis)
    return lax.ppermute(value, axis, [(i, (i + by) % size) for i in range(size)])


def with_halo(cells, sides, width):
    for axis, dim in sides:
        count = lax.axis_size(axis)
        head = lax.slice_in_dim(cells, 0, width, axis=dim)
        tail = lax.slice_in_dim(cells, cells.shape[dim] - width, cells.shape[dim], axis=dim)
        cells = jnp.concatenate(
            [
                lax.ppermute(tail, axis, [(i, (i + 1) % count) for i in range(count)]),
                cells,
                lax.ppermute(head, axis, [((i + 1) % count, i) for i in range(count)]),
            ],
            axis=dim,
        )
    return cells


def local(
    adjoint_state, east_wind, north_wind, east_diff, north_diff, mass_flux, region_map, cloud_top
):
    tags, levels, cols, lats = adjoint_state.shape
    level_ids = lax.broadcasted_iota(jnp.int32, mass_flux.shape, 0)
    active = mass_flux * (level_ids < cloud_top[None]).astype(jnp.float32)
    stacked = jnp.stack([east_wind, east_diff, north_wind, north_diff, active])
    margin = 1
    edge = stacked[0:2, :, cols - 1 : cols]
    left_edge = passed_along(edge, "dom", 1)
    lower_rim = jnp.concatenate(
        [left_edge, jnp.zeros((3,) + left_edge.shape[1:], jnp.float32)], axis=0
    )
    padded = jnp.concatenate([lower_rim, stacked, jnp.zeros_like(lower_rim)], axis=2)
    wind_e = padded[0]
    diff_e = padded[1]
    wind_n = padded[2]
    diff_n = padded[3]
    updraft = padded[4]
    east_coef = jnp.maximum(wind_e, 0.0) + diff_e
    west_prime = jnp.maximum(-wind_e, 0.0) + diff_e
    row_ids = lax.broadcasted_iota(jnp.int32, wind_n.shape, 2)
    north_coef = (jnp.maximum(wind_n, 0.0) + diff_n) * (row_ids < lats - 1).astype(jnp.float32)
    south_prime = jnp.maximum(-wind_n, 0.0) + diff_n
    south_coef = jnp.concatenate(
        [jnp.zeros_like(south_prime[..., :1]), south_prime[..., :-1]], axis=-1
    )
    lam = adjoint_state
    accum = jnp.zeros((tags, cols, lats), jnp.float32)
    for round_step in range(ITERS // margin):
        current = with_halo(lam, (("dom", 2),), 1)
        center = current[:, :, 1 : 1 + cols]
        east = current[:, :, 2 : 2 + cols]
        west = current[:, :, 0:cols]
        coef_e = east_coef[:, margin : margin + cols]
        coef_w = west_prime[:, margin - 1 : margin - 1 + cols]
        coef_n = north_coef[:, margin : margin + cols]
        coef_s = south_coef[:, margin : margin + cols]
        lift = updraft[:, margin : margin + cols]
        north = jnp.concatenate([center[..., 1:], center[..., -1:]], axis=-1)
        south = jnp.concatenate([center[..., :1], center[..., :-1]], axis=-1)
        h = (
            center
            + coef_e * (east - center)
            + coef_w * (west - center)
            + coef_n * (north - center)
            + coef_s * (south - center)
        )
        above = jnp.concatenate([h[:, 1:], h[:, -1:]], axis=1)
        current = h + lift * (above - h)
        accum = accum + current[:, 0, 0:cols]
        lam = current
    tag_ids = lax.axis_index("grp") * tags + lax.broadcasted_iota(jnp.int32, (tags, cols, lats), 0)
    select = (region_map[None] == tag_ids).astype(jnp.float32)
    local_grad = jnp.sum(select * accum, axis=0)
    flux_gradient = lax.psum(local_grad, "grp")
    return (lam, flux_gradient)


def solution(mesh):
    return jax.shard_map(
        local,
        mesh=mesh,
        in_specs=(
            P("grp", None, "dom", None),
            P(None, "dom", None),
            P(None, "dom", None),
            P(None, "dom", None),
            P(None, "dom", None),
            P(None, "dom", None),
            P("dom", None),
            P("dom", None),
        ),
        out_specs=(P("grp", None, "dom", None), P("dom", None)),
        check_vma=False,
    )
```

profile of v0, /device:TPU:0, one launch (start us, length us, event | category | flops | bytes accessed | tf_op | source)
XLA Modules:
  0.0 78.4 jit_solution(5576909689984771250)
XLA Ops:
  1.8 3.0 %collective-permute-start = (f32[2,16,1,256]{3,2,1,0:T(1,128)S(1)}, f32[2,16,1,256]{3,2,1,0:T(1,128)S(1)}, u32[]{:S(2)}, u32[]{:S(2)}) collective-permute-start(f32[2,16,1,256]{3,2,1,0:T(1,128)S(1)} %pad_maximum_fusion.8), channel_id=1, source_target_pairs={{0,4},{4,8},{8,12},{12,16},{16,20},{20,24},{24,28},{28,0},{1,5},{5... | collective-permute-start | bytes 98312 | tf_op jit(solution)/shard_map/ppermute | solution.py:11
  4.8 1.3 %fusion.63 = (f32[4,16,1,256]{3,2,1,0:T(1,128)S(1)}, f32[4,16,1,256]{3,2,1,0:T(1,128)S(1)}) fusion(f32[4,16,32,256]{3,2,1,0:T(8,128)} %param.8), kind=kLoop, calls=%fused_computation.104 | loop fusion | bytes 262144 | tf_op jit(solution)/shard_map/slice | solution.py:17
  6.1 3.1 %collective-permute-start.1 = (f32[4,16,1,256]{3,2,1,0:T(1,128)S(1)}, f32[4,16,1,256]{3,2,1,0:T(1,128)S(1)}, u32[]{:S(2)}, u32[]{:S(2)}) collective-permute-start(f32[4,16,1,256]{3,2,1,0:T(1,128)S(1)} %get-tuple-element.29), channel_id=1, source_target_pairs={{4,0},{8,4},{12,8},{16,12},{20,16},{24,20},{28,24},{0,28},{5,1},{9... | collective-permute-start | bytes 196616 | tf_op jit(solution)/shard_map/ppermute | solution.py:23
  9.2 1.9 %constant_dynamic-update-slice_fusion.1 = f32[5,16,32,256]{3,2,1,0:T(8,128)} fusion(f32[16,32,256]{2,1,0:T(8,128)} %param.9), kind=kLoop, calls=%fused_computation.90 | loop fusion | bytes 1048576
  11.1 2.8 %fusion.62 = (f32[4,16,32,255]{3,2,1,0:T(8,128)}, f32[4,16,32,255]{3,2,1,0:T(8,128)}) fusion(f32[4,16,32,256]{3,2,1,0:T(8,128)S(1)} %copy-done), kind=kLoop, calls=%fused_computation.103 | loop fusion | bytes 8355840 | tf_op jit(solution)/shard_map/slice | solution.py:70
  13.9 1.4 %fusion.61 = (f32[4,16,32,1]{3,2,1,0:T(8,128)S(1)}, f32[4,16,32,1]{3,2,1,0:T(8,128)}) fusion(f32[4,16,32,256]{3,2,1,0:T(8,128)S(1)} %copy-done), kind=kLoop, calls=%fused_computation.102 | loop fusion | bytes 32768 | tf_op jit(solution)/shard_map/slice | solution.py:70
  16.1 1.9 %bitcast_dynamic-update-slice_fusion.2 = f32[5,16,32,256]{3,2,1,0:T(8,128)} fusion(f32[5,16,32,256]{3,2,1,0:T(8,128)} %constant_dynamic-update-slice_fusion, f32[16,32,256]{2,1,0:T(8,128)} %param.10), kind=kLoop, calls=%fused_computation.80 | loop fusion | bytes 1048576
  18.0 1.9 %bitcast_dynamic-update-slice_fusion.1 = f32[5,16,32,256]{3,2,1,0:T(8,128)} fusion(f32[5,16,32,256]{3,2,1,0:T(8,128)} %bitcast_dynamic-update-slice_fusion.2, f32[16,32,256]{2,1,0:T(8,128)} %param.12), kind=kLoop, calls=%fused_computation.79 | loop fusion | bytes 1048576
  19.9 1.9 %bitcast_dynamic-update-slice_fusion = f32[5,16,32,256]{3,2,1,0:T(8,128)} fusion(f32[5,16,32,256]{3,2,1,0:T(8,128)} %bitcast_dynamic-update-slice_fusion.1, f32[16,32,256]{2,1,0:T(8,128)} %param.13, s32[32,256]{1,0:T(8,128)S(1)} %copy-done.6), kind=kLoop, calls=%fused_computation.78 | loop fusion | flops 262144 | bytes 1081344 | tf_op jit(solution)/shard_map/stack | solution.py:36
  21.8 2.2 %fusion = f32[5,16,34,256]{3,2,1,0:T(8,128)S(1)} fusion(f32[2,16,1,256]{3,2,1,0:T(1,128)S(1)} %collective-permute-done, f32[5,16,32,256]{3,2,1,0:T(8,128)} %bitcast_dynamic-update-slice_fusion, f32[34]{0:T(128)S(1)} %pad.44.clone), kind=kLoop, calls=%fused_computation.1 | loop fusion | flops 2785280 | bytes 5439624 | tf_op jit(solution)/shard_map/concatenate | solution.py:43
  26.9 1.9 %fusion.29 = f32[4,16,32,256]{3,2,1,0:T(8,128)S(1)} fusion(f32[4,16,32,256]{3,2,1,0:T(8,128)S(1)} %copy-done, f32[4,16,1,256]{3,2,1,0:T(1,128)S(1)} %collective-permute-done.2, f32[4,16,1,256]{3,2,1,0:T(1,128)S(1)} %collective-permute-done.1, f32[4,16,32,1]{3,2,1,0:T(8,128)S(1)} %copy-done.3, f32[4,16,32,255]{3,2,1,0:T(8,128)S(1)} %copy-done.2, ...), kind=kLoop, calls=%fused_computation.38 | loop fusion | flops 8388608 | bytes 10616832 | tf_op jit(solution)/shard_map/add | solution.py:72
  30.7 4.8 %collective-permute-start.3 = (f32[4,16,1,256]{3,2,1,0:T(1,128)S(1)}, f32[4,16,1,256]{3,2,1,0:T(1,128)S(1)}, u32[]{:S(2)}, u32[]{:S(2)}) collective-permute-start(f32[4,16,1,256]{3,2,1,0:T(1,128)S(1)} %get-tuple-element.23), channel_id=1, source_target_pairs={{4,0},{8,4},{12,8},{16,12},{20,16},{24,20},{28,24},{0,28},{5,1},{9... | collective-permute-start | bytes 196616 | tf_op jit(solution)/shard_map/ppermute | solution.py:23
  35.9 1.5 %collective-permute-done.3 = f32[4,16,1,256]{3,2,1,0:T(1,128)S(1)} collective-permute-done((f32[4,16,1,256]{3,2,1,0:T(1,128)S(1)}, f32[4,16,1,256]{3,2,1,0:T(1,128)S(1)}, u32[]{:S(2)}, u32[]{:S(2)}) %collective-permute-start.3) | collective-permute-done | bytes 65568 | tf_op jit(solution)/shard_map/ppermute | solution.py:23
  37.4 5.1 %collective-permute-done.4 = f32[4,16,1,256]{3,2,1,0:T(1,128)S(1)} collective-permute-done((f32[4,16,1,256]{3,2,1,0:T(1,128)S(1)}, f32[4,16,1,256]{3,2,1,0:T(1,128)S(1)}, u32[]{:S(2)}, u32[]{:S(2)}) %collective-permute-start.4) | collective-permute-done | bytes 65568 | tf_op jit(solution)/shard_map/ppermute | solution.py:21
  42.5 2.0 %fusion.21 = f32[4,16,32,256]{3,2,1,0:T(8,128)S(1)} fusion(f32[4,16,32,256]{3,2,1,0:T(8,128)S(1)} %fusion.36, f32[4,16,1,256]{3,2,1,0:T(1,128)S(1)} %collective-permute-done.4, f32[4,16,1,256]{3,2,1,0:T(1,128)S(1)} %collective-permute-done.3, f32[4,16,32,1]{3,2,1,0:T(8,128)S(1)} %get-tuple-element.20, f32[4,16,32,255]{3,2,1,0:T(8,128)S(1)} %get-tuple-element.22, ...), kind=kLoop, calls=%fused_computation.28 | loop fusion | flops 8388608 | bytes 10616832 | tf_op jit(solution)/shard_map/add | solution.py:72
  46.5 2.0 %collective-permute-start.6 = (f32[4,16,1,256]{3,2,1,0:T(1,128)S(1)}, f32[4,16,1,256]{3,2,1,0:T(1,128)S(1)}, u32[]{:S(2)}, u32[]{:S(2)}) collective-permute-start(f32[4,16,1,256]{3,2,1,0:T(1,128)S(1)} %get-tuple-element.18), channel_id=1, source_target_pairs={{0,4},{4,8},{8,12},{12,16},{16,20},{20,24},{24,28},{28,0},{1,5},{5... | collective-permute-start | bytes 196616 | tf_op jit(solution)/shard_map/ppermute | solution.py:21
  48.9 2.2 %collective-permute-done.5 = f32[4,16,1,256]{3,2,1,0:T(1,128)S(1)} collective-permute-done((f32[4,16,1,256]{3,2,1,0:T(1,128)S(1)}, f32[4,16,1,256]{3,2,1,0:T(1,128)S(1)}, u32[]{:S(2)}, u32[]{:S(2)}) %collective-permute-start.5) | collective-permute-done | bytes 65568 | tf_op jit(solution)/shard_map/ppermute | solution.py:23
  51.1 2.4 %collective-permute-done.6 = f32[4,16,1,256]{3,2,1,0:T(1,128)S(1)} collective-permute-done((f32[4,16,1,256]{3,2,1,0:T(1,128)S(1)}, f32[4,16,1,256]{3,2,1,0:T(1,128)S(1)}, u32[]{:S(2)}, u32[]{:S(2)}) %collective-permute-start.6) | collective-permute-done | bytes 65568 | tf_op jit(solution)/shard_map/ppermute | solution.py:21
  53.5 2.0 %fusion.13 = f32[4,16,32,256]{3,2,1,0:T(8,128)S(1)} fusion(f32[4,16,32,256]{3,2,1,0:T(8,128)S(1)} %fusion.40, f32[4,16,1,256]{3,2,1,0:T(1,128)S(1)} %collective-permute-done.6, f32[4,16,1,256]{3,2,1,0:T(1,128)S(1)} %collective-permute-done.5, f32[4,16,32,1]{3,2,1,0:T(8,128)S(1)} %get-tuple-element.14, f32[4,16,32,255]{3,2,1,0:T(8,128)S(1)} %get-tuple-element.16, ...), kind=kLoop, calls=%fused_computation.18 | loop fusion | flops 8388608 | bytes 10616832 | tf_op jit(solution)/shard_map/add | solution.py:72
  57.4 2.0 %collective-permute-start.8 = (f32[4,16,1,256]{3,2,1,0:T(1,128)S(1)}, f32[4,16,1,256]{3,2,1,0:T(1,128)S(1)}, u32[]{:S(2)}, u32[]{:S(2)}) collective-permute-start(f32[4,16,1,256]{3,2,1,0:T(1,128)S(1)} %get-tuple-element.12), channel_id=1, source_target_pairs={{0,4},{4,8},{8,12},{12,16},{16,20},{20,24},{24,28},{28,0},{1,5},{5... | collective-permute-start | bytes 196616 | tf_op jit(solution)/shard_map/ppermute | solution.py:21
  59.8 1.9 %collective-permute-done.7 = f32[4,16,1,256]{3,2,1,0:T(1,128)S(1)} collective-permute-done((f32[4,16,1,256]{3,2,1,0:T(1,128)S(1)}, f32[4,16,1,256]{3,2,1,0:T(1,128)S(1)}, u32[]{:S(2)}, u32[]{:S(2)}) %collective-permute-start.7) | collective-permute-done | bytes 65568 | tf_op jit(solution)/shard_map/ppermute | solution.py:23
  61.6 2.8 %collective-permute-done.8 = f32[4,16,1,256]{3,2,1,0:T(1,128)S(1)} collective-permute-done((f32[4,16,1,256]{3,2,1,0:T(1,128)S(1)}, f32[4,16,1,256]{3,2,1,0:T(1,128)S(1)}, u32[]{:S(2)}, u32[]{:S(2)}) %collective-permute-start.8) | collective-permute-done | bytes 65568 | tf_op jit(solution)/shard_map/ppermute | solution.py:21
  64.4 2.0 %fusion.5 = f32[4,16,32,256]{3,2,1,0:T(8,128)S(1)} fusion(f32[4,16,32,256]{3,2,1,0:T(8,128)S(1)} %fusion.44, f32[4,16,1,256]{3,2,1,0:T(1,128)S(1)} %collective-permute-done.8, f32[4,16,1,256]{3,2,1,0:T(1,128)S(1)} %collective-permute-done.7, f32[4,16,32,1]{3,2,1,0:T(8,128)S(1)} %get-tuple-element.8, f32[4,16,32,255]{3,2,1,0:T(8,128)S(1)} %get-tuple-element.10, ...), kind=kLoop, calls=%fused_computation.8 | loop fusion | flops 8388608 | bytes 10616832 | tf_op jit(solution)/shard_map/add | solution.py:72
  67.5 10.9 %psum.7 = f32[32,256]{1,0:T(8,128)} all-reduce(f32[32,256]{1,0:T(8,128)S(1)} %fusion.51), channel_id=1, replica_groups=mesh['dom'=8,'grp'=4] {'grp'}, use_global_device_ids=true, to_apply=%region_1.0 | all-reduce | flops 8192 | bytes 65536 | tf_op jit(solution)/shard_map/psum | solution.py:85
  (55 shorter events, 12.6 us)
Async XLA Ops:
  0.6 10.5 %copy-start = (f32[4,16,32,256]{3,2,1,0:T(8,128)S(1)}, f32[4,16,32,256]{3,2,1,0:T(8,128)}, u32[]{:S(2)}) copy-start(f32[4,16,32,256]{3,2,1,0:T(8,128)} %param.8) | copy-start | bytes 6291460
  1.8 20.1 %collective-permute-start = (f32[2,16,1,256]{3,2,1,0:T(1,128)S(1)}, f32[2,16,1,256]{3,2,1,0:T(1,128)S(1)}, u32[]{:S(2)}, u32[]{:S(2)}) collective-permute-start(f32[2,16,1,256]{3,2,1,0:T(1,128)S(1)} %pad_maximum_fusion.8), channel_id=1, source_target_pairs={{0,4},{4,8},{8,12},{12,16},{16,20},{20,24},{24,28},{28,0},{1,5},{5... | collective-permute-start | bytes 98312 | tf_op jit(solution)/shard_map/ppermute | solution.py:11
  6.1 18.7 %collective-permute-start.1 = (f32[4,16,1,256]{3,2,1,0:T(1,128)S(1)}, f32[4,16,1,256]{3,2,1,0:T(1,128)S(1)}, u32[]{:S(2)}, u32[]{:S(2)}) collective-permute-start(f32[4,16,1,256]{3,2,1,0:T(1,128)S(1)} %get-tuple-element.29), channel_id=1, source_target_pairs={{4,0},{8,4},{12,8},{16,12},{20,16},{24,20},{28,24},{0,28},{5,1},{9... | collective-permute-start | bytes 196616 | tf_op jit(solution)/shard_map/ppermute | solution.py:23
  9.2 15.6 %collective-permute-start.2 = (f32[4,16,1,256]{3,2,1,0:T(1,128)S(1)}, f32[4,16,1,256]{3,2,1,0:T(1,128)S(1)}, u32[]{:S(2)}, u32[]{:S(2)}) collective-permute-start(f32[4,16,1,256]{3,2,1,0:T(1,128)S(1)} %get-tuple-element.30), channel_id=1, source_target_pairs={{0,4},{4,8},{8,12},{12,16},{16,20},{20,24},{24,28},{28,0},{1,5},{5... | collective-permute-start | bytes 196616 | tf_op jit(solution)/shard_map/ppermute | solution.py:21
  13.9 1.4 %copy-start.5 = (f32[16,32,256]{2,1,0:T(8,128)S(1)}, f32[16,32,256]{2,1,0:T(8,128)}, u32[]{:S(2)}) copy-start(f32[16,32,256]{2,1,0:T(8,128)} %param.11) | copy-start | bytes 1572868
  15.2 4.6 %copy-start.6 = (s32[32,256]{1,0:T(8,128)S(1)}, s32[32,256]{1,0:T(8,128)}, u32[]{:S(2)}) copy-start(s32[32,256]{1,0:T(8,128)} %param.15) | copy-start | bytes 98308
  24.4 1.6 %copy-start.2 = (f32[4,16,32,255]{3,2,1,0:T(8,128)S(1)}, f32[4,16,32,255]{3,2,1,0:T(8,128)}, u32[]{:S(2)}) copy-start(f32[4,16,32,255]{3,2,1,0:T(8,128)} %get-tuple-element.28) | copy-start | bytes 6266884
  24.6 2.1 %copy-start.1 = (f32[4,16,32,255]{3,2,1,0:T(8,128)S(1)}, f32[4,16,32,255]{3,2,1,0:T(8,128)}, u32[]{:S(2)}) copy-start(f32[4,16,32,255]{3,2,1,0:T(8,128)} %get-tuple-element.27) | copy-start | bytes 6266884
  24.6 2.3 %copy-start.3 = (f32[4,16,32,1]{3,2,1,0:T(8,128)S(1)}, f32[4,16,32,1]{3,2,1,0:T(8,128)}, u32[]{:S(2)}) copy-start(f32[4,16,32,1]{3,2,1,0:T(8,128)} %get-tuple-element.26) | copy-start | bytes 24580
  30.7 6.7 %collective-permute-start.3 = (f32[4,16,1,256]{3,2,1,0:T(1,128)S(1)}, f32[4,16,1,256]{3,2,1,0:T(1,128)S(1)}, u32[]{:S(2)}, u32[]{:S(2)}) collective-permute-start(f32[4,16,1,256]{3,2,1,0:T(1,128)S(1)} %get-tuple-element.23), channel_id=1, source_target_pairs={{4,0},{8,4},{12,8},{16,12},{20,16},{24,20},{28,24},{0,28},{5,1},{9... | collective-permute-start | bytes 196616 | tf_op jit(solution)/shard_map/ppermute | solution.py:23
  35.5 7.0 %collective-permute-start.4 = (f32[4,16,1,256]{3,2,1,0:T(1,128)S(1)}, f32[4,16,1,256]{3,2,1,0:T(1,128)S(1)}, u32[]{:S(2)}, u32[]{:S(2)}) collective-permute-start(f32[4,16,1,256]{3,2,1,0:T(1,128)S(1)} %get-tuple-element.24), channel_id=1, source_target_pairs={{0,4},{4,8},{8,12},{12,16},{16,20},{20,24},{24,28},{28,0},{1,5},{5... | collective-permute-start | bytes 196616 | tf_op jit(solution)/shard_map/ppermute | solution.py:21
  46.4 4.7 %collective-permute-start.5 = (f32[4,16,1,256]{3,2,1,0:T(1,128)S(1)}, f32[4,16,1,256]{3,2,1,0:T(1,128)S(1)}, u32[]{:S(2)}, u32[]{:S(2)}) collective-permute-start(f32[4,16,1,256]{3,2,1,0:T(1,128)S(1)} %get-tuple-element.17), channel_id=1, source_target_pairs={{4,0},{8,4},{12,8},{16,12},{20,16},{24,20},{28,24},{0,28},{5,1},{9... | collective-permute-start | bytes 196616 | tf_op jit(solution)/shard_map/ppermute | solution.py:23
  46.5 7.0 %collective-permute-start.6 = (f32[4,16,1,256]{3,2,1,0:T(1,128)S(1)}, f32[4,16,1,256]{3,2,1,0:T(1,128)S(1)}, u32[]{:S(2)}, u32[]{:S(2)}) collective-permute-start(f32[4,16,1,256]{3,2,1,0:T(1,128)S(1)} %get-tuple-element.18), channel_id=1, source_target_pairs={{0,4},{4,8},{8,12},{12,16},{16,20},{20,24},{24,28},{28,0},{1,5},{5... | collective-permute-start | bytes 196616 | tf_op jit(solution)/shard_map/ppermute | solution.py:21
  57.3 4.3 %collective-permute-start.7 = (f32[4,16,1,256]{3,2,1,0:T(1,128)S(1)}, f32[4,16,1,256]{3,2,1,0:T(1,128)S(1)}, u32[]{:S(2)}, u32[]{:S(2)}) collective-permute-start(f32[4,16,1,256]{3,2,1,0:T(1,128)S(1)} %get-tuple-element.11), channel_id=1, source_target_pairs={{4,0},{8,4},{12,8},{16,12},{20,16},{24,20},{28,24},{0,28},{5,1},{9... | collective-permute-start | bytes 196616 | tf_op jit(solution)/shard_map/ppermute | solution.py:23
  57.4 7.0 %collective-permute-start.8 = (f32[4,16,1,256]{3,2,1,0:T(1,128)S(1)}, f32[4,16,1,256]{3,2,1,0:T(1,128)S(1)}, u32[]{:S(2)}, u32[]{:S(2)}) collective-permute-start(f32[4,16,1,256]{3,2,1,0:T(1,128)S(1)} %get-tuple-element.12), channel_id=1, source_target_pairs={{0,4},{4,8},{8,12},{12,16},{16,20},{20,24},{24,28},{28,0},{1,5},{5... | collective-permute-start | bytes 196616 | tf_op jit(solution)/shard_map/ppermute | solution.py:21
  66.7 0.8 copy-start.7
  67.4 10.9 %copy-start.4 = (f32[4,16,32,256]{3,2,1,0:T(8,128)}, f32[4,16,32,256]{3,2,1,0:T(8,128)S(1)}, u32[]{:S(2)}) copy-start(f32[4,16,32,256]{3,2,1,0:T(8,128)S(1)} %fusion.48) | copy-start | bytes 6291460
where the time goes:
time: 78.9 us; the launch traced here: 78.4 us
  local copies, waits for them, and re-layouts  19.3 us (24%)
  other arithmetic  16.4 us (21%)
  waiting for transfers between devices  15.8 us (20%)
  starting transfers between devices  15 us (19%)
  blocking collectives  10.9 us (14%)
  between operations  0.97 us (1%)
    psum x1, blocking collectives, local(): flux_gradient = lax.psum(local_grad, 'grp')  10.9 us
    ppermute x4, waiting for transfers between devices, with_halo(): lax.ppermute(tail, axis, [(i, (i + 1) % count) for i in range(count)])  10.2 us
    unnamed x20, local copies, waits for them, and re-layouts  8.83 us
    add x4, other arithmetic, local(): center + coef_e * (east - center) + coef_w * (west - center)  8 us
    ppermute x4, starting transfers between devices, with_halo(): lax.ppermute(head, axis, [((i + 1) % count, i) for i in range(count)])  8 us
    slice x8, local copies, waits for them, and re-layouts, local(): south = jnp.concatenate([center[..., :1], center[..., :-1]], axis=-1)  7.72 us
    ppermute x4, waiting for transfers between devices, with_halo(): lax.ppermute(head, axis, [((i + 1) % count, i) for i in range(count)])  5.59 us
    ppermute x4, starting transfers between devices, with_halo(): lax.ppermute(tail, axis, [(i, (i + 1) % count) for i in range(count)])  4.03 us
  transfers between devices with their start and end apart: 9, of which 6 were waited for; matrix products, arithmetic and copies ran while one was open for 23% of the time, Pallas kernels for 0%

commit v1 on v0

v1 whole, which is shorter than its diff:
```python
import functools

import jax
import jax.numpy as jnp
from jax import lax
from jax.experimental import pallas as pl
from jax.experimental.pallas import tpu as pltpu
from jax.sharding import PartitionSpec as P

ITERS = 4
EDGE = ITERS
PAD = 8


def shifted(value, axis, by):
    size = lax.axis_size(axis)
    return lax.ppermute(value, axis, [(i, (i + by) % size) for i in range(size)])


def faces(ew, ed, nw, nd):
    lats = ew.shape[-1]
    lat = lax.broadcasted_iota(jnp.int32, ew.shape, ew.ndim - 1)
    east = jnp.maximum(ew, 0.0) + ed
    west_next = jnp.maximum(-ew, 0.0) + ed
    north = jnp.where(lat < lats - 1, jnp.maximum(nw, 0.0) + nd, 0.0)
    south = jnp.maximum(-nw, 0.0) + nd
    south = jnp.where(lat > 0, pltpu.roll(south, 1, ew.ndim - 1), 0.0)
    return east, west_next, north, south


def pack_kernel(grp_ref, lam_lo, lam_hi, *refs):
    fields_lo, fields_hi = refs[0:6], refs[6:12]
    send_lo, send_hi, coef_lo, coef_hi = refs[12:]
    levels = lam_lo.shape[1]
    per = coef_lo.shape[1]
    send_lo[...] = lam_lo[:, :, 0:EDGE]
    send_hi[...] = lam_hi[:, :, 8 - EDGE : 8]
    base = grp_ref[0] * per
    for fields, dest, start in ((fields_lo, coef_lo, 0), (fields_hi, coef_hi, 8 - EDGE)):
        for i in range(per):
            ew, ed, nw, nd, mf = (ref[i] for ref in fields[:5])
            level = base + i
            lifted = jnp.where((level < fields[5][...]) & (level < levels - 1), mf, 0.0)
            for n, value in enumerate((*faces(ew, ed, nw, nd), lifted)):
                dest[n, i] = value[start : start + EDGE]


def pack(grp, lam, fields, top, groups):
    tags, levels, cols, lats = lam.shape
    per = levels // groups
    last = cols // 8 - 1
    lam_at = lambda c: pl.BlockSpec((tags, levels, 8, lats), lambda i, g: (0, 0, c, 0))
    field_at = lambda c: pl.BlockSpec((per, 8, lats), lambda i, g: (g[0], c, 0))
    top_at = lambda c: pl.BlockSpec((8, lats), lambda i, g: (c, 0))
    whole = lambda shape: pl.BlockSpec(shape, lambda i, g: (0,) * len(shape))
    lam_send = (tags, levels, EDGE, lats)
    coef_send = (5, per, EDGE, lats)
    shapes = [lam_send, lam_send, coef_send, coef_send]
    return pl.pallas_call(
        pack_kernel,
        grid_spec=pltpu.PrefetchScalarGridSpec(
            num_scalar_prefetch=1,
            grid=(1,),
            in_specs=[lam_at(0), lam_at(last)]
            + [field_at(0)] * 5
            + [top_at(0)]
            + [field_at(last)] * 5
            + [top_at(last)],
            out_specs=[whole(s) for s in shapes],
        ),
        out_shape=[jax.ShapeDtypeStruct(s, jnp.float32) for s in shapes],
        compiler_params=pltpu.CompilerParams(vmem_limit_bytes=24 << 20),
        name="pack_edges",
    )(grp, lam, lam, *fields, top, *fields, top)


def steps_kernel(groups, grp_ref, lam_ref, ew, ed, nw, nd, mf, top, region, from_west, from_east, *refs):
    gathered = refs[:groups]
    out_ref, grad_ref = refs[groups : groups + 2]
    coef, above, done, sems = refs[groups + 2 :]
    tags, levels, cols, lats = lam_ref.shape
    wide = cols + 2 * PAD
    per = levels // groups
    mine = grp_ref[0]
    gap = jnp.zeros((PAD - EDGE, lats), jnp.float32)

    def widen(west, own, east):
        return jnp.concatenate([gap, west, own, east, gap], axis=0)

    def prepare(source, piece):
        base = lax.rem(mine - source + groups, groups) * per

        @pl.loop(0, per)
        def _(i):
            level = base + i
            lifted = jnp.where((level < top[...]) & (level < levels - 1), mf[level], 0.0)
            own = (*faces(ew[level], ed[level], nw[level], nd[level]), lifted)
            e, w, n, s, u = (widen(piece[0, j, i], own[j], piece[1, j, i]) for j in range(5))
            w = pltpu.roll(w, 1, 0)
            for j, value in enumerate((1.0 - e - w - n - s, e, w, n, s, u)):
                coef[level, j] = value

    for source in range(groups):
        prepare(source, gathered[source])

    def column(tag, level, total):
        lam = widen(from_west[tag, level], lam_ref[tag, level], from_east[tag, level])
        for t in range(ITERS):
            h = (
                coef[level, 0] * lam
                + coef[level, 1] * pltpu.roll(lam, wide - 1, 0)
                + coef[level, 2] * pltpu.roll(lam, 1, 0)
                + coef[level, 3] * pltpu.roll(lam, lats - 1, 1)
                + coef[level, 4] * pltpu.roll(lam, 1, 1)
            )
            lam = h + coef[level, 5] * (above[t] - h)
            above[t] = h
            if total is not None:
                total = total + lam[PAD : PAD + cols]
        done[tag, level] = lam[PAD : PAD + cols]
        return total

    grad_ref[...] = jnp.zeros_like(grad_ref)

    @pl.loop(0, tags)
    def _(tag):
        above[...] = jnp.zeros_like(above)

        @pl.loop(0, levels - 1)
        def _(i):
            column(tag, levels - 1 - i, None)

        total = column(tag, 0, jnp.zeros((cols, lats), jnp.float32))
        grad_ref[...] += jnp.where(region[...] == mine * tags + tag, total, 0.0)
        pltpu.make_async_copy(done.at[tag], out_ref.at[tag], sems.at[tag]).start()

    @pl.loop(0, tags)
    def _(tag):
        pltpu.make_async_copy(done.at[tag], out_ref.at[tag], sems.at[tag]).wait()


def steps(groups, grp, lam, fields, top, region, from_west, from_east, gathered):
    tags, levels, cols, lats = lam.shape
    wide = cols + 2 * PAD
    vmem = pl.BlockSpec(memory_space=pltpu.VMEM)
    operands = [lam, *fields, top, region, from_west, from_east, *gathered]
    return pl.pallas_call(
        functools.partial(steps_kernel, groups),
        in_specs=[pl.BlockSpec(memory_space=pltpu.SMEM)] + [vmem] * len(operands),
        out_specs=[pl.BlockSpec(memory_space=pl.ANY), vmem],
        out_shape=[
            jax.ShapeDtypeStruct(lam.shape, jnp.float32),
            jax.ShapeDtypeStruct((cols, lats), jnp.float32),
        ],
        scratch_shapes=[
            pltpu.VMEM((levels, 6, wide, lats), jnp.float32),
            pltpu.VMEM((ITERS, wide, lats), jnp.float32),
            pltpu.VMEM(lam.shape, jnp.float32),
            pltpu.SemaphoreType.DMA((tags,)),
        ],
        compiler_params=pltpu.CompilerParams(vmem_limit_bytes=32 << 20),
        name="adjoint_steps",
    )(grp, *operands)


def local(lam, east_wind, north_wind, east_diff, north_diff, mass_flux, region, top):
    groups = lax.axis_size("grp")
    grp = lax.axis_index("grp").astype(jnp.int32).reshape(1)
    fields = (east_wind, east_diff, north_wind, north_diff, mass_flux)
    lam_lo, lam_hi, coef_lo, coef_hi = pack(grp, lam, fields, top, groups)
    coef_west = shifted(coef_hi, "dom", 1)
    coef_east = shifted(coef_lo, "dom", -1)
    from_west = shifted(lam_hi, "dom", 1)
    from_east = shifted(lam_lo, "dom", -1)
    mine = jnp.stack([coef_west, coef_east])
    gathered = [mine] + [shifted(mine, "grp", by) for by in range(1, groups)]
    final, grad = steps(groups, grp, lam, fields, top, region, from_west, from_east, gathered)
    share = grad
    for by in range(1, groups):
        grad = grad + shifted(share, "grp", by)
    return final, grad


def solution(mesh):
    return jax.shard_map(
        local,
        mesh=mesh,
        in_specs=(
            P("grp", None, "dom", None),
            P(None, "dom", None),
            P(None, "dom", None),
            P(None, "dom", None),
            P(None, "dom", None),
            P(None, "dom", None),
            P("dom", None),
            P("dom", None),
        ),
        out_specs=(P("grp", None, "dom", None), P("dom", None)),
        check_vma=False,
    )
```

time: 78.9 us -> 62.1 us (0.79)
  the two profiles are of different devices: /device:TPU:0 before, /device:TPU:16 now
where the time goes in v1:
time: 62.1 us; the launch traced here: 61.6 us
  Pallas kernels  25 us (40%)
  waiting for transfers between devices  18.4 us (30%)
  starting transfers between devices  9.14 us (15%)
  local copies, waits for them, and re-layouts  7.58 us (12%)
  between operations  0.79 us (1%)
  other arithmetic  0.66 us (1%)
    pallas_call x1, Pallas kernels, steps(): pl.pallas_call(functools.partial(steps_kernel, groups), in_specs=[pl.Bloc...  24.9 us
    ppermute x10, waiting for transfers between devices, shifted(): lax.ppermute(value, axis, [(i, (i + by) % size) for i in range(size)])  18.4 us
    ppermute x10, starting transfers between devices, shifted(): lax.ppermute(value, axis, [(i, (i + by) % size) for i in range(size)])  9.14 us
    unnamed x30, local copies, waits for them, and re-layouts  7.58 us
  transfers between devices with their start and end apart: 10, of which 6 were waited for; matrix products, arithmetic and copies ran while one was open for 0% of the time, Pallas kernels for 0%

profile of v1, /device:TPU:16, one launch (start us, length us, event | category | flops | bytes accessed | tf_op | source)
XLA Modules:
  0.0 61.6 jit_solution(5510221051347516712)
XLA Ops:
  0.6 1.6 %copy-done = f32[4,16,32,256]{3,2,1,0:T(8,128)S(1)} copy-done((f32[4,16,32,256]{3,2,1,0:T(8,128)S(1)}, f32[4,16,32,256]{3,2,1,0:T(8,128)}, u32[]{:S(2)}) %copy-start) | copy-done | bytes 2097176
  2.2 1.0 %copy-done.2 = f32[16,32,256]{2,1,0:T(8,128)S(1)} copy-done((f32[16,32,256]{2,1,0:T(8,128)S(1)}, f32[16,32,256]{2,1,0:T(8,128)}, u32[]{:S(2)}) %copy-start.2) | copy-done | bytes 524312
  3.3 1.0 %copy-done.4 = f32[16,32,256]{2,1,0:T(8,128)S(1)} copy-done((f32[16,32,256]{2,1,0:T(8,128)S(1)}, f32[16,32,256]{2,1,0:T(8,128)}, u32[]{:S(2)}) %copy-start.4) | copy-done | bytes 524312
  4.3 1.0 %copy-done.6 = f32[16,32,256]{2,1,0:T(8,128)S(1)} copy-done((f32[16,32,256]{2,1,0:T(8,128)S(1)}, f32[16,32,256]{2,1,0:T(8,128)}, u32[]{:S(2)}) %copy-start.6) | copy-done | bytes 524312
  5.4 1.0 %copy-done.8 = f32[16,32,256]{2,1,0:T(8,128)S(1)} copy-done((f32[16,32,256]{2,1,0:T(8,128)S(1)}, f32[16,32,256]{2,1,0:T(8,128)}, u32[]{:S(2)}) %copy-start.8) | copy-done | bytes 524312
  6.4 1.0 %copy-done.10 = f32[16,32,256]{2,1,0:T(8,128)S(1)} copy-done((f32[16,32,256]{2,1,0:T(8,128)S(1)}, f32[16,32,256]{2,1,0:T(8,128)}, u32[]{:S(2)}) %copy-start.10) | copy-done | bytes 524312
  7.4 0.8 %copy-done.12 = s32[32,256]{1,0:T(8,128)S(1)} copy-done((s32[32,256]{1,0:T(8,128)S(1)}, s32[32,256]{1,0:T(8,128)}, u32[]{:S(2)}) %copy-start.12) | copy-done | bytes 32792
  8.4 1.5 %collective-permute-start.2 = (f32[5,4,4,256]{3,2,1,0:T(4,128)S(1)}, f32[5,4,4,256]{3,2,1,0:T(4,128)S(1)}, u32[]{:S(2)}, u32[]{:S(2)}) collective-permute-start(f32[5,4,4,256]{3,2,1,0:T(4,128)S(1)} %get-tuple-element.10), channel_id=1, source_target_pairs={{0,4},{4,8},{8,12},{12,16},{16,20},{20,24},{24,28},{28,0},{1,5},{5... | collective-permute-start | bytes 245768 | tf_op jit(solution)/shard_map/ppermute | solution.py:17
  10.0 1.4 %collective-permute-start.3 = (f32[5,4,4,256]{3,2,1,0:T(4,128)S(1)}, f32[5,4,4,256]{3,2,1,0:T(4,128)S(1)}, u32[]{:S(2)}, u32[]{:S(2)}) collective-permute-start(f32[5,4,4,256]{3,2,1,0:T(4,128)S(1)} %get-tuple-element.11), channel_id=1, source_target_pairs={{0,28},{4,0},{8,4},{12,8},{16,12},{20,16},{24,20},{28,24},{1,29},{... | collective-permute-start | bytes 245768 | tf_op jit(solution)/shard_map/ppermute | solution.py:17
  11.4 0.6 collective-permute-start
  12.0 2.3 %collective-permute-start.1 = (f32[4,16,4,256]{3,2,1,0:T(4,128)S(1)}, f32[4,16,4,256]{3,2,1,0:T(4,128)S(1)}, u32[]{:S(2)}, u32[]{:S(2)}) collective-permute-start(f32[4,16,4,256]{3,2,1,0:T(4,128)S(1)} %get-tuple-element.9), channel_id=1, source_target_pairs={{0,28},{4,0},{8,4},{12,8},{16,12},{20,16},{24,20},{28,24},{1,29},{... | collective-permute-start | bytes 786440 | tf_op jit(solution)/shard_map/ppermute | solution.py:17
  14.3 6.9 %collective-permute-done.3 = f32[5,4,4,256]{3,2,1,0:T(4,128)S(1)} collective-permute-done((f32[5,4,4,256]{3,2,1,0:T(4,128)S(1)}, f32[5,4,4,256]{3,2,1,0:T(4,128)S(1)}, u32[]{:S(2)}, u32[]{:S(2)}) %collective-permute-start.3) | collective-permute-done | bytes 81952 | tf_op jit(solution)/shard_map/ppermute | solution.py:17
  21.3 0.7 %collective-permute-start.6 = (f32[2,5,4,4,256]{4,3,2,1,0:T(4,128)S(1)}, f32[2,5,4,4,256]{4,3,2,1,0:T(4,128)S(1)}, u32[]{:S(2)}, u32[]{:S(2)}) collective-permute-start(f32[2,5,4,4,256]{4,3,2,1,0:T(4,128)S(1)} %pad_maximum_fusion.refs_0_), channel_id=1, source_target_pairs={{0,3},{1,0},{2,1},{3,2},{4,7},{5,4},{6,5},{7,6},{8,11},{9,8},{10,9... | collective-permute-start | bytes 491528 | tf_op jit(solution)/shard_map/ppermute | solution.py:17
  22.0 1.0 %collective-permute-start.5 = (f32[2,5,4,4,256]{4,3,2,1,0:T(4,128)S(1)}, f32[2,5,4,4,256]{4,3,2,1,0:T(4,128)S(1)}, u32[]{:S(2)}, u32[]{:S(2)}) collective-permute-start(f32[2,5,4,4,256]{4,3,2,1,0:T(4,128)S(1)} %pad_maximum_fusion.refs_0_), channel_id=1, source_target_pairs={{0,2},{1,3},{2,0},{3,1},{4,6},{5,7},{6,4},{7,5},{8,10},{9,11},{10,... | collective-permute-start | bytes 491528 | tf_op jit(solution)/shard_map/ppermute | solution.py:17
  22.9 0.2 collective-permute-start.4
  23.1 3.1 %collective-permute-done.6.refs_3_ = f32[2,5,4,4,256]{4,3,2,1,0:T(4,128)S(1)} collective-permute-done((f32[2,5,4,4,256]{4,3,2,1,0:T(4,128)S(1)}, f32[2,5,4,4,256]{4,3,2,1,0:T(4,128)S(1)}, u32[]{:S(2)}, u32[]{:S(2)}) %collective-permute-start.6) | collective-permute-done | bytes 163872 | tf_op jit(solution)/shard_map/ppermute | solution.py:17
  26.2 5.2 %collective-permute-done.5.refs_2_ = f32[2,5,4,4,256]{4,3,2,1,0:T(4,128)S(1)} collective-permute-done((f32[2,5,4,4,256]{4,3,2,1,0:T(4,128)S(1)}, f32[2,5,4,4,256]{4,3,2,1,0:T(4,128)S(1)}, u32[]{:S(2)}, u32[]{:S(2)}) %collective-permute-start.5) | collective-permute-done | bytes 163872 | tf_op jit(solution)/shard_map/ppermute | solution.py:17
  31.5 24.9 %adjoint_steps.1 = (f32[4,16,32,256]{3,2,1,0:T(8,128)}, f32[32,256]{1,0:T(8,128)S(1)}) custom-call(s32[1]{0:T(128)} %bitcast.grp_ref, f32[4,16,32,256]{3,2,1,0:T(8,128)S(1)} %copy-done.1, f32[16,32,256]{2,1,0:T(8,128)S(1)} %copy-done.3, f32[16,32,256]{2,1,0:T(8,128)S(1)} %copy-done.5, f32[16,32,256]{2,1,0:T(8,128)S(1)} %copy-done.7, ...), custom_call_target="tpu_custom_call" | custom-call | tf_op jit(solution)/shard_map/adjoint_steps/pallas_call | solution.py:147
  56.5 1.2 %collective-permute-start.8 = (f32[32,256]{1,0:T(8,128)S(1)}, f32[32,256]{1,0:T(8,128)S(1)}, u32[]{:S(2)}, u32[]{:S(2)}) collective-permute-start(f32[32,256]{1,0:T(8,128)S(1)} %get-tuple-element.13), channel_id=1, source_target_pairs={{0,2},{1,3},{2,0},{3,1},{4,6},{5,7},{6,4},{7,5},{8,10},{9,11},{10,... | collective-permute-start | bytes 98312 | tf_op jit(solution)/shard_map/ppermute | solution.py:17
  57.6 0.2 collective-permute-start.7
  57.8 0.2 collective-permute-done.9
  58.0 2.4 %collective-permute-done.8 = f32[32,256]{1,0:T(8,128)S(1)} collective-permute-done((f32[32,256]{1,0:T(8,128)S(1)}, f32[32,256]{1,0:T(8,128)S(1)}, u32[]{:S(2)}, u32[]{:S(2)}) %collective-permute-start.8) | collective-permute-done | bytes 32800 | tf_op jit(solution)/shard_map/ppermute | solution.py:17
  60.4 0.6 collective-permute-done.7
  61.0 0.6 %add_add_fusion = f32[32,256]{1,0:T(8,128)} fusion(f32[32,256]{1,0:T(8,128)S(1)} %collective-permute-done.9, f32[32,256]{1,0:T(8,128)S(1)} %collective-permute-done.8, f32[32,256]{1,0:T(8,128)S(1)} %get-tuple-element.13, f32[32,256]{1,0:T(8,128)S(1)} %collective-permute-done.7), kind=kLoop, calls=%fused_computation.1 | loop fusion | flops 24576 | bytes 163840 | tf_op jit(solution)/shard_map/add | solution.py:180
  (30 shorter events, 0.3 us)
Async XLA Ops:
  0.6 1.6 %copy-start = (f32[4,16,32,256]{3,2,1,0:T(8,128)S(1)}, f32[4,16,32,256]{3,2,1,0:T(8,128)}, u32[]{:S(2)}) copy-start(f32[4,16,32,256]{3,2,1,0:T(8,128)} %lam_ref.1) | copy-start | bytes 6291460
  2.2 1.0 %copy-start.2 = (f32[16,32,256]{2,1,0:T(8,128)S(1)}, f32[16,32,256]{2,1,0:T(8,128)}, u32[]{:S(2)}) copy-start(f32[16,32,256]{2,1,0:T(8,128)} %ew.1) | copy-start | bytes 1572868
  3.3 1.0 %copy-start.4 = (f32[16,32,256]{2,1,0:T(8,128)S(1)}, f32[16,32,256]{2,1,0:T(8,128)}, u32[]{:S(2)}) copy-start(f32[16,32,256]{2,1,0:T(8,128)} %ed.1) | copy-start | bytes 1572868
  4.3 1.0 %copy-start.6 = (f32[16,32,256]{2,1,0:T(8,128)S(1)}, f32[16,32,256]{2,1,0:T(8,128)}, u32[]{:S(2)}) copy-start(f32[16,32,256]{2,1,0:T(8,128)} %nw.1) | copy-start | bytes 1572868
  5.4 1.0 %copy-start.8 = (f32[16,32,256]{2,1,0:T(8,128)S(1)}, f32[16,32,256]{2,1,0:T(8,128)}, u32[]{:S(2)}) copy-start(f32[16,32,256]{2,1,0:T(8,128)} %nd.1) | copy-start | bytes 1572868
  6.4 1.0 %copy-start.10 = (f32[16,32,256]{2,1,0:T(8,128)S(1)}, f32[16,32,256]{2,1,0:T(8,128)}, u32[]{:S(2)}) copy-start(f32[16,32,256]{2,1,0:T(8,128)} %mf.1) | copy-start | bytes 1572868
  8.2 23.2 %copy-start.1 = (f32[4,16,32,256]{3,2,1,0:T(8,128)S(1)}, f32[4,16,32,256]{3,2,1,0:T(8,128)}, u32[]{:S(2)}) copy-start(f32[4,16,32,256]{3,2,1,0:T(8,128)} %lam_ref.1) | copy-start | bytes 6291460
  8.2 23.2 %copy-start.3 = (f32[16,32,256]{2,1,0:T(8,128)S(1)}, f32[16,32,256]{2,1,0:T(8,128)}, u32[]{:S(2)}) copy-start(f32[16,32,256]{2,1,0:T(8,128)} %ew.1) | copy-start | bytes 1572868
  8.2 23.2 %copy-start.5 = (f32[16,32,256]{2,1,0:T(8,128)S(1)}, f32[16,32,256]{2,1,0:T(8,128)}, u32[]{:S(2)}) copy-start(f32[16,32,256]{2,1,0:T(8,128)} %ed.1) | copy-start | bytes 1572868
  8.2 23.2 %copy-start.7 = (f32[16,32,256]{2,1,0:T(8,128)S(1)}, f32[16,32,256]{2,1,0:T(8,128)}, u32[]{:S(2)}) copy-start(f32[16,32,256]{2,1,0:T(8,128)} %nw.1) | copy-start | bytes 1572868
  8.2 23.2 %copy-start.9 = (f32[16,32,256]{2,1,0:T(8,128)S(1)}, f32[16,32,256]{2,1,0:T(8,128)}, u32[]{:S(2)}) copy-start(f32[16,32,256]{2,1,0:T(8,128)} %nd.1) | copy-start | bytes 1572868
  8.2 23.2 %copy-start.11 = (f32[16,32,256]{2,1,0:T(8,128)S(1)}, f32[16,32,256]{2,1,0:T(8,128)}, u32[]{:S(2)}) copy-start(f32[16,32,256]{2,1,0:T(8,128)} %mf.1) | copy-start | bytes 1572868
  8.2 23.2 %copy-start.13 = (s32[32,256]{1,0:T(8,128)S(1)}, s32[32,256]{1,0:T(8,128)}, u32[]{:S(2)}) copy-start(s32[32,256]{1,0:T(8,128)} %top.1) | copy-start | bytes 98308
  8.2 23.2 %copy-start.14 = (s32[32,256]{1,0:T(8,128)S(1)}, s32[32,256]{1,0:T(8,128)}, u32[]{:S(2)}) copy-start(s32[32,256]{1,0:T(8,128)} %region.1) | copy-start | bytes 98308
  8.4 5.9 %collective-permute-start.2 = (f32[5,4,4,256]{3,2,1,0:T(4,128)S(1)}, f32[5,4,4,256]{3,2,1,0:T(4,128)S(1)}, u32[]{:S(2)}, u32[]{:S(2)}) collective-permute-start(f32[5,4,4,256]{3,2,1,0:T(4,128)S(1)} %get-tuple-element.10), channel_id=1, source_target_pairs={{0,4},{4,8},{8,12},{12,16},{16,20},{20,24},{24,28},{28,0},{1,5},{5... | collective-permute-start | bytes 245768 | tf_op jit(solution)/shard_map/ppermute | solution.py:17
  10.0 11.3 %collective-permute-start.3 = (f32[5,4,4,256]{3,2,1,0:T(4,128)S(1)}, f32[5,4,4,256]{3,2,1,0:T(4,128)S(1)}, u32[]{:S(2)}, u32[]{:S(2)}) collective-permute-start(f32[5,4,4,256]{3,2,1,0:T(4,128)S(1)} %get-tuple-element.11), channel_id=1, source_target_pairs={{0,28},{4,0},{8,4},{12,8},{16,12},{20,16},{24,20},{28,24},{1,29},{... | collective-permute-start | bytes 245768 | tf_op jit(solution)/shard_map/ppermute | solution.py:17
  11.4 20.0 %collective-permute-start = (f32[4,16,4,256]{3,2,1,0:T(4,128)S(1)}, f32[4,16,4,256]{3,2,1,0:T(4,128)S(1)}, u32[]{:S(2)}, u32[]{:S(2)}) collective-permute-start(f32[4,16,4,256]{3,2,1,0:T(4,128)S(1)} %get-tuple-element.8), channel_id=1, source_target_pairs={{0,4},{4,8},{8,12},{12,16},{16,20},{20,24},{24,28},{28,0},{1,5},{5... | collective-permute-start | bytes 786440 | tf_op jit(solution)/shard_map/ppermute | solution.py:17
  12.0 19.4 %collective-permute-start.1 = (f32[4,16,4,256]{3,2,1,0:T(4,128)S(1)}, f32[4,16,4,256]{3,2,1,0:T(4,128)S(1)}, u32[]{:S(2)}, u32[]{:S(2)}) collective-permute-start(f32[4,16,4,256]{3,2,1,0:T(4,128)S(1)} %get-tuple-element.9), channel_id=1, source_target_pairs={{0,28},{4,0},{8,4},{12,8},{16,12},{20,16},{24,20},{28,24},{1,29},{... | collective-permute-start | bytes 786440 | tf_op jit(solution)/shard_map/ppermute | solution.py:17
  21.3 4.9 %collective-permute-start.6 = (f32[2,5,4,4,256]{4,3,2,1,0:T(4,128)S(1)}, f32[2,5,4,4,256]{4,3,2,1,0:T(4,128)S(1)}, u32[]{:S(2)}, u32[]{:S(2)}) collective-permute-start(f32[2,5,4,4,256]{4,3,2,1,0:T(4,128)S(1)} %pad_maximum_fusion.refs_0_), channel_id=1, source_target_pairs={{0,3},{1,0},{2,1},{3,2},{4,7},{5,4},{6,5},{7,6},{8,11},{9,8},{10,9... | collective-permute-start | bytes 491528 | tf_op jit(solution)/shard_map/ppermute | solution.py:17
  22.0 9.4 %collective-permute-start.5 = (f32[2,5,4,4,256]{4,3,2,1,0:T(4,128)S(1)}, f32[2,5,4,4,256]{4,3,2,1,0:T(4,128)S(1)}, u32[]{:S(2)}, u32[]{:S(2)}) collective-permute-start(f32[2,5,4,4,256]{4,3,2,1,0:T(4,128)S(1)} %pad_maximum_fusion.refs_0_), channel_id=1, source_target_pairs={{0,2},{1,3},{2,0},{3,1},{4,6},{5,7},{6,4},{7,5},{8,10},{9,11},{10,... | collective-permute-start | bytes 491528 | tf_op jit(solution)/shard_map/ppermute | solution.py:17
  22.9 8.5 %collective-permute-start.4 = (f32[2,5,4,4,256]{4,3,2,1,0:T(4,128)S(1)}, f32[2,5,4,4,256]{4,3,2,1,0:T(4,128)S(1)}, u32[]{:S(2)}, u32[]{:S(2)}) collective-permute-start(f32[2,5,4,4,256]{4,3,2,1,0:T(4,128)S(1)} %pad_maximum_fusion.refs_0_), channel_id=1, source_target_pairs={{0,1},{1,2},{2,3},{3,0},{4,5},{5,6},{6,7},{7,4},{8,9},{9,10},{10,1... | collective-permute-start | bytes 491528 | tf_op jit(solution)/shard_map/ppermute | solution.py:17
  56.4 1.7 %collective-permute-start.9 = (f32[32,256]{1,0:T(8,128)S(1)}, f32[32,256]{1,0:T(8,128)S(1)}, u32[]{:S(2)}, u32[]{:S(2)}) collective-permute-start(f32[32,256]{1,0:T(8,128)S(1)} %get-tuple-element.13), channel_id=1, source_target_pairs={{0,3},{1,0},{2,1},{3,2},{4,7},{5,4},{6,5},{7,6},{8,11},{9,8},{10,9... | collective-permute-start | bytes 98312 | tf_op jit(solution)/shard_map/ppermute | solution.py:17
  56.5 4.0 %collective-permute-start.8 = (f32[32,256]{1,0:T(8,128)S(1)}, f32[32,256]{1,0:T(8,128)S(1)}, u32[]{:S(2)}, u32[]{:S(2)}) collective-permute-start(f32[32,256]{1,0:T(8,128)S(1)} %get-tuple-element.13), channel_id=1, source_target_pairs={{0,2},{1,3},{2,0},{3,1},{4,6},{5,7},{6,4},{7,5},{8,10},{9,11},{10,... | collective-permute-start | bytes 98312 | tf_op jit(solution)/shard_map/ppermute | solution.py:17
  57.6 3.3 %collective-permute-start.7 = (f32[32,256]{1,0:T(8,128)S(1)}, f32[32,256]{1,0:T(8,128)S(1)}, u32[]{:S(2)}, u32[]{:S(2)}) collective-permute-start(f32[32,256]{1,0:T(8,128)S(1)} %get-tuple-element.13), channel_id=1, source_target_pairs={{0,1},{1,2},{2,3},{3,0},{4,5},{5,6},{6,7},{7,4},{8,9},{9,10},{10,1... | collective-permute-start | bytes 98312 | tf_op jit(solution)/shard_map/ppermute | solution.py:17
  (1 other events, 0.8 us)

commit v2 on v0

v2 whole, which is shorter than its diff:
```python
import functools

import jax
import jax.numpy as jnp
from jax import lax
from jax.experimental import pallas as pl
from jax.experimental.pallas import tpu as pltpu
from jax.sharding import PartitionSpec as P

ITERS = 4
EDGE = ITERS
ENTRIES = 16
CHUNK = 6
LANES = 128


def shifted(value, axis, by):
    size = lax.axis_size(axis)
    return lax.ppermute(value, axis, [(i, (i + by) % size) for i in range(size)])


def shifted_in_blocks(value, axis, block, by):
    size = lax.axis_size(axis)
    return lax.ppermute(
        value, axis, [(i, i - i % block + (i + by) % block) for i in range(size)]
    )


def faces(ew, ed, nw, nd):
    lats = ew.shape[1]
    lat = lax.broadcasted_iota(jnp.int32, ew.shape, 1)
    east = jnp.maximum(ew, 0.0) + ed
    west_next = jnp.maximum(-ew, 0.0) + ed
    north = jnp.where(lat < lats - 1, jnp.maximum(nw, 0.0) + nd, 0.0)
    south = jnp.maximum(-nw, 0.0) + nd
    south = jnp.where(lat > 0, pltpu.roll(south, 1, 1), 0.0)
    return east, west_next, north, south


def updraft(mf, top_row):
    levels = mf.shape[0]
    level = lax.broadcasted_iota(jnp.int32, mf.shape, 0)
    return jnp.where((level < top_row) & (level < levels - 1), mf, 0.0)


def advance(coefs, mid, east, west):
    d, e, w, n, s, u = coefs
    levels, lats = mid.shape
    h = d * mid + e * east + w * west
    h = h + n * pltpu.roll(mid, lats - 1, 1) + s * pltpu.roll(mid, 1, 1)
    return h + u * (pltpu.roll(h, levels - 1, 0) - h)


def rows_of(ref):
    size = 1
    for n in ref.shape[:-1]:
        size *= n
    return ref.reshape(size, ref.shape[-1])


def halves(ref, start, levels, stride, apart):
    parts = [ref[pl.ds(start + apart * k, levels, stride=stride), :] for k in range(2)]
    return jnp.concatenate(parts, axis=1)


def pack_kernel(parts, grp_ref, lam, ew, ed, nw, nd, mf, top, lam_lo, lam_hi, coef_lo, coef_hi, lam_s, field_s, top_s, entry, sems):
    tags, levels, cols, lats = lam.shape
    copies = []

    def copy(src, dst):
        copies.append(pltpu.make_async_copy(src, dst, sems.at[len(copies)]))
        copies[-1].start()

    for side, first in enumerate((0, cols - 8)):
        copy(top.at[pl.ds(first, 8)], top_s.at[side])
        for k in range(2):
            lane = pl.ds(k * LANES, LANES)
            for f, field in enumerate((ew, ed, nw, nd, mf)):
                copy(field.at[:, pl.ds(first, 8), lane], field_s.at[f, side, k])
    fields_copies = len(copies)
    for side, first in enumerate((0, cols - 8)):
        for k in range(2):
            lane = pl.ds(k * LANES, LANES)
            copy(lam.at[:, :, pl.ds(first, 8), lane], lam_s.at[side, k])
    for c in copies[:fields_copies]:
        c.wait()

    field_rows = rows_of(field_s)
    slab = levels * 8

    def field(f, side, c):
        return halves(field_rows, (f * 2 + side) * 2 * slab + c, levels, 8, slab)

    for side in range(2):
        slot = 0
        for c in range(EDGE - 1) if side == 0 else range(8 - EDGE, 8):
            east, west, north, south = faces(*(field(f, side, c) for f in range(4)))
            lift = updraft(field(4, side, c), top_s[side, pl.ds(c, 1), :])
            wanted = (east, west, north, south, lift)
            if side == 1 and c == 8 - EDGE:
                wanted = (west,)
            for value in wanted:
                entry[side, slot] = value
                slot += 1
        for left in range(slot, ENTRIES):
            entry[side, left] = jnp.zeros((levels, lats), jnp.float32)
    per = ENTRIES // parts
    mine = lax.rem(grp_ref[0], parts) * per
    coef_lo[...] = entry[0, pl.ds(mine, per)]
    coef_hi[...] = entry[1, pl.ds(mine, per)]

    for c in copies[fields_copies:]:
        c.wait()
    lam_rows = rows_of(lam_s)
    for side, dest in enumerate((lam_lo, lam_hi)):
        for tag in range(tags):
            for c in range(EDGE):
                at = (side * 2 * tags + tag) * slab + c + (8 - EDGE) * side
                dest[tag, c] = halves(lam_rows, at, levels, 8, tags * slab)


def pack(parts, grp, lam, fields, top):
    tags, levels, cols, lats = lam.shape
    hbm = pl.BlockSpec(memory_space=pltpu.HBM)
    lam_send = pltpu.VMEM((tags, EDGE, levels, lats), jnp.float32)
    coef_send = pltpu.VMEM((ENTRIES // parts, levels, lats), jnp.float32)
    return pl.pallas_call(
        functools.partial(pack_kernel, parts),
        in_specs=[pl.BlockSpec(memory_space=pltpu.SMEM)] + [hbm] * 7,
        out_specs=[pl.BlockSpec(memory_space=pltpu.VMEM)] * 4,
        out_shape=[lam_send, lam_send, coef_send, coef_send],
        scratch_shapes=[
            pltpu.VMEM((3, 2, tags, levels, 8, LANES), jnp.float32),
            pltpu.VMEM((6, 2, 2, levels, 8, LANES), jnp.float32),
            pltpu.VMEM((2, 8, lats), jnp.int32),
            pltpu.VMEM((2, ENTRIES, levels, lats), jnp.float32),
            pltpu.SemaphoreType.DMA((26,)),
        ],
        compiler_params=pltpu.CompilerParams(vmem_limit_bytes=24 << 20),
        cost_estimate=pl.CostEstimate(flops=10**6, bytes_accessed=3 << 20, transcendentals=0),
        name="pack_edges",
    )(grp, lam, *fields, top)


def chosen(region_row, first_tag, values):
    row = jnp.zeros(region_row.shape, jnp.float32)
    for tag, value in enumerate(values):
        row = jnp.where(region_row == first_tag + tag, value[0:1], row)
    return row


def inner_kernel(grp_ref, lam, ew, ed, nw, nd, mf, top, region, out, coef, l0, l1, l2, l3, stage, rows, lam_s, field_s, sems):
    tags, levels, cols, lats = lam.shape
    first_tag = grp_ref[0] * tags
    copies = []

    def copy(src, dst):
        copies.append(pltpu.make_async_copy(src, dst, sems.at[len(copies)]))
        copies[-1].start()

    for k in range(2):
        for f, field in enumerate((ew, ed, nw, nd, mf)):
            copy(field.at[:, :, pl.ds(k * LANES, LANES)], field_s.at[f, k])
    for k in range(2):
        copy(lam.at[:, :, :, pl.ds(k * LANES, LANES)], lam_s.at[k])
    for c in copies[:10]:
        c.wait()
    field_rows = rows_of(field_s)
    lam_rows = rows_of(lam_s)
    slab = levels * cols

    def coefficients(c, west):
        ew, ed, nw, nd, mf = (
            halves(field_rows, f * 2 * slab + c, levels, cols, slab) for f in range(5)
        )
        e, next_west, n, s = faces(ew, ed, nw, nd)
        u = updraft(mf, top[pl.ds(c, 1), :])
        for j, value in enumerate((1.0 - e - west - n - s, e, west, n, s, u)):
            coef[c, j] = value
        return next_west

    def four(i, west):
        for j in range(4):
            west = coefficients(i * 4 + j, west)
        return west

    west = lax.fori_loop(0, cols // 4, four, jnp.zeros((levels, lats), jnp.float32))
    coef[cols, 2] = west
    for c in copies[10:]:
        c.wait()

    @pl.loop(0, cols // 4)
    def _(i):
        for j in range(4):
            c = i * 4 + j
            for tag in range(tags):
                l0[c, tag] = halves(lam_rows, tag * slab + c, levels, cols, tags * slab)

    stage_rows = rows_of(stage)
    store = (
        lambda c, tag, value: l1.__setitem__((c, tag), value),
        lambda c, tag, value: l2.__setitem__((c, tag), value),
        lambda c, tag, value: l3.__setitem__((c, tag), value),
        functools.partial(to_stage, stage_rows, tags, levels, cols),
    )
    sources = (l0, l1, l2, l3)
    for t in range(ITERS):
        src = sources[t]
        low, high = t + 1, cols - t - 1

        @pl.loop(0, -(-(high - low) // CHUNK))
        def _(i):
            start = jnp.minimum(low + i * CHUNK, high - CHUNK)
            for j in range(CHUNK):
                c = start + j
                coefs = [coef[c, n] for n in range(6)]
                new = [advance(coefs, src[c, k], src[c + 1, k], src[c - 1, k]) for k in range(tags)]
                for k in range(tags):
                    store[t](c, k, new[k])
                rows[t, pl.ds(c, 1), :] = chosen(region[pl.ds(c, 1), :], first_tag, new)

    inside = pl.ds(8, cols - 16)
    writes = [
        pltpu.make_async_copy(
            stage.at[k, :, :, inside],
            out.at[:, :, inside, pl.ds(k * LANES, LANES)],
            sems.at[len(copies) + k],
        )
        for k in range(2)
    ]
    for c in writes:
        c.start()
    for c in writes:
        c.wait()


def to_stage(stage_rows, tags, levels, cols, c, tag, value):
    slab = levels * cols
    for k in range(2):
        at = (k * tags + tag) * slab + c
        stage_rows[pl.ds(at, levels, stride=cols), :] = value[:, k * LANES : (k + 1) * LANES]


def inner(grp, lam, fields, top, region):
    tags, levels, cols, lats = lam.shape
    hbm = pl.BlockSpec(memory_space=pltpu.HBM)
    vmem = pl.BlockSpec(memory_space=pltpu.VMEM)
    state = pltpu.VMEM((cols, tags, levels, lats), jnp.float32)
    return pl.pallas_call(
        inner_kernel,
        in_specs=[pl.BlockSpec(memory_space=pltpu.SMEM)] + [hbm] * 6 + [vmem] * 2,
        out_specs=[hbm] + [vmem] * 7,
        out_shape=[
            pltpu.HBM(lam.shape, jnp.float32),
            pltpu.VMEM((cols + 1, 6, levels, lats), jnp.float32),
            *[state] * 4,
            pltpu.VMEM((3, tags, levels, cols, LANES), jnp.float32),
            pltpu.VMEM((ITERS, cols, lats), jnp.float32),
        ],
        scratch_shapes=[
            pltpu.VMEM((3, tags, levels, cols, LANES), jnp.float32),
            pltpu.VMEM((6, 2, levels, cols, LANES), jnp.float32),
            pltpu.SemaphoreType.DMA((14,)),
        ],
        compiler_params=pltpu.CompilerParams(vmem_limit_bytes=32 << 20),
        cost_estimate=pl.CostEstimate(flops=40 * 10**6, bytes_accessed=8 << 20, transcendentals=0),
        name="inner_steps",
    )(grp, lam, *fields, top, region)


def border_kernel(parts, grp_ref, region, coef, l0, l1, l2, l3, west, east, *refs):
    pieces = refs[:parts]
    stage_in, out_in, rows_in, stage, out, grad, entry, wide, work, rows, sems = refs[parts:]
    cols, tags, levels, lats = l0.shape
    first_tag = grp_ref[0] * tags
    per = ENTRIES // parts
    mine = lax.rem(grp_ref[0], parts)
    for by in range(parts):
        base = lax.rem(mine - by + parts, parts) * per
        for side in range(2):
            entry[side, pl.ds(base, per)] = pieces[by][side]

    def slot(c):
        return (0, c + EDGE - 1) if c < EDGE else (1, c - (cols - EDGE))

    def outside(c):
        if c < 0:
            at = 1 + 5 * (c + EDGE - 1)
            e, _, n, s, u = (entry[0, at + j] for j in range(5))
            w = entry[0, at - 4] if c > 1 - EDGE else entry[0, 0]
        else:
            at = 5 * (c - cols)
            e, _, n, s, u = (entry[1, at + j] for j in range(5))
            w = entry[1, at - 4] if c > cols else coef[cols, 2]
        return 1.0 - e - w - n - s, e, w, n, s, u

    for c in [*range(1 - EDGE, 0), *range(cols, cols + EDGE - 1)]:
        for j, value in enumerate(outside(c)):
            wide[*slot(c), j] = value
    first_west = entry[0, 1 + 5 * (EDGE - 2) + 1]
    first_mid = 1.0 - coef[0, 1] - first_west - coef[0, 3] - coef[0, 4]

    def coefs_at(c):
        if c < 0 or c >= cols:
            return [wide[*slot(c), j] for j in range(6)]
        if c == 0:
            return [first_mid, coef[0, 1], first_west, *(coef[0, j] for j in range(3, 6))]
        return [coef[c, j] for j in range(6)]

    kept = (l0, l1, l2, l3)

    def state(t, c, tag):
        if t <= c < cols - t:
            return kept[t][c, tag]
        if t == 0:
            return west[tag, c + EDGE] if c < 0 else east[tag, c - cols]
        return work[t, *slot(c), tag]

    rows[...] = rows_in[...]
    stage_rows = rows_of(stage)
    for t in range(ITERS):
        reach = EDGE - 1 - t
        for c in [*range(-reach, t + 1), *range(cols - t - 1, cols + reach)]:
            coefs = coefs_at(c)
            new = [
                advance(coefs, state(t, c, k), state(t, c + 1, k), state(t, c - 1, k))
                for k in range(tags)
            ]
            for k in range(tags):
                if t < ITERS - 1:
                    work[t + 1, *slot(c), k] = new[k]
                else:
                    to_stage(stage_rows, tags, levels, cols, c, k, new[k])
            if 0 <= c < cols:
                rows[t, c : c + 1, :] = chosen(region[c : c + 1, :], first_tag, new)
    writes = []
    for side, first in enumerate((0, cols - 8)):
        for k in range(2):
            writes.append(
                pltpu.make_async_copy(
                    stage.at[k, :, :, pl.ds(first, 8)],
                    out.at[:, :, pl.ds(first, 8), pl.ds(k * LANES, LANES)],
                    sems.at[side * 2 + k],
                )
            )
            writes[-1].start()
    total = rows[0]
    for t in range(1, ITERS):
        total = total + rows[t]
    grad[...] = total
    for c in writes:
        c.wait()


def border(parts, grp, region, coef, states, west, east, pieces, stage, out, rows):
    cols, tags, levels, lats = states[0].shape
    hbm = pl.BlockSpec(memory_space=pltpu.HBM)
    vmem = pl.BlockSpec(memory_space=pltpu.VMEM)
    operands = [region, coef, *states, west, east, *pieces, stage]
    n = len(operands)
    return pl.pallas_call(
        functools.partial(border_kernel, parts),
        in_specs=[pl.BlockSpec(memory_space=pltpu.SMEM)] + [vmem] * n + [hbm, vmem],
        out_specs=[vmem, hbm, vmem],
        out_shape=[
            pltpu.VMEM(stage.shape, jnp.float32),
            pltpu.HBM(out.shape, jnp.float32),
            pltpu.VMEM((cols, lats), jnp.float32),
        ],
        input_output_aliases={n: 0, n + 1: 1},
        scratch_shapes=[
            pltpu.VMEM((2, ENTRIES, levels, lats), jnp.float32),
            pltpu.VMEM((2, 2 * EDGE - 1, 6, levels, lats), jnp.float32),
            pltpu.VMEM((ITERS, 2, 2 * EDGE - 1, tags, levels, lats), jnp.float32),
            pltpu.VMEM((ITERS, cols, lats), jnp.float32),
            pltpu.SemaphoreType.DMA((4,)),
        ],
        compiler_params=pltpu.CompilerParams(vmem_limit_bytes=32 << 20),
        cost_estimate=pl.CostEstimate(flops=10 * 10**6, bytes_accessed=2 << 20, transcendentals=0),
        name="border_steps",
    )(grp, *operands, out, rows)


def local(lam, east_wind, north_wind, east_diff, north_diff, mass_flux, region, top):
    groups = lax.axis_size("grp")
    parts = 4 if groups % 4 == 0 else 1
    grp = lax.axis_index("grp").astype(jnp.int32).reshape(1)
    lam, *fields = (
        pltpu.with_memory_space_constraint(value, pltpu.HBM)
        for value in (lam, east_wind, east_diff, north_wind, north_diff, mass_flux)
    )
    far_top = pltpu.with_memory_space_constraint(top, pltpu.HBM)
    lam_lo, lam_hi, coef_lo, coef_hi = pack(parts, grp, lam, fields, far_top)
    coef_west = shifted(coef_hi, "dom", 1)
    coef_east = shifted(coef_lo, "dom", -1)
    west = shifted(lam_hi, "dom", 1)
    east = shifted(lam_lo, "dom", -1)
    out, coef, *states, stage, rows = inner(grp, lam, fields, top, region)
    coef_west, coef_east, rows = lax.optimization_barrier((coef_west, coef_east, rows))
    mine = jnp.stack([coef_west, coef_east])
    pieces = [mine] + [shifted_in_blocks(mine, "grp", parts, by) for by in range(1, parts)]
    _, final, grad = border(
        parts, grp, region, coef, states, west, east, pieces, stage, out, rows
    )
    share = grad
    for by in range(1, groups):
        grad = grad + shifted(share, "grp", by)
    return final, grad


def solution(mesh):
    return jax.shard_map(
        local,
        mesh=mesh,
        in_specs=(
            P("grp", None, "dom", None),
            P(None, "dom", None),
            P(None, "dom", None),
            P(None, "dom", None),
            P(None, "dom", None),
            P(None, "dom", None),
            P("dom", None),
            P("dom", None),
        ),
        out_specs=(P("grp", None, "dom", None), P("dom", None)),
        check_vma=False,
    )
```

time: 78.9 us -> 44.2 us (0.56)
  local copies, waits for them, and re-layouts: 19.3 us -> 0.01 us
  Pallas kernels: 0 us -> 18.7 us
  other arithmetic: 16.4 us -> 0.64 us
  blocking collectives: 10.9 us -> 0 us
  waiting for transfers between devices: 15.8 us -> 10.4 us
  starting transfers between devices: 15 us -> 13.6 us
    pallas_call x0 -> x3, Pallas kernels: none -> 18.7 us  [the longest x1 13.7 us: inner(): pl.pallas_call(inner_kernel, in_specs=[pl.BlockSpec(memory_space=pltpu.SM...]
    psum x1 -> x0, blocking collectives: 10.9 us -> none  [local(): flux_gradient = lax.psum(local_grad, 'grp')]
    slice x23 -> x0, local copies, waits for them, and re-layouts: 10.4 us -> none  [the longest x8 7.72 us: local(): south = jnp.concatenate([center[..., :1], center[..., :-1]], axis=-1)]
    add x9 -> x1, other arithmetic: 10.5 us -> 0.63 us  [local(): grad = grad + shifted(share, 'grp', by)]
    unnamed x20 -> x4, local copies, waits for them, and re-layouts: 8.83 us -> 0.01 us
    ppermute x9 -> x10, waiting for transfers between devices: 15.8 us -> 10.4 us  [the longest x3 6.83 us: shifted_in_blocks(): lax.ppermute(value, axis, [(i, i - i % block + (i + by) % block) for i in...]
    another operation x2 -> x1, other arithmetic: 3.05 us -> 0.01 us  [local(): mine = jnp.stack([coef_west, coef_east])]
    concatenate x1 -> x0, other arithmetic: 2.2 us -> none  [local(): jnp.concatenate([lower_rim, stacked, jnp.zeros_like(lower_rim)], axis=2)]
  transfers between devices with their start and end apart: 9 -> 10, of which waited for: 6 -> 4; matrix products, arithmetic and copies ran while one was open for 23% -> 0% of each run, Pallas kernels for 0% -> 31%
where the time goes in v2:
time: 44.2 us; the launch traced here: 44.1 us
  Pallas kernels  18.7 us (42%)
  starting transfers between devices  13.6 us (31%)
  waiting for transfers between devices  10.4 us (24%)
  between operations  0.72 us (2%)
  other arithmetic  0.64 us (1%)
    pallas_call x1, Pallas kernels, inner(): pl.pallas_call(inner_kernel, in_specs=[pl.BlockSpec(memory_space=pltpu.SM...  13.7 us
    ppermute x7, starting transfers between devices, shifted(): lax.ppermute(value, axis, [(i, (i + by) % size) for i in range(size)])  11.7 us
    ppermute x3, waiting for transfers between devices, shifted_in_blocks(): lax.ppermute(value, axis, [(i, i - i % block + (i + by) % block) for i in...  6.83 us
    ppermute x7, waiting for transfers between devices, shifted(): lax.ppermute(value, axis, [(i, (i + by) % size) for i in range(size)])  3.54 us
    pallas_call x1, Pallas kernels, border(): pl.pallas_call(functools.partial(border_kernel, parts), in_specs=[pl.Bloc...  2.91 us
    pallas_call x1, Pallas kernels, pack(): pl.pallas_call(functools.partial(pack_kernel, parts), in_specs=[pl.BlockS...  2.08 us
    ppermute x3, starting transfers between devices, shifted_in_blocks(): lax.ppermute(value, axis, [(i, i - i % block + (i + by) % block) for i in...  1.94 us
  transfers between devices with their start and end apart: 10, of which 4 were waited for; matrix products, arithmetic and copies ran while one was open for 0% of the time, Pallas kernels for 31%

profile of v2, /device:TPU:0, one launch (start us, length us, event | category | flops | bytes accessed | tf_op | source)
XLA Modules:
  0.0 44.1 jit_solution(17864546389377481376)
XLA Ops:
  0.7 2.1 %pack_edges.1 = (f32[4,4,16,256]{3,2,1,0:T(8,128)S(1)}, f32[4,4,16,256]{3,2,1,0:T(8,128)S(1)}, f32[4,16,256]{2,1,0:T(8,128)S(1)}, f32[4,16,256]{2,1,0:T(8,128)S(1)}) custom-call(s32[1]{0:T(128)} %bitcast.grp_ref, f32[4,16,32,256]{3,2,1,0:T(8,128)} %lam.3, f32[16,32,256]{2,1,0:T(8,128)} %ew.3, f32[16,32,256]{2,1,0:T(8,128)} %ed.3, f32[16,32,256]{2,1,0:T(8,128)} %nw.3, ...), custom_call_target="tpu_custom_call" | custom-call | flops 1000000 | bytes 3145728 | tf_op jit(solution)/shard_map/pack_edges/pallas_call | solution.py:127
  2.7 3.0 %collective-permute-start.2 = (f32[4,16,256]{2,1,0:T(8,128)S(1)}, f32[4,16,256]{2,1,0:T(8,128)S(1)}, u32[]{:S(2)}, u32[]{:S(2)}) collective-permute-start(f32[4,16,256]{2,1,0:T(8,128)S(1)} %get-tuple-element.26), channel_id=1, source_target_pairs={{0,4},{4,8},{8,12},{12,16},{16,20},{20,24},{24,28},{28,0},{1,5},{5... | collective-permute-start | bytes 196616 | tf_op jit(solution)/shard_map/ppermute | solution.py:19
  5.7 3.1 %collective-permute-start.3 = (f32[4,16,256]{2,1,0:T(8,128)S(1)}, f32[4,16,256]{2,1,0:T(8,128)S(1)}, u32[]{:S(2)}, u32[]{:S(2)}) collective-permute-start(f32[4,16,256]{2,1,0:T(8,128)S(1)} %get-tuple-element.27), channel_id=1, source_target_pairs={{0,28},{4,0},{8,4},{12,8},{16,12},{20,16},{24,20},{28,24},{1,29},{... | collective-permute-start | bytes 196616 | tf_op jit(solution)/shard_map/ppermute | solution.py:19
  8.8 0.0 collective-permute-start
  8.8 4.7 %collective-permute-start.1 = (f32[4,4,16,256]{3,2,1,0:T(8,128)S(1)}, f32[4,4,16,256]{3,2,1,0:T(8,128)S(1)}, u32[]{:S(2)}, u32[]{:S(2)}) collective-permute-start(f32[4,4,16,256]{3,2,1,0:T(8,128)S(1)} %get-tuple-element.25), channel_id=1, source_target_pairs={{0,28},{4,0},{8,4},{12,8},{16,12},{20,16},{24,20},{28,24},{1,29},{... | collective-permute-start | bytes 786440 | tf_op jit(solution)/shard_map/ppermute | solution.py:19
  13.6 13.7 %inner_steps.1 = (f32[4,16,32,256]{3,2,1,0:T(8,128)}, f32[33,6,16,256]{3,2,1,0:T(8,128)S(1)}, f32[32,4,16,256]{3,2,1,0:T(8,128)S(1)}, f32[32,4,16,256]{3,2,1,0:T...) custom-call(s32[1]{0:T(128)} %bitcast.grp_ref, ...), custom_call_target="tpu_custom_call" | custom-call | flops 40000000 | bytes 8388608 | tf_op jit(solution)/shard_map/inner_steps/pallas_call | solution.py:249
  27.3 0.0 collective-permute-done.2
  27.3 0.0 collective-permute-done.3
  27.3 0.2 collective-permute-start.6
  27.5 1.6 %collective-permute-start.5 = (f32[2,4,16,256]{3,2,1,0:T(8,128)S(1)}, f32[2,4,16,256]{3,2,1,0:T(8,128)S(1)}, u32[]{:S(2)}, u32[]{:S(2)}) collective-permute-start(f32[2,4,16,256]{3,2,1,0:T(8,128)S(1)} %pad_maximum_fusion.refs_0_), channel_id=1, source_target_pairs={{0,2},{1,3},{2,0},{3,1},{4,6},{5,7},{6,4},{7,5},{8,10},{9,11},{10,... | collective-permute-start | bytes 393224 | tf_op jit(solution)/shard_map/ppermute | solution.py:24
  29.1 0.2 collective-permute-start.4
  29.3 1.0 %collective-permute-done.6.refs_3_ = f32[2,4,16,256]{3,2,1,0:T(8,128)S(1)} collective-permute-done((f32[2,4,16,256]{3,2,1,0:T(8,128)S(1)}, f32[2,4,16,256]{3,2,1,0:T(8,128)S(1)}, u32[]{:S(2)}, u32[]{:S(2)}) %collective-permute-start.6) | collective-permute-done | bytes 131104 | tf_op jit(solution)/shard_map/ppermute | solution.py:24
  30.3 5.8 %collective-permute-done.5.refs_2_ = f32[2,4,16,256]{3,2,1,0:T(8,128)S(1)} collective-permute-done((f32[2,4,16,256]{3,2,1,0:T(8,128)S(1)}, f32[2,4,16,256]{3,2,1,0:T(8,128)S(1)}, u32[]{:S(2)}, u32[]{:S(2)}) %collective-permute-start.5) | collective-permute-done | bytes 131104 | tf_op jit(solution)/shard_map/ppermute | solution.py:24
  36.1 0.0 collective-permute-done.4.refs_1_
  36.1 0.0 collective-permute-done.west
  36.1 0.0 collective-permute-done.1.east
  36.1 2.9 %border_steps.1 = (f32[3,4,16,32,128]{4,3,2,1,0:T(8,128)S(1)}, f32[4,16,32,256]{3,2,1,0:T(8,128)}, f32[32,256]{1,0:T(8,128)S(1)}) custom-call(s32[1]{0:T(128)} %bitcast.grp_ref, s32[32,256]{1,0:T(8,128)S(1)} %copy-done.1, f32[33,6,16,256]{3,2,1,0:T(8,128)S(1)} %get-tuple-element.19.coef, ...), custom_call_target="tpu_custom_call", output_to_operand_aliasing={{0}: (13, {}), {1}: (14, {})} | custom-call | flops 10000000 | bytes 2097152 | tf_op jit(solution)/shard_map/border_steps/pallas_call | solution.py:361
  39.0 0.1 collective-permute-start.9
  39.1 0.6 %collective-permute-start.8 = (f32[32,256]{1,0:T(8,128)S(1)}, f32[32,256]{1,0:T(8,128)S(1)}, u32[]{:S(2)}, u32[]{:S(2)}) collective-permute-start(f32[32,256]{1,0:T(8,128)S(1)} %get-tuple-element.35), channel_id=1, source_target_pairs={{0,2},{1,3},{2,0},{3,1},{4,6},{5,7},{6,4},{7,5},{8,10},{9,11},{10,... | collective-permute-start | bytes 98312 | tf_op jit(solution)/shard_map/ppermute | solution.py:19
  39.7 0.2 collective-permute-start.7
  39.9 0.9 %collective-permute-done.9 = f32[32,256]{1,0:T(8,128)S(1)} collective-permute-done((f32[32,256]{1,0:T(8,128)S(1)}, f32[32,256]{1,0:T(8,128)S(1)}, u32[]{:S(2)}, u32[]{:S(2)}) %collective-permute-start.9) | collective-permute-done | bytes 32800 | tf_op jit(solution)/shard_map/ppermute | solution.py:19
  40.8 2.7 %collective-permute-done.8 = f32[32,256]{1,0:T(8,128)S(1)} collective-permute-done((f32[32,256]{1,0:T(8,128)S(1)}, f32[32,256]{1,0:T(8,128)S(1)}, u32[]{:S(2)}, u32[]{:S(2)}) %collective-permute-start.8) | collective-permute-done | bytes 32800 | tf_op jit(solution)/shard_map/ppermute | solution.py:19
  43.4 0.0 collective-permute-done.7
  43.4 0.6 %add_add_fusion = f32[32,256]{1,0:T(8,128)} fusion(f32[32,256]{1,0:T(8,128)S(1)} %collective-permute-done.9, f32[32,256]{1,0:T(8,128)S(1)} %collective-permute-done.8, f32[32,256]{1,0:T(8,128)S(1)} %get-tuple-element.35, f32[32,256]{1,0:T(8,128)S(1)} %collective-permute-done.7), kind=kLoop, calls=%fused_computation.1 | loop fusion | flops 24576 | bytes 163840 | tf_op jit(solution)/shard_map/add | solution.py:407
  (5 shorter events, 0.0 us)
Async XLA Ops:
  0.6 12.9 %copy-start = (s32[32,256]{1,0:T(8,128)S(1)}, s32[32,256]{1,0:T(8,128)}, u32[]{:S(2)}) copy-start(s32[32,256]{1,0:T(8,128)} %top.3) | copy-start | bytes 98308
  0.6 12.9 %copy-start.1 = (s32[32,256]{1,0:T(8,128)S(1)}, s32[32,256]{1,0:T(8,128)}, u32[]{:S(2)}) copy-start(s32[32,256]{1,0:T(8,128)} %region.3) | copy-start | bytes 98308
  2.7 24.6 %collective-permute-start.2 = (f32[4,16,256]{2,1,0:T(8,128)S(1)}, f32[4,16,256]{2,1,0:T(8,128)S(1)}, u32[]{:S(2)}, u32[]{:S(2)}) collective-permute-start(f32[4,16,256]{2,1,0:T(8,128)S(1)} %get-tuple-element.26), channel_id=1, source_target_pairs={{0,4},{4,8},{8,12},{12,16},{16,20},{20,24},{24,28},{28,0},{1,5},{5... | collective-permute-start | bytes 196616 | tf_op jit(solution)/shard_map/ppermute | solution.py:19
  5.7 21.6 %collective-permute-start.3 = (f32[4,16,256]{2,1,0:T(8,128)S(1)}, f32[4,16,256]{2,1,0:T(8,128)S(1)}, u32[]{:S(2)}, u32[]{:S(2)}) collective-permute-start(f32[4,16,256]{2,1,0:T(8,128)S(1)} %get-tuple-element.27), channel_id=1, source_target_pairs={{0,28},{4,0},{8,4},{12,8},{16,12},{20,16},{24,20},{28,24},{1,29},{... | collective-permute-start | bytes 196616 | tf_op jit(solution)/shard_map/ppermute | solution.py:19
  8.8 27.3 %collective-permute-start = (f32[4,4,16,256]{3,2,1,0:T(8,128)S(1)}, f32[4,4,16,256]{3,2,1,0:T(8,128)S(1)}, u32[]{:S(2)}, u32[]{:S(2)}) collective-permute-start(f32[4,4,16,256]{3,2,1,0:T(8,128)S(1)} %get-tuple-element.24), channel_id=1, source_target_pairs={{0,4},{4,8},{8,12},{12,16},{16,20},{20,24},{24,28},{28,0},{1,5},{5... | collective-permute-start | bytes 786440 | tf_op jit(solution)/shard_map/ppermute | solution.py:19
  8.8 27.3 %collective-permute-start.1 = (f32[4,4,16,256]{3,2,1,0:T(8,128)S(1)}, f32[4,4,16,256]{3,2,1,0:T(8,128)S(1)}, u32[]{:S(2)}, u32[]{:S(2)}) collective-permute-start(f32[4,4,16,256]{3,2,1,0:T(8,128)S(1)} %get-tuple-element.25), channel_id=1, source_target_pairs={{0,28},{4,0},{8,4},{12,8},{16,12},{20,16},{24,20},{28,24},{1,29},{... | collective-permute-start | bytes 786440 | tf_op jit(solution)/shard_map/ppermute | solution.py:19
  27.3 3.0 %collective-permute-start.6 = (f32[2,4,16,256]{3,2,1,0:T(8,128)S(1)}, f32[2,4,16,256]{3,2,1,0:T(8,128)S(1)}, u32[]{:S(2)}, u32[]{:S(2)}) collective-permute-start(f32[2,4,16,256]{3,2,1,0:T(8,128)S(1)} %pad_maximum_fusion.refs_0_), channel_id=1, source_target_pairs={{0,3},{1,0},{2,1},{3,2},{4,7},{5,4},{6,5},{7,6},{8,11},{9,8},{10,9... | collective-permute-start | bytes 393224 | tf_op jit(solution)/shard_map/ppermute | solution.py:24
  27.5 8.6 %collective-permute-start.5 = (f32[2,4,16,256]{3,2,1,0:T(8,128)S(1)}, f32[2,4,16,256]{3,2,1,0:T(8,128)S(1)}, u32[]{:S(2)}, u32[]{:S(2)}) collective-permute-start(f32[2,4,16,256]{3,2,1,0:T(8,128)S(1)} %pad_maximum_fusion.refs_0_), channel_id=1, source_target_pairs={{0,2},{1,3},{2,0},{3,1},{4,6},{5,7},{6,4},{7,5},{8,10},{9,11},{10,... | collective-permute-start | bytes 393224 | tf_op jit(solution)/shard_map/ppermute | solution.py:24
  29.1 7.0 %collective-permute-start.4 = (f32[2,4,16,256]{3,2,1,0:T(8,128)S(1)}, f32[2,4,16,256]{3,2,1,0:T(8,128)S(1)}, u32[]{:S(2)}, u32[]{:S(2)}) collective-permute-start(f32[2,4,16,256]{3,2,1,0:T(8,128)S(1)} %pad_maximum_fusion.refs_0_), channel_id=1, source_target_pairs={{0,1},{1,2},{2,3},{3,0},{4,5},{5,6},{6,7},{7,4},{8,9},{9,10},{10,1... | collective-permute-start | bytes 393224 | tf_op jit(solution)/shard_map/ppermute | solution.py:24
  39.0 1.7 %collective-permute-start.9 = (f32[32,256]{1,0:T(8,128)S(1)}, f32[32,256]{1,0:T(8,128)S(1)}, u32[]{:S(2)}, u32[]{:S(2)}) collective-permute-start(f32[32,256]{1,0:T(8,128)S(1)} %get-tuple-element.35), channel_id=1, source_target_pairs={{0,3},{1,0},{2,1},{3,2},{4,7},{5,4},{6,5},{7,6},{8,11},{9,8},{10,9... | collective-permute-start | bytes 98312 | tf_op jit(solution)/shard_map/ppermute | solution.py:19
  39.1 4.3 %collective-permute-start.8 = (f32[32,256]{1,0:T(8,128)S(1)}, f32[32,256]{1,0:T(8,128)S(1)}, u32[]{:S(2)}, u32[]{:S(2)}) collective-permute-start(f32[32,256]{1,0:T(8,128)S(1)} %get-tuple-element.35), channel_id=1, source_target_pairs={{0,2},{1,3},{2,0},{3,1},{4,6},{5,7},{6,4},{7,5},{8,10},{9,11},{10,... | collective-permute-start | bytes 98312 | tf_op jit(solution)/shard_map/ppermute | solution.py:19
  39.7 3.7 %collective-permute-start.7 = (f32[32,256]{1,0:T(8,128)S(1)}, f32[32,256]{1,0:T(8,128)S(1)}, u32[]{:S(2)}, u32[]{:S(2)}) collective-permute-start(f32[32,256]{1,0:T(8,128)S(1)} %get-tuple-element.35), channel_id=1, source_target_pairs={{0,1},{1,2},{2,3},{3,0},{4,5},{5,6},{6,7},{7,4},{8,9},{9,10},{10,1... | collective-permute-start | bytes 98312 | tf_op jit(solution)/shard_map/ppermute | solution.py:19

commit v3 on v2

--- a/solution.py
+++ b/solution.py
@@ -19,11 +19,8 @@
     return lax.ppermute(value, axis, [(i, (i + by) % size) for i in range(size)])
 
 
-def shifted_in_blocks(value, axis, block, by):
-    size = lax.axis_size(axis)
-    return lax.ppermute(
-        value, axis, [(i, i - i % block + (i + by) % block) for i in range(size)]
-    )
+def swapped(value, axis, bit):
+    return lax.ppermute(value, axis, [(i, i ^ bit) for i in range(lax.axis_size(axis))])
 
 
 def faces(ew, ed, nw, nd):
@@ -51,11 +48,8 @@
     return h + u * (pltpu.roll(h, levels - 1, 0) - h)
 
 
-def rows_of(ref):
-    size = 1
-    for n in ref.shape[:-1]:
-        size *= n
-    return ref.reshape(size, ref.shape[-1])
+def pitched(slabs, levels, width):
+    return -(-(slabs * levels * (width + 1) + width + 8) // 8) * 8
 
 
 def halves(ref, start, levels, stride, apart):
@@ -63,7 +57,7 @@
     return jnp.concatenate(parts, axis=1)
 
 
-def pack_kernel(parts, grp_ref, lam, ew, ed, nw, nd, mf, top, lam_lo, lam_hi, coef_lo, coef_hi, lam_s, field_s, top_s, entry, sems):
+def pack_kernel(parts, grp_ref, lam, ew, ed, nw, nd, mf, top, lam_lo, lam_hi, coef_lo, coef_hi, lam_s, field_s, top_s, entry, lam_p, field_p, sems):
     tags, levels, cols, lats = lam.shape
     copies = []
 
@@ -85,11 +79,19 @@
     for c in copies[:fields_copies]:
         c.wait()
 
-    field_rows = rows_of(field_s)
-    slab = levels * 8
+    pitch = 9
+    slab = levels * pitch
+
+    @pl.loop(0, levels)
+    def _(level):
+        for f in range(5):
+            for side in range(2):
+                for k in range(2):
+                    at = ((f * 2 + side) * 2 + k) * slab
+                    field_p[pl.ds(at + level * pitch, 8), :] = field_s[f, side, k, level]
 
     def field(f, side, c):
-        return halves(field_rows, (f * 2 + side) * 2 * slab + c, levels, 8, slab)
+        return halves(field_p, (f * 2 + side) * 2 * slab + c, levels, pitch, slab)
 
     for side in range(2):
         slot = 0
@@ -111,12 +113,20 @@
 
     for c in copies[fields_copies:]:
         c.wait()
-    lam_rows = rows_of(lam_s)
+
+    @pl.loop(0, levels)
+    def _(level):
+        for side in range(2):
+            for k in range(2):
+                for tag in range(tags):
+                    at = ((side * 2 + k) * tags + tag) * slab
+                    lam_p[pl.ds(at + level * pitch, 8), :] = lam_s[side, k, tag, level]
+
     for side, dest in enumerate((lam_lo, lam_hi)):
         for tag in range(tags):
             for c in range(EDGE):
                 at = (side * 2 * tags + tag) * slab + c + (8 - EDGE) * side
-                dest[tag, c] = halves(lam_rows, at, levels, 8, tags * slab)
+                dest[tag, c] = halves(lam_p, at, levels, pitch, tags * slab)
 
 
 def pack(parts, grp, lam, fields, top):
@@ -130,10 +140,12 @@
         out_specs=[pl.BlockSpec(memory_space=pltpu.VMEM)] * 4,
         out_shape=[lam_send, lam_send, coef_send, coef_send],
         scratch_shapes=[
-            pltpu.VMEM((3, 2, tags, levels, 8, LANES), jnp.float32),
-            pltpu.VMEM((6, 2, 2, levels, 8, LANES), jnp.float32),
+            pltpu.VMEM((2, 2, tags, levels, 8, LANES), jnp.float32),
+            pltpu.VMEM((5, 2, 2, levels, 8, LANES), jnp.float32),
             pltpu.VMEM((2, 8, lats), jnp.int32),
             pltpu.VMEM((2, ENTRIES, levels, lats), jnp.float32),
+            pltpu.VMEM((pitched(4 * tags, levels, 8), LANES), jnp.float32),
+            pltpu.VMEM((pitched(20, levels, 8), LANES), jnp.float32),
             pltpu.SemaphoreType.DMA((26,)),
         ],
         compiler_params=pltpu.CompilerParams(vmem_limit_bytes=24 << 20),
@@ -149,7 +161,7 @@
     return row
 
 
-def inner_kernel(grp_ref, lam, ew, ed, nw, nd, mf, top, region, out, coef, l0, l1, l2, l3, stage, rows, lam_s, field_s, sems):
+def inner_kernel(grp_ref, lam, ew, ed, nw, nd, mf, top, region, out, coef, l0, l1, l2, l3, stage, rows, lam_s, field_s, lam_p, field_p, inside, sems):
     tags, levels, cols, lats = lam.shape
     first_tag = grp_ref[0] * tags
     copies = []
@@ -165,13 +177,18 @@
         copy(lam.at[:, :, :, pl.ds(k * LANES, LANES)], lam_s.at[k])
     for c in copies[:10]:
         c.wait()
-    field_rows = rows_of(field_s)
-    lam_rows = rows_of(lam_s)
-    slab = levels * cols
+    pitch = cols + 1
+    slab = levels * pitch
+
+    @pl.loop(0, levels)
+    def _(level):
+        for f in range(5):
+            for k in range(2):
+                field_p[pl.ds((f * 2 + k) * slab + level * pitch, cols), :] = field_s[f, k, level]
 
     def coefficients(c, west):
         ew, ed, nw, nd, mf = (
-            halves(field_rows, f * 2 * slab + c, levels, cols, slab) for f in range(5)
+            halves(field_p, f * 2 * slab + c, levels, pitch, slab) for f in range(5)
         )
         e, next_west, n, s = faces(ew, ed, nw, nd)
         u = updraft(mf, top[pl.ds(c, 1), :])
@@ -189,19 +206,24 @@
     for c in copies[10:]:
         c.wait()
 
+    @pl.loop(0, levels)
+    def _(level):
+        for k in range(2):
+            for tag in range(tags):
+                lam_p[pl.ds((k * tags + tag) * slab + level * pitch, cols), :] = lam_s[k, tag, level]
+
     @pl.loop(0, cols // 4)
     def _(i):
         for j in range(4):
             c = i * 4 + j
             for tag in range(tags):
-                l0[c, tag] = halves(lam_rows, tag * slab + c, levels, cols, tags * slab)
-
-    stage_rows = rows_of(stage)
+                l0[c, tag] = halves(lam_p, tag * slab + c, levels, pitch, tags * slab)
+
     store = (
         lambda c, tag, value: l1.__setitem__((c, tag), value),
         lambda c, tag, value: l2.__setitem__((c, tag), value),
         lambda c, tag, value: l3.__setitem__((c, tag), value),
-        functools.partial(to_stage, stage_rows, tags, levels, cols),
+        functools.partial(to_stage, stage, tags, levels, pitch),
     )
     sources = (l0, l1, l2, l3)
     for t in range(ITERS):
@@ -219,11 +241,17 @@
                     store[t](c, k, new[k])
                 rows[t, pl.ds(c, 1), :] = chosen(region[pl.ds(c, 1), :], first_tag, new)
 
-    inside = pl.ds(8, cols - 16)
+    @pl.loop(0, levels)
+    def _(level):
+        for k in range(2):
+            for tag in range(tags):
+                at = (k * tags + tag) * slab + level * pitch + 8
+                inside[k, tag, level] = stage[pl.ds(at, cols - 16), :]
+
     writes = [
         pltpu.make_async_copy(
-            stage.at[k, :, :, inside],
-            out.at[:, :, inside, pl.ds(k * LANES, LANES)],
+            inside.at[k],
+            out.at[:, :, pl.ds(8, cols - 16), pl.ds(k * LANES, LANES)],
             sems.at[len(copies) + k],
         )
         for k in range(2)
@@ -234,11 +262,10 @@
         c.wait()
 
 
-def to_stage(stage_rows, tags, levels, cols, c, tag, value):
-    slab = levels * cols
+def to_stage(stage, tags, levels, pitch, c, tag, value):
     for k in range(2):
-        at = (k * tags + tag) * slab + c
-        stage_rows[pl.ds(at, levels, stride=cols), :] = value[:, k * LANES : (k + 1) * LANES]
+        at = (k * tags + tag) * levels * pitch + c
+        stage[pl.ds(at, levels, stride=pitch), :] = value[:, k * LANES : (k + 1) * LANES]
 
 
 def inner(grp, lam, fields, top, region):
@@ -254,12 +281,15 @@
             pltpu.HBM(lam.shape, jnp.float32),
             pltpu.VMEM((cols + 1, 6, levels, lats), jnp.float32),
             *[state] * 4,
-            pltpu.VMEM((3, tags, levels, cols, LANES), jnp.float32),
+            pltpu.VMEM((pitched(2 * tags, levels, cols), LANES), jnp.float32),
             pltpu.VMEM((ITERS, cols, lats), jnp.float32),
         ],
         scratch_shapes=[
-            pltpu.VMEM((3, tags, levels, cols, LANES), jnp.float32),
-            pltpu.VMEM((6, 2, levels, cols, LANES), jnp.float32),
+            pltpu.VMEM((2, tags, levels, cols, LANES), jnp.float32),
+            pltpu.VMEM((5, 2, levels, cols, LANES), jnp.float32),
+            pltpu.VMEM((pitched(2 * tags, levels, cols), LANES), jnp.float32),
+            pltpu.VMEM((pitched(10, levels, cols), LANES), jnp.float32),
+            pltpu.VMEM((2, tags, levels, cols - 16, LANES), jnp.float32),
             pltpu.SemaphoreType.DMA((14,)),
         ],
         compiler_params=pltpu.CompilerParams(vmem_limit_bytes=32 << 20),
@@ -270,13 +300,13 @@
 
 def border_kernel(parts, grp_ref, region, coef, l0, l1, l2, l3, west, east, *refs):
     pieces = refs[:parts]
-    stage_in, out_in, rows_in, stage, out, grad, entry, wide, work, rows, sems = refs[parts:]
+    stage_in, out_in, rows_in, stage, out, grad, entry, wide, work, rows, sides, sems = refs[parts:]
     cols, tags, levels, lats = l0.shape
     first_tag = grp_ref[0] * tags
     per = ENTRIES // parts
     mine = lax.rem(grp_ref[0], parts)
     for by in range(parts):
-        base = lax.rem(mine - by + parts, parts) * per
+        base = (mine ^ by) * per
         for side in range(2):
             entry[side, pl.ds(base, per)] = pieces[by][side]
 
@@ -317,7 +347,7 @@
         return work[t, *slot(c), tag]
 
     rows[...] = rows_in[...]
-    stage_rows = rows_of(stage)
+    pitch = cols + 1
     for t in range(ITERS):
         reach = EDGE - 1 - t
         for c in [*range(-reach, t + 1), *range(cols - t - 1, cols + reach)]:
@@ -330,15 +360,24 @@
                 if t < ITERS - 1:
                     work[t + 1, *slot(c), k] = new[k]
                 else:
-                    to_stage(stage_rows, tags, levels, cols, c, k, new[k])
+                    to_stage(stage, tags, levels, pitch, c, k, new[k])
             if 0 <= c < cols:
                 rows[t, c : c + 1, :] = chosen(region[c : c + 1, :], first_tag, new)
+
+    @pl.loop(0, levels)
+    def _(level):
+        for side, first in enumerate((0, cols - 8)):
+            for k in range(2):
+                for tag in range(tags):
+                    at = ((k * tags + tag) * levels + level) * pitch + first
+                    sides[side, k, tag, level] = stage[pl.ds(at, 8), :]
+
     writes = []
     for side, first in enumerate((0, cols - 8)):
         for k in range(2):
             writes.append(
                 pltpu.make_async_copy(
-                    stage.at[k, :, :, pl.ds(first, 8)],
+                    sides.at[side, k],
                     out.at[:, :, pl.ds(first, 8), pl.ds(k * LANES, LANES)],
                     sems.at[side * 2 + k],
                 )
@@ -373,6 +412,7 @@
             pltpu.VMEM((2, 2 * EDGE - 1, 6, levels, lats), jnp.float32),
             pltpu.VMEM((ITERS, 2, 2 * EDGE - 1, tags, levels, lats), jnp.float32),
             pltpu.VMEM((ITERS, cols, lats), jnp.float32),
+            pltpu.VMEM((2, 2, tags, levels, 8, LANES), jnp.float32),
             pltpu.SemaphoreType.DMA((4,)),
         ],
         compiler_params=pltpu.CompilerParams(vmem_limit_bytes=32 << 20),
@@ -392,13 +432,16 @@
     far_top = pltpu.with_memory_space_constraint(top, pltpu.HBM)
     lam_lo, lam_hi, coef_lo, coef_hi = pack(parts, grp, lam, fields, far_top)
     coef_west = shifted(coef_hi, "dom", 1)
+    west = shifted(lam_hi, "dom", 1)
     coef_east = shifted(coef_lo, "dom", -1)
-    west = shifted(lam_hi, "dom", 1)
     east = shifted(lam_lo, "dom", -1)
     out, coef, *states, stage, rows = inner(grp, lam, fields, top, region)
     coef_west, coef_east, rows = lax.optimization_barrier((coef_west, coef_east, rows))
     mine = jnp.stack([coef_west, coef_east])
-    pieces = [mine] + [shifted_in_blocks(mine, "grp", parts, by) for by in range(1, parts)]
+    pieces = [mine]
+    if parts == 4:
+        across = swapped(mine, "grp", 2)
+        pieces += [swapped(mine, "grp", 1), across, swapped(across, "grp", 1)]
     _, final, grad = border(
         parts, grp, region, coef, states, west, east, pieces, stage, out, rows
     )

time: 44.2 us -> 39.1 us (0.88)
  Pallas kernels: 18.7 us -> 14.9 us
  waiting for transfers between devices: 10.4 us -> 8.27 us
  starting transfers between devices: 13.6 us -> 14.5 us
    pallas_call x1, Pallas kernels: 13.7 us -> 10.1 us  [inner(): pl.pallas_call(inner_kernel, in_specs=[pl.BlockSpec(memory_space=pltpu.SM...]
    ppermute x3, waiting for transfers between devices: 6.83 us -> 4.64 us  [swapped(): lax.ppermute(value, axis, [(i, i ^ bit) for i in range(lax.axis_size(axis...]
    ppermute x7, starting transfers between devices: 11.7 us -> 12.7 us  [shifted(): lax.ppermute(value, axis, [(i, (i + by) % size) for i in range(size)])]
  transfers between devices with their start and end apart: 10 -> 10, of which waited for: 4 -> 4; matrix products, arithmetic and copies ran while one was open for 0% -> 0% of each run, Pallas kernels for 31% -> 26%
where the time goes in v3:
time: 39.1 us; the launch traced here: 39 us
  Pallas kernels  14.9 us (38%)
  starting transfers between devices  14.5 us (37%)
  waiting for transfers between devices  8.27 us (21%)
  between operations  0.72 us (2%)
  other arithmetic  0.64 us (2%)
    ppermute x7, starting transfers between devices, shifted(): lax.ppermute(value, axis, [(i, (i + by) % size) for i in range(size)])  12.7 us
    pallas_call x1, Pallas kernels, inner(): pl.pallas_call(inner_kernel, in_specs=[pl.BlockSpec(memory_space=pltpu.SM...  10.1 us
    ppermute x3, waiting for transfers between devices, swapped(): lax.ppermute(value, axis, [(i, i ^ bit) for i in range(lax.axis_size(axis...  4.64 us
    ppermute x7, waiting for transfers between devices, shifted(): lax.ppermute(value, axis, [(i, (i + by) % size) for i in range(size)])  3.62 us
    pallas_call x1, Pallas kernels, border(): pl.pallas_call(functools.partial(border_kernel, parts), in_specs=[pl.Bloc...  2.59 us
    pallas_call x1, Pallas kernels, pack(): pl.pallas_call(functools.partial(pack_kernel, parts), in_specs=[pl.BlockS...  2.17 us
    ppermute x3, starting transfers between devices, swapped(): lax.ppermute(value, axis, [(i, i ^ bit) for i in range(lax.axis_size(axis...  1.72 us
  transfers between devices with their start and end apart: 10, of which 4 were waited for; matrix products, arithmetic and copies ran while one was open for 0% of the time, Pallas kernels for 26%

profile of v3, /device:TPU:0, one launch (start us, length us, event | category | flops | bytes accessed | tf_op | source)
XLA Modules:
  0.0 39.0 jit_solution(10777843226253881766)
XLA Ops:
  0.7 2.2 %pack_edges.1 = (f32[4,4,16,256]{3,2,1,0:T(8,128)S(1)}, f32[4,4,16,256]{3,2,1,0:T(8,128)S(1)}, f32[4,16,256]{2,1,0:T(8,128)S(1)}, f32[4,16,256]{2,1,0:T(8,128)S(1)}) custom-call(s32[1]{0:T(128)} %bitcast.grp_ref, f32[4,16,32,256]{3,2,1,0:T(8,128)} %lam.3, f32[16,32,256]{2,1,0:T(8,128)} %ew.3, f32[16,32,256]{2,1,0:T(8,128)} %ed.3, f32[16,32,256]{2,1,0:T(8,128)} %nw.3, ...), custom_call_target="tpu_custom_call" | custom-call | flops 1000000 | bytes 3145728 | tf_op jit(solution)/shard_map/pack_edges/pallas_call | solution.py:137
  2.8 3.0 %collective-permute-start.2 = (f32[4,16,256]{2,1,0:T(8,128)S(1)}, f32[4,16,256]{2,1,0:T(8,128)S(1)}, u32[]{:S(2)}, u32[]{:S(2)}) collective-permute-start(f32[4,16,256]{2,1,0:T(8,128)S(1)} %get-tuple-element.26), channel_id=1, source_target_pairs={{0,4},{4,8},{8,12},{12,16},{16,20},{20,24},{24,28},{28,0},{1,5},{5... | collective-permute-start | bytes 196616 | tf_op jit(solution)/shard_map/ppermute | solution.py:19
  5.8 3.1 %collective-permute-start.3 = (f32[4,16,256]{2,1,0:T(8,128)S(1)}, f32[4,16,256]{2,1,0:T(8,128)S(1)}, u32[]{:S(2)}, u32[]{:S(2)}) collective-permute-start(f32[4,16,256]{2,1,0:T(8,128)S(1)} %get-tuple-element.27), channel_id=1, source_target_pairs={{0,28},{4,0},{8,4},{12,8},{16,12},{20,16},{24,20},{28,24},{1,29},{... | collective-permute-start | bytes 196616 | tf_op jit(solution)/shard_map/ppermute | solution.py:19
  8.9 0.0 collective-permute-start
  8.9 4.7 %collective-permute-start.1 = (f32[4,4,16,256]{3,2,1,0:T(8,128)S(1)}, f32[4,4,16,256]{3,2,1,0:T(8,128)S(1)}, u32[]{:S(2)}, u32[]{:S(2)}) collective-permute-start(f32[4,4,16,256]{3,2,1,0:T(8,128)S(1)} %get-tuple-element.25), channel_id=1, source_target_pairs={{0,28},{4,0},{8,4},{12,8},{16,12},{20,16},{24,20},{28,24},{1,29},{... | collective-permute-start | bytes 786440 | tf_op jit(solution)/shard_map/ppermute | solution.py:19
  13.7 10.1 %inner_steps.1 = (f32[4,16,32,256]{3,2,1,0:T(8,128)}, f32[33,6,16,256]{3,2,1,0:T(8,128)S(1)}, f32[32,4,16,256]{3,2,1,0:T(8,128)S(1)}, f32[32,4,16,256]{3,2,1,0:T...) custom-call(s32[1]{0:T(128)} %bitcast.grp_ref, ...), custom_call_target="tpu_custom_call" | custom-call | flops 40000000 | bytes 8388608 | tf_op jit(solution)/shard_map/inner_steps/pallas_call | solution.py:276
  23.8 0.0 collective-permute-done.2
  23.8 0.0 collective-permute-done.3
  23.8 1.7 %collective-permute-start.5 = (f32[2,4,16,256]{3,2,1,0:T(8,128)S(1)}, f32[2,4,16,256]{3,2,1,0:T(8,128)S(1)}, u32[]{:S(2)}, u32[]{:S(2)}) collective-permute-start(f32[2,4,16,256]{3,2,1,0:T(8,128)S(1)} %pad_maximum_fusion.refs_0_), channel_id=1, source_target_pairs={{0,2},{1,3},{2,0},{3,1},{4,6},{5,7},{6,4},{7,5},{8,10},{9,11},{10,... | collective-permute-start | bytes 393224 | tf_op jit(solution)/shard_map/ppermute | solution.py:23
  25.5 0.0 collective-permute-start.4
  25.6 3.3 %collective-permute-done.5.refs_2_ = f32[2,4,16,256]{3,2,1,0:T(8,128)S(1)} collective-permute-done((f32[2,4,16,256]{3,2,1,0:T(8,128)S(1)}, f32[2,4,16,256]{3,2,1,0:T(8,128)S(1)}, u32[]{:S(2)}, u32[]{:S(2)}) %collective-permute-start.5) | collective-permute-done | bytes 131104 | tf_op jit(solution)/shard_map/ppermute | solution.py:23
  28.9 0.0 collective-permute-start.6
  28.9 0.0 collective-permute-done.4.refs_1_
  28.9 0.0 collective-permute-done.west
  28.9 0.0 collective-permute-done.1.east
  28.9 1.3 %collective-permute-done.6.refs_3_ = f32[2,4,16,256]{3,2,1,0:T(8,128)S(1)} collective-permute-done((f32[2,4,16,256]{3,2,1,0:T(8,128)S(1)}, f32[2,4,16,256]{3,2,1,0:T(8,128)S(1)}, u32[]{:S(2)}, u32[]{:S(2)}) %collective-permute-start.6) | collective-permute-done | bytes 131104 | tf_op jit(solution)/shard_map/ppermute | solution.py:23
  30.2 2.6 %border_steps.1 = (f32[4264,128]{1,0:T(8,128)S(1)}, f32[4,16,32,256]{3,2,1,0:T(8,128)}, f32[32,256]{1,0:T(8,128)S(1)}) custom-call(s32[1]{0:T(128)} %bitcast.grp_ref, s32[32,256]{1,0:T(8,128)S(1)} %copy-done.1, f32[33,6,16,256]{3,2,1,0:T(8,128)S(1)} %get-tuple-element.19.coef, ...), custom_call_target="tpu_custom_call", output_to_operand_aliasing={{0}: (13, {}), {1}: (14, {})} | custom-call | flops 10000000 | bytes 2097152 | tf_op jit(solution)/shard_map/border_steps/pallas_call | solution.py:400
  32.8 1.5 %collective-permute-start.9 = (f32[32,256]{1,0:T(8,128)S(1)}, f32[32,256]{1,0:T(8,128)S(1)}, u32[]{:S(2)}, u32[]{:S(2)}) collective-permute-start(f32[32,256]{1,0:T(8,128)S(1)} %get-tuple-element.35), channel_id=1, source_target_pairs={{0,3},{1,0},{2,1},{3,2},{4,7},{5,4},{6,5},{7,6},{8,11},{9,8},{10,9... | collective-permute-start | bytes 98312 | tf_op jit(solution)/shard_map/ppermute | solution.py:19
  34.3 0.4 %collective-permute-start.8 = (f32[32,256]{1,0:T(8,128)S(1)}, f32[32,256]{1,0:T(8,128)S(1)}, u32[]{:S(2)}, u32[]{:S(2)}) collective-permute-start(f32[32,256]{1,0:T(8,128)S(1)} %get-tuple-element.35), channel_id=1, source_target_pairs={{0,2},{1,3},{2,0},{3,1},{4,6},{5,7},{6,4},{7,5},{8,10},{9,11},{10,... | collective-permute-start | bytes 98312 | tf_op jit(solution)/shard_map/ppermute | solution.py:19
  34.7 0.1 collective-permute-start.7
  34.7 1.1 %collective-permute-done.9 = f32[32,256]{1,0:T(8,128)S(1)} collective-permute-done((f32[32,256]{1,0:T(8,128)S(1)}, f32[32,256]{1,0:T(8,128)S(1)}, u32[]{:S(2)}, u32[]{:S(2)}) %collective-permute-start.9) | collective-permute-done | bytes 32800 | tf_op jit(solution)/shard_map/ppermute | solution.py:19
  35.9 2.5 %collective-permute-done.8 = f32[32,256]{1,0:T(8,128)S(1)} collective-permute-done((f32[32,256]{1,0:T(8,128)S(1)}, f32[32,256]{1,0:T(8,128)S(1)}, u32[]{:S(2)}, u32[]{:S(2)}) %collective-permute-start.8) | collective-permute-done | bytes 32800 | tf_op jit(solution)/shard_map/ppermute | solution.py:19
  38.4 0.0 collective-permute-done.7
  38.4 0.6 %add_add_fusion = f32[32,256]{1,0:T(8,128)} fusion(f32[32,256]{1,0:T(8,128)S(1)} %collective-permute-done.9, f32[32,256]{1,0:T(8,128)S(1)} %collective-permute-done.8, f32[32,256]{1,0:T(8,128)S(1)} %get-tuple-element.35, f32[32,256]{1,0:T(8,128)S(1)} %collective-permute-done.7), kind=kLoop, calls=%fused_computation.1 | loop fusion | flops 24576 | bytes 163840 | tf_op jit(solution)/shard_map/add | solution.py:450
  (5 shorter events, 0.0 us)
Async XLA Ops:
  0.6 13.0 %copy-start = (s32[32,256]{1,0:T(8,128)S(1)}, s32[32,256]{1,0:T(8,128)}, u32[]{:S(2)}) copy-start(s32[32,256]{1,0:T(8,128)} %top.3) | copy-start | bytes 98308
  0.6 13.0 %copy-start.1 = (s32[32,256]{1,0:T(8,128)S(1)}, s32[32,256]{1,0:T(8,128)}, u32[]{:S(2)}) copy-start(s32[32,256]{1,0:T(8,128)} %region.3) | copy-start | bytes 98308
  2.8 21.0 %collective-permute-start.2 = (f32[4,16,256]{2,1,0:T(8,128)S(1)}, f32[4,16,256]{2,1,0:T(8,128)S(1)}, u32[]{:S(2)}, u32[]{:S(2)}) collective-permute-start(f32[4,16,256]{2,1,0:T(8,128)S(1)} %get-tuple-element.26), channel_id=1, source_target_pairs={{0,4},{4,8},{8,12},{12,16},{16,20},{20,24},{24,28},{28,0},{1,5},{5... | collective-permute-start | bytes 196616 | tf_op jit(solution)/shard_map/ppermute | solution.py:19
  5.8 18.0 %collective-permute-start.3 = (f32[4,16,256]{2,1,0:T(8,128)S(1)}, f32[4,16,256]{2,1,0:T(8,128)S(1)}, u32[]{:S(2)}, u32[]{:S(2)}) collective-permute-start(f32[4,16,256]{2,1,0:T(8,128)S(1)} %get-tuple-element.27), channel_id=1, source_target_pairs={{0,28},{4,0},{8,4},{12,8},{16,12},{20,16},{24,20},{28,24},{1,29},{... | collective-permute-start | bytes 196616 | tf_op jit(solution)/shard_map/ppermute | solution.py:19
  8.9 19.9 %collective-permute-start = (f32[4,4,16,256]{3,2,1,0:T(8,128)S(1)}, f32[4,4,16,256]{3,2,1,0:T(8,128)S(1)}, u32[]{:S(2)}, u32[]{:S(2)}) collective-permute-start(f32[4,4,16,256]{3,2,1,0:T(8,128)S(1)} %get-tuple-element.24), channel_id=1, source_target_pairs={{0,4},{4,8},{8,12},{12,16},{16,20},{20,24},{24,28},{28,0},{1,5},{5... | collective-permute-start | bytes 786440 | tf_op jit(solution)/shard_map/ppermute | solution.py:19
  8.9 20.0 %collective-permute-start.1 = (f32[4,4,16,256]{3,2,1,0:T(8,128)S(1)}, f32[4,4,16,256]{3,2,1,0:T(8,128)S(1)}, u32[]{:S(2)}, u32[]{:S(2)}) collective-permute-start(f32[4,4,16,256]{3,2,1,0:T(8,128)S(1)} %get-tuple-element.25), channel_id=1, source_target_pairs={{0,28},{4,0},{8,4},{12,8},{16,12},{20,16},{24,20},{28,24},{1,29},{... | collective-permute-start | bytes 786440 | tf_op jit(solution)/shard_map/ppermute | solution.py:19
  23.8 5.0 %collective-permute-start.5 = (f32[2,4,16,256]{3,2,1,0:T(8,128)S(1)}, f32[2,4,16,256]{3,2,1,0:T(8,128)S(1)}, u32[]{:S(2)}, u32[]{:S(2)}) collective-permute-start(f32[2,4,16,256]{3,2,1,0:T(8,128)S(1)} %pad_maximum_fusion.refs_0_), channel_id=1, source_target_pairs={{0,2},{1,3},{2,0},{3,1},{4,6},{5,7},{6,4},{7,5},{8,10},{9,11},{10,... | collective-permute-start | bytes 393224 | tf_op jit(solution)/shard_map/ppermute | solution.py:23
  25.5 3.3 %collective-permute-start.4 = (f32[2,4,16,256]{3,2,1,0:T(8,128)S(1)}, f32[2,4,16,256]{3,2,1,0:T(8,128)S(1)}, u32[]{:S(2)}, u32[]{:S(2)}) collective-permute-start(f32[2,4,16,256]{3,2,1,0:T(8,128)S(1)} %pad_maximum_fusion.refs_0_), channel_id=1, source_target_pairs={{0,1},{1,0},{2,3},{3,2},{4,5},{5,4},{6,7},{7,6},{8,9},{9,8},{10,11... | collective-permute-start | bytes 393224 | tf_op jit(solution)/shard_map/ppermute | solution.py:23
  28.9 1.3 %collective-permute-start.6 = (f32[2,4,16,256]{3,2,1,0:T(8,128)S(1)}, f32[2,4,16,256]{3,2,1,0:T(8,128)S(1)}, u32[]{:S(2)}, u32[]{:S(2)}) collective-permute-start(f32[2,4,16,256]{3,2,1,0:T(8,128)S(1)} %collective-permute-done.5.refs_2_), channel_id=1, source_target_pairs={{0,1},{1,0},{2,3},{3,2},{4,5},{5,4},{6,7},{7,6},{8,9},{9,8},{10,11... | collective-permute-start | bytes 393224 | tf_op jit(solution)/shard_map/ppermute | solution.py:23
  32.8 3.1 %collective-permute-start.9 = (f32[32,256]{1,0:T(8,128)S(1)}, f32[32,256]{1,0:T(8,128)S(1)}, u32[]{:S(2)}, u32[]{:S(2)}) collective-permute-start(f32[32,256]{1,0:T(8,128)S(1)} %get-tuple-element.35), channel_id=1, source_target_pairs={{0,3},{1,0},{2,1},{3,2},{4,7},{5,4},{6,5},{7,6},{8,11},{9,8},{10,9... | collective-permute-start | bytes 98312 | tf_op jit(solution)/shard_map/ppermute | solution.py:19
  34.3 4.1 %collective-permute-start.8 = (f32[32,256]{1,0:T(8,128)S(1)}, f32[32,256]{1,0:T(8,128)S(1)}, u32[]{:S(2)}, u32[]{:S(2)}) collective-permute-start(f32[32,256]{1,0:T(8,128)S(1)} %get-tuple-element.35), channel_id=1, source_target_pairs={{0,2},{1,3},{2,0},{3,1},{4,6},{5,7},{6,4},{7,5},{8,10},{9,11},{10,... | collective-permute-start | bytes 98312 | tf_op jit(solution)/shard_map/ppermute | solution.py:19
  34.7 3.7 %collective-permute-start.7 = (f32[32,256]{1,0:T(8,128)S(1)}, f32[32,256]{1,0:T(8,128)S(1)}, u32[]{:S(2)}, u32[]{:S(2)}) collective-permute-start(f32[32,256]{1,0:T(8,128)S(1)} %get-tuple-element.35), channel_id=1, source_target_pairs={{0,1},{1,2},{2,3},{3,0},{4,5},{5,6},{6,7},{7,4},{8,9},{9,10},{10,1... | collective-permute-start | bytes 98312 | tf_op jit(solution)/shard_map/ppermute | solution.py:19

commit v4 on v3

v4 whole, which is shorter than its diff:
```python
import functools

import jax
import jax.numpy as jnp
from jax import lax
from jax.experimental import pallas as pl
from jax.experimental.pallas import tpu as pltpu
from jax.sharding import PartitionSpec as P

ITERS = 4
EDGE = ITERS
ENTRIES = 16
CHUNKS = 3
LANES = 128
SHORT = pl.CostEstimate(flops=1000, bytes_accessed=1000, transcendentals=0)
LOW, HIGH = 0, 1


def swapped(value, axis, partner):
    return lax.ppermute(value, axis, [(i, partner(i)) for i in range(lax.axis_size(axis))])


def level_of(shape):
    row = lax.broadcasted_iota(jnp.int32, shape, 0)
    half = shape[0] // 2
    return jnp.where(row < half, 2 * row, 2 * (row - half) + 1)


def place_of(level, levels):
    return (level % 2) * (levels // 2) + level // 2


def faces(ew, ed, nw, nd):
    lats = ew.shape[1]
    lat = lax.broadcasted_iota(jnp.int32, ew.shape, 1)
    east = jnp.maximum(ew, 0.0) + ed
    west_next = jnp.maximum(-ew, 0.0) + ed
    north = jnp.where(lat < lats - 1, jnp.maximum(nw, 0.0) + nd, 0.0)
    south = jnp.maximum(-nw, 0.0) + nd
    south = jnp.where(lat > 0, pltpu.roll(south, 1, 1), 0.0)
    return east, west_next, north, south


def updraft(mf, top_row):
    levels = mf.shape[0]
    level = level_of(mf.shape)
    return jnp.where((level < top_row) & (level < levels - 1), mf, 0.0)


def advance(coefs, mid, east, west):
    d, e, w, n, s, u = coefs
    levels, lats = mid.shape
    half = levels // 2
    h = d * mid + e * east + w * west
    h = h + n * pltpu.roll(mid, lats - 1, 1) + s * pltpu.roll(mid, 1, 1)
    above = jnp.concatenate([h[half:], pltpu.roll(h[:half], half - 1, 0)], axis=0)
    return h + u * (above - h)


def pitched(slabs, levels, width):
    return -(-(slabs * levels * (width + 1) + width + 8) // 8) * 8


def column_at(ref, start, levels, pitch, apart):
    parts = [ref[pl.ds(start + apart * k, levels, stride=pitch), :] for k in range(2)]
    return jnp.concatenate(parts, axis=1)


def pack_coefs_kernel(parts, place, ew, ed, nw, nd, mf, top, first, second, field_s, top_s, entry, field_p, sems):
    levels, cols, lats = ew.shape
    copies = []

    def copy(src, dst):
        copies.append(pltpu.make_async_copy(src, dst, sems.at[len(copies)]))
        copies[-1].start()

    for side, at in ((LOW, 0), (HIGH, cols - 8)):
        copy(top.at[pl.ds(at, 8)], top_s.at[side])
        for k in range(2):
            for f, field in enumerate((ew, ed, nw, nd, mf)):
                copy(field.at[:, pl.ds(at, 8), pl.ds(k * LANES, LANES)], field_s.at[f, side, k])
    for c in copies:
        c.wait()
    pitch = 9
    slab = levels * pitch

    @pl.loop(0, levels)
    def _(level):
        row = place_of(level, levels) * pitch
        for f in range(5):
            for side in range(2):
                for k in range(2):
                    at = ((f * 2 + side) * 2 + k) * slab
                    field_p[pl.ds(at + row, 8), :] = field_s[f, side, k, level]

    def field(f, side, c):
        return column_at(field_p, (f * 2 + side) * 2 * slab + c, levels, pitch, slab)

    for side in (LOW, HIGH):
        slot = 0
        for c in range(EDGE - 1) if side == LOW else range(8 - EDGE, 8):
            east, west, north, south = faces(*(field(f, side, c) for f in range(4)))
            lift = updraft(field(4, side, c), top_s[side, pl.ds(c, 1), :])
            wanted = (east, west, north, south, lift)
            if side == HIGH and c == 8 - EDGE:
                wanted = (west,)
            for value in wanted:
                entry[side, slot] = value
                slot += 1
        for left in range(slot, ENTRIES):
            entry[side, left] = jnp.zeros((levels, lats), jnp.float32)
    per = ENTRIES // parts
    mine = lax.rem(place[0], parts) * per
    odd = place[1]
    first[...] = entry[1 - odd, pl.ds(mine, per)]
    second[...] = entry[odd, pl.ds(mine, per)]


def pack_coefs(parts, place, fields, top):
    levels, cols, lats = fields[0].shape
    hbm = pl.BlockSpec(memory_space=pltpu.HBM)
    send = pltpu.VMEM((ENTRIES // parts, levels, lats), jnp.float32)
    return pl.pallas_call(
        functools.partial(pack_coefs_kernel, parts),
        in_specs=[pl.BlockSpec(memory_space=pltpu.SMEM)] + [hbm] * 6,
        out_specs=[pl.BlockSpec(memory_space=pltpu.VMEM)] * 2,
        out_shape=[send, send],
        scratch_shapes=[
            pltpu.VMEM((5, 2, 2, levels, 8, LANES), jnp.float32),
            pltpu.VMEM((2, 8, lats), jnp.int32),
            pltpu.VMEM((2, ENTRIES, levels, lats), jnp.float32),
            pltpu.VMEM((pitched(20, levels, 8), LANES), jnp.float32),
            pltpu.SemaphoreType.DMA((22,)),
        ],
        compiler_params=pltpu.CompilerParams(vmem_limit_bytes=24 << 20),
        cost_estimate=SHORT,
        name="pack_coefs",
    )(place, *fields, top)


def pack_lam_kernel(place, lam, first, second, lam_s, lam_p, sems):
    tags, levels, cols, lats = lam.shape
    copies = []
    for side, at in ((LOW, 0), (HIGH, cols - 8)):
        for k in range(2):
            copies.append(
                pltpu.make_async_copy(
                    lam.at[:, :, pl.ds(at, 8), pl.ds(k * LANES, LANES)],
                    lam_s.at[side, k],
                    sems.at[side * 2 + k],
                )
            )
            copies[-1].start()
    for c in copies:
        c.wait()
    pitch = 9
    slab = levels * pitch

    @pl.loop(0, levels)
    def _(level):
        row = place_of(level, levels) * pitch
        for side in range(2):
            for k in range(2):
                for tag in range(tags):
                    at = ((side * 2 + k) * tags + tag) * slab
                    lam_p[pl.ds(at + row, 8), :] = lam_s[side, k, tag, level]

    odd = place[1]
    for dest, side in ((first, 1 - odd), (second, odd)):
        start = side * (2 * tags * slab + 8 - EDGE)
        for tag in range(tags):
            for c in range(EDGE):
                dest[tag, c] = column_at(lam_p, start + tag * slab + c, levels, pitch, tags * slab)


def pack_lam(place, lam):
    tags, levels, cols, lats = lam.shape
    send = pltpu.VMEM((tags, EDGE, levels, lats), jnp.float32)
    return pl.pallas_call(
        pack_lam_kernel,
        in_specs=[pl.BlockSpec(memory_space=pltpu.SMEM), pl.BlockSpec(memory_space=pltpu.HBM)],
        out_specs=[pl.BlockSpec(memory_space=pltpu.VMEM)] * 2,
        out_shape=[send, send],
        scratch_shapes=[
            pltpu.VMEM((2, 2, tags, levels, 8, LANES), jnp.float32),
            pltpu.VMEM((pitched(4 * tags, levels, 8), LANES), jnp.float32),
            pltpu.SemaphoreType.DMA((4,)),
        ],
        compiler_params=pltpu.CompilerParams(vmem_limit_bytes=24 << 20),
        cost_estimate=SHORT,
        name="pack_lam",
    )(place, lam)


def chosen(region_row, first_tag, values):
    row = jnp.zeros(region_row.shape, jnp.float32)
    for tag, value in enumerate(values):
        row = jnp.where(region_row == first_tag + tag, value[0:1], row)
    return row


def sweep(t, first_tag, region, coef, src, store, rows):
    cols, tags = src.shape[:2]
    low, high = t + 1, cols - t - 1
    chunk = -(-(high - low) // CHUNKS)

    @pl.loop(0, CHUNKS)
    def _(i):
        start = jnp.minimum(low + i * chunk, high - chunk)
        for j in range(chunk):
            c = start + j
            coefs = [coef[c, n] for n in range(6)]
            new = [advance(coefs, src[c, k], src[c + 1, k], src[c - 1, k]) for k in range(tags)]
            for k in range(tags):
                store(c, k, new[k])
            rows[t, pl.ds(c, 1), :] = chosen(region[pl.ds(c, 1), :], first_tag, new)


def storing(ref):
    def store(c, tag, value):
        ref[c, tag] = value

    return store


def storing_rows(ref, tags, levels, pitch):
    def store(c, tag, value):
        for k in range(2):
            at = (k * tags + tag) * levels * pitch + c
            ref[pl.ds(at, levels, stride=pitch), :] = value[:, k * LANES : (k + 1) * LANES]

    return store


def inner_kernel(place, lam, ew, ed, nw, nd, mf, top, region, coef, l0, l1, l2, l3, final, rows, lam_p, field_p):
    tags, levels, cols, lats = lam.shape
    pitch = cols + 1
    slab = levels * pitch
    halves = [slice(k * LANES, (k + 1) * LANES) for k in range(2)]

    @pl.loop(0, levels)
    def _(level):
        row = place_of(level, levels) * pitch
        for f, field in enumerate((ew, ed, nw, nd, mf)):
            for k in range(2):
                field_p[pl.ds((f * 2 + k) * slab + row, cols), :] = field[level, :, halves[k]]
        for tag in range(tags):
            for k in range(2):
                lam_p[pl.ds((k * tags + tag) * slab + row, cols), :] = lam[tag, level, :, halves[k]]

    def coefficients(c, west):
        ew, ed, nw, nd, mf = (
            column_at(field_p, f * 2 * slab + c, levels, pitch, slab) for f in range(5)
        )
        e, next_west, n, s = faces(ew, ed, nw, nd)
        u = updraft(mf, top[pl.ds(c, 1), :])
        for j, value in enumerate((1.0 - e - west - n - s, e, west, n, s, u)):
            coef[c, j] = value
        return next_west

    def some(i, west):
        for j in range(8):
            c = i * 8 + j
            west = coefficients(c, west)
            for tag in range(tags):
                l0[c, tag] = column_at(lam_p, tag * slab + c, levels, pitch, tags * slab)
        return west

    west = lax.fori_loop(0, cols // 8, some, jnp.zeros((levels, lats), jnp.float32))
    coef[cols, 2] = west
    first_tag = place[0] * tags
    sweep(0, first_tag, region, coef, l0, storing(l1), rows)
    sweep(1, first_tag, region, coef, l1, storing(l2), rows)
    sweep(2, first_tag, region, coef, l2, storing(l3), rows)
    sweep(3, first_tag, region, coef, l3, storing_rows(final, tags, levels, pitch), rows)


def inner(place, lam, fields, top, region):
    tags, levels, cols, lats = lam.shape
    vmem = pl.BlockSpec(memory_space=pltpu.VMEM)
    state = pltpu.VMEM((cols, tags, levels, lats), jnp.float32)
    return pl.pallas_call(
        inner_kernel,
        in_specs=[pl.BlockSpec(memory_space=pltpu.SMEM)] + [vmem] * 8,
        out_specs=[vmem] * 7,
        out_shape=[
            pltpu.VMEM((cols + 1, 6, levels, lats), jnp.float32),
            *[state] * 4,
            pltpu.VMEM((pitched(2 * tags, levels, cols), LANES), jnp.float32),
            pltpu.VMEM((ITERS, cols, lats), jnp.float32),
        ],
        scratch_shapes=[
            pltpu.VMEM((pitched(2 * tags, levels, cols), LANES), jnp.float32),
            pltpu.VMEM((pitched(10, levels, cols), LANES), jnp.float32),
        ],
        compiler_params=pltpu.CompilerParams(vmem_limit_bytes=32 << 20),
        cost_estimate=SHORT,
        name="inner_steps",
    )(place, lam, *fields, top, region)


def border_kernel(parts, place, region, coef, l0, l1, l2, l3, first, second, *refs):
    pieces = refs[:parts]
    final_in, rows_in, final, grad, entry, halo, wide, work, rows = refs[parts:]
    cols, tags, levels, lats = l0.shape
    first_tag = place[0] * tags
    per = ENTRIES // parts
    mine = lax.rem(place[0], parts)
    odd = place[1]
    halo[1 - odd] = first[...]
    halo[odd] = second[...]
    for by in range(parts):
        base = (mine ^ by) * per
        entry[1 - odd, pl.ds(base, per)] = pieces[by][0]
        entry[odd, pl.ds(base, per)] = pieces[by][1]

    def slot(c):
        return (LOW, c + EDGE - 1) if c < EDGE else (HIGH, c - (cols - EDGE))

    def outside(c):
        if c < 0:
            at = 1 + 5 * (c + EDGE - 1)
            e, _, n, s, u = (entry[LOW, at + j] for j in range(5))
            w = entry[LOW, at - 4] if c > 1 - EDGE else entry[LOW, 0]
        else:
            at = 5 * (c - cols)
            e, _, n, s, u = (entry[HIGH, at + j] for j in range(5))
            w = entry[HIGH, at - 4] if c > cols else coef[cols, 2]
        return 1.0 - e - w - n - s, e, w, n, s, u

    for c in [*range(1 - EDGE, 0), *range(cols, cols + EDGE - 1)]:
        for j, value in enumerate(outside(c)):
            wide[*slot(c), j] = value
    first_west = entry[LOW, 1 + 5 * (EDGE - 2) + 1]
    first_mid = 1.0 - coef[0, 1] - first_west - coef[0, 3] - coef[0, 4]
    for j, value in enumerate((first_mid, coef[0, 1], first_west, *(coef[0, j] for j in range(3, 6)))):
        wide[*slot(0), j] = value

    def coefs_at(c):
        if 0 < c < cols:
            return [coef[c, j] for j in range(6)]
        return [wide[*slot(c), j] for j in range(6)]

    kept = (l0, l1, l2, l3)

    def state(t, c, tag):
        if t <= c < cols - t:
            return kept[t][c, tag]
        if t == 0:
            return halo[LOW, tag, c + EDGE] if c < 0 else halo[HIGH, tag, c - cols]
        return work[t, *slot(c), tag]

    rows[...] = rows_in[...]
    store = storing_rows(final, tags, levels, cols + 1)
    for t in range(ITERS):
        reach = EDGE - 1 - t
        for c in [*range(-reach, t + 1), *range(cols - t - 1, cols + reach)]:
            coefs = coefs_at(c)
            new = [
                advance(coefs, state(t, c, k), state(t, c + 1, k), state(t, c - 1, k))
                for k in range(tags)
            ]
            for k in range(tags):
                if t < ITERS - 1:
                    work[t + 1, *slot(c), k] = new[k]
                else:
                    store(c, k, new[k])
            if 0 <= c < cols:
                rows[t, c : c + 1, :] = chosen(region[c : c + 1, :], first_tag, new)
    total = rows[0]
    for t in range(1, ITERS):
        total = total + rows[t]
    grad[...] = total


def border(parts, place, region, coef, states, first, second, pieces, final, rows):
    cols, tags, levels, lats = states[0].shape
    vmem = pl.BlockSpec(memory_space=pltpu.VMEM)
    operands = [region, coef, *states, first, second, *pieces]
    return pl.pallas_call(
        functools.partial(border_kernel, parts),
        in_specs=[pl.BlockSpec(memory_space=pltpu.SMEM)] + [vmem] * (len(operands) + 2),
        out_specs=[vmem] * 2,
        out_shape=[
            pltpu.VMEM(final.shape, jnp.float32),
            pltpu.VMEM((cols, lats), jnp.float32),
        ],
        input_output_aliases={len(operands) + 1: 0},
        scratch_shapes=[
            pltpu.VMEM((2, ENTRIES, levels, lats), jnp.float32),
            pltpu.VMEM((2, tags, EDGE, levels, lats), jnp.float32),
            pltpu.VMEM((2, 2 * EDGE - 1, 6, levels, lats), jnp.float32),
            pltpu.VMEM((ITERS, 2, 2 * EDGE - 1, tags, levels, lats), jnp.float32),
            pltpu.VMEM((ITERS, cols, lats), jnp.float32),
        ],
        compiler_params=pltpu.CompilerParams(vmem_limit_bytes=32 << 20),
        cost_estimate=SHORT,
        name="border_steps",
    )(place, *operands, final, rows)


def write_kernel(final, out, block, sems):
    tags, levels, cols, _ = out.shape
    pitch = cols + 1
    copies = []
    for tag in range(tags):

        @pl.loop(0, levels)
        def _(level):
            row = place_of(level, levels) * pitch
            for k in range(2):
                at = (k * tags + tag) * levels * pitch + row
                block[tag, level, :, k * LANES : (k + 1) * LANES] = final[pl.ds(at, cols), :]

        copies.append(pltpu.make_async_copy(block.at[tag], out.at[tag], sems.at[tag]))
        copies[-1].start()
    for c in copies:
        c.wait()


def write(final, shape):
    return pl.pallas_call(
        write_kernel,
        in_specs=[pl.BlockSpec(memory_space=pltpu.VMEM)],
        out_specs=pl.BlockSpec(memory_space=pltpu.HBM),
        out_shape=pltpu.HBM(shape, jnp.float32),
        scratch_shapes=[
            pltpu.VMEM(shape, jnp.float32),
            pltpu.SemaphoreType.DMA((shape[0],)),
        ],
        compiler_params=pltpu.CompilerParams(vmem_limit_bytes=24 << 20),
        cost_estimate=SHORT,
        name="write_final",
    )(final)


def local(lam, east_wind, north_wind, east_diff, north_diff, mass_flux, region, top):
    groups, tiles = lax.axis_size("grp"), lax.axis_size("dom")
    parts = 4 if groups % 4 == 0 else 1
    grp, dom = lax.axis_index("grp"), lax.axis_index("dom")
    place = jnp.stack([grp, dom % 2]).astype(jnp.int32)
    own = (lam, east_wind, east_diff, north_wind, north_diff, mass_flux)
    far = [pltpu.with_memory_space_constraint(value, pltpu.HBM) for value in (*own, top)]

    pairs = lambda i: i ^ 1
    turn = lambda i: (((i - 1) % tiles ^ 1) + 1) % tiles
    coef_first, coef_second = pack_coefs(parts, place, far[1:6], far[6])
    coef_first, coef_second, far_lam, *own = lax.optimization_barrier(
        (coef_first, coef_second, far[0], *own)
    )
    lam_first, lam_second = pack_lam(place, far_lam)
    coef_first = swapped(coef_first, "dom", pairs)
    coef_second = swapped(coef_second, "dom", turn)
    coef_first, coef_second, _ = lax.optimization_barrier((coef_first, coef_second, lam_first))
    first = swapped(lam_first, "dom", pairs)
    second = swapped(lam_second, "dom", turn)
    pieces = [jnp.stack([coef_first, coef_second])]
    for by in range(1, parts):
        pieces.append(swapped(pieces[0], "grp", lambda i: i ^ by))
    coef, *states, final, rows = inner(place, own[0], own[1:], top, region)
    final, grad = border(parts, place, region, coef, states, first, second, pieces, final, rows)
    share = grad
    for by in range(1, groups):
        grad = grad + swapped(share, "grp", lambda i: (i + by) % groups)
    return write(final, lam.shape), grad


def solution(mesh):
    return jax.shard_map(
        local,
        mesh=mesh,
        in_specs=(
            P("grp", None, "dom", None),
            P(None, "dom", None),
            P(None, "dom", None),
            P(None, "dom", None),
            P(None, "dom", None),
            P(None, "dom", None),
            P("dom", None),
            P("dom", None),
        ),
        out_specs=(P("grp", None, "dom", None), P("dom", None)),
        check_vma=False,
    )
```

time: 39.1 us -> 34 us (0.87)
  starting transfers between devices: 14.5 us -> 11.5 us
  waiting for transfers between devices: 8.27 us -> 5.47 us
  Pallas kernels: 14.9 us -> 15.3 us
    pallas_call x1 -> x3, Pallas kernels: 2.17 us -> 6.34 us  [the longest x1 2.74 us: pack_coefs(): pl.pallas_call(functools.partial(pack_coefs_kernel, parts), in_specs=[pl....]
    pallas_call x1, Pallas kernels: 10.1 us -> 6.91 us  [inner(): pl.pallas_call(inner_kernel, in_specs=[pl.BlockSpec(memory_space=pltpu.SM...]
    ppermute x10, starting transfers between devices: 14.5 us -> 11.5 us  [swapped(): lax.ppermute(value, axis, [(i, partner(i)) for i in range(lax.axis_size(a...]
    ppermute x10, waiting for transfers between devices: 8.27 us -> 5.47 us  [swapped(): lax.ppermute(value, axis, [(i, partner(i)) for i in range(lax.axis_size(a...]
    pallas_call x1, Pallas kernels: 2.59 us -> 2.01 us  [border(): pl.pallas_call(functools.partial(border_kernel, parts), in_specs=[pl.Bloc...]
  transfers between devices with their start and end apart: 10 -> 10, of which waited for: 4 -> 5; matrix products, arithmetic and copies ran while one was open for 0% -> 0% of each run, Pallas kernels for 26% -> 31%
where the time goes in v4:
time: 34 us; the launch traced here: 33.8 us
  Pallas kernels  15.3 us (45%)
  starting transfers between devices  11.5 us (34%)
  waiting for transfers between devices  5.47 us (16%)
  between operations  0.81 us (2%)
  other arithmetic  0.71 us (2%)
    ppermute x10, starting transfers between devices, swapped(): lax.ppermute(value, axis, [(i, partner(i)) for i in range(lax.axis_size(a...  11.5 us
    pallas_call x1, Pallas kernels, inner(): pl.pallas_call(inner_kernel, in_specs=[pl.BlockSpec(memory_space=pltpu.SM...  6.91 us
    ppermute x10, waiting for transfers between devices, swapped(): lax.ppermute(value, axis, [(i, partner(i)) for i in range(lax.axis_size(a...  5.47 us
    pallas_call x1, Pallas kernels, pack_coefs(): pl.pallas_call(functools.partial(pack_coefs_kernel, parts), in_specs=[pl....  2.74 us
    pallas_call x1, Pallas kernels, pack_lam(): pl.pallas_call(pack_lam_kernel, in_specs=[pl.BlockSpec(memory_space=pltpu...  2.03 us
    pallas_call x1, Pallas kernels, border(): pl.pallas_call(functools.partial(border_kernel, parts), in_specs=[pl.Bloc...  2.01 us
    pallas_call x1, Pallas kernels, write(): pl.pallas_call(write_kernel, in_specs=[pl.BlockSpec(memory_space=pltpu.VM...  1.57 us
  transfers between devices with their start and end apart: 10, of which 5 were waited for; matrix products, arithmetic and copies ran while one was open for 0% of the time, Pallas kernels for 31%

profile of v4, /device:TPU:0, one launch (start us, length us, event | category | flops | bytes accessed | tf_op | source)
XLA Modules:
  0.0 33.8 jit_solution(14469929629187063714)
XLA Ops:
  0.6 0.1 pad_add_fusion.place
  0.7 0.0 copy-start.4
  0.7 0.0 copy-start.5
  0.8 0.0 copy-start.7
  0.8 2.7 %pack_coefs.1 = (f32[4,16,256]{2,1,0:T(8,128)S(1)}, f32[4,16,256]{2,1,0:T(8,128)S(1)}) custom-call(s32[2]{0:T(128)S(1)} %pad_add_fusion.place, f32[16,32,256]{2,1,0:T(8,128)} %ew.2, f32[16,32,256]{2,1,0:T(8,128)} %ed.2, f32[16,32,256]{2,1,0:T(8,128)} %nw.2, f32[16,32,256]{2,1,0:T(8,128)} %nd.2, f32[16,32,256]{2,1,0:T(8,128)} %mf.2, s32[32,256]{1,0:T(8,128)} %top.3), custom_call_target="tpu_custom_call" | custom-call | flops 1000 | bytes 1000 | tf_op jit(solution)/shard_map/pack_coefs/pallas_call | solution.py:123
  3.5 3.0 %collective-permute-start.2 = (f32[4,16,256]{2,1,0:T(8,128)S(1)}, f32[4,16,256]{2,1,0:T(8,128)S(1)}, u32[]{:S(2)}, u32[]{:S(2)}) collective-permute-start(f32[4,16,256]{2,1,0:T(8,128)S(1)} %get-tuple-element.42), channel_id=1, source_target_pairs={{0,4},{4,0},{8,12},{12,8},{16,20},{20,16},{24,28},{28,24},{1,5},{5... | collective-permute-start | bytes 196616 | tf_op jit(solution)/shard_map/ppermute | solution.py:20
  6.5 3.6 %collective-permute-start.3 = (f32[4,16,256]{2,1,0:T(8,128)S(1)}, f32[4,16,256]{2,1,0:T(8,128)S(1)}, u32[]{:S(2)}, u32[]{:S(2)}) collective-permute-start(f32[4,16,256]{2,1,0:T(8,128)S(1)} %get-tuple-element.43), channel_id=1, source_target_pairs={{0,28},{4,8},{8,4},{12,16},{16,12},{20,24},{24,20},{28,0},{1,29},{... | collective-permute-start | bytes 196616 | tf_op jit(solution)/shard_map/ppermute | solution.py:20
  10.1 2.0 %pack_lam.1 = (f32[4,4,16,256]{3,2,1,0:T(8,128)S(1)}, f32[4,4,16,256]{3,2,1,0:T(8,128)S(1)}) custom-call(s32[2]{0:T(128)S(1)} %pad_add_fusion.place, f32[4,16,32,256]{3,2,1,0:T(8,128)} %lam.1), custom_call_target="tpu_custom_call" | custom-call | flops 1000 | bytes 1000 | tf_op jit(solution)/shard_map/pack_lam/pallas_call | solution.py:179
  12.1 1.2 %collective-permute-start.1 = (f32[4,4,16,256]{3,2,1,0:T(8,128)S(1)}, f32[4,4,16,256]{3,2,1,0:T(8,128)S(1)}, u32[]{:S(2)}, u32[]{:S(2)}) collective-permute-start(f32[4,4,16,256]{3,2,1,0:T(8,128)S(1)} %get-tuple-element.41), channel_id=1, source_target_pairs={{0,28},{4,8},{8,4},{12,16},{16,12},{20,24},{24,20},{28,0},{1,29},{... | collective-permute-start | bytes 786440 | tf_op jit(solution)/shard_map/ppermute | solution.py:20
  13.4 0.1 collective-permute-done.3
  13.5 0.1 collective-permute-start.6
  13.6 1.6 %collective-permute-start.5 = (f32[2,4,16,256]{3,2,1,0:T(8,128)S(1)}, f32[2,4,16,256]{3,2,1,0:T(8,128)S(1)}, u32[]{:S(2)}, u32[]{:S(2)}) collective-permute-start(f32[2,4,16,256]{3,2,1,0:T(8,128)S(1)} %pad_maximum_fusion.refs_0_), channel_id=1, source_target_pairs={{0,2},{1,3},{2,0},{3,1},{4,6},{5,7},{6,4},{7,5},{8,10},{9,11},{10,... | collective-permute-start | bytes 393224 | tf_op jit(solution)/shard_map/ppermute | solution.py:20
  15.2 0.3 collective-permute-start.4
  15.5 6.9 %inner_steps.1 = (f32[33,6,16,256]{3,2,1,0:T(8,128)S(1)}, f32[32,4,16,256]{3,2,1,0:T(8,128)S(1)}, f32[32,4,16,256]{3,2,1,0:T(8,128)S(1)}, f32[32,4,16,256]{3,2,1...) custom-call(s32[2]{0:T(128)S(1)} %pad_add_fusion.place, ...), custom_call_target="tpu_custom_call" | custom-call | flops 1000 | bytes 1000 | tf_op jit(solution)/shard_map/inner_steps/pallas_call | solution.py:282
  22.4 0.1 collective-permute-done.1.second
  22.5 3.7 %collective-permute-done.first = f32[4,4,16,256]{3,2,1,0:T(8,128)S(1)} collective-permute-done((f32[4,4,16,256]{3,2,1,0:T(8,128)S(1)}, f32[4,4,16,256]{3,2,1,0:T(8,128)S(1)}, u32[]{:S(2)}, u32[]{:S(2)}) %collective-permute-start) | collective-permute-done | bytes 262176 | tf_op jit(solution)/shard_map/ppermute | solution.py:20
  26.2 2.0 %border_steps.1 = (f32[4264,128]{1,0:T(8,128)S(1)}, f32[32,256]{1,0:T(8,128)S(1)}) custom-call(s32[2]{0:T(128)S(1)} %pad_add_fusion.place, s32[32,256]{1,0:T(8,128)S(1)} %copy-done.7, f32[33,6,16,256]{3,2,1,0:T(8,128)S(1)} %get-tuple-element.34.coef, f32[32,4,16,256]{3,2,1,0:T(8,128)S(1)} %get-tuple-element.35.l0, ...), custom_call_target="tpu_custom_call", output_to_operand_aliasing={{0}: (13, {})} | custom-call | flops 1000 | bytes 1000 | tf_op jit(solution)/shard_map/border_steps/pallas_call | solution.py:380
  28.2 0.1 collective-permute-start.9
  28.3 1.6 %collective-permute-start.8 = (f32[32,256]{1,0:T(8,128)S(1)}, f32[32,256]{1,0:T(8,128)S(1)}, u32[]{:S(2)}, u32[]{:S(2)}) collective-permute-start(f32[32,256]{1,0:T(8,128)S(1)} %get-tuple-element.49), channel_id=1, source_target_pairs={{0,2},{1,3},{2,0},{3,1},{4,6},{5,7},{6,4},{7,5},{8,10},{9,11},{10,... | collective-permute-start | bytes 98312 | tf_op jit(solution)/shard_map/ppermute | solution.py:20
  29.8 0.2 collective-permute-start.7
  30.0 1.6 %write_final.1 = f32[4,16,32,256]{3,2,1,0:T(8,128)} custom-call(f32[4264,128]{1,0:T(8,128)S(1)} %get-tuple-element.48.final), custom_call_target="tpu_custom_call" | custom-call | flops 1000 | bytes 1000 | tf_op jit(solution)/shard_map/write_final/pallas_call | solution.py:422
  31.6 0.8 %collective-permute-done.8 = f32[32,256]{1,0:T(8,128)S(1)} collective-permute-done((f32[32,256]{1,0:T(8,128)S(1)}, f32[32,256]{1,0:T(8,128)S(1)}, u32[]{:S(2)}, u32[]{:S(2)}) %collective-permute-start.8) | collective-permute-done | bytes 32800 | tf_op jit(solution)/shard_map/ppermute | solution.py:20
  32.4 0.8 %collective-permute-done.7 = f32[32,256]{1,0:T(8,128)S(1)} collective-permute-done((f32[32,256]{1,0:T(8,128)S(1)}, f32[32,256]{1,0:T(8,128)S(1)}, u32[]{:S(2)}, u32[]{:S(2)}) %collective-permute-start.7) | collective-permute-done | bytes 32800 | tf_op jit(solution)/shard_map/ppermute | solution.py:20
  33.2 0.6 %add_add_fusion = f32[32,256]{1,0:T(8,128)} fusion(f32[32,256]{1,0:T(8,128)S(1)} %collective-permute-done.9, f32[32,256]{1,0:T(8,128)S(1)} %collective-permute-done.8, f32[32,256]{1,0:T(8,128)S(1)} %get-tuple-element.49, f32[32,256]{1,0:T(8,128)S(1)} %collective-permute-done.7), kind=kLoop, calls=%fused_computation.1 | loop fusion | flops 24576 | bytes 163840 | tf_op jit(solution)/shard_map/add | solution.py:464
  (20 shorter events, 0.1 us)
Async XLA Ops:
  0.7 14.7 %copy-start = (f32[4,16,32,256]{3,2,1,0:T(8,128)S(1)}, f32[4,16,32,256]{3,2,1,0:T(8,128)}, u32[]{:S(2)}) copy-start(f32[4,16,32,256]{3,2,1,0:T(8,128)} %lam.1) | copy-start | bytes 6291460
  0.7 14.7 %copy-start.1 = (f32[16,32,256]{2,1,0:T(8,128)S(1)}, f32[16,32,256]{2,1,0:T(8,128)}, u32[]{:S(2)}) copy-start(f32[16,32,256]{2,1,0:T(8,128)} %ew.2) | copy-start | bytes 1572868
  0.7 14.7 %copy-start.2 = (f32[16,32,256]{2,1,0:T(8,128)S(1)}, f32[16,32,256]{2,1,0:T(8,128)}, u32[]{:S(2)}) copy-start(f32[16,32,256]{2,1,0:T(8,128)} %ed.2) | copy-start | bytes 1572868
  0.7 14.7 %copy-start.3 = (f32[16,32,256]{2,1,0:T(8,128)S(1)}, f32[16,32,256]{2,1,0:T(8,128)}, u32[]{:S(2)}) copy-start(f32[16,32,256]{2,1,0:T(8,128)} %nw.2) | copy-start | bytes 1572868
  0.7 14.7 %copy-start.4 = (f32[16,32,256]{2,1,0:T(8,128)S(1)}, f32[16,32,256]{2,1,0:T(8,128)}, u32[]{:S(2)}) copy-start(f32[16,32,256]{2,1,0:T(8,128)} %nd.2) | copy-start | bytes 1572868
  0.7 14.7 %copy-start.5 = (f32[16,32,256]{2,1,0:T(8,128)S(1)}, f32[16,32,256]{2,1,0:T(8,128)}, u32[]{:S(2)}) copy-start(f32[16,32,256]{2,1,0:T(8,128)} %mf.2) | copy-start | bytes 1572868
  0.8 14.7 %copy-start.6 = (s32[32,256]{1,0:T(8,128)S(1)}, s32[32,256]{1,0:T(8,128)}, u32[]{:S(2)}) copy-start(s32[32,256]{1,0:T(8,128)} %top.3) | copy-start | bytes 98308
  0.8 14.7 %copy-start.7 = (s32[32,256]{1,0:T(8,128)S(1)}, s32[32,256]{1,0:T(8,128)}, u32[]{:S(2)}) copy-start(s32[32,256]{1,0:T(8,128)} %region.3) | copy-start | bytes 98308
  3.5 9.8 %collective-permute-start.2 = (f32[4,16,256]{2,1,0:T(8,128)S(1)}, f32[4,16,256]{2,1,0:T(8,128)S(1)}, u32[]{:S(2)}, u32[]{:S(2)}) collective-permute-start(f32[4,16,256]{2,1,0:T(8,128)S(1)} %get-tuple-element.42), channel_id=1, source_target_pairs={{0,4},{4,0},{8,12},{12,8},{16,20},{20,16},{24,28},{28,24},{1,5},{5... | collective-permute-start | bytes 196616 | tf_op jit(solution)/shard_map/ppermute | solution.py:20
  6.5 7.0 %collective-permute-start.3 = (f32[4,16,256]{2,1,0:T(8,128)S(1)}, f32[4,16,256]{2,1,0:T(8,128)S(1)}, u32[]{:S(2)}, u32[]{:S(2)}) collective-permute-start(f32[4,16,256]{2,1,0:T(8,128)S(1)} %get-tuple-element.43), channel_id=1, source_target_pairs={{0,28},{4,8},{8,4},{12,16},{16,12},{20,24},{24,20},{28,0},{1,29},{... | collective-permute-start | bytes 196616 | tf_op jit(solution)/shard_map/ppermute | solution.py:20
  12.1 10.4 %collective-permute-start.1 = (f32[4,4,16,256]{3,2,1,0:T(8,128)S(1)}, f32[4,4,16,256]{3,2,1,0:T(8,128)S(1)}, u32[]{:S(2)}, u32[]{:S(2)}) collective-permute-start(f32[4,4,16,256]{3,2,1,0:T(8,128)S(1)} %get-tuple-element.41), channel_id=1, source_target_pairs={{0,28},{4,8},{8,4},{12,16},{16,12},{20,24},{24,20},{28,0},{1,29},{... | collective-permute-start | bytes 786440 | tf_op jit(solution)/shard_map/ppermute | solution.py:20
  13.4 12.8 %collective-permute-start = (f32[4,4,16,256]{3,2,1,0:T(8,128)S(1)}, f32[4,4,16,256]{3,2,1,0:T(8,128)S(1)}, u32[]{:S(2)}, u32[]{:S(2)}) collective-permute-start(f32[4,4,16,256]{3,2,1,0:T(8,128)S(1)} %get-tuple-element.40), channel_id=1, source_target_pairs={{0,4},{4,0},{8,12},{12,8},{16,20},{20,16},{24,28},{28,24},{1,5},{5... | collective-permute-start | bytes 786440 | tf_op jit(solution)/shard_map/ppermute | solution.py:20
  13.5 8.9 %collective-permute-start.6 = (f32[2,4,16,256]{3,2,1,0:T(8,128)S(1)}, f32[2,4,16,256]{3,2,1,0:T(8,128)S(1)}, u32[]{:S(2)}, u32[]{:S(2)}) collective-permute-start(f32[2,4,16,256]{3,2,1,0:T(8,128)S(1)} %pad_maximum_fusion.refs_0_), channel_id=1, source_target_pairs={{0,3},{1,2},{2,1},{3,0},{4,7},{5,6},{6,5},{7,4},{8,11},{9,10},{10,... | collective-permute-start | bytes 393224 | tf_op jit(solution)/shard_map/ppermute | solution.py:20
  13.6 8.8 %collective-permute-start.5 = (f32[2,4,16,256]{3,2,1,0:T(8,128)S(1)}, f32[2,4,16,256]{3,2,1,0:T(8,128)S(1)}, u32[]{:S(2)}, u32[]{:S(2)}) collective-permute-start(f32[2,4,16,256]{3,2,1,0:T(8,128)S(1)} %pad_maximum_fusion.refs_0_), channel_id=1, source_target_pairs={{0,2},{1,3},{2,0},{3,1},{4,6},{5,7},{6,4},{7,5},{8,10},{9,11},{10,... | collective-permute-start | bytes 393224 | tf_op jit(solution)/shard_map/ppermute | solution.py:20
  15.2 7.3 %collective-permute-start.4 = (f32[2,4,16,256]{3,2,1,0:T(8,128)S(1)}, f32[2,4,16,256]{3,2,1,0:T(8,128)S(1)}, u32[]{:S(2)}, u32[]{:S(2)}) collective-permute-start(f32[2,4,16,256]{3,2,1,0:T(8,128)S(1)} %pad_maximum_fusion.refs_0_), channel_id=1, source_target_pairs={{0,1},{1,0},{2,3},{3,2},{4,5},{5,4},{6,7},{7,6},{8,9},{9,8},{10,11... | collective-permute-start | bytes 393224 | tf_op jit(solution)/shard_map/ppermute | solution.py:20
  28.2 3.4 %collective-permute-start.9 = (f32[32,256]{1,0:T(8,128)S(1)}, f32[32,256]{1,0:T(8,128)S(1)}, u32[]{:S(2)}, u32[]{:S(2)}) collective-permute-start(f32[32,256]{1,0:T(8,128)S(1)} %get-tuple-element.49), channel_id=1, source_target_pairs={{0,3},{1,0},{2,1},{3,2},{4,7},{5,4},{6,5},{7,6},{8,11},{9,8},{10,9... | collective-permute-start | bytes 98312 | tf_op jit(solution)/shard_map/ppermute | solution.py:20
  28.3 4.1 %collective-permute-start.8 = (f32[32,256]{1,0:T(8,128)S(1)}, f32[32,256]{1,0:T(8,128)S(1)}, u32[]{:S(2)}, u32[]{:S(2)}) collective-permute-start(f32[32,256]{1,0:T(8,128)S(1)} %get-tuple-element.49), channel_id=1, source_target_pairs={{0,2},{1,3},{2,0},{3,1},{4,6},{5,7},{6,4},{7,5},{8,10},{9,11},{10,... | collective-permute-start | bytes 98312 | tf_op jit(solution)/shard_map/ppermute | solution.py:20
  29.8 3.3 %collective-permute-start.7 = (f32[32,256]{1,0:T(8,128)S(1)}, f32[32,256]{1,0:T(8,128)S(1)}, u32[]{:S(2)}, u32[]{:S(2)}) collective-permute-start(f32[32,256]{1,0:T(8,128)S(1)} %get-tuple-element.49), channel_id=1, source_target_pairs={{0,1},{1,2},{2,3},{3,0},{4,5},{5,6},{6,7},{7,4},{8,9},{9,10},{10,1... | collective-permute-start | bytes 98312 | tf_op jit(solution)/shard_map/ppermute | solution.py:20

commit v5 on v4

--- a/solution.py
+++ b/solution.py
@@ -12,6 +12,7 @@
 ENTRIES = 16
 CHUNKS = 3
 LANES = 128
+HALVES = (slice(0, LANES), slice(LANES, 2 * LANES))
 SHORT = pl.CostEstimate(flops=1000, bytes_accessed=1000, transcendentals=0)
 LOW, HIGH = 0, 1
 
@@ -49,10 +50,14 @@
 
 def advance(coefs, mid, east, west):
     d, e, w, n, s, u = coefs
-    levels, lats = mid.shape
-    half = levels // 2
+    half = mid.shape[0] // 2
     h = d * mid + e * east + w * west
-    h = h + n * pltpu.roll(mid, lats - 1, 1) + s * pltpu.roll(mid, 1, 1)
+    lane = lax.broadcasted_iota(jnp.int32, (mid.shape[0], LANES), 1)
+    north = [pltpu.roll(mid[:, part], LANES - 1, 1) for part in HALVES]
+    south = [pltpu.roll(mid[:, part], 1, 1) for part in HALVES]
+    north = jnp.concatenate([jnp.where(lane < LANES - 1, *north), north[1]], axis=1)
+    south = jnp.concatenate([south[0], jnp.where(lane > 0, south[1], south[0])], axis=1)
+    h = h + n * north + s * south
     above = jnp.concatenate([h[half:], pltpu.roll(h[:half], half - 1, 0)], axis=0)
     return h + u * (above - h)
 
@@ -66,8 +71,10 @@
     return jnp.concatenate(parts, axis=1)
 
 
-def pack_coefs_kernel(parts, place, ew, ed, nw, nd, mf, top, first, second, field_s, top_s, entry, field_p, sems):
-    levels, cols, lats = ew.shape
+def pack_kernel(parts, place, lam, ew, ed, nw, nd, mf, top, *refs):
+    coef_first, coef_second, lam_first, lam_second = refs[:4]
+    field_s, top_s, lam_s, entry, field_p, lam_p, sems = refs[4:]
+    tags, levels, cols, lats = lam.shape
     copies = []
 
     def copy(src, dst):
@@ -75,11 +82,13 @@
         copies[-1].start()
 
     for side, at in ((LOW, 0), (HIGH, cols - 8)):
+        for f, field in enumerate((ew, ed, nw, nd, mf)):
+            copy(field.at[:, pl.ds(at, 8)], field_s.at[f, side])
         copy(top.at[pl.ds(at, 8)], top_s.at[side])
-        for k in range(2):
-            for f, field in enumerate((ew, ed, nw, nd, mf)):
-                copy(field.at[:, pl.ds(at, 8), pl.ds(k * LANES, LANES)], field_s.at[f, side, k])
-    for c in copies:
+    field_copies = len(copies)
+    for side, at in ((LOW, 0), (HIGH, cols - 8)):
+        copy(lam.at[:, :, pl.ds(at, 8)], lam_s.at[side])
+    for c in copies[:field_copies]:
         c.wait()
     pitch = 9
     slab = levels * pitch
@@ -91,7 +100,7 @@
             for side in range(2):
                 for k in range(2):
                     at = ((f * 2 + side) * 2 + k) * slab
-                    field_p[pl.ds(at + row, 8), :] = field_s[f, side, k, level]
+                    field_p[pl.ds(at + row, 8), :] = field_s[f, side, level, :, HALVES[k]]
 
     def field(f, side, c):
         return column_at(field_p, (f * 2 + side) * 2 * slab + c, levels, pitch, slab)
@@ -112,84 +121,51 @@
     per = ENTRIES // parts
     mine = lax.rem(place[0], parts) * per
     odd = place[1]
-    first[...] = entry[1 - odd, pl.ds(mine, per)]
-    second[...] = entry[odd, pl.ds(mine, per)]
-
-
-def pack_coefs(parts, place, fields, top):
-    levels, cols, lats = fields[0].shape
-    hbm = pl.BlockSpec(memory_space=pltpu.HBM)
-    send = pltpu.VMEM((ENTRIES // parts, levels, lats), jnp.float32)
-    return pl.pallas_call(
-        functools.partial(pack_coefs_kernel, parts),
-        in_specs=[pl.BlockSpec(memory_space=pltpu.SMEM)] + [hbm] * 6,
-        out_specs=[pl.BlockSpec(memory_space=pltpu.VMEM)] * 2,
-        out_shape=[send, send],
-        scratch_shapes=[
-            pltpu.VMEM((5, 2, 2, levels, 8, LANES), jnp.float32),
-            pltpu.VMEM((2, 8, lats), jnp.int32),
-            pltpu.VMEM((2, ENTRIES, levels, lats), jnp.float32),
-            pltpu.VMEM((pitched(20, levels, 8), LANES), jnp.float32),
-            pltpu.SemaphoreType.DMA((22,)),
-        ],
-        compiler_params=pltpu.CompilerParams(vmem_limit_bytes=24 << 20),
-        cost_estimate=SHORT,
-        name="pack_coefs",
-    )(place, *fields, top)
-
-
-def pack_lam_kernel(place, lam, first, second, lam_s, lam_p, sems):
-    tags, levels, cols, lats = lam.shape
-    copies = []
-    for side, at in ((LOW, 0), (HIGH, cols - 8)):
-        for k in range(2):
-            copies.append(
-                pltpu.make_async_copy(
-                    lam.at[:, :, pl.ds(at, 8), pl.ds(k * LANES, LANES)],
-                    lam_s.at[side, k],
-                    sems.at[side * 2 + k],
-                )
-            )
-            copies[-1].start()
-    for c in copies:
+    coef_first[...] = entry[1 - odd, pl.ds(mine, per)]
+    coef_second[...] = entry[odd, pl.ds(mine, per)]
+
+    for c in copies[field_copies:]:
         c.wait()
-    pitch = 9
-    slab = levels * pitch
 
     @pl.loop(0, levels)
     def _(level):
         row = place_of(level, levels) * pitch
         for side in range(2):
-            for k in range(2):
-                for tag in range(tags):
+            for tag in range(tags):
+                for k in range(2):
                     at = ((side * 2 + k) * tags + tag) * slab
-                    lam_p[pl.ds(at + row, 8), :] = lam_s[side, k, tag, level]
-
-    odd = place[1]
-    for dest, side in ((first, 1 - odd), (second, odd)):
+                    lam_p[pl.ds(at + row, 8), :] = lam_s[side, tag, level, :, HALVES[k]]
+
+    for dest, side in ((lam_first, 1 - odd), (lam_second, odd)):
         start = side * (2 * tags * slab + 8 - EDGE)
         for tag in range(tags):
             for c in range(EDGE):
                 dest[tag, c] = column_at(lam_p, start + tag * slab + c, levels, pitch, tags * slab)
 
 
-def pack_lam(place, lam):
+def pack(parts, place, lam, fields, top):
     tags, levels, cols, lats = lam.shape
-    send = pltpu.VMEM((tags, EDGE, levels, lats), jnp.float32)
+    hbm = pl.BlockSpec(memory_space=pltpu.HBM)
+    coef_send = pltpu.VMEM((ENTRIES // parts, levels, lats), jnp.float32)
+    lam_send = pltpu.VMEM((tags, EDGE, levels, lats), jnp.float32)
     return pl.pallas_call(
-        pack_lam_kernel,
-        in_specs=[pl.BlockSpec(memory_space=pltpu.SMEM), pl.BlockSpec(memory_space=pltpu.HBM)],
-        out_specs=[pl.BlockSpec(memory_space=pltpu.VMEM)] * 2,
-        out_shape=[send, send],
+        functools.partial(pack_kernel, parts),
+        in_specs=[pl.BlockSpec(memory_space=pltpu.SMEM)] + [hbm] * 7,
+        out_specs=[pl.BlockSpec(memory_space=pltpu.VMEM)] * 4,
+        out_shape=[coef_send, coef_send, lam_send, lam_send],
         scratch_shapes=[
-            pltpu.VMEM((2, 2, tags, levels, 8, LANES), jnp.float32),
+            pltpu.VMEM((5, 2, levels, 8, lats), jnp.float32),
+            pltpu.VMEM((2, 8, lats), jnp.int32),
+            pltpu.VMEM((2, tags, levels, 8, lats), jnp.float32),
+            pltpu.VMEM((2, ENTRIES, levels, lats), jnp.float32),
+            pltpu.VMEM((pitched(20, levels, 8), LANES), jnp.float32),
             pltpu.VMEM((pitched(4 * tags, levels, 8), LANES), jnp.float32),
-            pltpu.SemaphoreType.DMA((4,)),
+            pltpu.SemaphoreType.DMA((14,)),
         ],
         compiler_params=pltpu.CompilerParams(vmem_limit_bytes=24 << 20),
         cost_estimate=SHORT,
-        name="pack_lam",
-    )(place, lam)
+        name="pack_edges",
+    )(place, lam, *fields, top)
 
 
 def chosen(region_row, first_tag, values):
@@ -227,26 +203,26 @@
     def store(c, tag, value):
         for k in range(2):
             at = (k * tags + tag) * levels * pitch + c
-            ref[pl.ds(at, levels, stride=pitch), :] = value[:, k * LANES : (k + 1) * LANES]
+            ref[pl.ds(at, levels, stride=pitch), :] = value[:, HALVES[k]]
 
     return store
 
 
-def inner_kernel(place, lam, ew, ed, nw, nd, mf, top, region, coef, l0, l1, l2, l3, final, rows, lam_p, field_p):
+def inner_kernel(place, lam, ew, ed, nw, nd, mf, top, region, *refs):
+    coef, l0, l1, l2, l3, final, rows, lam_s, lam_p, field_p, sems = refs
     tags, levels, cols, lats = lam.shape
     pitch = cols + 1
     slab = levels * pitch
-    halves = [slice(k * LANES, (k + 1) * LANES) for k in range(2)]
+    loads = [pltpu.make_async_copy(lam.at[k], lam_s.at[k], sems.at[k]) for k in range(tags)]
+    for c in loads:
+        c.start()
 
     @pl.loop(0, levels)
     def _(level):
         row = place_of(level, levels) * pitch
         for f, field in enumerate((ew, ed, nw, nd, mf)):
             for k in range(2):
-                field_p[pl.ds((f * 2 + k) * slab + row, cols), :] = field[level, :, halves[k]]
-        for tag in range(tags):
-            for k in range(2):
-                lam_p[pl.ds((k * tags + tag) * slab + row, cols), :] = lam[tag, level, :, halves[k]]
+                field_p[pl.ds((f * 2 + k) * slab + row, cols), :] = field[level, :, HALVES[k]]
 
     def coefficients(c, west):
         ew, ed, nw, nd, mf = (
@@ -262,12 +238,28 @@
         for j in range(8):
             c = i * 8 + j
             west = coefficients(c, west)
+        return west
+
+    west = lax.fori_loop(0, cols // 8, some, jnp.zeros((levels, lats), jnp.float32))
+    coef[cols, 2] = west
+    for c in loads:
+        c.wait()
+
+    @pl.loop(0, levels)
+    def _(level):
+        row = place_of(level, levels) * pitch
+        for tag in range(tags):
+            for k in range(2):
+                at = (k * tags + tag) * slab + row
+                lam_p[pl.ds(at, cols), :] = lam_s[tag, level, :, HALVES[k]]
+
+    @pl.loop(0, cols // 8)
+    def _(i):
+        for j in range(8):
+            c = i * 8 + j
             for tag in range(tags):
                 l0[c, tag] = column_at(lam_p, tag * slab + c, levels, pitch, tags * slab)
-        return west
-
-    west = lax.fori_loop(0, cols // 8, some, jnp.zeros((levels, lats), jnp.float32))
-    coef[cols, 2] = west
+
     first_tag = place[0] * tags
     sweep(0, first_tag, region, coef, l0, storing(l1), rows)
     sweep(1, first_tag, region, coef, l1, storing(l2), rows)
@@ -281,7 +273,11 @@
     state = pltpu.VMEM((cols, tags, levels, lats), jnp.float32)
     return pl.pallas_call(
         inner_kernel,
-        in_specs=[pl.BlockSpec(memory_space=pltpu.SMEM)] + [vmem] * 8,
+        in_specs=[
+            pl.BlockSpec(memory_space=pltpu.SMEM),
+            pl.BlockSpec(memory_space=pltpu.HBM),
+            *[vmem] * 7,
+        ],
         out_specs=[vmem] * 7,
         out_shape=[
             pltpu.VMEM((cols + 1, 6, levels, lats), jnp.float32),
@@ -290,8 +286,10 @@
             pltpu.VMEM((ITERS, cols, lats), jnp.float32),
         ],
         scratch_shapes=[
+            pltpu.VMEM(lam.shape, jnp.float32),
             pltpu.VMEM((pitched(2 * tags, levels, cols), LANES), jnp.float32),
             pltpu.VMEM((pitched(10, levels, cols), LANES), jnp.float32),
+            pltpu.SemaphoreType.DMA((tags,)),
         ],
         compiler_params=pltpu.CompilerParams(vmem_limit_bytes=32 << 20),
         cost_estimate=SHORT,
@@ -410,7 +408,7 @@
             row = place_of(level, levels) * pitch
             for k in range(2):
                 at = (k * tags + tag) * levels * pitch + row
-                block[tag, level, :, k * LANES : (k + 1) * LANES] = final[pl.ds(at, cols), :]
+                block[tag, level, :, HALVES[k]] = final[pl.ds(at, cols), :]
 
         copies.append(pltpu.make_async_copy(block.at[tag], out.at[tag], sems.at[tag]))
         copies[-1].start()
@@ -444,20 +442,15 @@
 
     pairs = lambda i: i ^ 1
     turn = lambda i: (((i - 1) % tiles ^ 1) + 1) % tiles
-    coef_first, coef_second = pack_coefs(parts, place, far[1:6], far[6])
-    coef_first, coef_second, far_lam, *own = lax.optimization_barrier(
-        (coef_first, coef_second, far[0], *own)
-    )
-    lam_first, lam_second = pack_lam(place, far_lam)
+    coef_first, coef_second, lam_first, lam_second = pack(parts, place, far[0], far[1:6], far[6])
     coef_first = swapped(coef_first, "dom", pairs)
     coef_second = swapped(coef_second, "dom", turn)
-    coef_first, coef_second, _ = lax.optimization_barrier((coef_first, coef_second, lam_first))
     first = swapped(lam_first, "dom", pairs)
     second = swapped(lam_second, "dom", turn)
     pieces = [jnp.stack([coef_first, coef_second])]
     for by in range(1, parts):
         pieces.append(swapped(pieces[0], "grp", lambda i: i ^ by))
-    coef, *states, final, rows = inner(place, own[0], own[1:], top, region)
+    coef, *states, final, rows = inner(place, far[0], own[1:], top, region)
     final, grad = border(parts, place, region, coef, states, first, second, pieces, final, rows)
     share = grad
     for by in range(1, groups):

time: 34 us -> 31.9 us (0.938)
  waiting for transfers between devices: 5.47 us -> 3.74 us
  Pallas kernels: 15.3 us -> 14.3 us
  starting transfers between devices: 11.5 us -> 12.2 us
    pallas_call x2 -> x1, Pallas kernels: 4.77 us -> 2.86 us  [pack(): pl.pallas_call(functools.partial(pack_kernel, parts), in_specs=[pl.BlockS...]
    ppermute x10, waiting for transfers between devices: 5.47 us -> 3.74 us  [swapped(): lax.ppermute(value, axis, [(i, partner(i)) for i in range(lax.axis_size(a...]
    pallas_call x1, Pallas kernels: 6.91 us -> 7.83 us  [inner(): pl.pallas_call(inner_kernel, in_specs=[pl.BlockSpec(memory_space=pltpu.SM...]
    ppermute x10, starting transfers between devices: 11.5 us -> 12.2 us  [swapped(): lax.ppermute(value, axis, [(i, partner(i)) for i in range(lax.axis_size(a...]
  transfers between devices with their start and end apart: 10 -> 10, of which waited for: 5 -> 4; matrix products, arithmetic and copies ran while one was open for 0% -> 0% of each run, Pallas kernels for 31% -> 30%
where the time goes in v5:
time: 31.9 us; the launch traced here: 31.7 us
  Pallas kernels  14.3 us (45%)
  starting transfers between devices  12.2 us (38%)
  waiting for transfers between devices  3.74 us (12%)
  between operations  0.77 us (2%)
  other arithmetic  0.71 us (2%)
    ppermute x10, starting transfers between devices, swapped(): lax.ppermute(value, axis, [(i, partner(i)) for i in range(lax.axis_size(a...  12.2 us
    pallas_call x1, Pallas kernels, inner(): pl.pallas_call(inner_kernel, in_specs=[pl.BlockSpec(memory_space=pltpu.SM...  7.83 us
    ppermute x10, waiting for transfers between devices, swapped(): lax.ppermute(value, axis, [(i, partner(i)) for i in range(lax.axis_size(a...  3.74 us
    pallas_call x1, Pallas kernels, pack(): pl.pallas_call(functools.partial(pack_kernel, parts), in_specs=[pl.BlockS...  2.86 us
    pallas_call x1, Pallas kernels, border(): pl.pallas_call(functools.partial(border_kernel, parts), in_specs=[pl.Bloc...  2 us
    pallas_call x1, Pallas kernels, write(): pl.pallas_call(write_kernel, in_specs=[pl.BlockSpec(memory_space=pltpu.VM...  1.57 us
  transfers between devices with their start and end apart: 10, of which 4 were waited for; matrix products, arithmetic and copies ran while one was open for 0% of the time, Pallas kernels for 30%

profile of v5, /device:TPU:0, one launch (start us, length us, event | category | flops | bytes accessed | tf_op | source)
XLA Modules:
  0.0 31.7 jit_solution(6413622831977244928)
XLA Ops:
  0.6 0.1 pad_add_fusion.place
  0.7 0.0 copy-start.4
  0.7 0.0 copy-start.5
  0.8 0.0 copy-start.6
  0.8 2.9 %pack_edges.1 = (f32[4,16,256]{2,1,0:T(8,128)S(1)}, f32[4,16,256]{2,1,0:T(8,128)S(1)}, f32[4,4,16,256]{3,2,1,0:T(8,128)S(1)}, f32[4,4,16,256]{3,2,1,0:T(8,128)S(1)}) custom-call(s32[2]{0:T(128)S(1)} %pad_add_fusion.place, f32[4,16,32,256]{3,2,1,0:T(8,128)} %lam.3, f32[16,32,256]{2,1,0:T(8,128)} %ew.3, f32[16,32,256]{2,1,0:T(8,128)} %ed.3, ...), custom_call_target="tpu_custom_call" | custom-call | flops 1000 | bytes 1000 | tf_op jit(solution)/shard_map/pack_edges/pallas_call | solution.py:151
  3.6 3.0 %collective-permute-start.2 = (f32[4,16,256]{2,1,0:T(8,128)S(1)}, f32[4,16,256]{2,1,0:T(8,128)S(1)}, u32[]{:S(2)}, u32[]{:S(2)}) collective-permute-start(f32[4,16,256]{2,1,0:T(8,128)S(1)} %get-tuple-element.22), channel_id=1, source_target_pairs={{0,4},{4,0},{8,12},{12,8},{16,20},{20,16},{24,28},{28,24},{1,5},{5... | collective-permute-start | bytes 196616 | tf_op jit(solution)/shard_map/ppermute | solution.py:21
  6.6 3.6 %collective-permute-start.3 = (f32[4,16,256]{2,1,0:T(8,128)S(1)}, f32[4,16,256]{2,1,0:T(8,128)S(1)}, u32[]{:S(2)}, u32[]{:S(2)}) collective-permute-start(f32[4,16,256]{2,1,0:T(8,128)S(1)} %get-tuple-element.23), channel_id=1, source_target_pairs={{0,28},{4,8},{8,4},{12,16},{16,12},{20,24},{24,20},{28,0},{1,29},{... | collective-permute-start | bytes 196616 | tf_op jit(solution)/shard_map/ppermute | solution.py:21
  10.2 1.9 %collective-permute-start.1 = (f32[4,4,16,256]{3,2,1,0:T(8,128)S(1)}, f32[4,4,16,256]{3,2,1,0:T(8,128)S(1)}, u32[]{:S(2)}, u32[]{:S(2)}) collective-permute-start(f32[4,4,16,256]{3,2,1,0:T(8,128)S(1)} %get-tuple-element.21), channel_id=1, source_target_pairs={{0,28},{4,8},{8,4},{12,16},{16,12},{20,24},{24,20},{28,0},{1,29},{... | collective-permute-start | bytes 786440 | tf_op jit(solution)/shard_map/ppermute | solution.py:21
  12.1 0.0 collective-permute-done.2
  12.1 1.6 %collective-permute-done.3 = f32[4,16,256]{2,1,0:T(8,128)S(1)} collective-permute-done((f32[4,16,256]{2,1,0:T(8,128)S(1)}, f32[4,16,256]{2,1,0:T(8,128)S(1)}, u32[]{:S(2)}, u32[]{:S(2)}) %collective-permute-start.3) | collective-permute-done | bytes 65568 | tf_op jit(solution)/shard_map/ppermute | solution.py:21
  13.7 0.1 collective-permute-start.6
  13.8 1.6 %collective-permute-start.5 = (f32[2,4,16,256]{3,2,1,0:T(8,128)S(1)}, f32[2,4,16,256]{3,2,1,0:T(8,128)S(1)}, u32[]{:S(2)}, u32[]{:S(2)}) collective-permute-start(f32[2,4,16,256]{3,2,1,0:T(8,128)S(1)} %pad_maximum_fusion.refs_0_), channel_id=1, source_target_pairs={{0,2},{1,3},{2,0},{3,1},{4,6},{5,7},{6,4},{7,5},{8,10},{9,11},{10,... | collective-permute-start | bytes 393224 | tf_op jit(solution)/shard_map/ppermute | solution.py:21
  15.4 0.3 collective-permute-start.4
  15.7 7.8 %inner_steps.1 = (f32[33,6,16,256]{3,2,1,0:T(8,128)S(1)}, f32[32,4,16,256]{3,2,1,0:T(8,128)S(1)}, f32[32,4,16,256]{3,2,1,0:T(8,128)S(1)}, f32[32,4,16,256]{3,2,1...) custom-call(s32[2]{0:T(128)S(1)} %pad_add_fusion.place, ...), custom_call_target="tpu_custom_call" | custom-call | flops 1000 | bytes 1000 | tf_op jit(solution)/shard_map/inner_steps/pallas_call | solution.py:274
  23.5 0.0 collective-permute-done.5.refs_2_
  23.6 0.6 %collective-permute-done.first = f32[4,4,16,256]{3,2,1,0:T(8,128)S(1)} collective-permute-done((f32[4,4,16,256]{3,2,1,0:T(8,128)S(1)}, f32[4,4,16,256]{3,2,1,0:T(8,128)S(1)}, u32[]{:S(2)}, u32[]{:S(2)}) %collective-permute-start) | collective-permute-done | bytes 262176 | tf_op jit(solution)/shard_map/ppermute | solution.py:21
  24.1 2.0 %border_steps.1 = (f32[4264,128]{1,0:T(8,128)S(1)}, f32[32,256]{1,0:T(8,128)S(1)}) custom-call(s32[2]{0:T(128)S(1)} %pad_add_fusion.place, s32[32,256]{1,0:T(8,128)S(1)} %copy-done.6, f32[33,6,16,256]{3,2,1,0:T(8,128)S(1)} %get-tuple-element.15.coef, f32[32,4,16,256]{3,2,1,0:T(8,128)S(1)} %get-tuple-element.16.l0, ...), custom_call_target="tpu_custom_call", output_to_operand_aliasing={{0}: (13, {})} | custom-call | flops 1000 | bytes 1000 | tf_op jit(solution)/shard_map/border_steps/pallas_call | solution.py:378
  26.1 0.7 %collective-permute-start.9 = (f32[32,256]{1,0:T(8,128)S(1)}, f32[32,256]{1,0:T(8,128)S(1)}, u32[]{:S(2)}, u32[]{:S(2)}) collective-permute-start(f32[32,256]{1,0:T(8,128)S(1)} %get-tuple-element.27), channel_id=1, source_target_pairs={{0,3},{1,0},{2,1},{3,2},{4,7},{5,4},{6,5},{7,6},{8,11},{9,8},{10,9... | collective-permute-start | bytes 98312 | tf_op jit(solution)/shard_map/ppermute | solution.py:21
  26.8 1.0 %collective-permute-start.8 = (f32[32,256]{1,0:T(8,128)S(1)}, f32[32,256]{1,0:T(8,128)S(1)}, u32[]{:S(2)}, u32[]{:S(2)}) collective-permute-start(f32[32,256]{1,0:T(8,128)S(1)} %get-tuple-element.27), channel_id=1, source_target_pairs={{0,2},{1,3},{2,0},{3,1},{4,6},{5,7},{6,4},{7,5},{8,10},{9,11},{10,... | collective-permute-start | bytes 98312 | tf_op jit(solution)/shard_map/ppermute | solution.py:21
  27.8 0.2 collective-permute-start.7
  27.9 1.6 %write_final.1 = f32[4,16,32,256]{3,2,1,0:T(8,128)} custom-call(f32[4264,128]{1,0:T(8,128)S(1)} %get-tuple-element.26.final), custom_call_target="tpu_custom_call" | custom-call | flops 1000 | bytes 1000 | tf_op jit(solution)/shard_map/write_final/pallas_call | solution.py:420
  29.5 1.2 %collective-permute-done.8 = f32[32,256]{1,0:T(8,128)S(1)} collective-permute-done((f32[32,256]{1,0:T(8,128)S(1)}, f32[32,256]{1,0:T(8,128)S(1)}, u32[]{:S(2)}, u32[]{:S(2)}) %collective-permute-start.8) | collective-permute-done | bytes 32800 | tf_op jit(solution)/shard_map/ppermute | solution.py:21
  30.7 0.4 %collective-permute-done.7 = f32[32,256]{1,0:T(8,128)S(1)} collective-permute-done((f32[32,256]{1,0:T(8,128)S(1)}, f32[32,256]{1,0:T(8,128)S(1)}, u32[]{:S(2)}, u32[]{:S(2)}) %collective-permute-start.7) | collective-permute-done | bytes 32800 | tf_op jit(solution)/shard_map/ppermute | solution.py:21
  31.1 0.6 %add_add_fusion = f32[32,256]{1,0:T(8,128)} fusion(f32[32,256]{1,0:T(8,128)S(1)} %collective-permute-done.9, f32[32,256]{1,0:T(8,128)S(1)} %collective-permute-done.8, f32[32,256]{1,0:T(8,128)S(1)} %get-tuple-element.27, f32[32,256]{1,0:T(8,128)S(1)} %collective-permute-done.7), kind=kLoop, calls=%fused_computation.1 | loop fusion | flops 24576 | bytes 163840 | tf_op jit(solution)/shard_map/add | solution.py:457
  (17 shorter events, 0.0 us)
Async XLA Ops:
  0.7 14.9 %copy-start = (f32[16,32,256]{2,1,0:T(8,128)S(1)}, f32[16,32,256]{2,1,0:T(8,128)}, u32[]{:S(2)}) copy-start(f32[16,32,256]{2,1,0:T(8,128)} %ew.3) | copy-start | bytes 1572868
  0.7 14.9 %copy-start.1 = (f32[16,32,256]{2,1,0:T(8,128)S(1)}, f32[16,32,256]{2,1,0:T(8,128)}, u32[]{:S(2)}) copy-start(f32[16,32,256]{2,1,0:T(8,128)} %ed.3) | copy-start | bytes 1572868
  0.7 14.9 %copy-start.2 = (f32[16,32,256]{2,1,0:T(8,128)S(1)}, f32[16,32,256]{2,1,0:T(8,128)}, u32[]{:S(2)}) copy-start(f32[16,32,256]{2,1,0:T(8,128)} %nw.3) | copy-start | bytes 1572868
  0.7 14.9 %copy-start.3 = (f32[16,32,256]{2,1,0:T(8,128)S(1)}, f32[16,32,256]{2,1,0:T(8,128)}, u32[]{:S(2)}) copy-start(f32[16,32,256]{2,1,0:T(8,128)} %nd.3) | copy-start | bytes 1572868
  0.7 14.9 %copy-start.4 = (f32[16,32,256]{2,1,0:T(8,128)S(1)}, f32[16,32,256]{2,1,0:T(8,128)}, u32[]{:S(2)}) copy-start(f32[16,32,256]{2,1,0:T(8,128)} %mf.3) | copy-start | bytes 1572868
  0.7 14.9 %copy-start.5 = (s32[32,256]{1,0:T(8,128)S(1)}, s32[32,256]{1,0:T(8,128)}, u32[]{:S(2)}) copy-start(s32[32,256]{1,0:T(8,128)} %top.3) | copy-start | bytes 98308
  0.8 14.9 %copy-start.6 = (s32[32,256]{1,0:T(8,128)S(1)}, s32[32,256]{1,0:T(8,128)}, u32[]{:S(2)}) copy-start(s32[32,256]{1,0:T(8,128)} %region.3) | copy-start | bytes 98308
  3.6 8.5 %collective-permute-start.2 = (f32[4,16,256]{2,1,0:T(8,128)S(1)}, f32[4,16,256]{2,1,0:T(8,128)S(1)}, u32[]{:S(2)}, u32[]{:S(2)}) collective-permute-start(f32[4,16,256]{2,1,0:T(8,128)S(1)} %get-tuple-element.22), channel_id=1, source_target_pairs={{0,4},{4,0},{8,12},{12,8},{16,20},{20,16},{24,28},{28,24},{1,5},{5... | collective-permute-start | bytes 196616 | tf_op jit(solution)/shard_map/ppermute | solution.py:21
  6.6 7.1 %collective-permute-start.3 = (f32[4,16,256]{2,1,0:T(8,128)S(1)}, f32[4,16,256]{2,1,0:T(8,128)S(1)}, u32[]{:S(2)}, u32[]{:S(2)}) collective-permute-start(f32[4,16,256]{2,1,0:T(8,128)S(1)} %get-tuple-element.23), channel_id=1, source_target_pairs={{0,28},{4,8},{8,4},{12,16},{16,12},{20,24},{24,20},{28,0},{1,29},{... | collective-permute-start | bytes 196616 | tf_op jit(solution)/shard_map/ppermute | solution.py:21
  10.2 13.9 %collective-permute-start = (f32[4,4,16,256]{3,2,1,0:T(8,128)S(1)}, f32[4,4,16,256]{3,2,1,0:T(8,128)S(1)}, u32[]{:S(2)}, u32[]{:S(2)}) collective-permute-start(f32[4,4,16,256]{3,2,1,0:T(8,128)S(1)} %get-tuple-element.20), channel_id=1, source_target_pairs={{0,4},{4,0},{8,12},{12,8},{16,20},{20,16},{24,28},{28,24},{1,5},{5... | collective-permute-start | bytes 786440 | tf_op jit(solution)/shard_map/ppermute | solution.py:21
  10.2 13.9 %collective-permute-start.1 = (f32[4,4,16,256]{3,2,1,0:T(8,128)S(1)}, f32[4,4,16,256]{3,2,1,0:T(8,128)S(1)}, u32[]{:S(2)}, u32[]{:S(2)}) collective-permute-start(f32[4,4,16,256]{3,2,1,0:T(8,128)S(1)} %get-tuple-element.21), channel_id=1, source_target_pairs={{0,28},{4,8},{8,4},{12,16},{16,12},{20,24},{24,20},{28,0},{1,29},{... | collective-permute-start | bytes 786440 | tf_op jit(solution)/shard_map/ppermute | solution.py:21
  13.7 9.8 %collective-permute-start.6 = (f32[2,4,16,256]{3,2,1,0:T(8,128)S(1)}, f32[2,4,16,256]{3,2,1,0:T(8,128)S(1)}, u32[]{:S(2)}, u32[]{:S(2)}) collective-permute-start(f32[2,4,16,256]{3,2,1,0:T(8,128)S(1)} %pad_maximum_fusion.refs_0_), channel_id=1, source_target_pairs={{0,3},{1,2},{2,1},{3,0},{4,7},{5,6},{6,5},{7,4},{8,11},{9,10},{10,... | collective-permute-start | bytes 393224 | tf_op jit(solution)/shard_map/ppermute | solution.py:21
  13.8 9.7 %collective-permute-start.5 = (f32[2,4,16,256]{3,2,1,0:T(8,128)S(1)}, f32[2,4,16,256]{3,2,1,0:T(8,128)S(1)}, u32[]{:S(2)}, u32[]{:S(2)}) collective-permute-start(f32[2,4,16,256]{3,2,1,0:T(8,128)S(1)} %pad_maximum_fusion.refs_0_), channel_id=1, source_target_pairs={{0,2},{1,3},{2,0},{3,1},{4,6},{5,7},{6,4},{7,5},{8,10},{9,11},{10,... | collective-permute-start | bytes 393224 | tf_op jit(solution)/shard_map/ppermute | solution.py:21
  15.4 8.2 %collective-permute-start.4 = (f32[2,4,16,256]{3,2,1,0:T(8,128)S(1)}, f32[2,4,16,256]{3,2,1,0:T(8,128)S(1)}, u32[]{:S(2)}, u32[]{:S(2)}) collective-permute-start(f32[2,4,16,256]{3,2,1,0:T(8,128)S(1)} %pad_maximum_fusion.refs_0_), channel_id=1, source_target_pairs={{0,1},{1,0},{2,3},{3,2},{4,5},{5,4},{6,7},{7,6},{8,9},{9,8},{10,11... | collective-permute-start | bytes 393224 | tf_op jit(solution)/shard_map/ppermute | solution.py:21
  26.1 3.4 %collective-permute-start.9 = (f32[32,256]{1,0:T(8,128)S(1)}, f32[32,256]{1,0:T(8,128)S(1)}, u32[]{:S(2)}, u32[]{:S(2)}) collective-permute-start(f32[32,256]{1,0:T(8,128)S(1)} %get-tuple-element.27), channel_id=1, source_target_pairs={{0,3},{1,0},{2,1},{3,2},{4,7},{5,4},{6,5},{7,6},{8,11},{9,8},{10,9... | collective-permute-start | bytes 98312 | tf_op jit(solution)/shard_map/ppermute | solution.py:21
  26.8 3.9 %collective-permute-start.8 = (f32[32,256]{1,0:T(8,128)S(1)}, f32[32,256]{1,0:T(8,128)S(1)}, u32[]{:S(2)}, u32[]{:S(2)}) collective-permute-start(f32[32,256]{1,0:T(8,128)S(1)} %get-tuple-element.27), channel_id=1, source_target_pairs={{0,2},{1,3},{2,0},{3,1},{4,6},{5,7},{6,4},{7,5},{8,10},{9,11},{10,... | collective-permute-start | bytes 98312 | tf_op jit(solution)/shard_map/ppermute | solution.py:21
  27.8 3.3 %collective-permute-start.7 = (f32[32,256]{1,0:T(8,128)S(1)}, f32[32,256]{1,0:T(8,128)S(1)}, u32[]{:S(2)}, u32[]{:S(2)}) collective-permute-start(f32[32,256]{1,0:T(8,128)S(1)} %get-tuple-element.27), channel_id=1, source_target_pairs={{0,1},{1,2},{2,3},{3,0},{4,5},{5,6},{6,7},{7,4},{8,9},{9,10},{10,1... | collective-permute-start | bytes 98312 | tf_op jit(solution)/shard_map/ppermute | solution.py:21

commit v6 on v5

--- a/solution.py
+++ b/solution.py
@@ -140,19 +140,19 @@
         start = side * (2 * tags * slab + 8 - EDGE)
         for tag in range(tags):
             for c in range(EDGE):
-                dest[tag, c] = column_at(lam_p, start + tag * slab + c, levels, pitch, tags * slab)
+                dest[tag * EDGE + c] = column_at(lam_p, start + tag * slab + c, levels, pitch, tags * slab)
 
 
 def pack(parts, place, lam, fields, top):
     tags, levels, cols, lats = lam.shape
     hbm = pl.BlockSpec(memory_space=pltpu.HBM)
-    coef_send = pltpu.VMEM((ENTRIES // parts, levels, lats), jnp.float32)
-    lam_send = pltpu.VMEM((tags, EDGE, levels, lats), jnp.float32)
+    send = lambda slabs: pltpu.VMEM((slabs, levels, lats), jnp.float32)
+    few, many = ENTRIES // parts, tags * EDGE
     return pl.pallas_call(
         functools.partial(pack_kernel, parts),
         in_specs=[pl.BlockSpec(memory_space=pltpu.SMEM)] + [hbm] * 7,
         out_specs=[pl.BlockSpec(memory_space=pltpu.VMEM)] * 4,
-        out_shape=[coef_send, coef_send, lam_send, lam_send],
+        out_shape=[send(few), send(few), send(many), send(many)],
         scratch_shapes=[
             pltpu.VMEM((5, 2, levels, 8, lats), jnp.float32),
             pltpu.VMEM((2, 8, lats), jnp.int32),
@@ -175,21 +175,29 @@
     return row
 
 
-def sweep(t, first_tag, region, coef, src, store, rows):
-    cols, tags = src.shape[:2]
+def sweep(t, shape, first_tag, region, coef, load, store, rows):
+    tags, _, cols, _ = shape
     low, high = t + 1, cols - t - 1
     chunk = -(-(high - low) // CHUNKS)
+    column = lambda c: [load(c, k) for k in range(tags)]
 
     @pl.loop(0, CHUNKS)
     def _(i):
         start = jnp.minimum(low + i * chunk, high - chunk)
+        west, mid = column(start - 1), column(start)
         for j in range(chunk):
             c = start + j
+            east = column(c + 1)
             coefs = [coef[c, n] for n in range(6)]
-            new = [advance(coefs, src[c, k], src[c + 1, k], src[c - 1, k]) for k in range(tags)]
+            new = [advance(coefs, mid[k], east[k], west[k]) for k in range(tags)]
             for k in range(tags):
                 store(c, k, new[k])
             rows[t, pl.ds(c, 1), :] = chosen(region[pl.ds(c, 1), :], first_tag, new)
+            west, mid = mid, east
+
+
+def loading(ref):
+    return lambda c, tag: ref[c, tag]
 
 
 def storing(ref):
@@ -209,13 +217,10 @@
 
 
 def inner_kernel(place, lam, ew, ed, nw, nd, mf, top, region, *refs):
-    coef, l0, l1, l2, l3, final, rows, lam_s, lam_p, field_p, sems = refs
+    coef, l0, l1, l2, l3, final, rows, lam_p, field_p = refs
     tags, levels, cols, lats = lam.shape
     pitch = cols + 1
     slab = levels * pitch
-    loads = [pltpu.make_async_copy(lam.at[k], lam_s.at[k], sems.at[k]) for k in range(tags)]
-    for c in loads:
-        c.start()
 
     @pl.loop(0, levels)
     def _(level):
@@ -223,6 +228,10 @@
         for f, field in enumerate((ew, ed, nw, nd, mf)):
             for k in range(2):
                 field_p[pl.ds((f * 2 + k) * slab + row, cols), :] = field[level, :, HALVES[k]]
+        for tag in range(tags):
+            for k in range(2):
+                at = (k * tags + tag) * slab + row
+                lam_p[pl.ds(at, cols), :] = lam[tag, level, :, HALVES[k]]
 
     def coefficients(c, west):
         ew, ed, nw, nd, mf = (
@@ -236,35 +245,23 @@
 
     def some(i, west):
         for j in range(8):
-            c = i * 8 + j
-            west = coefficients(c, west)
+            west = coefficients(i * 8 + j, west)
         return west
 
     west = lax.fori_loop(0, cols // 8, some, jnp.zeros((levels, lats), jnp.float32))
     coef[cols, 2] = west
-    for c in loads:
-        c.wait()
-
-    @pl.loop(0, levels)
-    def _(level):
-        row = place_of(level, levels) * pitch
+
+    def given(c, tag):
+        return column_at(lam_p, tag * slab + c, levels, pitch, tags * slab)
+
+    for at, c in enumerate((0, 1, cols - 2, cols - 1)):
         for tag in range(tags):
-            for k in range(2):
-                at = (k * tags + tag) * slab + row
-                lam_p[pl.ds(at, cols), :] = lam_s[tag, level, :, HALVES[k]]
-
-    @pl.loop(0, cols // 8)
-    def _(i):
-        for j in range(8):
-            c = i * 8 + j
-            for tag in range(tags):
-                l0[c, tag] = column_at(lam_p, tag * slab + c, levels, pitch, tags * slab)
-
-    first_tag = place[0] * tags
-    sweep(0, first_tag, region, coef, l0, storing(l1), rows)
-    sweep(1, first_tag, region, coef, l1, storing(l2), rows)
-    sweep(2, first_tag, region, coef, l2, storing(l3), rows)
-    sweep(3, first_tag, region, coef, l3, storing_rows(final, tags, levels, pitch), rows)
+            l0[at, tag] = given(c, tag)
+    last = storing_rows(final, tags, levels, pitch)
+    loads = (given, loading(l1), loading(l2), loading(l3))
+    stores = (storing(l1), storing(l2), storing(l3), last)
+    for t in range(ITERS):
+        sweep(t, lam.shape, place[0] * tags, region, coef, loads[t], stores[t], rows)
 
 
 def inner(place, lam, fields, top, region):
@@ -273,23 +270,18 @@
     state = pltpu.VMEM((cols, tags, levels, lats), jnp.float32)
     return pl.pallas_call(
         inner_kernel,
-        in_specs=[
-            pl.BlockSpec(memory_space=pltpu.SMEM),
-            pl.BlockSpec(memory_space=pltpu.HBM),
-            *[vmem] * 7,
-        ],
+        in_specs=[pl.BlockSpec(memory_space=pltpu.SMEM)] + [vmem] * 8,
         out_specs=[vmem] * 7,
         out_shape=[
             pltpu.VMEM((cols + 1, 6, levels, lats), jnp.float32),
-            *[state] * 4,
+            pltpu.VMEM((4, tags, levels, lats), jnp.float32),
+            *[state] * 3,
             pltpu.VMEM((pitched(2 * tags, levels, cols), LANES), jnp.float32),
             pltpu.VMEM((ITERS, cols, lats), jnp.float32),
         ],
         scratch_shapes=[
-            pltpu.VMEM(lam.shape, jnp.float32),
             pltpu.VMEM((pitched(2 * tags, levels, cols), LANES), jnp.float32),
             pltpu.VMEM((pitched(10, levels, cols), LANES), jnp.float32),
-            pltpu.SemaphoreType.DMA((tags,)),
         ],
         compiler_params=pltpu.CompilerParams(vmem_limit_bytes=32 << 20),
         cost_estimate=SHORT,
@@ -297,23 +289,19 @@
     )(place, lam, *fields, top, region)
 
 
-def border_kernel(parts, place, region, coef, l0, l1, l2, l3, first, second, *refs):
-    pieces = refs[:parts]
-    final_in, rows_in, final, grad, entry, halo, wide, work, rows = refs[parts:]
-    cols, tags, levels, lats = l0.shape
-    first_tag = place[0] * tags
+def slot(c, cols):
+    return (LOW, c + EDGE - 1) if c < EDGE else (HIGH, c - (cols - EDGE))
+
+
+def outer_kernel(parts, cols, place, coef, *refs):
+    pieces, wide, entry = refs[:parts], refs[parts], refs[parts + 1]
     per = ENTRIES // parts
     mine = lax.rem(place[0], parts)
     odd = place[1]
-    halo[1 - odd] = first[...]
-    halo[odd] = second[...]
     for by in range(parts):
         base = (mine ^ by) * per
         entry[1 - odd, pl.ds(base, per)] = pieces[by][0]
         entry[odd, pl.ds(base, per)] = pieces[by][1]
-
-    def slot(c):
-        return (LOW, c + EDGE - 1) if c < EDGE else (HIGH, c - (cols - EDGE))
 
     def outside(c):
         if c < 0:
@@ -324,59 +312,90 @@
             at = 5 * (c - cols)
             e, _, n, s, u = (entry[HIGH, at + j] for j in range(5))
             w = entry[HIGH, at - 4] if c > cols else coef[cols, 2]
-        return 1.0 - e - w - n - s, e, w, n, s, u
-
-    for c in [*range(1 - EDGE, 0), *range(cols, cols + EDGE - 1)]:
-        for j, value in enumerate(outside(c)):
-            wide[*slot(c), j] = value
+        return e, w, n, s, u
+
     first_west = entry[LOW, 1 + 5 * (EDGE - 2) + 1]
-    first_mid = 1.0 - coef[0, 1] - first_west - coef[0, 3] - coef[0, 4]
-    for j, value in enumerate((first_mid, coef[0, 1], first_west, *(coef[0, j] for j in range(3, 6)))):
-        wide[*slot(0), j] = value
+    for c in [*range(1 - EDGE, 1), *range(cols, cols + EDGE - 1)]:
+        if c == 0:
+            e, w, n, s, u = coef[0, 1], first_west, coef[0, 3], coef[0, 4], coef[0, 5]
+        else:
+            e, w, n, s, u = outside(c)
+        for j, value in enumerate((1.0 - e - w - n - s, e, w, n, s, u)):
+            wide[*slot(c, cols), j] = value
+
+
+def outer_coefs(parts, cols, place, coef, pieces):
+    _, _, levels, lats = coef.shape
+    vmem = pl.BlockSpec(memory_space=pltpu.VMEM)
+    return pl.pallas_call(
+        functools.partial(outer_kernel, parts, cols),
+        in_specs=[pl.BlockSpec(memory_space=pltpu.SMEM)] + [vmem] * (1 + parts),
+        out_specs=vmem,
+        out_shape=pltpu.VMEM((2, 2 * EDGE - 1, 6, levels, lats), jnp.float32),
+        scratch_shapes=[pltpu.VMEM((2, ENTRIES, levels, lats), jnp.float32)],
+        compiler_params=pltpu.CompilerParams(vmem_limit_bytes=24 << 20),
+        cost_estimate=SHORT,
+        name="outer_coefs",
+    )(place, coef, *pieces)
+
+
+def border_kernel(place, region, coef, wide, l0, l1, l2, l3, first, second, *refs):
+    final_in, rows_in, final, grad, halo, work, rows = refs
+    cols, tags, levels, lats = l1.shape
+    first_tag = place[0] * tags
+    odd = place[1]
+    halo[1 - odd] = first[...]
+    halo[odd] = second[...]
 
     def coefs_at(c):
         if 0 < c < cols:
             return [coef[c, j] for j in range(6)]
-        return [wide[*slot(c), j] for j in range(6)]
-
-    kept = (l0, l1, l2, l3)
+        return [wide[*slot(c, cols), j] for j in range(6)]
+
+    kept = (None, l1, l2, l3)
 
     def state(t, c, tag):
-        if t <= c < cols - t:
-            return kept[t][c, tag]
         if t == 0:
-            return halo[LOW, tag, c + EDGE] if c < 0 else halo[HIGH, tag, c - cols]
-        return work[t, *slot(c), tag]
+            if c < 0:
+                return halo[LOW, tag * EDGE + c + EDGE]
+            if c >= cols:
+                return halo[HIGH, tag * EDGE + c - cols]
+            return l0[c if c < 2 else c - (cols - 4), tag]
+        return kept[t][c, tag] if t <= c < cols - t else work[t, *slot(c, cols), tag]
+
+    def column(t, c):
+        return [state(t, c, tag) for tag in range(tags)]
 
     rows[...] = rows_in[...]
     store = storing_rows(final, tags, levels, cols + 1)
     for t in range(ITERS):
         reach = EDGE - 1 - t
-        for c in [*range(-reach, t + 1), *range(cols - t - 1, cols + reach)]:
-            coefs = coefs_at(c)
-            new = [
-                advance(coefs, state(t, c, k), state(t, c + 1, k), state(t, c - 1, k))
-                for k in range(tags)
-            ]
-            for k in range(tags):
-                if t < ITERS - 1:
-                    work[t + 1, *slot(c), k] = new[k]
-                else:
-                    store(c, k, new[k])
-            if 0 <= c < cols:
-                rows[t, c : c + 1, :] = chosen(region[c : c + 1, :], first_tag, new)
+        for run in (range(-reach, t + 1), range(cols - t - 1, cols + reach)):
+            west, mid = column(t, run[0] - 1), column(t, run[0])
+            for c in run:
+                east = column(t, c + 1)
+                coefs = coefs_at(c)
+                new = [advance(coefs, mid[k], east[k], west[k]) for k in range(tags)]
+                for k in range(tags):
+                    if t < ITERS - 1:
+                        work[t + 1, *slot(c, cols), k] = new[k]
+                    else:
+                        store(c, k, new[k])
+                if 0 <= c < cols:
+                    rows[t, c : c + 1, :] = chosen(region[c : c + 1, :], first_tag, new)
+                west, mid = mid, east
     total = rows[0]
     for t in range(1, ITERS):
         total = total + rows[t]
     grad[...] = total
 
 
-def border(parts, place, region, coef, states, first, second, pieces, final, rows):
-    cols, tags, levels, lats = states[0].shape
+def border(place, region, coef, wide, states, first, second, final, rows):
+    cols, tags, levels, lats = states[1].shape
     vmem = pl.BlockSpec(memory_space=pltpu.VMEM)
-    operands = [region, coef, *states, first, second, *pieces]
+    operands = [region, coef, wide, *states, first, second]
     return pl.pallas_call(
-        functools.partial(border_kernel, parts),
+        border_kernel,
         in_specs=[pl.BlockSpec(memory_space=pltpu.SMEM)] + [vmem] * (len(operands) + 2),
         out_specs=[vmem] * 2,
         out_shape=[
@@ -385,9 +404,7 @@
         ],
         input_output_aliases={len(operands) + 1: 0},
         scratch_shapes=[
-            pltpu.VMEM((2, ENTRIES, levels, lats), jnp.float32),
-            pltpu.VMEM((2, tags, EDGE, levels, lats), jnp.float32),
-            pltpu.VMEM((2, 2 * EDGE - 1, 6, levels, lats), jnp.float32),
+            pltpu.VMEM((2, tags * EDGE, levels, lats), jnp.float32),
             pltpu.VMEM((ITERS, 2, 2 * EDGE - 1, tags, levels, lats), jnp.float32),
             pltpu.VMEM((ITERS, cols, lats), jnp.float32),
         ],
@@ -442,16 +459,17 @@
 
     pairs = lambda i: i ^ 1
     turn = lambda i: (((i - 1) % tiles ^ 1) + 1) % tiles
-    coef_first, coef_second, lam_first, lam_second = pack(parts, place, far[0], far[1:6], far[6])
+    coef_first, coef_second, first, second = pack(parts, place, far[0], far[1:6], far[6])
     coef_first = swapped(coef_first, "dom", pairs)
     coef_second = swapped(coef_second, "dom", turn)
-    first = swapped(lam_first, "dom", pairs)
-    second = swapped(lam_second, "dom", turn)
+    first = swapped(first, "dom", pairs)
+    second = swapped(second, "dom", turn)
     pieces = [jnp.stack([coef_first, coef_second])]
     for by in range(1, parts):
         pieces.append(swapped(pieces[0], "grp", lambda i: i ^ by))
-    coef, *states, final, rows = inner(place, far[0], own[1:], top, region)
-    final, grad = border(parts, place, region, coef, states, first, second, pieces, final, rows)
+    coef, *states, final, rows = inner(place, own[0], own[1:], top, region)
+    wide = outer_coefs(parts, lam.shape[2], place, coef, pieces)
+    final, grad = border(place, region, coef, wide, states, first, second, final, rows)
     share = grad
     for by in range(1, groups):
         grad = grad + swapped(share, "grp", lambda i: (i + by) % groups)

time: 31.9 us -> 32 us (level)
  Pallas kernels: 14.3 us -> 13.8 us
  waiting for transfers between devices: 3.74 us -> 4.24 us
    pallas_call x1, Pallas kernels: 7.83 us -> 6.68 us  [inner(): pl.pallas_call(inner_kernel, in_specs=[pl.BlockSpec(memory_space=pltpu.SM...]
    pallas_call x1 -> x2, Pallas kernels: 2 us -> 2.64 us  [the longest x1 2.01 us: border(): pl.pallas_call(border_kernel, in_specs=[pl.BlockSpec(memory_space=pltpu.S...]
    ppermute x10, waiting for transfers between devices: 3.74 us -> 4.24 us  [swapped(): lax.ppermute(value, axis, [(i, partner(i)) for i in range(lax.axis_size(a...]
  transfers between devices with their start and end apart: 10 -> 10, of which waited for: 4 -> 4; matrix products, arithmetic and copies ran while one was open for 0% -> 0% of each run, Pallas kernels for 30% -> 28%
where the time goes in v6:
time: 32 us; the launch traced here: 31.8 us
  Pallas kernels  13.8 us (43%)
  starting transfers between devices  12.2 us (38%)
  waiting for transfers between devices  4.24 us (13%)
  between operations  0.8 us (2%)
  other arithmetic  0.71 us (2%)
    ppermute x10, starting transfers between devices, swapped(): lax.ppermute(value, axis, [(i, partner(i)) for i in range(lax.axis_size(a...  12.2 us
    pallas_call x1, Pallas kernels, inner(): pl.pallas_call(inner_kernel, in_specs=[pl.BlockSpec(memory_space=pltpu.SM...  6.68 us
    ppermute x10, waiting for transfers between devices, swapped(): lax.ppermute(value, axis, [(i, partner(i)) for i in range(lax.axis_size(a...  4.24 us
    pallas_call x1, Pallas kernels, pack(): pl.pallas_call(functools.partial(pack_kernel, parts), in_specs=[pl.BlockS...  2.93 us
    pallas_call x1, Pallas kernels, border(): pl.pallas_call(border_kernel, in_specs=[pl.BlockSpec(memory_space=pltpu.S...  2.01 us
    pallas_call x1, Pallas kernels, write(): pl.pallas_call(write_kernel, in_specs=[pl.BlockSpec(memory_space=pltpu.VM...  1.57 us
  transfers between devices with their start and end apart: 10, of which 4 were waited for; matrix products, arithmetic and copies ran while one was open for 0% of the time, Pallas kernels for 28%

profile of v6, /device:TPU:0, one launch (start us, length us, event | category | flops | bytes accessed | tf_op | source)
XLA Modules:
  0.0 31.8 jit_solution(14067914321374658795)
XLA Ops:
  0.6 0.1 pad_add_fusion.place
  0.7 0.0 copy-start.4
  0.7 0.0 copy-start.5
  0.8 0.0 copy-start.6
  0.8 0.0 copy-start.7
  0.8 2.9 %pack_edges.1 = (f32[4,16,256]{2,1,0:T(8,128)S(1)}, f32[4,16,256]{2,1,0:T(8,128)S(1)}, f32[16,16,256]{2,1,0:T(8,128)S(1)}, f32[16,16,256]{2,1,0:T(8,128)S(1)}) custom-call(s32[2]{0:T(128)S(1)} %pad_add_fusion.place, f32[4,16,32,256]{3,2,1,0:T(8,128)} %lam.3, f32[16,32,256]{2,1,0:T(8,128)} %ew.3, f32[16,32,256]{2,1,0:T(8,128)} %ed.3, f32[16,32,256]{2,1,0:T(8,128)} %nw.3, ...), custom_call_target="tpu_custom_call" | custom-call | flops 1000 | bytes 1000 | tf_op jit(solution)/shard_map/pack_edges/pallas_call | solution.py:151
  3.7 3.0 %collective-permute-start = (f32[4,16,256]{2,1,0:T(8,128)S(1)}, f32[4,16,256]{2,1,0:T(8,128)S(1)}, u32[]{:S(2)}, u32[]{:S(2)}) collective-permute-start(f32[4,16,256]{2,1,0:T(8,128)S(1)} %get-tuple-element.16), channel_id=1, source_target_pairs={{0,4},{4,0},{8,12},{12,8},{16,20},{20,16},{24,28},{28,24},{1,5},{5... | collective-permute-start | bytes 196616 | tf_op jit(solution)/shard_map/ppermute | solution.py:21
  6.7 3.6 %collective-permute-start.1 = (f32[4,16,256]{2,1,0:T(8,128)S(1)}, f32[4,16,256]{2,1,0:T(8,128)S(1)}, u32[]{:S(2)}, u32[]{:S(2)}) collective-permute-start(f32[4,16,256]{2,1,0:T(8,128)S(1)} %get-tuple-element.17), channel_id=1, source_target_pairs={{0,28},{4,8},{8,4},{12,16},{16,12},{20,24},{24,20},{28,0},{1,29},{... | collective-permute-start | bytes 196616 | tf_op jit(solution)/shard_map/ppermute | solution.py:21
  10.3 1.9 %collective-permute-start.6 = (f32[16,16,256]{2,1,0:T(8,128)S(1)}, f32[16,16,256]{2,1,0:T(8,128)S(1)}, u32[]{:S(2)}, u32[]{:S(2)}) collective-permute-start(f32[16,16,256]{2,1,0:T(8,128)S(1)} %get-tuple-element.23), channel_id=1, source_target_pairs={{0,28},{4,8},{8,4},{12,16},{16,12},{20,24},{24,20},{28,0},{1,29},{... | collective-permute-start | bytes 786440 | tf_op jit(solution)/shard_map/ppermute | solution.py:21
  12.2 1.6 %collective-permute-done.1 = f32[4,16,256]{2,1,0:T(8,128)S(1)} collective-permute-done((f32[4,16,256]{2,1,0:T(8,128)S(1)}, f32[4,16,256]{2,1,0:T(8,128)S(1)}, u32[]{:S(2)}, u32[]{:S(2)}) %collective-permute-start.1) | collective-permute-done | bytes 65568 | tf_op jit(solution)/shard_map/ppermute | solution.py:21
  13.8 0.1 collective-permute-start.4
  13.9 1.6 %collective-permute-start.3 = (f32[2,4,16,256]{3,2,1,0:T(8,128)S(1)}, f32[2,4,16,256]{3,2,1,0:T(8,128)S(1)}, u32[]{:S(2)}, u32[]{:S(2)}) collective-permute-start(f32[2,4,16,256]{3,2,1,0:T(8,128)S(1)} %pad_maximum_fusion.refs_0_), channel_id=1, source_target_pairs={{0,2},{1,3},{2,0},{3,1},{4,6},{5,7},{6,4},{7,5},{8,10},{9,11},{10,... | collective-permute-start | bytes 393224 | tf_op jit(solution)/shard_map/ppermute | solution.py:21
  15.5 0.3 collective-permute-start.2
  15.8 6.7 %inner_steps.1 = (f32[33,6,16,256]{3,2,1,0:T(8,128)S(1)}, f32[4,4,16,256]{3,2,1,0:T(8,128)S(1)}, f32[32,4,16,256]{3,2,1,0:T(8,128)S(1)}, f32[32,4,16,256]{3,2,1,...) custom-call(s32[2]{0:T(128)S(1)} %pad_add_fusion.place, ...), custom_call_target="tpu_custom_call" | custom-call | flops 1000 | bytes 1000 | tf_op jit(solution)/shard_map/inner_steps/pallas_call | solution.py:271
  22.5 0.6 %outer_coefs.1.wide = f32[2,7,6,16,256]{4,3,2,1,0:T(8,128)S(1)} custom-call(s32[2]{0:T(128)S(1)} %pad_add_fusion.place, f32[33,6,16,256]{3,2,1,0:T(8,128)S(1)} %get-tuple-element.15.coef, f32[2,4,16,256]{3,2,1,0:T(8,128)S(1)} %pad_maximum_fusion.refs_0_, f32[2,4,16,256]{3,2,1,0:T(8,128)S(1)} %collective-permute-done.2.refs_1_, ...), custom_call_target="tpu_custom_call" | custom-call | flops 1000 | bytes 1000 | tf_op jit(solution)/shard_map/outer_coefs/pallas_call | solution.py:330
  23.1 1.1 %collective-permute-done.5.first = f32[16,16,256]{2,1,0:T(8,128)S(1)} collective-permute-done((f32[16,16,256]{2,1,0:T(8,128)S(1)}, f32[16,16,256]{2,1,0:T(8,128)S(1)}, u32[]{:S(2)}, u32[]{:S(2)}) %collective-permute-start.5) | collective-permute-done | bytes 262176 | tf_op jit(solution)/shard_map/ppermute | solution.py:21
  24.2 2.0 %border_steps.1 = (f32[4264,128]{1,0:T(8,128)S(1)}, f32[32,256]{1,0:T(8,128)S(1)}) custom-call(s32[2]{0:T(128)S(1)} %pad_add_fusion.place, s32[32,256]{1,0:T(8,128)S(1)} %copy-done.7, f32[33,6,16,256]{3,2,1,0:T(8,128)S(1)} %get-tuple-element.15.coef, f32[2,7,6,16,256]{4,3,2,1,0:T(8,128)S(1)} %outer_coefs.1.wide, ...), custom_call_target="tpu_custom_call", output_to_operand_aliasing={{0}: (10, {})} | custom-call | flops 1000 | bytes 1000 | tf_op jit(solution)/shard_map/border_steps/pallas_call | solution.py:397
  26.2 0.3 %collective-permute-start.9 = (f32[32,256]{1,0:T(8,128)S(1)}, f32[32,256]{1,0:T(8,128)S(1)}, u32[]{:S(2)}, u32[]{:S(2)}) collective-permute-start(f32[32,256]{1,0:T(8,128)S(1)} %get-tuple-element.27), channel_id=1, source_target_pairs={{0,3},{1,0},{2,1},{3,2},{4,7},{5,4},{6,5},{7,6},{8,11},{9,8},{10,9... | collective-permute-start | bytes 98312 | tf_op jit(solution)/shard_map/ppermute | solution.py:21
  26.6 1.3 %collective-permute-start.8 = (f32[32,256]{1,0:T(8,128)S(1)}, f32[32,256]{1,0:T(8,128)S(1)}, u32[]{:S(2)}, u32[]{:S(2)}) collective-permute-start(f32[32,256]{1,0:T(8,128)S(1)} %get-tuple-element.27), channel_id=1, source_target_pairs={{0,2},{1,3},{2,0},{3,1},{4,6},{5,7},{6,4},{7,5},{8,10},{9,11},{10,... | collective-permute-start | bytes 98312 | tf_op jit(solution)/shard_map/ppermute | solution.py:21
  27.9 0.2 collective-permute-start.7
  28.0 1.6 %write_final.1 = f32[4,16,32,256]{3,2,1,0:T(8,128)} custom-call(f32[4264,128]{1,0:T(8,128)S(1)} %get-tuple-element.26.final), custom_call_target="tpu_custom_call" | custom-call | flops 1000 | bytes 1000 | tf_op jit(solution)/shard_map/write_final/pallas_call | solution.py:437
  29.6 0.8 %collective-permute-done.8 = f32[32,256]{1,0:T(8,128)S(1)} collective-permute-done((f32[32,256]{1,0:T(8,128)S(1)}, f32[32,256]{1,0:T(8,128)S(1)}, u32[]{:S(2)}, u32[]{:S(2)}) %collective-permute-start.8) | collective-permute-done | bytes 32800 | tf_op jit(solution)/shard_map/ppermute | solution.py:21
  30.5 0.7 %collective-permute-done.7 = f32[32,256]{1,0:T(8,128)S(1)} collective-permute-done((f32[32,256]{1,0:T(8,128)S(1)}, f32[32,256]{1,0:T(8,128)S(1)}, u32[]{:S(2)}, u32[]{:S(2)}) %collective-permute-start.7) | collective-permute-done | bytes 32800 | tf_op jit(solution)/shard_map/ppermute | solution.py:21
  31.2 0.6 %add_add_fusion = f32[32,256]{1,0:T(8,128)} fusion(f32[32,256]{1,0:T(8,128)S(1)} %collective-permute-done.9, f32[32,256]{1,0:T(8,128)S(1)} %collective-permute-done.8, f32[32,256]{1,0:T(8,128)S(1)} %get-tuple-element.27, f32[32,256]{1,0:T(8,128)S(1)} %collective-permute-done.7), kind=kLoop, calls=%fused_computation.1 | loop fusion | flops 24576 | bytes 163840 | tf_op jit(solution)/shard_map/add | solution.py:475
  (20 shorter events, 0.1 us)
Async XLA Ops:
  0.7 15.0 %copy-start = (f32[4,16,32,256]{3,2,1,0:T(8,128)S(1)}, f32[4,16,32,256]{3,2,1,0:T(8,128)}, u32[]{:S(2)}) copy-start(f32[4,16,32,256]{3,2,1,0:T(8,128)} %lam.3) | copy-start | bytes 6291460
  0.7 15.0 %copy-start.1 = (f32[16,32,256]{2,1,0:T(8,128)S(1)}, f32[16,32,256]{2,1,0:T(8,128)}, u32[]{:S(2)}) copy-start(f32[16,32,256]{2,1,0:T(8,128)} %ew.3) | copy-start | bytes 1572868
  0.7 15.0 %copy-start.2 = (f32[16,32,256]{2,1,0:T(8,128)S(1)}, f32[16,32,256]{2,1,0:T(8,128)}, u32[]{:S(2)}) copy-start(f32[16,32,256]{2,1,0:T(8,128)} %ed.3) | copy-start | bytes 1572868
  0.7 15.0 %copy-start.3 = (f32[16,32,256]{2,1,0:T(8,128)S(1)}, f32[16,32,256]{2,1,0:T(8,128)}, u32[]{:S(2)}) copy-start(f32[16,32,256]{2,1,0:T(8,128)} %nw.3) | copy-start | bytes 1572868
  0.7 15.0 %copy-start.4 = (f32[16,32,256]{2,1,0:T(8,128)S(1)}, f32[16,32,256]{2,1,0:T(8,128)}, u32[]{:S(2)}) copy-start(f32[16,32,256]{2,1,0:T(8,128)} %nd.3) | copy-start | bytes 1572868
  0.7 15.0 %copy-start.5 = (f32[16,32,256]{2,1,0:T(8,128)S(1)}, f32[16,32,256]{2,1,0:T(8,128)}, u32[]{:S(2)}) copy-start(f32[16,32,256]{2,1,0:T(8,128)} %mf.3) | copy-start | bytes 1572868
  0.8 15.0 %copy-start.6 = (s32[32,256]{1,0:T(8,128)S(1)}, s32[32,256]{1,0:T(8,128)}, u32[]{:S(2)}) copy-start(s32[32,256]{1,0:T(8,128)} %top.3) | copy-start | bytes 98308
  0.8 15.0 %copy-start.7 = (s32[32,256]{1,0:T(8,128)S(1)}, s32[32,256]{1,0:T(8,128)}, u32[]{:S(2)}) copy-start(s32[32,256]{1,0:T(8,128)} %region.3) | copy-start | bytes 98308
  3.7 8.5 %collective-permute-start = (f32[4,16,256]{2,1,0:T(8,128)S(1)}, f32[4,16,256]{2,1,0:T(8,128)S(1)}, u32[]{:S(2)}, u32[]{:S(2)}) collective-permute-start(f32[4,16,256]{2,1,0:T(8,128)S(1)} %get-tuple-element.16), channel_id=1, source_target_pairs={{0,4},{4,0},{8,12},{12,8},{16,20},{20,16},{24,28},{28,24},{1,5},{5... | collective-permute-start | bytes 196616 | tf_op jit(solution)/shard_map/ppermute | solution.py:21
  6.7 7.1 %collective-permute-start.1 = (f32[4,16,256]{2,1,0:T(8,128)S(1)}, f32[4,16,256]{2,1,0:T(8,128)S(1)}, u32[]{:S(2)}, u32[]{:S(2)}) collective-permute-start(f32[4,16,256]{2,1,0:T(8,128)S(1)} %get-tuple-element.17), channel_id=1, source_target_pairs={{0,28},{4,8},{8,4},{12,16},{16,12},{20,24},{24,20},{28,0},{1,29},{... | collective-permute-start | bytes 196616 | tf_op jit(solution)/shard_map/ppermute | solution.py:21
  10.3 13.9 %collective-permute-start.5 = (f32[16,16,256]{2,1,0:T(8,128)S(1)}, f32[16,16,256]{2,1,0:T(8,128)S(1)}, u32[]{:S(2)}, u32[]{:S(2)}) collective-permute-start(f32[16,16,256]{2,1,0:T(8,128)S(1)} %get-tuple-element.22), channel_id=1, source_target_pairs={{0,4},{4,0},{8,12},{12,8},{16,20},{20,16},{24,28},{28,24},{1,5},{5... | collective-permute-start | bytes 786440 | tf_op jit(solution)/shard_map/ppermute | solution.py:21
  10.3 13.9 %collective-permute-start.6 = (f32[16,16,256]{2,1,0:T(8,128)S(1)}, f32[16,16,256]{2,1,0:T(8,128)S(1)}, u32[]{:S(2)}, u32[]{:S(2)}) collective-permute-start(f32[16,16,256]{2,1,0:T(8,128)S(1)} %get-tuple-element.23), channel_id=1, source_target_pairs={{0,28},{4,8},{8,4},{12,16},{16,12},{20,24},{24,20},{28,0},{1,29},{... | collective-permute-start | bytes 786440 | tf_op jit(solution)/shard_map/ppermute | solution.py:21
  13.8 8.7 %collective-permute-start.4 = (f32[2,4,16,256]{3,2,1,0:T(8,128)S(1)}, f32[2,4,16,256]{3,2,1,0:T(8,128)S(1)}, u32[]{:S(2)}, u32[]{:S(2)}) collective-permute-start(f32[2,4,16,256]{3,2,1,0:T(8,128)S(1)} %pad_maximum_fusion.refs_0_), channel_id=1, source_target_pairs={{0,3},{1,2},{2,1},{3,0},{4,7},{5,6},{6,5},{7,4},{8,11},{9,10},{10,... | collective-permute-start | bytes 393224 | tf_op jit(solution)/shard_map/ppermute | solution.py:21
  13.9 8.6 %collective-permute-start.3 = (f32[2,4,16,256]{3,2,1,0:T(8,128)S(1)}, f32[2,4,16,256]{3,2,1,0:T(8,128)S(1)}, u32[]{:S(2)}, u32[]{:S(2)}) collective-permute-start(f32[2,4,16,256]{3,2,1,0:T(8,128)S(1)} %pad_maximum_fusion.refs_0_), channel_id=1, source_target_pairs={{0,2},{1,3},{2,0},{3,1},{4,6},{5,7},{6,4},{7,5},{8,10},{9,11},{10,... | collective-permute-start | bytes 393224 | tf_op jit(solution)/shard_map/ppermute | solution.py:21
  15.5 7.0 %collective-permute-start.2 = (f32[2,4,16,256]{3,2,1,0:T(8,128)S(1)}, f32[2,4,16,256]{3,2,1,0:T(8,128)S(1)}, u32[]{:S(2)}, u32[]{:S(2)}) collective-permute-start(f32[2,4,16,256]{3,2,1,0:T(8,128)S(1)} %pad_maximum_fusion.refs_0_), channel_id=1, source_target_pairs={{0,1},{1,0},{2,3},{3,2},{4,5},{5,4},{6,7},{7,6},{8,9},{9,8},{10,11... | collective-permute-start | bytes 393224 | tf_op jit(solution)/shard_map/ppermute | solution.py:21
  26.2 3.4 %collective-permute-start.9 = (f32[32,256]{1,0:T(8,128)S(1)}, f32[32,256]{1,0:T(8,128)S(1)}, u32[]{:S(2)}, u32[]{:S(2)}) collective-permute-start(f32[32,256]{1,0:T(8,128)S(1)} %get-tuple-element.27), channel_id=1, source_target_pairs={{0,3},{1,0},{2,1},{3,2},{4,7},{5,4},{6,5},{7,6},{8,11},{9,8},{10,9... | collective-permute-start | bytes 98312 | tf_op jit(solution)/shard_map/ppermute | solution.py:21
  26.6 3.9 %collective-permute-start.8 = (f32[32,256]{1,0:T(8,128)S(1)}, f32[32,256]{1,0:T(8,128)S(1)}, u32[]{:S(2)}, u32[]{:S(2)}) collective-permute-start(f32[32,256]{1,0:T(8,128)S(1)} %get-tuple-element.27), channel_id=1, source_target_pairs={{0,2},{1,3},{2,0},{3,1},{4,6},{5,7},{6,4},{7,5},{8,10},{9,11},{10,... | collective-permute-start | bytes 98312 | tf_op jit(solution)/shard_map/ppermute | solution.py:21
  27.9 3.3 %collective-permute-start.7 = (f32[32,256]{1,0:T(8,128)S(1)}, f32[32,256]{1,0:T(8,128)S(1)}, u32[]{:S(2)}, u32[]{:S(2)}) collective-permute-start(f32[32,256]{1,0:T(8,128)S(1)} %get-tuple-element.27), channel_id=1, source_target_pairs={{0,1},{1,2},{2,3},{3,0},{4,5},{5,6},{6,7},{7,4},{8,9},{9,10},{10,1... | collective-permute-start | bytes 98312 | tf_op jit(solution)/shard_map/ppermute | solution.py:21

commit v7 on v6

--- a/solution.py
+++ b/solution.py
@@ -10,7 +10,7 @@
 ITERS = 4
 EDGE = ITERS
 ENTRIES = 16
-CHUNKS = 3
+CHUNKS = 5
 LANES = 128
 HALVES = (slice(0, LANES), slice(LANES, 2 * LANES))
 SHORT = pl.CostEstimate(flops=1000, bytes_accessed=1000, transcendentals=0)
@@ -72,23 +72,28 @@
 
 
 def pack_kernel(parts, place, lam, ew, ed, nw, nd, mf, top, *refs):
-    coef_first, coef_second, lam_first, lam_second = refs[:4]
-    field_s, top_s, lam_s, entry, field_p, lam_p, sems = refs[4:]
+    coef_first, coef_second, lam_first, lam_second, lam_v, field_v = refs[:6]
+    top_v, entry, field_p, lam_p, sems = refs[6:]
     tags, levels, cols, lats = lam.shape
+    edges = (pl.ds(0, 8), pl.ds(cols - 8, 8))
+    middle = pl.ds(8, cols - 16)
     copies = []
 
     def copy(src, dst):
         copies.append(pltpu.make_async_copy(src, dst, sems.at[len(copies)]))
         copies[-1].start()
 
-    for side, at in ((LOW, 0), (HIGH, cols - 8)):
-        for f, field in enumerate((ew, ed, nw, nd, mf)):
-            copy(field.at[:, pl.ds(at, 8)], field_s.at[f, side])
-        copy(top.at[pl.ds(at, 8)], top_s.at[side])
-    field_copies = len(copies)
-    for side, at in ((LOW, 0), (HIGH, cols - 8)):
-        copy(lam.at[:, :, pl.ds(at, 8)], lam_s.at[side])
-    for c in copies[:field_copies]:
+    copy(top, top_v)
+    fields = list(enumerate((ew, ed, nw, nd, mf)))
+    for part in edges:
+        for f, field in fields:
+            copy(field.at[:, part], field_v.at[f, :, part])
+    for part in edges:
+        copy(lam.at[:, :, part], lam_v.at[:, :, part])
+    for f, field in fields:
+        copy(field.at[:, middle], field_v.at[f, :, middle])
+    copy(lam.at[:, :, middle], lam_v.at[:, :, middle])
+    for c in copies[:11]:
         c.wait()
     pitch = 9
     slab = levels * pitch
@@ -97,50 +102,55 @@
     def _(level):
         row = place_of(level, levels) * pitch
         for f in range(5):
-            for side in range(2):
+            for side, part in enumerate(edges):
                 for k in range(2):
                     at = ((f * 2 + side) * 2 + k) * slab
-                    field_p[pl.ds(at + row, 8), :] = field_s[f, side, level, :, HALVES[k]]
+                    field_p[pl.ds(at + row, 8), :] = field_v[f, level, part, HALVES[k]]
 
     def field(f, side, c):
         return column_at(field_p, (f * 2 + side) * 2 * slab + c, levels, pitch, slab)
 
-    for side in (LOW, HIGH):
-        slot = 0
-        for c in range(EDGE - 1) if side == LOW else range(8 - EDGE, 8):
+    entry[LOW, 0] = jnp.zeros((levels, lats), jnp.float32)
+    start = 8 - EDGE
+    entry[HIGH, 0] = jnp.maximum(-field(0, HIGH, start), 0.0) + field(1, HIGH, start)
+
+    @pl.loop(0, EDGE - 1)
+    def _(j):
+        for side in (LOW, HIGH):
+            c = j + (start + 1) * side
             east, west, north, south = faces(*(field(f, side, c) for f in range(4)))
-            lift = updraft(field(4, side, c), top_s[side, pl.ds(c, 1), :])
-            wanted = (east, west, north, south, lift)
-            if side == HIGH and c == 8 - EDGE:
-                wanted = (west,)
-            for value in wanted:
-                entry[side, slot] = value
-                slot += 1
-        for left in range(slot, ENTRIES):
-            entry[side, left] = jnp.zeros((levels, lats), jnp.float32)
+            row = top_v[pl.ds(c + (cols - 8) * side, 1), :]
+            lift = updraft(field(4, side, c), row)
+            for n, value in enumerate((east, north, south, lift, west)):
+                entry[side, 5 * j + 1 + n] = value
+
     per = ENTRIES // parts
     mine = lax.rem(place[0], parts) * per
     odd = place[1]
     coef_first[...] = entry[1 - odd, pl.ds(mine, per)]
     coef_second[...] = entry[odd, pl.ds(mine, per)]
 
-    for c in copies[field_copies:]:
+    for c in copies[11:13]:
         c.wait()
 
     @pl.loop(0, levels)
     def _(level):
         row = place_of(level, levels) * pitch
-        for side in range(2):
+        for side, part in enumerate(edges):
             for tag in range(tags):
                 for k in range(2):
                     at = ((side * 2 + k) * tags + tag) * slab
-                    lam_p[pl.ds(at + row, 8), :] = lam_s[side, tag, level, :, HALVES[k]]
-
-    for dest, side in ((lam_first, 1 - odd), (lam_second, odd)):
-        start = side * (2 * tags * slab + 8 - EDGE)
-        for tag in range(tags):
+                    lam_p[pl.ds(at + row, 8), :] = lam_v[tag, level, part, HALVES[k]]
+
+    @pl.loop(0, tags)
+    def _(tag):
+        for dest, side in ((lam_first, 1 - odd), (lam_second, odd)):
+            at = side * (2 * tags * slab + start) + tag * slab
             for c in range(EDGE):
-                dest[tag * EDGE + c] = column_at(lam_p, start + tag * slab + c, levels, pitch, tags * slab)
+                dest[tag * EDGE + c] = column_at(lam_p, at + c, levels, pitch, tags * slab)
+
+    for c in copies[13:]:
+        c.wait()
 
 
 def pack(parts, place, lam, fields, top):
@@ -151,16 +161,21 @@
     return pl.pallas_call(
         functools.partial(pack_kernel, parts),
         in_specs=[pl.BlockSpec(memory_space=pltpu.SMEM)] + [hbm] * 7,
-        out_specs=[pl.BlockSpec(memory_space=pltpu.VMEM)] * 4,
-        out_shape=[send(few), send(few), send(many), send(many)],
+        out_specs=[pl.BlockSpec(memory_space=pltpu.VMEM)] * 6,
+        out_shape=[
+            send(few),
+            send(few),
+            send(many),
+            send(many),
+            pltpu.VMEM(lam.shape, jnp.float32),
+            pltpu.VMEM((5, levels, cols, lats), jnp.float32),
+        ],
         scratch_shapes=[
-            pltpu.VMEM((5, 2, levels, 8, lats), jnp.float32),
-            pltpu.VMEM((2, 8, lats), jnp.int32),
-            pltpu.VMEM((2, tags, levels, 8, lats), jnp.float32),
+            pltpu.VMEM((cols, lats), jnp.int32),
             pltpu.VMEM((2, ENTRIES, levels, lats), jnp.float32),
             pltpu.VMEM((pitched(20, levels, 8), LANES), jnp.float32),
             pltpu.VMEM((pitched(4 * tags, levels, 8), LANES), jnp.float32),
-            pltpu.SemaphoreType.DMA((14,)),
+            pltpu.SemaphoreType.DMA((19,)),
         ],
         compiler_params=pltpu.CompilerParams(vmem_limit_bytes=24 << 20),
         cost_estimate=SHORT,
@@ -216,7 +231,7 @@
     return store
 
 
-def inner_kernel(place, lam, ew, ed, nw, nd, mf, top, region, *refs):
+def inner_kernel(place, lam, fields, top, region, *refs):
     coef, l0, l1, l2, l3, final, rows, lam_p, field_p = refs
     tags, levels, cols, lats = lam.shape
     pitch = cols + 1
@@ -225,9 +240,9 @@
     @pl.loop(0, levels)
     def _(level):
         row = place_of(level, levels) * pitch
-        for f, field in enumerate((ew, ed, nw, nd, mf)):
+        for f in range(5):
             for k in range(2):
-                field_p[pl.ds((f * 2 + k) * slab + row, cols), :] = field[level, :, HALVES[k]]
+                field_p[pl.ds((f * 2 + k) * slab + row, cols), :] = fields[f, level, :, HALVES[k]]
         for tag in range(tags):
             for k in range(2):
                 at = (k * tags + tag) * slab + row
@@ -270,7 +285,7 @@
     state = pltpu.VMEM((cols, tags, levels, lats), jnp.float32)
     return pl.pallas_call(
         inner_kernel,
-        in_specs=[pl.BlockSpec(memory_space=pltpu.SMEM)] + [vmem] * 8,
+        in_specs=[pl.BlockSpec(memory_space=pltpu.SMEM)] + [vmem] * 4,
         out_specs=[vmem] * 7,
         out_shape=[
             pltpu.VMEM((cols + 1, 6, levels, lats), jnp.float32),
@@ -286,7 +301,7 @@
         compiler_params=pltpu.CompilerParams(vmem_limit_bytes=32 << 20),
         cost_estimate=SHORT,
         name="inner_steps",
-    )(place, lam, *fields, top, region)
+    )(place, lam, fields, top, region)
 
 
 def slot(c, cols):
@@ -303,25 +318,19 @@
         entry[1 - odd, pl.ds(base, per)] = pieces[by][0]
         entry[odd, pl.ds(base, per)] = pieces[by][1]
 
-    def outside(c):
-        if c < 0:
-            at = 1 + 5 * (c + EDGE - 1)
-            e, _, n, s, u = (entry[LOW, at + j] for j in range(5))
-            w = entry[LOW, at - 4] if c > 1 - EDGE else entry[LOW, 0]
-        else:
-            at = 5 * (c - cols)
-            e, _, n, s, u = (entry[HIGH, at + j] for j in range(5))
-            w = entry[HIGH, at - 4] if c > cols else coef[cols, 2]
-        return e, w, n, s, u
-
-    first_west = entry[LOW, 1 + 5 * (EDGE - 2) + 1]
-    for c in [*range(1 - EDGE, 1), *range(cols, cols + EDGE - 1)]:
-        if c == 0:
-            e, w, n, s, u = coef[0, 1], first_west, coef[0, 3], coef[0, 4], coef[0, 5]
-        else:
-            e, w, n, s, u = outside(c)
-        for j, value in enumerate((1.0 - e - w - n - s, e, w, n, s, u)):
-            wide[*slot(c, cols), j] = value
+    entry[HIGH, 0] = coef[cols, 2]
+
+    @pl.loop(0, EDGE - 1)
+    def _(j):
+        for side in (LOW, HIGH):
+            w, e, n, s, u = (entry[side, 5 * j + i] for i in range(5))
+            for i, value in enumerate((1.0 - e - w - n - s, e, w, n, s, u)):
+                wide[side, j + EDGE * side, i] = value
+
+    first_west = entry[LOW, ENTRIES - 1]
+    e, n, s, u = (coef[0, i] for i in (1, 3, 4, 5))
+    for i, value in enumerate((1.0 - e - first_west - n - s, e, first_west, n, s, u)):
+        wide[*slot(0, cols), i] = value
 
 
 def outer_coefs(parts, cols, place, coef, pieces):
@@ -454,12 +463,16 @@
     parts = 4 if groups % 4 == 0 else 1
     grp, dom = lax.axis_index("grp"), lax.axis_index("dom")
     place = jnp.stack([grp, dom % 2]).astype(jnp.int32)
-    own = (lam, east_wind, east_diff, north_wind, north_diff, mass_flux)
-    far = [pltpu.with_memory_space_constraint(value, pltpu.HBM) for value in (*own, top)]
+    far_lam, *far = (
+        pltpu.with_memory_space_constraint(value, pltpu.HBM)
+        for value in (lam, east_wind, east_diff, north_wind, north_diff, mass_flux, top)
+    )
 
     pairs = lambda i: i ^ 1
     turn = lambda i: (((i - 1) % tiles ^ 1) + 1) % tiles
-    coef_first, coef_second, first, second = pack(parts, place, far[0], far[1:6], far[6])
+    coef_first, coef_second, first, second, own_lam, own_fields = pack(
+        parts, place, far_lam, far[:5], far[5]
+    )
     coef_first = swapped(coef_first, "dom", pairs)
     coef_second = swapped(coef_second, "dom", turn)
     first = swapped(first, "dom", pairs)
@@ -467,7 +480,7 @@
     pieces = [jnp.stack([coef_first, coef_second])]
     for by in range(1, parts):
         pieces.append(swapped(pieces[0], "grp", lambda i: i ^ by))
-    coef, *states, final, rows = inner(place, own[0], own[1:], top, region)
+    coef, *states, final, rows = inner(place, own_lam, own_fields, top, region)
     wide = outer_coefs(parts, lam.shape[2], place, coef, pieces)
     final, grad = border(place, region, coef, wide, states, first, second, final, rows)
     share = grad

time: 32 us -> 32 us (level)
  waiting for transfers between devices: 4.24 us -> 1.88 us
  starting transfers between devices: 12.2 us -> 13.5 us
  Pallas kernels: 13.8 us -> 14.9 us
    ppermute x10, waiting for transfers between devices: 4.24 us -> 1.88 us  [swapped(): lax.ppermute(value, axis, [(i, partner(i)) for i in range(lax.axis_size(a...]
    ppermute x10, starting transfers between devices: 12.2 us -> 13.5 us  [swapped(): lax.ppermute(value, axis, [(i, partner(i)) for i in range(lax.axis_size(a...]
    pallas_call x1, Pallas kernels: 6.68 us -> 7.49 us  [inner(): pl.pallas_call(inner_kernel, in_specs=[pl.BlockSpec(memory_space=pltpu.SM...]
  transfers between devices with their start and end apart: 10 -> 10, of which waited for: 4 -> 2; matrix products, arithmetic and copies ran while one was open for 0% -> 0% of each run, Pallas kernels for 28% -> 31%
where the time goes in v7:
time: 32 us; the launch traced here: 31.7 us
  Pallas kernels  14.9 us (47%)
  starting transfers between devices  13.5 us (42%)
  waiting for transfers between devices  1.88 us (6%)
  between operations  0.74 us (2%)
  other arithmetic  0.71 us (2%)
    ppermute x10, starting transfers between devices, swapped(): lax.ppermute(value, axis, [(i, partner(i)) for i in range(lax.axis_size(a...  13.5 us
    pallas_call x1, Pallas kernels, inner(): pl.pallas_call(inner_kernel, in_specs=[pl.BlockSpec(memory_space=pltpu.SM...  7.49 us
    pallas_call x1, Pallas kernels, pack(): pl.pallas_call(functools.partial(pack_kernel, parts), in_specs=[pl.BlockS...  3.18 us
    pallas_call x1, Pallas kernels, border(): pl.pallas_call(border_kernel, in_specs=[pl.BlockSpec(memory_space=pltpu.S...  2.01 us
    ppermute x10, waiting for transfers between devices, swapped(): lax.ppermute(value, axis, [(i, partner(i)) for i in range(lax.axis_size(a...  1.88 us
    pallas_call x1, Pallas kernels, write(): pl.pallas_call(write_kernel, in_specs=[pl.BlockSpec(memory_space=pltpu.VM...  1.57 us
  transfers between devices with their start and end apart: 10, of which 2 were waited for; matrix products, arithmetic and copies ran while one was open for 0% of the time, Pallas kernels for 31%

profile of v7, /device:TPU:0, one launch (start us, length us, event | category | flops | bytes accessed | tf_op | source)
XLA Modules:
  0.0 31.7 jit_solution(6750026571595724963)
XLA Ops:
  0.6 0.1 pad_add_fusion.place
  0.7 3.2 %pack_edges.1 = (f32[4,16,256]{2,1,0:T(8,128)S(1)}, f32[4,16,256]{2,1,0:T(8,128)S(1)}, f32[16,16,256]{2,1,0:T(8,128)S(1)}, f32[16,16,256]{2,1,0:T(8,128)S(1)}, f...) custom-call(s32[2]{0:T(128)S(1)} %pad_add_fusion.place, f32[4,16,32,256]{3,2,1,0:T(8,128)} %lam.1, ...), custom_call_target="tpu_custom_call" | custom-call | flops 1000 | bytes 1000 | tf_op jit(solution)/shard_map/pack_edges/pallas_call | solution.py:161
  3.9 3.0 %collective-permute-start = (f32[4,16,256]{2,1,0:T(8,128)S(1)}, f32[4,16,256]{2,1,0:T(8,128)S(1)}, u32[]{:S(2)}, u32[]{:S(2)}) collective-permute-start(f32[4,16,256]{2,1,0:T(8,128)S(1)} %get-tuple-element.20), channel_id=1, source_target_pairs={{0,4},{4,0},{8,12},{12,8},{16,20},{20,16},{24,28},{28,24},{1,5},{5... | collective-permute-start | bytes 196616 | tf_op jit(solution)/shard_map/ppermute | solution.py:21
  6.9 3.6 %collective-permute-start.1 = (f32[4,16,256]{2,1,0:T(8,128)S(1)}, f32[4,16,256]{2,1,0:T(8,128)S(1)}, u32[]{:S(2)}, u32[]{:S(2)}) collective-permute-start(f32[4,16,256]{2,1,0:T(8,128)S(1)} %get-tuple-element.21), channel_id=1, source_target_pairs={{0,28},{4,8},{8,4},{12,16},{16,12},{20,24},{24,20},{28,0},{1,29},{... | collective-permute-start | bytes 196616 | tf_op jit(solution)/shard_map/ppermute | solution.py:21
  10.5 0.0 collective-permute-start.5
  10.5 1.9 %collective-permute-start.6 = (f32[16,16,256]{2,1,0:T(8,128)S(1)}, f32[16,16,256]{2,1,0:T(8,128)S(1)}, u32[]{:S(2)}, u32[]{:S(2)}) collective-permute-start(f32[16,16,256]{2,1,0:T(8,128)S(1)} %get-tuple-element.27), channel_id=1, source_target_pairs={{0,28},{4,8},{8,4},{12,16},{16,12},{20,24},{24,20},{28,0},{1,29},{... | collective-permute-start | bytes 786440 | tf_op jit(solution)/shard_map/ppermute | solution.py:21
  12.4 0.0 collective-permute-done
  12.4 1.6 %collective-permute-done.1 = f32[4,16,256]{2,1,0:T(8,128)S(1)} collective-permute-done((f32[4,16,256]{2,1,0:T(8,128)S(1)}, f32[4,16,256]{2,1,0:T(8,128)S(1)}, u32[]{:S(2)}, u32[]{:S(2)}) %collective-permute-start.1) | collective-permute-done | bytes 65568 | tf_op jit(solution)/shard_map/ppermute | solution.py:21
  14.0 0.1 collective-permute-start.2
  14.1 1.6 %collective-permute-start.3 = (f32[2,4,16,256]{3,2,1,0:T(8,128)S(1)}, f32[2,4,16,256]{3,2,1,0:T(8,128)S(1)}, u32[]{:S(2)}, u32[]{:S(2)}) collective-permute-start(f32[2,4,16,256]{3,2,1,0:T(8,128)S(1)} %pad_maximum_fusion.refs_0_), channel_id=1, source_target_pairs={{0,2},{1,3},{2,0},{3,1},{4,6},{5,7},{6,4},{7,5},{8,10},{9,11},{10,... | collective-permute-start | bytes 393224 | tf_op jit(solution)/shard_map/ppermute | solution.py:21
  15.7 0.3 collective-permute-start.4
  15.9 7.5 %inner_steps.1 = (f32[33,6,16,256]{3,2,1,0:T(8,128)S(1)}, f32[4,4,16,256]{3,2,1,0:T(8,128)S(1)}, f32[32,4,16,256]{3,2,1,0:T(8,128)S(1)}, f32[32,4,16,256]{3,2,1,...) custom-call(s32[2]{0:T(128)S(1)} %pad_add_fusion.place, ...), custom_call_target="tpu_custom_call" | custom-call | flops 1000 | bytes 1000 | tf_op jit(solution)/shard_map/inner_steps/pallas_call | solution.py:286
  23.4 0.0 collective-permute-done.2.refs_1_
  23.5 0.0 collective-permute-done.4.refs_3_
  23.5 0.6 %outer_coefs.1.wide = f32[2,7,6,16,256]{4,3,2,1,0:T(8,128)S(1)} custom-call(s32[2]{0:T(128)S(1)} %pad_add_fusion.place, f32[33,6,16,256]{3,2,1,0:T(8,128)S(1)} %get-tuple-element.19.coef, f32[2,4,16,256]{3,2,1,0:T(8,128)S(1)} %pad_maximum_fusion.refs_0_, f32[2,4,16,256]{3,2,1,0:T(8,128)S(1)} %collective-permute-done.2.refs_1_, ...), custom_call_target="tpu_custom_call" | custom-call | flops 1000 | bytes 1000 | tf_op jit(solution)/shard_map/outer_coefs/pallas_call | solution.py:339
  24.1 0.3 collective-permute-done.5.first
  24.4 2.0 %border_steps.1 = (f32[4264,128]{1,0:T(8,128)S(1)}, f32[32,256]{1,0:T(8,128)S(1)}) custom-call(s32[2]{0:T(128)S(1)} %pad_add_fusion.place, s32[32,256]{1,0:T(8,128)S(1)} %copy-done.1, f32[33,6,16,256]{3,2,1,0:T(8,128)S(1)} %get-tuple-element.19.coef, f32[2,7,6,16,256]{4,3,2,1,0:T(8,128)S(1)} %outer_coefs.1.wide, ...), custom_call_target="tpu_custom_call", output_to_operand_aliasing={{0}: (10, {})} | custom-call | flops 1000 | bytes 1000 | tf_op jit(solution)/shard_map/border_steps/pallas_call | solution.py:406
  26.4 0.1 collective-permute-start.7
  26.6 1.5 %collective-permute-start.8 = (f32[32,256]{1,0:T(8,128)S(1)}, f32[32,256]{1,0:T(8,128)S(1)}, u32[]{:S(2)}, u32[]{:S(2)}) collective-permute-start(f32[32,256]{1,0:T(8,128)S(1)} %get-tuple-element.31), channel_id=1, source_target_pairs={{0,2},{1,3},{2,0},{3,1},{4,6},{5,7},{6,4},{7,5},{8,10},{9,11},{10,... | collective-permute-start | bytes 98312 | tf_op jit(solution)/shard_map/ppermute | solution.py:21
  28.1 1.4 %collective-permute-start.9 = (f32[32,256]{1,0:T(8,128)S(1)}, f32[32,256]{1,0:T(8,128)S(1)}, u32[]{:S(2)}, u32[]{:S(2)}) collective-permute-start(f32[32,256]{1,0:T(8,128)S(1)} %get-tuple-element.31), channel_id=1, source_target_pairs={{0,3},{1,0},{2,1},{3,2},{4,7},{5,4},{6,5},{7,6},{8,11},{9,8},{10,9... | collective-permute-start | bytes 98312 | tf_op jit(solution)/shard_map/ppermute | solution.py:21
  29.5 1.6 %write_final.1 = f32[4,16,32,256]{3,2,1,0:T(8,128)} custom-call(f32[4264,128]{1,0:T(8,128)S(1)} %get-tuple-element.30.final), custom_call_target="tpu_custom_call" | custom-call | flops 1000 | bytes 1000 | tf_op jit(solution)/shard_map/write_final/pallas_call | solution.py:446
  31.0 0.0 collective-permute-done.7
  31.0 0.0 collective-permute-done.8
  31.1 0.6 %add_add_fusion = f32[32,256]{1,0:T(8,128)} fusion(f32[32,256]{1,0:T(8,128)S(1)} %collective-permute-done.9, f32[32,256]{1,0:T(8,128)S(1)} %collective-permute-done.8, f32[32,256]{1,0:T(8,128)S(1)} %get-tuple-element.31, f32[32,256]{1,0:T(8,128)S(1)} %collective-permute-done.7), kind=kLoop, calls=%fused_computation.1 | loop fusion | flops 24576 | bytes 163840 | tf_op jit(solution)/shard_map/add | solution.py:488
  (8 shorter events, 0.0 us)
Async XLA Ops:
  0.7 15.2 %copy-start = (s32[32,256]{1,0:T(8,128)S(1)}, s32[32,256]{1,0:T(8,128)}, u32[]{:S(2)}) copy-start(s32[32,256]{1,0:T(8,128)} %top.3) | copy-start | bytes 98308
  0.7 15.2 %copy-start.1 = (s32[32,256]{1,0:T(8,128)S(1)}, s32[32,256]{1,0:T(8,128)}, u32[]{:S(2)}) copy-start(s32[32,256]{1,0:T(8,128)} %region.3) | copy-start | bytes 98308
  3.9 8.5 %collective-permute-start = (f32[4,16,256]{2,1,0:T(8,128)S(1)}, f32[4,16,256]{2,1,0:T(8,128)S(1)}, u32[]{:S(2)}, u32[]{:S(2)}) collective-permute-start(f32[4,16,256]{2,1,0:T(8,128)S(1)} %get-tuple-element.20), channel_id=1, source_target_pairs={{0,4},{4,0},{8,12},{12,8},{16,20},{20,16},{24,28},{28,24},{1,5},{5... | collective-permute-start | bytes 196616 | tf_op jit(solution)/shard_map/ppermute | solution.py:21
  6.9 7.1 %collective-permute-start.1 = (f32[4,16,256]{2,1,0:T(8,128)S(1)}, f32[4,16,256]{2,1,0:T(8,128)S(1)}, u32[]{:S(2)}, u32[]{:S(2)}) collective-permute-start(f32[4,16,256]{2,1,0:T(8,128)S(1)} %get-tuple-element.21), channel_id=1, source_target_pairs={{0,28},{4,8},{8,4},{12,16},{16,12},{20,24},{24,20},{28,0},{1,29},{... | collective-permute-start | bytes 196616 | tf_op jit(solution)/shard_map/ppermute | solution.py:21
  10.5 13.9 %collective-permute-start.5 = (f32[16,16,256]{2,1,0:T(8,128)S(1)}, f32[16,16,256]{2,1,0:T(8,128)S(1)}, u32[]{:S(2)}, u32[]{:S(2)}) collective-permute-start(f32[16,16,256]{2,1,0:T(8,128)S(1)} %get-tuple-element.26), channel_id=1, source_target_pairs={{0,4},{4,0},{8,12},{12,8},{16,20},{20,16},{24,28},{28,24},{1,5},{5... | collective-permute-start | bytes 786440 | tf_op jit(solution)/shard_map/ppermute | solution.py:21
  10.5 13.9 %collective-permute-start.6 = (f32[16,16,256]{2,1,0:T(8,128)S(1)}, f32[16,16,256]{2,1,0:T(8,128)S(1)}, u32[]{:S(2)}, u32[]{:S(2)}) collective-permute-start(f32[16,16,256]{2,1,0:T(8,128)S(1)} %get-tuple-element.27), channel_id=1, source_target_pairs={{0,28},{4,8},{8,4},{12,16},{16,12},{20,24},{24,20},{28,0},{1,29},{... | collective-permute-start | bytes 786440 | tf_op jit(solution)/shard_map/ppermute | solution.py:21
  14.0 9.4 %collective-permute-start.2 = (f32[2,4,16,256]{3,2,1,0:T(8,128)S(1)}, f32[2,4,16,256]{3,2,1,0:T(8,128)S(1)}, u32[]{:S(2)}, u32[]{:S(2)}) collective-permute-start(f32[2,4,16,256]{3,2,1,0:T(8,128)S(1)} %pad_maximum_fusion.refs_0_), channel_id=1, source_target_pairs={{0,1},{1,0},{2,3},{3,2},{4,5},{5,4},{6,7},{7,6},{8,9},{9,8},{10,11... | collective-permute-start | bytes 393224 | tf_op jit(solution)/shard_map/ppermute | solution.py:21
  14.1 9.4 %collective-permute-start.3 = (f32[2,4,16,256]{3,2,1,0:T(8,128)S(1)}, f32[2,4,16,256]{3,2,1,0:T(8,128)S(1)}, u32[]{:S(2)}, u32[]{:S(2)}) collective-permute-start(f32[2,4,16,256]{3,2,1,0:T(8,128)S(1)} %pad_maximum_fusion.refs_0_), channel_id=1, source_target_pairs={{0,2},{1,3},{2,0},{3,1},{4,6},{5,7},{6,4},{7,5},{8,10},{9,11},{10,... | collective-permute-start | bytes 393224 | tf_op jit(solution)/shard_map/ppermute | solution.py:21
  15.7 7.8 %collective-permute-start.4 = (f32[2,4,16,256]{3,2,1,0:T(8,128)S(1)}, f32[2,4,16,256]{3,2,1,0:T(8,128)S(1)}, u32[]{:S(2)}, u32[]{:S(2)}) collective-permute-start(f32[2,4,16,256]{3,2,1,0:T(8,128)S(1)} %pad_maximum_fusion.refs_0_), channel_id=1, source_target_pairs={{0,3},{1,2},{2,1},{3,0},{4,7},{5,6},{6,5},{7,4},{8,11},{9,10},{10,... | collective-permute-start | bytes 393224 | tf_op jit(solution)/shard_map/ppermute | solution.py:21
  26.4 4.6 %collective-permute-start.7 = (f32[32,256]{1,0:T(8,128)S(1)}, f32[32,256]{1,0:T(8,128)S(1)}, u32[]{:S(2)}, u32[]{:S(2)}) collective-permute-start(f32[32,256]{1,0:T(8,128)S(1)} %get-tuple-element.31), channel_id=1, source_target_pairs={{0,1},{1,2},{2,3},{3,0},{4,5},{5,6},{6,7},{7,4},{8,9},{9,10},{10,1... | collective-permute-start | bytes 98312 | tf_op jit(solution)/shard_map/ppermute | solution.py:21
  26.6 4.5 %collective-permute-start.8 = (f32[32,256]{1,0:T(8,128)S(1)}, f32[32,256]{1,0:T(8,128)S(1)}, u32[]{:S(2)}, u32[]{:S(2)}) collective-permute-start(f32[32,256]{1,0:T(8,128)S(1)} %get-tuple-element.31), channel_id=1, source_target_pairs={{0,2},{1,3},{2,0},{3,1},{4,6},{5,7},{6,4},{7,5},{8,10},{9,11},{10,... | collective-permute-start | bytes 98312 | tf_op jit(solution)/shard_map/ppermute | solution.py:21
  28.1 3.0 %collective-permute-start.9 = (f32[32,256]{1,0:T(8,128)S(1)}, f32[32,256]{1,0:T(8,128)S(1)}, u32[]{:S(2)}, u32[]{:S(2)}) collective-permute-start(f32[32,256]{1,0:T(8,128)S(1)} %get-tuple-element.31), channel_id=1, source_target_pairs={{0,3},{1,0},{2,1},{3,2},{4,7},{5,4},{6,5},{7,6},{8,11},{9,8},{10,9... | collective-permute-start | bytes 98312 | tf_op jit(solution)/shard_map/ppermute | solution.py:21

commit v8 on v7

--- a/solution.py
+++ b/solution.py
@@ -10,7 +10,7 @@
 ITERS = 4
 EDGE = ITERS
 ENTRIES = 16
-CHUNKS = 5
+CHUNKS = 2
 LANES = 128
 HALVES = (slice(0, LANES), slice(LANES, 2 * LANES))
 SHORT = pl.CostEstimate(flops=1000, bytes_accessed=1000, transcendentals=0)
@@ -72,7 +72,7 @@
 
 
 def pack_kernel(parts, place, lam, ew, ed, nw, nd, mf, top, *refs):
-    coef_first, coef_second, lam_first, lam_second, lam_v, field_v = refs[:6]
+    first, coef_second, lam_first, lam_second, lam_v, field_v = refs[:6]
     top_v, entry, field_p, lam_p, sems = refs[6:]
     tags, levels, cols, lats = lam.shape
     edges = (pl.ds(0, 8), pl.ds(cols - 8, 8))
@@ -84,16 +84,11 @@
         copies[-1].start()
 
     copy(top, top_v)
-    fields = list(enumerate((ew, ed, nw, nd, mf)))
-    for part in edges:
-        for f, field in fields:
-            copy(field.at[:, part], field_v.at[f, :, part])
-    for part in edges:
+    for f, field in enumerate((ew, ed, nw, nd, mf)):
+        copy(field, field_v.at[f])
+    for part in (*edges, middle):
         copy(lam.at[:, :, part], lam_v.at[:, :, part])
-    for f, field in fields:
-        copy(field.at[:, middle], field_v.at[f, :, middle])
-    copy(lam.at[:, :, middle], lam_v.at[:, :, middle])
-    for c in copies[:11]:
+    for c in copies[:6]:
         c.wait()
     pitch = 9
     slab = levels * pitch
@@ -127,10 +122,11 @@
     per = ENTRIES // parts
     mine = lax.rem(place[0], parts) * per
     odd = place[1]
-    coef_first[...] = entry[1 - odd, pl.ds(mine, per)]
+    half = tags // 2 * EDGE
+    first[half:] = entry[1 - odd, pl.ds(mine, per)]
     coef_second[...] = entry[odd, pl.ds(mine, per)]
 
-    for c in copies[11:13]:
+    for c in copies[6:8]:
         c.wait()
 
     @pl.loop(0, levels)
@@ -142,14 +138,23 @@
                     at = ((side * 2 + k) * tags + tag) * slab
                     lam_p[pl.ds(at + row, 8), :] = lam_v[tag, level, part, HALVES[k]]
 
+    def columns(tag, side):
+        at = side * (2 * tags * slab + start) + tag * slab
+        return [column_at(lam_p, at + c, levels, pitch, tags * slab) for c in range(EDGE)]
+
+    @pl.loop(0, tags // 2)
+    def _(i):
+        for c, value in enumerate(columns(i, 1 - odd)):
+            first[i * EDGE + c] = value
+        for c, value in enumerate(columns(tags // 2 + i, 1 - odd)):
+            lam_first[i * EDGE + c] = value
+
     @pl.loop(0, tags)
     def _(tag):
-        for dest, side in ((lam_first, 1 - odd), (lam_second, odd)):
-            at = side * (2 * tags * slab + start) + tag * slab
-            for c in range(EDGE):
-                dest[tag * EDGE + c] = column_at(lam_p, at + c, levels, pitch, tags * slab)
-
-    for c in copies[13:]:
+        for c, value in enumerate(columns(tag, odd)):
+            lam_second[tag * EDGE + c] = value
+
+    for c in copies[8:]:
         c.wait()
 
 
@@ -163,9 +168,9 @@
         in_specs=[pl.BlockSpec(memory_space=pltpu.SMEM)] + [hbm] * 7,
         out_specs=[pl.BlockSpec(memory_space=pltpu.VMEM)] * 6,
         out_shape=[
+            send(many // 2 + few),
             send(few),
-            send(few),
-            send(many),
+            send(many // 2),
             send(many),
             pltpu.VMEM(lam.shape, jnp.float32),
             pltpu.VMEM((5, levels, cols, lats), jnp.float32),
@@ -175,7 +180,7 @@
             pltpu.VMEM((2, ENTRIES, levels, lats), jnp.float32),
             pltpu.VMEM((pitched(20, levels, 8), LANES), jnp.float32),
             pltpu.VMEM((pitched(4 * tags, levels, 8), LANES), jnp.float32),
-            pltpu.SemaphoreType.DMA((19,)),
+            pltpu.SemaphoreType.DMA((9,)),
         ],
         compiler_params=pltpu.CompilerParams(vmem_limit_bytes=24 << 20),
         cost_estimate=SHORT,
@@ -348,12 +353,14 @@
     )(place, coef, *pieces)
 
 
-def border_kernel(place, region, coef, wide, l0, l1, l2, l3, first, second, *refs):
+def border_kernel(place, region, coef, wide, l0, l1, l2, l3, first, rest, second, *refs):
     final_in, rows_in, final, grad, halo, work, rows = refs
     cols, tags, levels, lats = l1.shape
     first_tag = place[0] * tags
     odd = place[1]
-    halo[1 - odd] = first[...]
+    half = rest.shape[0]
+    halo[1 - odd, :half] = first[:half]
+    halo[1 - odd, half:] = rest[...]
     halo[odd] = second[...]
 
     def coefs_at(c):
@@ -399,10 +406,10 @@
     grad[...] = total
 
 
-def border(place, region, coef, wide, states, first, second, final, rows):
+def border(place, region, coef, wide, states, halos, final, rows):
     cols, tags, levels, lats = states[1].shape
     vmem = pl.BlockSpec(memory_space=pltpu.VMEM)
-    operands = [region, coef, wide, *states, first, second]
+    operands = [region, coef, wide, *states, *halos]
     return pl.pallas_call(
         border_kernel,
         in_specs=[pl.BlockSpec(memory_space=pltpu.SMEM)] + [vmem] * (len(operands) + 2),
@@ -470,19 +477,19 @@
 
     pairs = lambda i: i ^ 1
     turn = lambda i: (((i - 1) % tiles ^ 1) + 1) % tiles
-    coef_first, coef_second, first, second, own_lam, own_fields = pack(
+    first, coef_second, rest, second, own_lam, own_fields = pack(
         parts, place, far_lam, far[:5], far[5]
     )
-    coef_first = swapped(coef_first, "dom", pairs)
+    first = swapped(first, "dom", pairs)
     coef_second = swapped(coef_second, "dom", turn)
-    first = swapped(first, "dom", pairs)
+    rest = swapped(rest, "dom", pairs)
     second = swapped(second, "dom", turn)
-    pieces = [jnp.stack([coef_first, coef_second])]
+    pieces = [jnp.stack([first[rest.shape[0] :], coef_second])]
     for by in range(1, parts):
         pieces.append(swapped(pieces[0], "grp", lambda i: i ^ by))
     coef, *states, final, rows = inner(place, own_lam, own_fields, top, region)
     wide = outer_coefs(parts, lam.shape[2], place, coef, pieces)
-    final, grad = border(place, region, coef, wide, states, first, second, final, rows)
+    final, grad = border(place, region, coef, wide, states, (first, rest, second), final, rows)
     share = grad
     for by in range(1, groups):
         grad = grad + swapped(share, "grp", lambda i: (i + by) % groups)

time: 32 us -> 37 us (1.16)
  waiting for transfers between devices: 1.88 us -> 6.48 us
  starting transfers between devices: 13.5 us -> 15.2 us
  Pallas kernels: 14.9 us -> 13.6 us
    ppermute x10, waiting for transfers between devices: 1.88 us -> 6.48 us  [swapped(): lax.ppermute(value, axis, [(i, partner(i)) for i in range(lax.axis_size(a...]
    ppermute x10, starting transfers between devices: 13.5 us -> 15.2 us  [swapped(): lax.ppermute(value, axis, [(i, partner(i)) for i in range(lax.axis_size(a...]
    pallas_call x1, Pallas kernels: 7.49 us -> 6.25 us  [inner(): pl.pallas_call(inner_kernel, in_specs=[pl.BlockSpec(memory_space=pltpu.SM...]
  transfers between devices with their start and end apart: 10 -> 10, of which waited for: 2 -> 1; matrix products, arithmetic and copies ran while one was open for 0% -> 0% of each run, Pallas kernels for 31% -> 23%
where the time goes in v8:
time: 37 us; the launch traced here: 36.7 us
  starting transfers between devices  15.2 us (41%)
  Pallas kernels  13.6 us (37%)
  waiting for transfers between devices  6.48 us (18%)
  between operations  0.76 us (2%)
  other arithmetic  0.72 us (2%)
    ppermute x10, starting transfers between devices, swapped(): lax.ppermute(value, axis, [(i, partner(i)) for i in range(lax.axis_size(a...  15.2 us
    ppermute x10, waiting for transfers between devices, swapped(): lax.ppermute(value, axis, [(i, partner(i)) for i in range(lax.axis_size(a...  6.48 us
    pallas_call x1, Pallas kernels, inner(): pl.pallas_call(inner_kernel, in_specs=[pl.BlockSpec(memory_space=pltpu.SM...  6.25 us
    pallas_call x1, Pallas kernels, pack(): pl.pallas_call(functools.partial(pack_kernel, parts), in_specs=[pl.BlockS...  3.11 us
    pallas_call x1, Pallas kernels, border(): pl.pallas_call(border_kernel, in_specs=[pl.BlockSpec(memory_space=pltpu.S...  2.02 us
    pallas_call x1, Pallas kernels, write(): pl.pallas_call(write_kernel, in_specs=[pl.BlockSpec(memory_space=pltpu.VM...  1.57 us
  transfers between devices with their start and end apart: 10, of which 1 were waited for; matrix products, arithmetic and copies ran while one was open for 0% of the time, Pallas kernels for 23%

profile of v8, /device:TPU:0, one launch (start us, length us, event | category | flops | bytes accessed | tf_op | source)
XLA Modules:
  0.0 36.7 jit_solution(1723555468990317136)
XLA Ops:
  0.6 0.1 pad_add_fusion.place
  0.7 3.1 %pack_edges.1 = (f32[12,16,256]{2,1,0:T(8,128)S(1)}, f32[4,16,256]{2,1,0:T(8,128)S(1)}, f32[8,16,256]{2,1,0:T(8,128)S(1)}, f32[16,16,256]{2,1,0:T(8,128)S(1)}, f...) custom-call(s32[2]{0:T(128)S(1)} %pad_add_fusion.place, f32[4,16,32,256]{3,2,1,0:T(8,128)} %lam.1, ...), custom_call_target="tpu_custom_call" | custom-call | flops 1000 | bytes 1000 | tf_op jit(solution)/shard_map/pack_edges/pallas_call | solution.py:166
  3.8 3.0 %collective-permute-start = (f32[12,16,256]{2,1,0:T(8,128)S(1)}, f32[12,16,256]{2,1,0:T(8,128)S(1)}, u32[]{:S(2)}, u32[]{:S(2)}) collective-permute-start(f32[12,16,256]{2,1,0:T(8,128)S(1)} %get-tuple-element.20), channel_id=1, source_target_pairs={{0,4},{4,0},{8,12},{12,8},{16,20},{20,16},{24,28},{28,24},{1,5},{5... | collective-permute-start | bytes 589832 | tf_op jit(solution)/shard_map/ppermute | solution.py:21
  6.8 3.6 %collective-permute-start.1 = (f32[4,16,256]{2,1,0:T(8,128)S(1)}, f32[4,16,256]{2,1,0:T(8,128)S(1)}, u32[]{:S(2)}, u32[]{:S(2)}) collective-permute-start(f32[4,16,256]{2,1,0:T(8,128)S(1)} %get-tuple-element.21), channel_id=1, source_target_pairs={{0,28},{4,8},{8,4},{12,16},{16,12},{20,24},{24,20},{28,0},{1,29},{... | collective-permute-start | bytes 196616 | tf_op jit(solution)/shard_map/ppermute | solution.py:21
  10.4 1.1 %collective-permute-start.6 = (f32[16,16,256]{2,1,0:T(8,128)S(1)}, f32[16,16,256]{2,1,0:T(8,128)S(1)}, u32[]{:S(2)}, u32[]{:S(2)}) collective-permute-start(f32[16,16,256]{2,1,0:T(8,128)S(1)} %get-tuple-element.27), channel_id=1, source_target_pairs={{0,28},{4,8},{8,4},{12,16},{16,12},{20,24},{24,20},{28,0},{1,29},{... | collective-permute-start | bytes 786440 | tf_op jit(solution)/shard_map/ppermute | solution.py:21
  11.6 6.5 %collective-permute-done.first = f32[12,16,256]{2,1,0:T(8,128)S(1)} collective-permute-done((f32[12,16,256]{2,1,0:T(8,128)S(1)}, f32[12,16,256]{2,1,0:T(8,128)S(1)}, u32[]{:S(2)}, u32[]{:S(2)}) %collective-permute-start) | collective-permute-done | bytes 196640 | tf_op jit(solution)/shard_map/ppermute | solution.py:21
  18.0 0.0 collective-permute-done.1
  18.1 0.1 collective-permute-start.2
  18.1 1.6 %collective-permute-start.3 = (f32[2,4,16,256]{3,2,1,0:T(8,128)S(1)}, f32[2,4,16,256]{3,2,1,0:T(8,128)S(1)}, u32[]{:S(2)}, u32[]{:S(2)}) collective-permute-start(f32[2,4,16,256]{3,2,1,0:T(8,128)S(1)} %pad_maximum_fusion.refs_0_), channel_id=1, source_target_pairs={{0,2},{1,3},{2,0},{3,1},{4,6},{5,7},{6,4},{7,5},{8,10},{9,11},{10,... | collective-permute-start | bytes 393224 | tf_op jit(solution)/shard_map/ppermute | solution.py:21
  19.7 0.3 collective-permute-start.4
  20.0 2.5 %collective-permute-start.5 = (f32[8,16,256]{2,1,0:T(8,128)S(1)}, f32[8,16,256]{2,1,0:T(8,128)S(1)}, u32[]{:S(2)}, u32[]{:S(2)}) collective-permute-start(f32[8,16,256]{2,1,0:T(8,128)S(1)} %get-tuple-element.26), channel_id=1, source_target_pairs={{0,4},{4,0},{8,12},{12,8},{16,20},{20,16},{24,28},{28,24},{1,5},{5... | collective-permute-start | bytes 393224 | tf_op jit(solution)/shard_map/ppermute | solution.py:21
  22.5 6.3 %inner_steps.1 = (f32[33,6,16,256]{3,2,1,0:T(8,128)S(1)}, f32[4,4,16,256]{3,2,1,0:T(8,128)S(1)}, f32[32,4,16,256]{3,2,1,0:T(8,128)S(1)}, f32[32,4,16,256]{3,2,1,...) custom-call(s32[2]{0:T(128)S(1)} %pad_add_fusion.place, ...), custom_call_target="tpu_custom_call" | custom-call | flops 1000 | bytes 1000 | tf_op jit(solution)/shard_map/inner_steps/pallas_call | solution.py:291
  28.7 0.0 collective-permute-done.2.refs_1_
  28.8 0.0 collective-permute-done.4.refs_3_
  28.8 0.6 %outer_coefs.1.wide = f32[2,7,6,16,256]{4,3,2,1,0:T(8,128)S(1)} custom-call(s32[2]{0:T(128)S(1)} %pad_add_fusion.place, f32[33,6,16,256]{3,2,1,0:T(8,128)S(1)} %get-tuple-element.19.coef, f32[2,4,16,256]{3,2,1,0:T(8,128)S(1)} %pad_maximum_fusion.refs_0_, f32[2,4,16,256]{3,2,1,0:T(8,128)S(1)} %collective-permute-done.2.refs_1_, ...), custom_call_target="tpu_custom_call" | custom-call | flops 1000 | bytes 1000 | tf_op jit(solution)/shard_map/outer_coefs/pallas_call | solution.py:344
  29.4 0.0 collective-permute-done.6.second
  29.4 2.0 %border_steps.1 = (f32[4264,128]{1,0:T(8,128)S(1)}, f32[32,256]{1,0:T(8,128)S(1)}) custom-call(s32[2]{0:T(128)S(1)} %pad_add_fusion.place, s32[32,256]{1,0:T(8,128)S(1)} %copy-done.1, f32[33,6,16,256]{3,2,1,0:T(8,128)S(1)} %get-tuple-element.19.coef, f32[2,7,6,16,256]{4,3,2,1,0:T(8,128)S(1)} %outer_coefs.1.wide, ...), custom_call_target="tpu_custom_call", output_to_operand_aliasing={{0}: (11, {})} | custom-call | flops 1000 | bytes 1000 | tf_op jit(solution)/shard_map/border_steps/pallas_call | solution.py:413
  31.5 0.1 collective-permute-start.7
  31.6 1.5 %collective-permute-start.8 = (f32[32,256]{1,0:T(8,128)S(1)}, f32[32,256]{1,0:T(8,128)S(1)}, u32[]{:S(2)}, u32[]{:S(2)}) collective-permute-start(f32[32,256]{1,0:T(8,128)S(1)} %get-tuple-element.31), channel_id=1, source_target_pairs={{0,2},{1,3},{2,0},{3,1},{4,6},{5,7},{6,4},{7,5},{8,10},{9,11},{10,... | collective-permute-start | bytes 98312 | tf_op jit(solution)/shard_map/ppermute | solution.py:21
  33.1 1.4 %collective-permute-start.9 = (f32[32,256]{1,0:T(8,128)S(1)}, f32[32,256]{1,0:T(8,128)S(1)}, u32[]{:S(2)}, u32[]{:S(2)}) collective-permute-start(f32[32,256]{1,0:T(8,128)S(1)} %get-tuple-element.31), channel_id=1, source_target_pairs={{0,3},{1,0},{2,1},{3,2},{4,7},{5,4},{6,5},{7,6},{8,11},{9,8},{10,9... | collective-permute-start | bytes 98312 | tf_op jit(solution)/shard_map/ppermute | solution.py:21
  34.5 1.6 %write_final.1 = f32[4,16,32,256]{3,2,1,0:T(8,128)} custom-call(f32[4264,128]{1,0:T(8,128)S(1)} %get-tuple-element.30.final), custom_call_target="tpu_custom_call" | custom-call | flops 1000 | bytes 1000 | tf_op jit(solution)/shard_map/write_final/pallas_call | solution.py:453
  36.1 0.0 collective-permute-done.7
  36.1 0.0 collective-permute-done.8
  36.1 0.6 %add_add_fusion = f32[32,256]{1,0:T(8,128)} fusion(f32[32,256]{1,0:T(8,128)S(1)} %collective-permute-done.9, f32[32,256]{1,0:T(8,128)S(1)} %collective-permute-done.8, f32[32,256]{1,0:T(8,128)S(1)} %get-tuple-element.31, f32[32,256]{1,0:T(8,128)S(1)} %collective-permute-done.7), kind=kLoop, calls=%fused_computation.2 | loop fusion | flops 24576 | bytes 163840 | tf_op jit(solution)/shard_map/add | solution.py:495
  (9 shorter events, 0.0 us)
Async XLA Ops:
  0.7 21.8 %copy-start = (s32[32,256]{1,0:T(8,128)S(1)}, s32[32,256]{1,0:T(8,128)}, u32[]{:S(2)}) copy-start(s32[32,256]{1,0:T(8,128)} %top.3) | copy-start | bytes 98308
  0.7 21.8 %copy-start.1 = (s32[32,256]{1,0:T(8,128)S(1)}, s32[32,256]{1,0:T(8,128)}, u32[]{:S(2)}) copy-start(s32[32,256]{1,0:T(8,128)} %region.3) | copy-start | bytes 98308
  3.8 14.2 %collective-permute-start = (f32[12,16,256]{2,1,0:T(8,128)S(1)}, f32[12,16,256]{2,1,0:T(8,128)S(1)}, u32[]{:S(2)}, u32[]{:S(2)}) collective-permute-start(f32[12,16,256]{2,1,0:T(8,128)S(1)} %get-tuple-element.20), channel_id=1, source_target_pairs={{0,4},{4,0},{8,12},{12,8},{16,20},{20,16},{24,28},{28,24},{1,5},{5... | collective-permute-start | bytes 589832 | tf_op jit(solution)/shard_map/ppermute | solution.py:21
  6.8 11.2 %collective-permute-start.1 = (f32[4,16,256]{2,1,0:T(8,128)S(1)}, f32[4,16,256]{2,1,0:T(8,128)S(1)}, u32[]{:S(2)}, u32[]{:S(2)}) collective-permute-start(f32[4,16,256]{2,1,0:T(8,128)S(1)} %get-tuple-element.21), channel_id=1, source_target_pairs={{0,28},{4,8},{8,4},{12,16},{16,12},{20,24},{24,20},{28,0},{1,29},{... | collective-permute-start | bytes 196616 | tf_op jit(solution)/shard_map/ppermute | solution.py:21
  10.4 19.0 %collective-permute-start.6 = (f32[16,16,256]{2,1,0:T(8,128)S(1)}, f32[16,16,256]{2,1,0:T(8,128)S(1)}, u32[]{:S(2)}, u32[]{:S(2)}) collective-permute-start(f32[16,16,256]{2,1,0:T(8,128)S(1)} %get-tuple-element.27), channel_id=1, source_target_pairs={{0,28},{4,8},{8,4},{12,16},{16,12},{20,24},{24,20},{28,0},{1,29},{... | collective-permute-start | bytes 786440 | tf_op jit(solution)/shard_map/ppermute | solution.py:21
  18.1 10.7 %collective-permute-start.2 = (f32[2,4,16,256]{3,2,1,0:T(8,128)S(1)}, f32[2,4,16,256]{3,2,1,0:T(8,128)S(1)}, u32[]{:S(2)}, u32[]{:S(2)}) collective-permute-start(f32[2,4,16,256]{3,2,1,0:T(8,128)S(1)} %pad_maximum_fusion.refs_0_), channel_id=1, source_target_pairs={{0,1},{1,0},{2,3},{3,2},{4,5},{5,4},{6,7},{7,6},{8,9},{9,8},{10,11... | collective-permute-start | bytes 393224 | tf_op jit(solution)/shard_map/ppermute | solution.py:21
  18.1 10.6 %collective-permute-start.3 = (f32[2,4,16,256]{3,2,1,0:T(8,128)S(1)}, f32[2,4,16,256]{3,2,1,0:T(8,128)S(1)}, u32[]{:S(2)}, u32[]{:S(2)}) collective-permute-start(f32[2,4,16,256]{3,2,1,0:T(8,128)S(1)} %pad_maximum_fusion.refs_0_), channel_id=1, source_target_pairs={{0,2},{1,3},{2,0},{3,1},{4,6},{5,7},{6,4},{7,5},{8,10},{9,11},{10,... | collective-permute-start | bytes 393224 | tf_op jit(solution)/shard_map/ppermute | solution.py:21
  19.7 9.1 %collective-permute-start.4 = (f32[2,4,16,256]{3,2,1,0:T(8,128)S(1)}, f32[2,4,16,256]{3,2,1,0:T(8,128)S(1)}, u32[]{:S(2)}, u32[]{:S(2)}) collective-permute-start(f32[2,4,16,256]{3,2,1,0:T(8,128)S(1)} %pad_maximum_fusion.refs_0_), channel_id=1, source_target_pairs={{0,3},{1,2},{2,1},{3,0},{4,7},{5,6},{6,5},{7,4},{8,11},{9,10},{10,... | collective-permute-start | bytes 393224 | tf_op jit(solution)/shard_map/ppermute | solution.py:21
  20.0 9.4 %collective-permute-start.5 = (f32[8,16,256]{2,1,0:T(8,128)S(1)}, f32[8,16,256]{2,1,0:T(8,128)S(1)}, u32[]{:S(2)}, u32[]{:S(2)}) collective-permute-start(f32[8,16,256]{2,1,0:T(8,128)S(1)} %get-tuple-element.26), channel_id=1, source_target_pairs={{0,4},{4,0},{8,12},{12,8},{16,20},{20,16},{24,28},{28,24},{1,5},{5... | collective-permute-start | bytes 393224 | tf_op jit(solution)/shard_map/ppermute | solution.py:21
  31.5 4.6 %collective-permute-start.7 = (f32[32,256]{1,0:T(8,128)S(1)}, f32[32,256]{1,0:T(8,128)S(1)}, u32[]{:S(2)}, u32[]{:S(2)}) collective-permute-start(f32[32,256]{1,0:T(8,128)S(1)} %get-tuple-element.31), channel_id=1, source_target_pairs={{0,1},{1,2},{2,3},{3,0},{4,5},{5,6},{6,7},{7,4},{8,9},{9,10},{10,1... | collective-permute-start | bytes 98312 | tf_op jit(solution)/shard_map/ppermute | solution.py:21
  31.6 4.5 %collective-permute-start.8 = (f32[32,256]{1,0:T(8,128)S(1)}, f32[32,256]{1,0:T(8,128)S(1)}, u32[]{:S(2)}, u32[]{:S(2)}) collective-permute-start(f32[32,256]{1,0:T(8,128)S(1)} %get-tuple-element.31), channel_id=1, source_target_pairs={{0,2},{1,3},{2,0},{3,1},{4,6},{5,7},{6,4},{7,5},{8,10},{9,11},{10,... | collective-permute-start | bytes 98312 | tf_op jit(solution)/shard_map/ppermute | solution.py:21
  33.1 3.0 %collective-permute-start.9 = (f32[32,256]{1,0:T(8,128)S(1)}, f32[32,256]{1,0:T(8,128)S(1)}, u32[]{:S(2)}, u32[]{:S(2)}) collective-permute-start(f32[32,256]{1,0:T(8,128)S(1)} %get-tuple-element.31), channel_id=1, source_target_pairs={{0,3},{1,0},{2,1},{3,2},{4,7},{5,4},{6,5},{7,6},{8,11},{9,8},{10,9... | collective-permute-start | bytes 98312 | tf_op jit(solution)/shard_map/ppermute | solution.py:21

commit v9 on v7

--- a/solution.py
+++ b/solution.py
@@ -10,7 +10,7 @@
 ITERS = 4
 EDGE = ITERS
 ENTRIES = 16
-CHUNKS = 5
+CHUNKS = 2
 LANES = 128
 HALVES = (slice(0, LANES), slice(LANES, 2 * LANES))
 SHORT = pl.CostEstimate(flops=1000, bytes_accessed=1000, transcendentals=0)
@@ -72,28 +72,22 @@
 
 
 def pack_kernel(parts, place, lam, ew, ed, nw, nd, mf, top, *refs):
-    coef_first, coef_second, lam_first, lam_second, lam_v, field_v = refs[:6]
-    top_v, entry, field_p, lam_p, sems = refs[6:]
+    coef_first, coef_second, lam_first, lam_second = refs[:4]
+    field_s, top_s, lam_s, entry, field_p, lam_p, sems = refs[4:]
     tags, levels, cols, lats = lam.shape
-    edges = (pl.ds(0, 8), pl.ds(cols - 8, 8))
-    middle = pl.ds(8, cols - 16)
     copies = []
 
     def copy(src, dst):
         copies.append(pltpu.make_async_copy(src, dst, sems.at[len(copies)]))
         copies[-1].start()
 
-    copy(top, top_v)
-    fields = list(enumerate((ew, ed, nw, nd, mf)))
-    for part in edges:
-        for f, field in fields:
-            copy(field.at[:, part], field_v.at[f, :, part])
-    for part in edges:
-        copy(lam.at[:, :, part], lam_v.at[:, :, part])
-    for f, field in fields:
-        copy(field.at[:, middle], field_v.at[f, :, middle])
-    copy(lam.at[:, :, middle], lam_v.at[:, :, middle])
-    for c in copies[:11]:
+    for side, at in ((LOW, 0), (HIGH, cols - 8)):
+        for f, field in enumerate((ew, ed, nw, nd, mf)):
+            copy(field.at[:, pl.ds(at, 8)], field_s.at[f, side])
+        copy(top.at[pl.ds(at, 8)], top_s.at[side])
+    for side, at in ((LOW, 0), (HIGH, cols - 8)):
+        copy(lam.at[:, :, pl.ds(at, 8)], lam_s.at[side])
+    for c in copies[:12]:
         c.wait()
     pitch = 9
     slab = levels * pitch
@@ -102,10 +96,10 @@
     def _(level):
         row = place_of(level, levels) * pitch
         for f in range(5):
-            for side, part in enumerate(edges):
+            for side in (LOW, HIGH):
                 for k in range(2):
                     at = ((f * 2 + side) * 2 + k) * slab
-                    field_p[pl.ds(at + row, 8), :] = field_v[f, level, part, HALVES[k]]
+                    field_p[pl.ds(at + row, 8), :] = field_s[f, side, level, :, HALVES[k]]
 
     def field(f, side, c):
         return column_at(field_p, (f * 2 + side) * 2 * slab + c, levels, pitch, slab)
@@ -119,28 +113,26 @@
         for side in (LOW, HIGH):
             c = j + (start + 1) * side
             east, west, north, south = faces(*(field(f, side, c) for f in range(4)))
-            row = top_v[pl.ds(c + (cols - 8) * side, 1), :]
-            lift = updraft(field(4, side, c), row)
+            lift = updraft(field(4, side, c), top_s[side, pl.ds(c, 1), :])
             for n, value in enumerate((east, north, south, lift, west)):
                 entry[side, 5 * j + 1 + n] = value
 
     per = ENTRIES // parts
     mine = lax.rem(place[0], parts) * per
     odd = place[1]
-    coef_first[...] = entry[1 - odd, pl.ds(mine, per)]
-    coef_second[...] = entry[odd, pl.ds(mine, per)]
-
-    for c in copies[11:13]:
+    copy(entry.at[1 - odd, pl.ds(mine, per)], coef_first)
+    copy(entry.at[odd, pl.ds(mine, per)], coef_second)
+    for c in copies[12:14]:
         c.wait()
 
     @pl.loop(0, levels)
     def _(level):
         row = place_of(level, levels) * pitch
-        for side, part in enumerate(edges):
+        for side in (LOW, HIGH):
             for tag in range(tags):
                 for k in range(2):
                     at = ((side * 2 + k) * tags + tag) * slab
-                    lam_p[pl.ds(at + row, 8), :] = lam_v[tag, level, part, HALVES[k]]
+                    lam_p[pl.ds(at + row, 8), :] = lam_s[side, tag, level, :, HALVES[k]]
 
     @pl.loop(0, tags)
     def _(tag):
@@ -149,33 +141,29 @@
             for c in range(EDGE):
                 dest[tag * EDGE + c] = column_at(lam_p, at + c, levels, pitch, tags * slab)
 
-    for c in copies[13:]:
+    for c in copies[14:]:
         c.wait()
 
 
 def pack(parts, place, lam, fields, top):
     tags, levels, cols, lats = lam.shape
     hbm = pl.BlockSpec(memory_space=pltpu.HBM)
-    send = lambda slabs: pltpu.VMEM((slabs, levels, lats), jnp.float32)
-    few, many = ENTRIES // parts, tags * EDGE
+    vmem = pl.BlockSpec(memory_space=pltpu.VMEM)
+    coef_send = pltpu.HBM((ENTRIES // parts, levels, lats), jnp.float32)
+    lam_send = pltpu.VMEM((tags * EDGE, levels, lats), jnp.float32)
     return pl.pallas_call(
         functools.partial(pack_kernel, parts),
         in_specs=[pl.BlockSpec(memory_space=pltpu.SMEM)] + [hbm] * 7,
-        out_specs=[pl.BlockSpec(memory_space=pltpu.VMEM)] * 6,
-        out_shape=[
-            send(few),
-            send(few),
-            send(many),
-            send(many),
-            pltpu.VMEM(lam.shape, jnp.float32),
-            pltpu.VMEM((5, levels, cols, lats), jnp.float32),
-        ],
+        out_specs=[hbm, hbm, vmem, vmem],
+        out_shape=[coef_send, coef_send, lam_send, lam_send],
         scratch_shapes=[
-            pltpu.VMEM((cols, lats), jnp.int32),
+            pltpu.VMEM((5, 2, levels, 8, lats), jnp.float32),
+            pltpu.VMEM((2, 8, lats), jnp.int32),
+            pltpu.VMEM((2, tags, levels, 8, lats), jnp.float32),
             pltpu.VMEM((2, ENTRIES, levels, lats), jnp.float32),
             pltpu.VMEM((pitched(20, levels, 8), LANES), jnp.float32),
             pltpu.VMEM((pitched(4 * tags, levels, 8), LANES), jnp.float32),
-            pltpu.SemaphoreType.DMA((19,)),
+            pltpu.SemaphoreType.DMA((16,)),
         ],
         compiler_params=pltpu.CompilerParams(vmem_limit_bytes=24 << 20),
         cost_estimate=SHORT,
@@ -231,22 +219,29 @@
     return store
 
 
-def inner_kernel(place, lam, fields, top, region, *refs):
-    coef, l0, l1, l2, l3, final, rows, lam_p, field_p = refs
+def inner_kernel(place, lam, ew, ed, nw, nd, mf, top, region, *refs):
+    coef, l0, l1, l2, l3, final, rows, lam_s, field_s, lam_p, field_p, sems = refs
     tags, levels, cols, lats = lam.shape
     pitch = cols + 1
     slab = levels * pitch
+
+    loads = [
+        pltpu.make_async_copy(field, field_s.at[f], sems.at[f])
+        for f, field in enumerate((ew, ed, nw, nd, mf))
+    ]
+    loads.append(pltpu.make_async_copy(lam, lam_s, sems.at[5]))
+    for c in loads:
+        c.start()
+    for c in loads[:5]:
+        c.wait()
 
     @pl.loop(0, levels)
     def _(level):
         row = place_of(level, levels) * pitch
         for f in range(5):
             for k in range(2):
-                field_p[pl.ds((f * 2 + k) * slab + row, cols), :] = fields[f, level, :, HALVES[k]]
-        for tag in range(tags):
-            for k in range(2):
-                at = (k * tags + tag) * slab + row
-                lam_p[pl.ds(at, cols), :] = lam[tag, level, :, HALVES[k]]
+                at = (f * 2 + k) * slab + row
+                field_p[pl.ds(at, cols), :] = field_s[f, level, :, HALVES[k]]
 
     def coefficients(c, west):
         ew, ed, nw, nd, mf = (
@@ -265,6 +260,15 @@
 
     west = lax.fori_loop(0, cols // 8, some, jnp.zeros((levels, lats), jnp.float32))
     coef[cols, 2] = west
+    loads[5].wait()
+
+    @pl.loop(0, levels)
+    def _(level):
+        row = place_of(level, levels) * pitch
+        for tag in range(tags):
+            for k in range(2):
+                at = (k * tags + tag) * slab + row
+                lam_p[pl.ds(at, cols), :] = lam_s[tag, level, :, HALVES[k]]
 
     def given(c, tag):
         return column_at(lam_p, tag * slab + c, levels, pitch, tags * slab)
@@ -273,19 +277,20 @@
         for tag in range(tags):
             l0[at, tag] = given(c, tag)
     last = storing_rows(final, tags, levels, pitch)
-    loads = (given, loading(l1), loading(l2), loading(l3))
+    sources = (given, loading(l1), loading(l2), loading(l3))
     stores = (storing(l1), storing(l2), storing(l3), last)
     for t in range(ITERS):
-        sweep(t, lam.shape, place[0] * tags, region, coef, loads[t], stores[t], rows)
+        sweep(t, lam.shape, place[0] * tags, region, coef, sources[t], stores[t], rows)
 
 
 def inner(place, lam, fields, top, region):
     tags, levels, cols, lats = lam.shape
     vmem = pl.BlockSpec(memory_space=pltpu.VMEM)
+    hbm = pl.BlockSpec(memory_space=pltpu.HBM)
     state = pltpu.VMEM((cols, tags, levels, lats), jnp.float32)
     return pl.pallas_call(
         inner_kernel,
-        in_specs=[pl.BlockSpec(memory_space=pltpu.SMEM)] + [vmem] * 4,
+        in_specs=[pl.BlockSpec(memory_space=pltpu.SMEM)] + [hbm] * 6 + [vmem] * 2,
         out_specs=[vmem] * 7,
         out_shape=[
             pltpu.VMEM((cols + 1, 6, levels, lats), jnp.float32),
@@ -295,29 +300,37 @@
             pltpu.VMEM((ITERS, cols, lats), jnp.float32),
         ],
         scratch_shapes=[
+            pltpu.VMEM(lam.shape, jnp.float32),
+            pltpu.VMEM((5, levels, cols, lats), jnp.float32),
             pltpu.VMEM((pitched(2 * tags, levels, cols), LANES), jnp.float32),
             pltpu.VMEM((pitched(10, levels, cols), LANES), jnp.float32),
+            pltpu.SemaphoreType.DMA((6,)),
         ],
         compiler_params=pltpu.CompilerParams(vmem_limit_bytes=32 << 20),
         cost_estimate=SHORT,
         name="inner_steps",
-    )(place, lam, fields, top, region)
+    )(place, lam, *fields, top, region)
 
 
 def slot(c, cols):
     return (LOW, c + EDGE - 1) if c < EDGE else (HIGH, c - (cols - EDGE))
 
 
-def outer_kernel(parts, cols, place, coef, *refs):
-    pieces, wide, entry = refs[:parts], refs[parts], refs[parts + 1]
-    per = ENTRIES // parts
-    mine = lax.rem(place[0], parts)
-    odd = place[1]
-    for by in range(parts):
-        base = (mine ^ by) * per
-        entry[1 - odd, pl.ds(base, per)] = pieces[by][0]
-        entry[odd, pl.ds(base, per)] = pieces[by][1]
-
+def outer_kernel(place, coef, first, second, wide, entry, sems):
+    cols = coef.shape[0] - 1
+    odd, before = place[1], place[2]
+    copies = [
+        pltpu.make_async_copy(
+            first.at[pl.ds((1 - odd) * ENTRIES, ENTRIES)], entry.at[1 - odd], sems.at[0]
+        ),
+        pltpu.make_async_copy(
+            second.at[pl.ds(before * ENTRIES, ENTRIES)], entry.at[odd], sems.at[1]
+        ),
+    ]
+    for c in copies:
+        c.start()
+    for c in copies:
+        c.wait()
     entry[HIGH, 0] = coef[cols, 2]
 
     @pl.loop(0, EDGE - 1)
@@ -333,19 +346,23 @@
         wide[*slot(0, cols), i] = value
 
 
-def outer_coefs(parts, cols, place, coef, pieces):
+def outer_coefs(place, coef, first, second):
     _, _, levels, lats = coef.shape
     vmem = pl.BlockSpec(memory_space=pltpu.VMEM)
+    hbm = pl.BlockSpec(memory_space=pltpu.HBM)
     return pl.pallas_call(
-        functools.partial(outer_kernel, parts, cols),
-        in_specs=[pl.BlockSpec(memory_space=pltpu.SMEM)] + [vmem] * (1 + parts),
+        outer_kernel,
+        in_specs=[pl.BlockSpec(memory_space=pltpu.SMEM), vmem, hbm, hbm],
         out_specs=vmem,
         out_shape=pltpu.VMEM((2, 2 * EDGE - 1, 6, levels, lats), jnp.float32),
-        scratch_shapes=[pltpu.VMEM((2, ENTRIES, levels, lats), jnp.float32)],
+        scratch_shapes=[
+            pltpu.VMEM((2, ENTRIES, levels, lats), jnp.float32),
+            pltpu.SemaphoreType.DMA((2,)),
+        ],
         compiler_params=pltpu.CompilerParams(vmem_limit_bytes=24 << 20),
         cost_estimate=SHORT,
         name="outer_coefs",
-    )(place, coef, *pieces)
+    )(place, coef, first, second)
 
 
 def border_kernel(place, region, coef, wide, l0, l1, l2, l3, first, second, *refs):
@@ -460,28 +477,31 @@
 
 def local(lam, east_wind, north_wind, east_diff, north_diff, mass_flux, region, top):
     groups, tiles = lax.axis_size("grp"), lax.axis_size("dom")
-    parts = 4 if groups % 4 == 0 else 1
     grp, dom = lax.axis_index("grp"), lax.axis_index("dom")
-    place = jnp.stack([grp, dom % 2]).astype(jnp.int32)
-    far_lam, *far = (
+    odd = dom % 2
+    before = jnp.where((dom > 0) & (dom < tiles - 1), odd, 1 - odd)
+    place = jnp.stack([grp, odd, before]).astype(jnp.int32)
+    lam, *fields, far_top = (
         pltpu.with_memory_space_constraint(value, pltpu.HBM)
         for value in (lam, east_wind, east_diff, north_wind, north_diff, mass_flux, top)
     )
+    coef_first, coef_second, first, second = pack(groups, place, lam, fields, far_top)
 
     pairs = lambda i: i ^ 1
     turn = lambda i: (((i - 1) % tiles ^ 1) + 1) % tiles
-    coef_first, coef_second, first, second, own_lam, own_fields = pack(
-        parts, place, far_lam, far[:5], far[5]
-    )
-    coef_first = swapped(coef_first, "dom", pairs)
-    coef_second = swapped(coef_second, "dom", turn)
+
+    def gathered(value, partner):
+        sets = sorted({tuple(sorted((i, partner(i)))) for i in range(tiles)})
+        members = [[i * groups + rank for i in both for rank in range(groups)] for both in sets]
+        value = lax.all_gather(value, ("dom", "grp"), axis_index_groups=members, tiled=True)
+        return pltpu.with_memory_space_constraint(value, pltpu.HBM)
+
+    coef_first = gathered(coef_first, pairs)
+    coef_second = gathered(coef_second, turn)
     first = swapped(first, "dom", pairs)
     second = swapped(second, "dom", turn)
-    pieces = [jnp.stack([coef_first, coef_second])]
-    for by in range(1, parts):
-        pieces.append(swapped(pieces[0], "grp", lambda i: i ^ by))
-    coef, *states, final, rows = inner(place, own_lam, own_fields, top, region)
-    wide = outer_coefs(parts, lam.shape[2], place, coef, pieces)
+    coef, *states, final, rows = inner(place, lam, fields, top, region)
+    wide = outer_coefs(place, coef, coef_first, coef_second)
     final, grad = border(place, region, coef, wide, states, first, second, final, rows)
     share = grad
     for by in range(1, groups):

time: 32 us -> 63.1 us (1.97)
  blocking collectives: 0 us -> 34.5 us
  starting transfers between devices: 13.5 us -> 8.61 us
  Pallas kernels: 14.9 us -> 16.6 us
    all_gather x0 -> x2, blocking collectives: none -> 34.5 us  [gathered(): lax.all_gather(value, ('dom', 'grp'), axis_index_groups=members, tiled=True)]
    ppermute x10 -> x5, starting transfers between devices: 13.5 us -> 8.61 us  [swapped(): lax.ppermute(value, axis, [(i, partner(i)) for i in range(lax.axis_size(a...]
    pallas_call x1, Pallas kernels: 0.64 us -> 1.64 us  [outer_coefs(): pl.pallas_call(outer_kernel, in_specs=[pl.BlockSpec(memory_space=pltpu.SM...]
    pallas_call x1, Pallas kernels: 7.49 us -> 8.16 us  [inner(): pl.pallas_call(inner_kernel, in_specs=[pl.BlockSpec(memory_space=pltpu.SM...]
    ppermute x10 -> x5, waiting for transfers between devices: 1.88 us -> 1.75 us  [swapped(): lax.ppermute(value, axis, [(i, partner(i)) for i in range(lax.axis_size(a...]
  transfers between devices with their start and end apart: 10 -> 5, of which waited for: 2 -> 2; matrix products, arithmetic and copies ran while one was open for 0% -> 0% of each run, Pallas kernels for 31% -> 18%
where the time goes in v9:
time: 63.1 us; the launch traced here: 62.9 us
  blocking collectives  34.5 us (55%)
  Pallas kernels  16.6 us (26%)
  starting transfers between devices  8.61 us (14%)
  waiting for transfers between devices  1.75 us (3%)
  between operations  0.72 us (1%)
  other arithmetic  0.7 us (1%)
    all_gather x2, blocking collectives, gathered(): lax.all_gather(value, ('dom', 'grp'), axis_index_groups=members, tiled=True)  34.5 us
    ppermute x5, starting transfers between devices, swapped(): lax.ppermute(value, axis, [(i, partner(i)) for i in range(lax.axis_size(a...  8.61 us
    pallas_call x1, Pallas kernels, inner(): pl.pallas_call(inner_kernel, in_specs=[pl.BlockSpec(memory_space=pltpu.SM...  8.16 us
    pallas_call x1, Pallas kernels, pack(): pl.pallas_call(functools.partial(pack_kernel, parts), in_specs=[pl.BlockS...  3.22 us
    pallas_call x1, Pallas kernels, border(): pl.pallas_call(border_kernel, in_specs=[pl.BlockSpec(memory_space=pltpu.S...  2.02 us
    ppermute x5, waiting for transfers between devices, swapped(): lax.ppermute(value, axis, [(i, partner(i)) for i in range(lax.axis_size(a...  1.75 us
    pallas_call x1, Pallas kernels, outer_coefs(): pl.pallas_call(outer_kernel, in_specs=[pl.BlockSpec(memory_space=pltpu.SM...  1.64 us
    pallas_call x1, Pallas kernels, write(): pl.pallas_call(write_kernel, in_specs=[pl.BlockSpec(memory_space=pltpu.VM...  1.58 us
  transfers between devices with their start and end apart: 5, of which 2 were waited for; matrix products, arithmetic and copies ran while one was open for 0% of the time, Pallas kernels for 18%

profile of v9, /device:TPU:0, one launch (start us, length us, event | category | flops | bytes accessed | tf_op | source)
XLA Modules:
  0.0 62.9 jit_solution(7247324256088222172)
XLA Ops:
  0.6 0.1 pad_add_fusion.place
  0.7 0.0 copy-start.1
  0.7 3.2 %pack_edges.1 = (f32[4,16,256]{2,1,0:T(8,128)}, f32[4,16,256]{2,1,0:T(8,128)}, f32[16,16,256]{2,1,0:T(8,128)S(1)}, f32[16,16,256]{2,1,0:T(8,128)S(1)}) custom-call(s32[3]{0:T(128)S(1)} %pad_add_fusion.place, f32[4,16,32,256]{3,2,1,0:T(8,128)} %lam.3, f32[16,32,256]{2,1,0:T(8,128)} %ew.3, f32[16,32,256]{2,1,0:T(8,128)} %ed.3, f32[16,32,256]{2,1,0:T(8,128)} %nw.3, ...), custom_call_target="tpu_custom_call" | custom-call | flops 1000 | bytes 1000 | tf_op jit(solution)/shard_map/pack_edges/pallas_call | solution.py:154
  4.0 3.0 %collective-permute-start = (f32[16,16,256]{2,1,0:T(8,128)S(1)}, f32[16,16,256]{2,1,0:T(8,128)S(1)}, u32[]{:S(2)}, u32[]{:S(2)}) collective-permute-start(f32[16,16,256]{2,1,0:T(8,128)S(1)} %get-tuple-element.22), channel_id=1, source_target_pairs={{0,4},{4,0},{8,12},{12,8},{16,20},{20,16},{24,28},{28,24},{1,5},{5... | collective-permute-start | bytes 786440 | tf_op jit(solution)/shard_map/ppermute | solution.py:21
  7.0 3.6 %collective-permute-start.1 = (f32[16,16,256]{2,1,0:T(8,128)S(1)}, f32[16,16,256]{2,1,0:T(8,128)S(1)}, u32[]{:S(2)}, u32[]{:S(2)}) collective-permute-start(f32[16,16,256]{2,1,0:T(8,128)S(1)} %get-tuple-element.23), channel_id=1, source_target_pairs={{0,28},{4,8},{8,4},{12,16},{16,12},{20,24},{24,20},{28,0},{1,29},{... | collective-permute-start | bytes 786440 | tf_op jit(solution)/shard_map/ppermute | solution.py:21
  10.5 14.7 %all_gather.6.first = f32[32,16,256]{2,1,0:T(8,128)} all-gather(f32[4,16,256]{2,1,0:T(8,128)} %get-tuple-element.16), channel_id=1, replica_groups={{0,1,2,3,4,5,6,7},{8,9,10,11,12,13,14,15},{16,17,18,19,20,21,22,23},{24..., dimensions={0}, use_global_device_ids=true | all-gather | bytes 589824 | tf_op jit(solution)/shard_map/all_gather | solution.py:496
  25.2 0.0 copy-done
  25.2 0.0 copy-done.1
  25.2 0.0 copy-start.2
  25.2 8.2 %inner_steps.1 = (f32[33,6,16,256]{3,2,1,0:T(8,128)S(1)}, f32[4,4,16,256]{3,2,1,0:T(8,128)S(1)}, f32[32,4,16,256]{3,2,1,0:T(8,128)S(1)}, f32[32,4,16,256]{3,2,1,...) custom-call(s32[3]{0:T(128)S(1)} %pad_add_fusion.place, ...), custom_call_target="tpu_custom_call" | custom-call | flops 1000 | bytes 1000 | tf_op jit(solution)/shard_map/inner_steps/pallas_call | solution.py:291
  33.4 0.0 copy-done.2
  33.4 19.8 %all_gather.7.second = f32[32,16,256]{2,1,0:T(8,128)} all-gather(f32[4,16,256]{2,1,0:T(8,128)S(1)} %copy-done.2), channel_id=1, replica_groups={{0,1,2,3,28,29,30,31},{4,5,6,7,8,9,10,11},{12,13,14,15,16,17,18,19},{20..., dimensions={0}, use_global_device_ids=true | all-gather | bytes 589824 | tf_op jit(solution)/shard_map/all_gather | solution.py:496
  53.2 1.6 %outer_coefs.1.wide = f32[2,7,6,16,256]{4,3,2,1,0:T(8,128)S(1)} custom-call(s32[3]{0:T(128)S(1)} %pad_add_fusion.place, f32[33,6,16,256]{3,2,1,0:T(8,128)S(1)} %get-tuple-element.15.coef, f32[32,16,256]{2,1,0:T(8,128)} %all_gather.6.first, f32[32,16,256]{2,1,0:T(8,128)} %all_gather.7.second), custom_call_target="tpu_custom_call" | custom-call | flops 1000 | bytes 1000 | tf_op jit(solution)/shard_map/outer_coefs/pallas_call | solution.py:353
  54.8 0.0 collective-permute-done.first
  54.8 0.0 collective-permute-done.1.second
  54.9 2.0 %border_steps.1 = (f32[4264,128]{1,0:T(8,128)S(1)}, f32[32,256]{1,0:T(8,128)S(1)}) custom-call(s32[3]{0:T(128)S(1)} %pad_add_fusion.place, s32[32,256]{1,0:T(8,128)S(1)} %copy-done.1, f32[33,6,16,256]{3,2,1,0:T(8,128)S(1)} %get-tuple-element.15.coef, f32[2,7,6,16,256]{4,3,2,1,0:T(8,128)S(1)} %outer_coefs.1.wide, ...), custom_call_target="tpu_custom_call", output_to_operand_aliasing={{0}: (10, {})} | custom-call | flops 1000 | bytes 1000 | tf_op jit(solution)/shard_map/border_steps/pallas_call | solution.py:423
  56.9 0.8 %collective-permute-start.4 = (f32[32,256]{1,0:T(8,128)S(1)}, f32[32,256]{1,0:T(8,128)S(1)}, u32[]{:S(2)}, u32[]{:S(2)}) collective-permute-start(f32[32,256]{1,0:T(8,128)S(1)} %get-tuple-element.27), channel_id=1, source_target_pairs={{0,3},{1,0},{2,1},{3,2},{4,7},{5,4},{6,5},{7,6},{8,11},{9,8},{10,9... | collective-permute-start | bytes 98312 | tf_op jit(solution)/shard_map/ppermute | solution.py:21
  57.6 1.3 %collective-permute-start.3 = (f32[32,256]{1,0:T(8,128)S(1)}, f32[32,256]{1,0:T(8,128)S(1)}, u32[]{:S(2)}, u32[]{:S(2)}) collective-permute-start(f32[32,256]{1,0:T(8,128)S(1)} %get-tuple-element.27), channel_id=1, source_target_pairs={{0,2},{1,3},{2,0},{3,1},{4,6},{5,7},{6,4},{7,5},{8,10},{9,11},{10,... | collective-permute-start | bytes 98312 | tf_op jit(solution)/shard_map/ppermute | solution.py:21
  58.9 0.0 collective-permute-start.2
  58.9 1.6 %write_final.1 = f32[4,16,32,256]{3,2,1,0:T(8,128)} custom-call(f32[4264,128]{1,0:T(8,128)S(1)} %get-tuple-element.26.final), custom_call_target="tpu_custom_call" | custom-call | flops 1000 | bytes 1000 | tf_op jit(solution)/shard_map/write_final/pallas_call | solution.py:463
  60.5 0.0 collective-permute-done.4
  60.5 1.1 %collective-permute-done.3 = f32[32,256]{1,0:T(8,128)S(1)} collective-permute-done((f32[32,256]{1,0:T(8,128)S(1)}, f32[32,256]{1,0:T(8,128)S(1)}, u32[]{:S(2)}, u32[]{:S(2)}) %collective-permute-start.3) | collective-permute-done | bytes 32800 | tf_op jit(solution)/shard_map/ppermute | solution.py:21
  61.6 0.7 %collective-permute-done.2 = f32[32,256]{1,0:T(8,128)S(1)} collective-permute-done((f32[32,256]{1,0:T(8,128)S(1)}, f32[32,256]{1,0:T(8,128)S(1)}, u32[]{:S(2)}, u32[]{:S(2)}) %collective-permute-start.2) | collective-permute-done | bytes 32800 | tf_op jit(solution)/shard_map/ppermute | solution.py:21
  62.2 0.6 add_add_fusion
  (1 shorter events, 0.0 us)
Async XLA Ops:
  0.7 24.5 %copy-start = (s32[32,256]{1,0:T(8,128)S(1)}, s32[32,256]{1,0:T(8,128)}, u32[]{:S(2)}) copy-start(s32[32,256]{1,0:T(8,128)} %top.3) | copy-start | bytes 98308
  0.7 24.5 %copy-start.1 = (s32[32,256]{1,0:T(8,128)S(1)}, s32[32,256]{1,0:T(8,128)}, u32[]{:S(2)}) copy-start(s32[32,256]{1,0:T(8,128)} %region.3) | copy-start | bytes 98308
  4.0 50.9 %collective-permute-start = (f32[16,16,256]{2,1,0:T(8,128)S(1)}, f32[16,16,256]{2,1,0:T(8,128)S(1)}, u32[]{:S(2)}, u32[]{:S(2)}) collective-permute-start(f32[16,16,256]{2,1,0:T(8,128)S(1)} %get-tuple-element.22), channel_id=1, source_target_pairs={{0,4},{4,0},{8,12},{12,8},{16,20},{20,16},{24,28},{28,24},{1,5},{5... | collective-permute-start | bytes 786440 | tf_op jit(solution)/shard_map/ppermute | solution.py:21
  7.0 47.9 %collective-permute-start.1 = (f32[16,16,256]{2,1,0:T(8,128)S(1)}, f32[16,16,256]{2,1,0:T(8,128)S(1)}, u32[]{:S(2)}, u32[]{:S(2)}) collective-permute-start(f32[16,16,256]{2,1,0:T(8,128)S(1)} %get-tuple-element.23), channel_id=1, source_target_pairs={{0,28},{4,8},{8,4},{12,16},{16,12},{20,24},{24,20},{28,0},{1,29},{... | collective-permute-start | bytes 786440 | tf_op jit(solution)/shard_map/ppermute | solution.py:21
  25.2 8.2 %copy-start.2 = (f32[4,16,256]{2,1,0:T(8,128)S(1)}, f32[4,16,256]{2,1,0:T(8,128)}, u32[]{:S(2)}) copy-start(f32[4,16,256]{2,1,0:T(8,128)} %get-tuple-element.17) | copy-start | bytes 196612
  56.9 3.6 %collective-permute-start.4 = (f32[32,256]{1,0:T(8,128)S(1)}, f32[32,256]{1,0:T(8,128)S(1)}, u32[]{:S(2)}, u32[]{:S(2)}) collective-permute-start(f32[32,256]{1,0:T(8,128)S(1)} %get-tuple-element.27), channel_id=1, source_target_pairs={{0,3},{1,0},{2,1},{3,2},{4,7},{5,4},{6,5},{7,6},{8,11},{9,8},{10,9... | collective-permute-start | bytes 98312 | tf_op jit(solution)/shard_map/ppermute | solution.py:21
  57.6 3.9 %collective-permute-start.3 = (f32[32,256]{1,0:T(8,128)S(1)}, f32[32,256]{1,0:T(8,128)S(1)}, u32[]{:S(2)}, u32[]{:S(2)}) collective-permute-start(f32[32,256]{1,0:T(8,128)S(1)} %get-tuple-element.27), channel_id=1, source_target_pairs={{0,2},{1,3},{2,0},{3,1},{4,6},{5,7},{6,4},{7,5},{8,10},{9,11},{10,... | collective-permute-start | bytes 98312 | tf_op jit(solution)/shard_map/ppermute | solution.py:21
  58.9 3.3 %collective-permute-start.2 = (f32[32,256]{1,0:T(8,128)S(1)}, f32[32,256]{1,0:T(8,128)S(1)}, u32[]{:S(2)}, u32[]{:S(2)}) collective-permute-start(f32[32,256]{1,0:T(8,128)S(1)} %get-tuple-element.27), channel_id=1, source_target_pairs={{0,1},{1,2},{2,3},{3,0},{4,5},{5,6},{6,7},{7,4},{8,9},{9,10},{10,1... | collective-permute-start | bytes 98312 | tf_op jit(solution)/shard_map/ppermute | solution.py:21

commit v10 on v8

--- a/solution.py
+++ b/solution.py
@@ -72,23 +72,23 @@
 
 
 def pack_kernel(parts, place, lam, ew, ed, nw, nd, mf, top, *refs):
-    first, coef_second, lam_first, lam_second, lam_v, field_v = refs[:6]
-    top_v, entry, field_p, lam_p, sems = refs[6:]
+    first, coef_second, lam_first, lam_second = refs[:4]
+    field_s, top_s, lam_s, entry, field_p, lam_p, sems = refs[4:]
     tags, levels, cols, lats = lam.shape
-    edges = (pl.ds(0, 8), pl.ds(cols - 8, 8))
-    middle = pl.ds(8, cols - 16)
     copies = []
 
     def copy(src, dst):
         copies.append(pltpu.make_async_copy(src, dst, sems.at[len(copies)]))
         copies[-1].start()
 
-    copy(top, top_v)
-    for f, field in enumerate((ew, ed, nw, nd, mf)):
-        copy(field, field_v.at[f])
-    for part in (*edges, middle):
-        copy(lam.at[:, :, part], lam_v.at[:, :, part])
-    for c in copies[:6]:
+    for side, at in ((LOW, 0), (HIGH, cols - 8)):
+        for f, field in enumerate((ew, ed, nw, nd, mf)):
+            copy(field.at[:, pl.ds(at, 8)], field_s.at[f, side])
+        copy(top.at[pl.ds(at, 8)], top_s.at[side])
+    for side, at in ((LOW, 0), (HIGH, cols - 8)):
+        for tag in range(tags):
+            copy(lam.at[tag, :, pl.ds(at, 8)], lam_s.at[side, tag])
+    for c in copies[:12]:
         c.wait()
     pitch = 9
     slab = levels * pitch
@@ -97,10 +97,10 @@
     def _(level):
         row = place_of(level, levels) * pitch
         for f in range(5):
-            for side, part in enumerate(edges):
+            for side in (LOW, HIGH):
                 for k in range(2):
                     at = ((f * 2 + side) * 2 + k) * slab
-                    field_p[pl.ds(at + row, 8), :] = field_v[f, level, part, HALVES[k]]
+                    field_p[pl.ds(at + row, 8), :] = field_s[f, side, level, :, HALVES[k]]
 
     def field(f, side, c):
         return column_at(field_p, (f * 2 + side) * 2 * slab + c, levels, pitch, slab)
@@ -114,48 +114,44 @@
         for side in (LOW, HIGH):
             c = j + (start + 1) * side
             east, west, north, south = faces(*(field(f, side, c) for f in range(4)))
-            row = top_v[pl.ds(c + (cols - 8) * side, 1), :]
-            lift = updraft(field(4, side, c), row)
+            lift = updraft(field(4, side, c), top_s[side, pl.ds(c, 1), :])
             for n, value in enumerate((east, north, south, lift, west)):
                 entry[side, 5 * j + 1 + n] = value
 
     per = ENTRIES // parts
     mine = lax.rem(place[0], parts) * per
     odd = place[1]
-    half = tags // 2 * EDGE
-    first[half:] = entry[1 - odd, pl.ds(mine, per)]
+    first[EDGE:] = entry[1 - odd, pl.ds(mine, per)]
     coef_second[...] = entry[odd, pl.ds(mine, per)]
 
-    for c in copies[6:8]:
+    for c in copies[12:]:
         c.wait()
 
     @pl.loop(0, levels)
     def _(level):
         row = place_of(level, levels) * pitch
-        for side, part in enumerate(edges):
+        for side in (LOW, HIGH):
             for tag in range(tags):
                 for k in range(2):
                     at = ((side * 2 + k) * tags + tag) * slab
-                    lam_p[pl.ds(at + row, 8), :] = lam_v[tag, level, part, HALVES[k]]
+                    lam_p[pl.ds(at + row, 8), :] = lam_s[side, tag, level, :, HALVES[k]]
 
     def columns(tag, side):
         at = side * (2 * tags * slab + start) + tag * slab
         return [column_at(lam_p, at + c, levels, pitch, tags * slab) for c in range(EDGE)]
 
-    @pl.loop(0, tags // 2)
-    def _(i):
-        for c, value in enumerate(columns(i, 1 - odd)):
-            first[i * EDGE + c] = value
-        for c, value in enumerate(columns(tags // 2 + i, 1 - odd)):
-            lam_first[i * EDGE + c] = value
+    for c, value in enumerate(columns(0, 1 - odd)):
+        first[c] = value
+
+    @pl.loop(1, tags)
+    def _(tag):
+        for c, value in enumerate(columns(tag, 1 - odd)):
+            lam_first[(tag - 1) * EDGE + c] = value
 
     @pl.loop(0, tags)
     def _(tag):
         for c, value in enumerate(columns(tag, odd)):
             lam_second[tag * EDGE + c] = value
-
-    for c in copies[8:]:
-        c.wait()
 
 
 def pack(parts, place, lam, fields, top):
@@ -166,21 +162,16 @@
     return pl.pallas_call(
         functools.partial(pack_kernel, parts),
         in_specs=[pl.BlockSpec(memory_space=pltpu.SMEM)] + [hbm] * 7,
-        out_specs=[pl.BlockSpec(memory_space=pltpu.VMEM)] * 6,
-        out_shape=[
-            send(many // 2 + few),
-            send(few),
-            send(many // 2),
-            send(many),
-            pltpu.VMEM(lam.shape, jnp.float32),
-            pltpu.VMEM((5, levels, cols, lats), jnp.float32),
-        ],
+        out_specs=[pl.BlockSpec(memory_space=pltpu.VMEM)] * 4,
+        out_shape=[send(EDGE + few), send(few), send(many - EDGE), send(many)],
         scratch_shapes=[
-            pltpu.VMEM((cols, lats), jnp.int32),
+            pltpu.VMEM((5, 2, levels, 8, lats), jnp.float32),
+            pltpu.VMEM((2, 8, lats), jnp.int32),
+            pltpu.VMEM((2, tags, levels, 8, lats), jnp.float32),
             pltpu.VMEM((2, ENTRIES, levels, lats), jnp.float32),
             pltpu.VMEM((pitched(20, levels, 8), LANES), jnp.float32),
             pltpu.VMEM((pitched(4 * tags, levels, 8), LANES), jnp.float32),
-            pltpu.SemaphoreType.DMA((9,)),
+            pltpu.SemaphoreType.DMA((12 + 2 * tags,)),
         ],
         compiler_params=pltpu.CompilerParams(vmem_limit_bytes=24 << 20),
         cost_estimate=SHORT,
@@ -236,7 +227,7 @@
     return store
 
 
-def inner_kernel(place, lam, fields, top, region, *refs):
+def inner_kernel(place, lam, ew, ed, nw, nd, mf, top, region, *refs):
     coef, l0, l1, l2, l3, final, rows, lam_p, field_p = refs
     tags, levels, cols, lats = lam.shape
     pitch = cols + 1
@@ -245,9 +236,9 @@
     @pl.loop(0, levels)
     def _(level):
         row = place_of(level, levels) * pitch
-        for f in range(5):
+        for f, field in enumerate((ew, ed, nw, nd, mf)):
             for k in range(2):
-                field_p[pl.ds((f * 2 + k) * slab + row, cols), :] = fields[f, level, :, HALVES[k]]
+                field_p[pl.ds((f * 2 + k) * slab + row, cols), :] = field[level, :, HALVES[k]]
         for tag in range(tags):
             for k in range(2):
                 at = (k * tags + tag) * slab + row
@@ -290,7 +281,7 @@
     state = pltpu.VMEM((cols, tags, levels, lats), jnp.float32)
     return pl.pallas_call(
         inner_kernel,
-        in_specs=[pl.BlockSpec(memory_space=pltpu.SMEM)] + [vmem] * 4,
+        in_specs=[pl.BlockSpec(memory_space=pltpu.SMEM)] + [vmem] * 8,
         out_specs=[vmem] * 7,
         out_shape=[
             pltpu.VMEM((cols + 1, 6, levels, lats), jnp.float32),
@@ -306,7 +297,7 @@
         compiler_params=pltpu.CompilerParams(vmem_limit_bytes=32 << 20),
         cost_estimate=SHORT,
         name="inner_steps",
-    )(place, lam, fields, top, region)
+    )(place, lam, *fields, top, region)
 
 
 def slot(c, cols):
@@ -358,9 +349,8 @@
     cols, tags, levels, lats = l1.shape
     first_tag = place[0] * tags
     odd = place[1]
-    half = rest.shape[0]
-    halo[1 - odd, :half] = first[:half]
-    halo[1 - odd, half:] = rest[...]
+    halo[1 - odd, :EDGE] = first[:EDGE]
+    halo[1 - odd, EDGE:] = rest[...]
     halo[odd] = second[...]
 
     def coefs_at(c):
@@ -470,24 +460,22 @@
     parts = 4 if groups % 4 == 0 else 1
     grp, dom = lax.axis_index("grp"), lax.axis_index("dom")
     place = jnp.stack([grp, dom % 2]).astype(jnp.int32)
+    own = (lam, east_wind, east_diff, north_wind, north_diff, mass_flux)
     far_lam, *far = (
-        pltpu.with_memory_space_constraint(value, pltpu.HBM)
-        for value in (lam, east_wind, east_diff, north_wind, north_diff, mass_flux, top)
+        pltpu.with_memory_space_constraint(value, pltpu.HBM) for value in (*own, top)
     )
 
     pairs = lambda i: i ^ 1
     turn = lambda i: (((i - 1) % tiles ^ 1) + 1) % tiles
-    first, coef_second, rest, second, own_lam, own_fields = pack(
-        parts, place, far_lam, far[:5], far[5]
-    )
+    first, coef_second, rest, second = pack(parts, place, far_lam, far[:5], far[5])
     first = swapped(first, "dom", pairs)
     coef_second = swapped(coef_second, "dom", turn)
     rest = swapped(rest, "dom", pairs)
     second = swapped(second, "dom", turn)
-    pieces = [jnp.stack([first[rest.shape[0] :], coef_second])]
+    pieces = [jnp.stack([first[EDGE:], coef_second])]
     for by in range(1, parts):
         pieces.append(swapped(pieces[0], "grp", lambda i: i ^ by))
-    coef, *states, final, rows = inner(place, own_lam, own_fields, top, region)
+    coef, *states, final, rows = inner(place, own[0], own[1:], top, region)
     wide = outer_coefs(parts, lam.shape[2], place, coef, pieces)
     final, grad = border(place, region, coef, wide, states, (first, rest, second), final, rows)
     share = grad

time: 37 us -> 34.7 us (0.938)
  the two profiles are of different devices: /device:TPU:0 before, /device:TPU:24 now
where the time goes in v10:
time: 34.7 us; the launch traced here: 34.5 us
  Pallas kernels  13.7 us (39%)
  waiting for transfers between devices  11.2 us (32%)
  starting transfers between devices  8.12 us (23%)
  between operations  0.81 us (2%)
  other arithmetic  0.71 us (2%)
    ppermute x10, waiting for transfers between devices, swapped(): lax.ppermute(value, axis, [(i, partner(i)) for i in range(lax.axis_size(a...  11.2 us
    ppermute x10, starting transfers between devices, swapped(): lax.ppermute(value, axis, [(i, partner(i)) for i in range(lax.axis_size(a...  8.12 us
    pallas_call x1, Pallas kernels, inner(): pl.pallas_call(inner_kernel, in_specs=[pl.BlockSpec(memory_space=pltpu.SM...  6.25 us
    pallas_call x1, Pallas kernels, pack(): pl.pallas_call(functools.partial(pack_kernel, parts), in_specs=[pl.BlockS...  3.19 us
    pallas_call x1, Pallas kernels, border(): pl.pallas_call(border_kernel, in_specs=[pl.BlockSpec(memory_space=pltpu.S...  2.02 us
    pallas_call x1, Pallas kernels, write(): pl.pallas_call(write_kernel, in_specs=[pl.BlockSpec(memory_space=pltpu.VM...  1.58 us
  transfers between devices with their start and end apart: 10, of which 4 were waited for; matrix products, arithmetic and copies ran while one was open for 0% of the time, Pallas kernels for 25%

profile of v10, /device:TPU:24, one launch (start us, length us, event | category | flops | bytes accessed | tf_op | source)
XLA Modules:
  0.0 34.5 jit_solution(17530754857114361590)
XLA Ops:
  0.6 0.1 pad_add_fusion.place
  0.7 0.0 copy-start.4
  0.7 0.0 copy-start.5
  0.8 0.0 copy-start.6
  0.8 0.0 copy-start.7
  0.8 3.2 %pack_edges.1 = (f32[8,16,256]{2,1,0:T(8,128)S(1)}, f32[4,16,256]{2,1,0:T(8,128)S(1)}, f32[12,16,256]{2,1,0:T(8,128)S(1)}, f32[16,16,256]{2,1,0:T(8,128)S(1)}) custom-call(s32[2]{0:T(128)S(1)} %pad_add_fusion.place, f32[4,16,32,256]{3,2,1,0:T(8,128)} %lam.3, f32[16,32,256]{2,1,0:T(8,128)} %ew.3, f32[16,32,256]{2,1,0:T(8,128)} %ed.3, f32[16,32,256]{2,1,0:T(8,128)} %nw.3, ...), custom_call_target="tpu_custom_call" | custom-call | flops 1000 | bytes 1000 | tf_op jit(solution)/shard_map/pack_edges/pallas_call | solution.py:162
  4.0 1.6 %collective-permute-start = (f32[8,16,256]{2,1,0:T(8,128)S(1)}, f32[8,16,256]{2,1,0:T(8,128)S(1)}, u32[]{:S(2)}, u32[]{:S(2)}) collective-permute-start(f32[8,16,256]{2,1,0:T(8,128)S(1)} %get-tuple-element.16), channel_id=1, source_target_pairs={{0,4},{4,0},{8,12},{12,8},{16,20},{20,16},{24,28},{28,24},{1,5},{5... | collective-permute-start | bytes 393224 | tf_op jit(solution)/shard_map/ppermute | solution.py:21
  5.5 0.4 %collective-permute-start.1 = (f32[4,16,256]{2,1,0:T(8,128)S(1)}, f32[4,16,256]{2,1,0:T(8,128)S(1)}, u32[]{:S(2)}, u32[]{:S(2)}) collective-permute-start(f32[4,16,256]{2,1,0:T(8,128)S(1)} %get-tuple-element.17), channel_id=1, source_target_pairs={{0,28},{4,8},{8,4},{12,16},{16,12},{20,24},{24,20},{28,0},{1,29},{... | collective-permute-start | bytes 196616 | tf_op jit(solution)/shard_map/ppermute | solution.py:21
  5.9 1.3 %collective-permute-start.5 = (f32[12,16,256]{2,1,0:T(8,128)S(1)}, f32[12,16,256]{2,1,0:T(8,128)S(1)}, u32[]{:S(2)}, u32[]{:S(2)}) collective-permute-start(f32[12,16,256]{2,1,0:T(8,128)S(1)} %get-tuple-element.22), channel_id=1, source_target_pairs={{0,4},{4,0},{8,12},{12,8},{16,20},{20,16},{24,28},{28,24},{1,5},{5... | collective-permute-start | bytes 589832 | tf_op jit(solution)/shard_map/ppermute | solution.py:21
  7.2 1.2 %collective-permute-start.6 = (f32[16,16,256]{2,1,0:T(8,128)S(1)}, f32[16,16,256]{2,1,0:T(8,128)S(1)}, u32[]{:S(2)}, u32[]{:S(2)}) collective-permute-start(f32[16,16,256]{2,1,0:T(8,128)S(1)} %get-tuple-element.23), channel_id=1, source_target_pairs={{0,28},{4,8},{8,4},{12,16},{16,12},{20,24},{24,20},{28,0},{1,29},{... | collective-permute-start | bytes 786440 | tf_op jit(solution)/shard_map/ppermute | solution.py:21
  8.5 9.0 %collective-permute-done.first = f32[8,16,256]{2,1,0:T(8,128)S(1)} collective-permute-done((f32[8,16,256]{2,1,0:T(8,128)S(1)}, f32[8,16,256]{2,1,0:T(8,128)S(1)}, u32[]{:S(2)}, u32[]{:S(2)}) %collective-permute-start) | collective-permute-done | bytes 131104 | tf_op jit(solution)/shard_map/ppermute | solution.py:21
  17.5 0.1 collective-permute-start.4
  17.6 1.6 %collective-permute-start.3 = (f32[2,4,16,256]{3,2,1,0:T(8,128)S(1)}, f32[2,4,16,256]{3,2,1,0:T(8,128)S(1)}, u32[]{:S(2)}, u32[]{:S(2)}) collective-permute-start(f32[2,4,16,256]{3,2,1,0:T(8,128)S(1)} %pad_maximum_fusion.refs_0_), channel_id=1, source_target_pairs={{0,2},{1,3},{2,0},{3,1},{4,6},{5,7},{6,4},{7,5},{8,10},{9,11},{10,... | collective-permute-start | bytes 393224 | tf_op jit(solution)/shard_map/ppermute | solution.py:21
  19.1 0.3 collective-permute-start.2
  19.5 6.3 %inner_steps.1 = (f32[33,6,16,256]{3,2,1,0:T(8,128)S(1)}, f32[4,4,16,256]{3,2,1,0:T(8,128)S(1)}, f32[32,4,16,256]{3,2,1,0:T(8,128)S(1)}, f32[32,4,16,256]{3,2,1,...) custom-call(s32[2]{0:T(128)S(1)} %pad_add_fusion.place, ...), custom_call_target="tpu_custom_call" | custom-call | flops 1000 | bytes 1000 | tf_op jit(solution)/shard_map/inner_steps/pallas_call | solution.py:282
  25.7 0.4 %collective-permute-done.3.refs_2_ = f32[2,4,16,256]{3,2,1,0:T(8,128)S(1)} collective-permute-done((f32[2,4,16,256]{3,2,1,0:T(8,128)S(1)}, f32[2,4,16,256]{3,2,1,0:T(8,128)S(1)}, u32[]{:S(2)}, u32[]{:S(2)}) %collective-permute-start.3) | collective-permute-done | bytes 131104 | tf_op jit(solution)/shard_map/ppermute | solution.py:21
  26.1 0.6 %outer_coefs.1.wide = f32[2,7,6,16,256]{4,3,2,1,0:T(8,128)S(1)} custom-call(s32[2]{0:T(128)S(1)} %pad_add_fusion.place, f32[33,6,16,256]{3,2,1,0:T(8,128)S(1)} %get-tuple-element.15.coef, f32[2,4,16,256]{3,2,1,0:T(8,128)S(1)} %pad_maximum_fusion.refs_0_, f32[2,4,16,256]{3,2,1,0:T(8,128)S(1)} %collective-permute-done.2.refs_1_, ...), custom_call_target="tpu_custom_call" | custom-call | flops 1000 | bytes 1000 | tf_op jit(solution)/shard_map/outer_coefs/pallas_call | solution.py:335
  26.8 2.0 %border_steps.1 = (f32[4264,128]{1,0:T(8,128)S(1)}, f32[32,256]{1,0:T(8,128)S(1)}) custom-call(s32[2]{0:T(128)S(1)} %pad_add_fusion.place, s32[32,256]{1,0:T(8,128)S(1)} %copy-done.7, f32[33,6,16,256]{3,2,1,0:T(8,128)S(1)} %get-tuple-element.15.coef, f32[2,7,6,16,256]{4,3,2,1,0:T(8,128)S(1)} %outer_coefs.1.wide, ...), custom_call_target="tpu_custom_call", output_to_operand_aliasing={{0}: (11, {})} | custom-call | flops 1000 | bytes 1000 | tf_op jit(solution)/shard_map/border_steps/pallas_call | solution.py:403
  28.8 0.8 %collective-permute-start.9 = (f32[32,256]{1,0:T(8,128)S(1)}, f32[32,256]{1,0:T(8,128)S(1)}, u32[]{:S(2)}, u32[]{:S(2)}) collective-permute-start(f32[32,256]{1,0:T(8,128)S(1)} %get-tuple-element.27), channel_id=1, source_target_pairs={{0,3},{1,0},{2,1},{3,2},{4,7},{5,4},{6,5},{7,6},{8,11},{9,8},{10,9... | collective-permute-start | bytes 98312 | tf_op jit(solution)/shard_map/ppermute | solution.py:21
  29.6 0.9 %collective-permute-start.8 = (f32[32,256]{1,0:T(8,128)S(1)}, f32[32,256]{1,0:T(8,128)S(1)}, u32[]{:S(2)}, u32[]{:S(2)}) collective-permute-start(f32[32,256]{1,0:T(8,128)S(1)} %get-tuple-element.27), channel_id=1, source_target_pairs={{0,2},{1,3},{2,0},{3,1},{4,6},{5,7},{6,4},{7,5},{8,10},{9,11},{10,... | collective-permute-start | bytes 98312 | tf_op jit(solution)/shard_map/ppermute | solution.py:21
  30.6 1.6 %write_final.1 = f32[4,16,32,256]{3,2,1,0:T(8,128)} custom-call(f32[4264,128]{1,0:T(8,128)S(1)} %get-tuple-element.26.final), custom_call_target="tpu_custom_call" | custom-call | flops 1000 | bytes 1000 | tf_op jit(solution)/shard_map/write_final/pallas_call | solution.py:443
  32.1 1.4 %collective-permute-done.8 = f32[32,256]{1,0:T(8,128)S(1)} collective-permute-done((f32[32,256]{1,0:T(8,128)S(1)}, f32[32,256]{1,0:T(8,128)S(1)}, u32[]{:S(2)}, u32[]{:S(2)}) %collective-permute-start.8) | collective-permute-done | bytes 32800 | tf_op jit(solution)/shard_map/ppermute | solution.py:21
  33.5 0.4 %collective-permute-done.7 = f32[32,256]{1,0:T(8,128)S(1)} collective-permute-done((f32[32,256]{1,0:T(8,128)S(1)}, f32[32,256]{1,0:T(8,128)S(1)}, u32[]{:S(2)}, u32[]{:S(2)}) %collective-permute-start.7) | collective-permute-done | bytes 32800 | tf_op jit(solution)/shard_map/ppermute | solution.py:21
  33.9 0.6 %add_add_fusion = f32[32,256]{1,0:T(8,128)} fusion(f32[32,256]{1,0:T(8,128)S(1)} %collective-permute-done.9, f32[32,256]{1,0:T(8,128)S(1)} %collective-permute-done.8, f32[32,256]{1,0:T(8,128)S(1)} %get-tuple-element.27, f32[32,256]{1,0:T(8,128)S(1)} %collective-permute-done.7), kind=kLoop, calls=%fused_computation.2 | loop fusion | flops 24576 | bytes 163840 | tf_op jit(solution)/shard_map/add | solution.py:483
  (21 shorter events, 0.1 us)
Async XLA Ops:
  0.7 18.7 %copy-start = (f32[4,16,32,256]{3,2,1,0:T(8,128)S(1)}, f32[4,16,32,256]{3,2,1,0:T(8,128)}, u32[]{:S(2)}) copy-start(f32[4,16,32,256]{3,2,1,0:T(8,128)} %lam.3) | copy-start | bytes 6291460
  0.7 18.7 %copy-start.1 = (f32[16,32,256]{2,1,0:T(8,128)S(1)}, f32[16,32,256]{2,1,0:T(8,128)}, u32[]{:S(2)}) copy-start(f32[16,32,256]{2,1,0:T(8,128)} %ew.3) | copy-start | bytes 1572868
  0.7 18.7 %copy-start.2 = (f32[16,32,256]{2,1,0:T(8,128)S(1)}, f32[16,32,256]{2,1,0:T(8,128)}, u32[]{:S(2)}) copy-start(f32[16,32,256]{2,1,0:T(8,128)} %ed.3) | copy-start | bytes 1572868
  0.7 18.7 %copy-start.3 = (f32[16,32,256]{2,1,0:T(8,128)S(1)}, f32[16,32,256]{2,1,0:T(8,128)}, u32[]{:S(2)}) copy-start(f32[16,32,256]{2,1,0:T(8,128)} %nw.3) | copy-start | bytes 1572868
  0.7 18.7 %copy-start.4 = (f32[16,32,256]{2,1,0:T(8,128)S(1)}, f32[16,32,256]{2,1,0:T(8,128)}, u32[]{:S(2)}) copy-start(f32[16,32,256]{2,1,0:T(8,128)} %nd.3) | copy-start | bytes 1572868
  0.7 18.7 %copy-start.5 = (f32[16,32,256]{2,1,0:T(8,128)S(1)}, f32[16,32,256]{2,1,0:T(8,128)}, u32[]{:S(2)}) copy-start(f32[16,32,256]{2,1,0:T(8,128)} %mf.3) | copy-start | bytes 1572868
  0.8 18.7 %copy-start.6 = (s32[32,256]{1,0:T(8,128)S(1)}, s32[32,256]{1,0:T(8,128)}, u32[]{:S(2)}) copy-start(s32[32,256]{1,0:T(8,128)} %top.3) | copy-start | bytes 98308
  0.8 18.7 %copy-start.7 = (s32[32,256]{1,0:T(8,128)S(1)}, s32[32,256]{1,0:T(8,128)}, u32[]{:S(2)}) copy-start(s32[32,256]{1,0:T(8,128)} %region.3) | copy-start | bytes 98308
  4.0 13.5 %collective-permute-start = (f32[8,16,256]{2,1,0:T(8,128)S(1)}, f32[8,16,256]{2,1,0:T(8,128)S(1)}, u32[]{:S(2)}, u32[]{:S(2)}) collective-permute-start(f32[8,16,256]{2,1,0:T(8,128)S(1)} %get-tuple-element.16), channel_id=1, source_target_pairs={{0,4},{4,0},{8,12},{12,8},{16,20},{20,16},{24,28},{28,24},{1,5},{5... | collective-permute-start | bytes 393224 | tf_op jit(solution)/shard_map/ppermute | solution.py:21
  5.5 11.9 %collective-permute-start.1 = (f32[4,16,256]{2,1,0:T(8,128)S(1)}, f32[4,16,256]{2,1,0:T(8,128)S(1)}, u32[]{:S(2)}, u32[]{:S(2)}) collective-permute-start(f32[4,16,256]{2,1,0:T(8,128)S(1)} %get-tuple-element.17), channel_id=1, source_target_pairs={{0,28},{4,8},{8,4},{12,16},{16,12},{20,24},{24,20},{28,0},{1,29},{... | collective-permute-start | bytes 196616 | tf_op jit(solution)/shard_map/ppermute | solution.py:21
  5.9 20.8 %collective-permute-start.5 = (f32[12,16,256]{2,1,0:T(8,128)S(1)}, f32[12,16,256]{2,1,0:T(8,128)S(1)}, u32[]{:S(2)}, u32[]{:S(2)}) collective-permute-start(f32[12,16,256]{2,1,0:T(8,128)S(1)} %get-tuple-element.22), channel_id=1, source_target_pairs={{0,4},{4,0},{8,12},{12,8},{16,20},{20,16},{24,28},{28,24},{1,5},{5... | collective-permute-start | bytes 589832 | tf_op jit(solution)/shard_map/ppermute | solution.py:21
  7.2 19.6 %collective-permute-start.6 = (f32[16,16,256]{2,1,0:T(8,128)S(1)}, f32[16,16,256]{2,1,0:T(8,128)S(1)}, u32[]{:S(2)}, u32[]{:S(2)}) collective-permute-start(f32[16,16,256]{2,1,0:T(8,128)S(1)} %get-tuple-element.23), channel_id=1, source_target_pairs={{0,28},{4,8},{8,4},{12,16},{16,12},{20,24},{24,20},{28,0},{1,29},{... | collective-permute-start | bytes 786440 | tf_op jit(solution)/shard_map/ppermute | solution.py:21
  17.5 8.2 %collective-permute-start.4 = (f32[2,4,16,256]{3,2,1,0:T(8,128)S(1)}, f32[2,4,16,256]{3,2,1,0:T(8,128)S(1)}, u32[]{:S(2)}, u32[]{:S(2)}) collective-permute-start(f32[2,4,16,256]{3,2,1,0:T(8,128)S(1)} %pad_maximum_fusion.refs_0_), channel_id=1, source_target_pairs={{0,3},{1,2},{2,1},{3,0},{4,7},{5,6},{6,5},{7,4},{8,11},{9,10},{10,... | collective-permute-start | bytes 393224 | tf_op jit(solution)/shard_map/ppermute | solution.py:21
  17.6 8.6 %collective-permute-start.3 = (f32[2,4,16,256]{3,2,1,0:T(8,128)S(1)}, f32[2,4,16,256]{3,2,1,0:T(8,128)S(1)}, u32[]{:S(2)}, u32[]{:S(2)}) collective-permute-start(f32[2,4,16,256]{3,2,1,0:T(8,128)S(1)} %pad_maximum_fusion.refs_0_), channel_id=1, source_target_pairs={{0,2},{1,3},{2,0},{3,1},{4,6},{5,7},{6,4},{7,5},{8,10},{9,11},{10,... | collective-permute-start | bytes 393224 | tf_op jit(solution)/shard_map/ppermute | solution.py:21
  19.1 7.0 %collective-permute-start.2 = (f32[2,4,16,256]{3,2,1,0:T(8,128)S(1)}, f32[2,4,16,256]{3,2,1,0:T(8,128)S(1)}, u32[]{:S(2)}, u32[]{:S(2)}) collective-permute-start(f32[2,4,16,256]{3,2,1,0:T(8,128)S(1)} %pad_maximum_fusion.refs_0_), channel_id=1, source_target_pairs={{0,1},{1,0},{2,3},{3,2},{4,5},{5,4},{6,7},{7,6},{8,9},{9,8},{10,11... | collective-permute-start | bytes 393224 | tf_op jit(solution)/shard_map/ppermute | solution.py:21
  28.8 3.3 %collective-permute-start.9 = (f32[32,256]{1,0:T(8,128)S(1)}, f32[32,256]{1,0:T(8,128)S(1)}, u32[]{:S(2)}, u32[]{:S(2)}) collective-permute-start(f32[32,256]{1,0:T(8,128)S(1)} %get-tuple-element.27), channel_id=1, source_target_pairs={{0,3},{1,0},{2,1},{3,2},{4,7},{5,4},{6,5},{7,6},{8,11},{9,8},{10,9... | collective-permute-start | bytes 98312 | tf_op jit(solution)/shard_map/ppermute | solution.py:21
  29.6 3.9 %collective-permute-start.8 = (f32[32,256]{1,0:T(8,128)S(1)}, f32[32,256]{1,0:T(8,128)S(1)}, u32[]{:S(2)}, u32[]{:S(2)}) collective-permute-start(f32[32,256]{1,0:T(8,128)S(1)} %get-tuple-element.27), channel_id=1, source_target_pairs={{0,2},{1,3},{2,0},{3,1},{4,6},{5,7},{6,4},{7,5},{8,10},{9,11},{10,... | collective-permute-start | bytes 98312 | tf_op jit(solution)/shard_map/ppermute | solution.py:21
  30.5 3.3 %collective-permute-start.7 = (f32[32,256]{1,0:T(8,128)S(1)}, f32[32,256]{1,0:T(8,128)S(1)}, u32[]{:S(2)}, u32[]{:S(2)}) collective-permute-start(f32[32,256]{1,0:T(8,128)S(1)} %get-tuple-element.27), channel_id=1, source_target_pairs={{0,1},{1,2},{2,3},{3,0},{4,5},{5,6},{6,7},{7,4},{8,9},{9,10},{10,1... | collective-permute-start | bytes 98312 | tf_op jit(solution)/shard_map/ppermute | solution.py:21

commit v11 on v6

--- a/solution.py
+++ b/solution.py
@@ -10,25 +10,14 @@
 ITERS = 4
 EDGE = ITERS
 ENTRIES = 16
-CHUNKS = 3
+CHUNKS = 2
 LANES = 128
 HALVES = (slice(0, LANES), slice(LANES, 2 * LANES))
 SHORT = pl.CostEstimate(flops=1000, bytes_accessed=1000, transcendentals=0)
 LOW, HIGH = 0, 1
 
-
 def swapped(value, axis, partner):
     return lax.ppermute(value, axis, [(i, partner(i)) for i in range(lax.axis_size(axis))])
-
-
-def level_of(shape):
-    row = lax.broadcasted_iota(jnp.int32, shape, 0)
-    half = shape[0] // 2
-    return jnp.where(row < half, 2 * row, 2 * (row - half) + 1)
-
-
-def place_of(level, levels):
-    return (level % 2) * (levels // 2) + level // 2
 
 
 def faces(ew, ed, nw, nd):
@@ -44,13 +33,21 @@
 
 def updraft(mf, top_row):
     levels = mf.shape[0]
-    level = level_of(mf.shape)
+    level = lax.broadcasted_iota(jnp.int32, mf.shape, 0)
     return jnp.where((level < top_row) & (level < levels - 1), mf, 0.0)
+
+
+def level_above(h):
+    if h.shape[0] == 8:
+        return pltpu.roll(h, 7, 0)
+    parts = [pltpu.roll(h[at : at + 8], 7, 0) for at in range(0, h.shape[0], 8)]
+    inside = lax.broadcasted_iota(jnp.int32, parts[0].shape, 0) < 7
+    joined = [jnp.where(inside, low, high) for low, high in zip(parts, parts[1:])]
+    return jnp.concatenate([*joined, parts[-1]], axis=0)
 
 
 def advance(coefs, mid, east, west):
     d, e, w, n, s, u = coefs
-    half = mid.shape[0] // 2
     h = d * mid + e * east + w * west
     lane = lax.broadcasted_iota(jnp.int32, (mid.shape[0], LANES), 1)
     north = [pltpu.roll(mid[:, part], LANES - 1, 1) for part in HALVES]
@@ -58,8 +55,7 @@
     north = jnp.concatenate([jnp.where(lane < LANES - 1, *north), north[1]], axis=1)
     south = jnp.concatenate([south[0], jnp.where(lane > 0, south[1], south[0])], axis=1)
     h = h + n * north + s * south
-    above = jnp.concatenate([h[half:], pltpu.roll(h[:half], half - 1, 0)], axis=0)
-    return h + u * (above - h)
+    return h + u * (level_above(h) - h)
 
 
 def pitched(slabs, levels, width):
@@ -87,7 +83,8 @@
         copy(top.at[pl.ds(at, 8)], top_s.at[side])
     field_copies = len(copies)
     for side, at in ((LOW, 0), (HIGH, cols - 8)):
-        copy(lam.at[:, :, pl.ds(at, 8)], lam_s.at[side])
+        for tag in range(tags):
+            copy(lam.at[tag, :, pl.ds(at, 8)], lam_s.at[side, tag])
     for c in copies[:field_copies]:
         c.wait()
     pitch = 9
@@ -95,7 +92,7 @@
 
     @pl.loop(0, levels)
     def _(level):
-        row = place_of(level, levels) * pitch
+        row = level * pitch
         for f in range(5):
             for side in range(2):
                 for k in range(2):
@@ -129,7 +126,7 @@
 
     @pl.loop(0, levels)
     def _(level):
-        row = place_of(level, levels) * pitch
+        row = level * pitch
         for side in range(2):
             for tag in range(tags):
                 for k in range(2):
@@ -160,7 +157,7 @@
             pltpu.VMEM((2, ENTRIES, levels, lats), jnp.float32),
             pltpu.VMEM((pitched(20, levels, 8), LANES), jnp.float32),
             pltpu.VMEM((pitched(4 * tags, levels, 8), LANES), jnp.float32),
-            pltpu.SemaphoreType.DMA((14,)),
+            pltpu.SemaphoreType.DMA((12 + 2 * tags,)),
         ],
         compiler_params=pltpu.CompilerParams(vmem_limit_bytes=24 << 20),
         cost_estimate=SHORT,
@@ -224,7 +221,7 @@
 
     @pl.loop(0, levels)
     def _(level):
-        row = place_of(level, levels) * pitch
+        row = level * pitch
         for f, field in enumerate((ew, ed, nw, nd, mf)):
             for k in range(2):
                 field_p[pl.ds((f * 2 + k) * slab + row, cols), :] = field[level, :, HALVES[k]]
@@ -339,20 +336,17 @@
     )(place, coef, *pieces)
 
 
-def border_kernel(place, region, coef, wide, l0, l1, l2, l3, first, second, *refs):
-    final_in, rows_in, final, grad, halo, work, rows = refs
-    cols, tags, levels, lats = l1.shape
+def border_steps(depth, place, region, coef, wide, kept, l0, halos, halo, work, store, rows):
+    cols, tags, levels, lats = kept[1].shape
     first_tag = place[0] * tags
-    odd = place[1]
-    halo[1 - odd] = first[...]
-    halo[odd] = second[...]
+    part = slice(0, depth)
+    halo[1 - place[1]] = halos[0][:, part]
+    halo[place[1]] = halos[1][:, part]
 
     def coefs_at(c):
         if 0 < c < cols:
-            return [coef[c, j] for j in range(6)]
-        return [wide[*slot(c, cols), j] for j in range(6)]
-
-    kept = (None, l1, l2, l3)
+            return [coef[c, j, part] for j in range(6)]
+        return [wide[*slot(c, cols), j, part] for j in range(6)]
 
     def state(t, c, tag):
         if t == 0:
@@ -360,14 +354,14 @@
                 return halo[LOW, tag * EDGE + c + EDGE]
             if c >= cols:
                 return halo[HIGH, tag * EDGE + c - cols]
-            return l0[c if c < 2 else c - (cols - 4), tag]
-        return kept[t][c, tag] if t <= c < cols - t else work[t, *slot(c, cols), tag]
+            return l0[c if c < 2 else c - (cols - 4), tag, part]
+        if t <= c < cols - t:
+            return kept[t][c, tag, part]
+        return work[t, *slot(c, cols), tag]
 
     def column(t, c):
         return [state(t, c, tag) for tag in range(tags)]
 
-    rows[...] = rows_in[...]
-    store = storing_rows(final, tags, levels, cols + 1)
     for t in range(ITERS):
         reach = EDGE - 1 - t
         for run in (range(-reach, t + 1), range(cols - t - 1, cols + reach)):
@@ -379,39 +373,107 @@
                 for k in range(tags):
                     if t < ITERS - 1:
                         work[t + 1, *slot(c, cols), k] = new[k]
-                    else:
+                    elif store is not None:
                         store(c, k, new[k])
-                if 0 <= c < cols:
+                if rows is not None and 0 <= c < cols:
                     rows[t, c : c + 1, :] = chosen(region[c : c + 1, :], first_tag, new)
                 west, mid = mid, east
+
+
+def low_kernel(place, region, coef, wide, l0, l1, l2, l3, first, second, rows_in, grad, halo, work, rows):
+    rows[...] = rows_in[...]
+    kept = (None, l1, l2, l3)
+    border_steps(
+        8, place, region, coef, wide, kept, l0, (first, second), halo, work, None, rows
+    )
     total = rows[0]
     for t in range(1, ITERS):
         total = total + rows[t]
     grad[...] = total
 
 
-def border(place, region, coef, wide, states, first, second, final, rows):
+def border_scratch(tags, depth, lats):
+    return [
+        pltpu.VMEM((2, tags * EDGE, depth, lats), jnp.float32),
+        pltpu.VMEM((ITERS, 2, 2 * EDGE - 1, tags, depth, lats), jnp.float32),
+    ]
+
+
+def gradient(place, region, coef, wide, states, halos, rows):
     cols, tags, levels, lats = states[1].shape
     vmem = pl.BlockSpec(memory_space=pltpu.VMEM)
-    operands = [region, coef, wide, *states, first, second]
+    operands = [region, coef, wide, *states, *halos, rows]
+    return pl.pallas_call(
+        low_kernel,
+        in_specs=[pl.BlockSpec(memory_space=pltpu.SMEM)] + [vmem] * len(operands),
+        out_specs=vmem,
+        out_shape=pltpu.VMEM((cols, lats), jnp.float32),
+        scratch_shapes=[
+            *border_scratch(tags, 8, lats),
+            pltpu.VMEM((ITERS, cols, lats), jnp.float32),
+        ],
+        compiler_params=pltpu.CompilerParams(vmem_limit_bytes=32 << 20),
+        cost_estimate=SHORT,
+        name="border_low_levels",
+    )(place, *operands)
+
+
+def border_kernel(place, coef, wide, l0, l1, l2, l3, first, second, *refs):
+    final_in, out_in, final, out, halo, work, sides, sems = refs
+    cols, tags, levels, lats = l1.shape
+    pitch = cols + 1
+    store = storing_rows(final, tags, levels, pitch)
+    kept = (None, l1, l2, l3)
+    border_steps(
+        levels, place, None, coef, wide, kept, l0, (first, second), halo, work, store, None
+    )
+    edges = (0, cols - 8)
+
+    @pl.loop(0, levels)
+    def _(level):
+        for tag in range(tags):
+            for k in range(2):
+                at = ((k * tags + tag) * levels + level) * pitch
+                for side, c in enumerate(edges):
+                    sides[side, tag, level, :, HALVES[k]] = final[pl.ds(at + c, 8), :]
+
+    copies = []
+    for side, c in enumerate(edges):
+        for tag in range(tags):
+            copies.append(
+                pltpu.make_async_copy(
+                    sides.at[side, tag], out.at[tag, :, pl.ds(c, 8)], sems.at[len(copies)]
+                )
+            )
+            copies[-1].start()
+    for c in copies:
+        c.wait()
+
+
+def border(place, coef, wide, states, halos, final, out):
+    cols, tags, levels, lats = states[1].shape
+    vmem = pl.BlockSpec(memory_space=pltpu.VMEM)
+    hbm = pl.BlockSpec(memory_space=pltpu.HBM)
+    operands = [coef, wide, *states, *halos]
+    n = len(operands) + 1
     return pl.pallas_call(
         border_kernel,
-        in_specs=[pl.BlockSpec(memory_space=pltpu.SMEM)] + [vmem] * (len(operands) + 2),
-        out_specs=[vmem] * 2,
+        in_specs=[pl.BlockSpec(memory_space=pltpu.SMEM)] + [vmem] * n + [hbm],
+        out_specs=[vmem, hbm],
         out_shape=[
             pltpu.VMEM(final.shape, jnp.float32),
-            pltpu.VMEM((cols, lats), jnp.float32),
-        ],
-        input_output_aliases={len(operands) + 1: 0},
+            pltpu.HBM(out.shape, jnp.float32),
+        ],
+        input_output_aliases={n: 0, n + 1: 1},
         scratch_shapes=[
-            pltpu.VMEM((2, tags * EDGE, levels, lats), jnp.float32),
-            pltpu.VMEM((ITERS, 2, 2 * EDGE - 1, tags, levels, lats), jnp.float32),
-            pltpu.VMEM((ITERS, cols, lats), jnp.float32),
+            *border_scratch(tags, levels, lats),
+            pltpu.VMEM((2, tags, levels, 8, lats), jnp.float32),
+            pltpu.SemaphoreType.DMA((2 * tags,)),
         ],
         compiler_params=pltpu.CompilerParams(vmem_limit_bytes=32 << 20),
         cost_estimate=SHORT,
-        name="border_steps",
-    )(place, *operands, final, rows)
+        name="border_all_levels",
+    )(place, *operands, final, out)[1]
 
 
 def write_kernel(final, out, block, sems):
@@ -422,30 +484,34 @@
 
         @pl.loop(0, levels)
         def _(level):
-            row = place_of(level, levels) * pitch
             for k in range(2):
-                at = (k * tags + tag) * levels * pitch + row
-                block[tag, level, :, HALVES[k]] = final[pl.ds(at, cols), :]
-
-        copies.append(pltpu.make_async_copy(block.at[tag], out.at[tag], sems.at[tag]))
+                at = ((k * tags + tag) * levels + level) * pitch + 8
+                block[tag, level, :, HALVES[k]] = final[pl.ds(at, cols - 16), :]
+
+        copies.append(
+            pltpu.make_async_copy(
+                block.at[tag], out.at[tag, :, pl.ds(8, cols - 16)], sems.at[tag]
+            )
+        )
         copies[-1].start()
     for c in copies:
         c.wait()
 
 
-def write(final, shape):
+def write_inner(final, shape):
+    tags, levels, cols, lats = shape
     return pl.pallas_call(
         write_kernel,
         in_specs=[pl.BlockSpec(memory_space=pltpu.VMEM)],
         out_specs=pl.BlockSpec(memory_space=pltpu.HBM),
         out_shape=pltpu.HBM(shape, jnp.float32),
         scratch_shapes=[
-            pltpu.VMEM(shape, jnp.float32),
-            pltpu.SemaphoreType.DMA((shape[0],)),
+            pltpu.VMEM((tags, levels, cols - 16, lats), jnp.float32),
+            pltpu.SemaphoreType.DMA((tags,)),
         ],
         compiler_params=pltpu.CompilerParams(vmem_limit_bytes=24 << 20),
         cost_estimate=SHORT,
-        name="write_final",
+        name="write_inner",
     )(final)
 
 
@@ -469,11 +535,15 @@
         pieces.append(swapped(pieces[0], "grp", lambda i: i ^ by))
     coef, *states, final, rows = inner(place, own[0], own[1:], top, region)
     wide = outer_coefs(parts, lam.shape[2], place, coef, pieces)
-    final, grad = border(place, region, coef, wide, states, first, second, final, rows)
+    out = write_inner(final, lam.shape)
+    wide, out = lax.optimization_barrier((wide, out))
+    grad = gradient(place, region, coef, wide, states, (first, second), rows)
+    grad, wide = lax.optimization_barrier((grad, wide))
+    out = border(place, coef, wide, states, (first, second), final, out)
     share = grad
     for by in range(1, groups):
         grad = grad + swapped(share, "grp", lambda i: (i + by) % groups)
-    return write(final, lam.shape), grad
+    return out, grad
 
 
 def solution(mesh):

time: 32 us -> 32 us (level)
  the two profiles are of different devices: /device:TPU:0 before, /device:TPU:1 now
where the time goes in v11:
time: 32 us; the launch traced here: 31.8 us
  Pallas kernels  15.3 us (48%)
  starting transfers between devices  13.7 us (43%)
  waiting for transfers between devices  1.19 us (4%)
  between operations  0.83 us (3%)
  other arithmetic  0.71 us (2%)
    ppermute x10, starting transfers between devices, swapped(): lax.ppermute(value, axis, [(i, partner(i)) for i in range(lax.axis_size(a...  13.7 us
    pallas_call x1, Pallas kernels, inner(): pl.pallas_call(inner_kernel, in_specs=[pl.BlockSpec(memory_space=pltpu.SM...  6.29 us
    pallas_call x1, Pallas kernels, border(): pl.pallas_call(border_kernel, in_specs=[pl.BlockSpec(memory_space=pltpu.S...  3.18 us
    pallas_call x1, Pallas kernels, pack(): pl.pallas_call(functools.partial(pack_kernel, parts), in_specs=[pl.BlockS...  2.83 us
    pallas_call x1, Pallas kernels, gradient(): pl.pallas_call(low_kernel, in_specs=[pl.BlockSpec(memory_space=pltpu.SMEM...  1.27 us
    ppermute x10, waiting for transfers between devices, swapped(): lax.ppermute(value, axis, [(i, partner(i)) for i in range(lax.axis_size(a...  1.19 us
    pallas_call x1, Pallas kernels, write_inner(): pl.pallas_call(write_kernel, in_specs=[pl.BlockSpec(memory_space=pltpu.VM...  1.14 us
  transfers between devices with their start and end apart: 10, of which 1 were waited for; matrix products, arithmetic and copies ran while one was open for 0% of the time, Pallas kernels for 35%

profile of v11, /device:TPU:1, one launch (start us, length us, event | category | flops | bytes accessed | tf_op | source)
XLA Modules:
  0.0 31.8 jit_solution(7520346129286670571)
XLA Ops:
  0.6 0.1 pad_add_fusion.place
  0.7 0.0 copy-start.4
  0.7 0.0 copy-start.5
  0.8 0.0 copy-start.6
  0.8 0.0 copy-start.7
  0.8 2.8 %pack_edges.1 = (f32[4,16,256]{2,1,0:T(8,128)S(1)}, f32[4,16,256]{2,1,0:T(8,128)S(1)}, f32[16,16,256]{2,1,0:T(8,128)S(1)}, f32[16,16,256]{2,1,0:T(8,128)S(1)}) custom-call(s32[2]{0:T(128)S(1)} %pad_add_fusion.place, f32[4,16,32,256]{3,2,1,0:T(8,128)} %lam.3, f32[16,32,256]{2,1,0:T(8,128)} %ew.3, f32[16,32,256]{2,1,0:T(8,128)} %ed.3, f32[16,32,256]{2,1,0:T(8,128)} %nw.3, ...), custom_call_target="tpu_custom_call" | custom-call | flops 1000 | bytes 1000 | tf_op jit(solution)/shard_map/pack_edges/pallas_call | solution.py:148
  3.6 2.1 %collective-permute-start = (f32[4,16,256]{2,1,0:T(8,128)S(1)}, f32[4,16,256]{2,1,0:T(8,128)S(1)}, u32[]{:S(2)}, u32[]{:S(2)}) collective-permute-start(f32[4,16,256]{2,1,0:T(8,128)S(1)} %get-tuple-element.19), channel_id=1, source_target_pairs={{0,4},{4,0},{8,12},{12,8},{16,20},{20,16},{24,28},{28,24},{1,5},{5... | collective-permute-start | bytes 196616 | tf_op jit(solution)/shard_map/ppermute | solution.py:20
  5.7 3.3 %collective-permute-start.1 = (f32[4,16,256]{2,1,0:T(8,128)S(1)}, f32[4,16,256]{2,1,0:T(8,128)S(1)}, u32[]{:S(2)}, u32[]{:S(2)}) collective-permute-start(f32[4,16,256]{2,1,0:T(8,128)S(1)} %get-tuple-element.20), channel_id=1, source_target_pairs={{0,28},{4,8},{8,4},{12,16},{16,12},{20,24},{24,20},{28,0},{1,29},{... | collective-permute-start | bytes 196616 | tf_op jit(solution)/shard_map/ppermute | solution.py:20
  9.0 1.3 %collective-permute-start.6 = (f32[16,16,256]{2,1,0:T(8,128)S(1)}, f32[16,16,256]{2,1,0:T(8,128)S(1)}, u32[]{:S(2)}, u32[]{:S(2)}) collective-permute-start(f32[16,16,256]{2,1,0:T(8,128)S(1)} %get-tuple-element.28), channel_id=1, source_target_pairs={{0,28},{4,8},{8,4},{12,16},{16,12},{20,24},{24,20},{28,0},{1,29},{... | collective-permute-start | bytes 786440 | tf_op jit(solution)/shard_map/ppermute | solution.py:20
  10.4 0.0 collective-permute-done
  10.4 1.2 %collective-permute-done.1 = f32[4,16,256]{2,1,0:T(8,128)S(1)} collective-permute-done((f32[4,16,256]{2,1,0:T(8,128)S(1)}, f32[4,16,256]{2,1,0:T(8,128)S(1)}, u32[]{:S(2)}, u32[]{:S(2)}) %collective-permute-start.1) | collective-permute-done | bytes 65568 | tf_op jit(solution)/shard_map/ppermute | solution.py:20
  11.6 3.4 %collective-permute-start.4 = (f32[2,4,16,256]{3,2,1,0:T(8,128)S(1)}, f32[2,4,16,256]{3,2,1,0:T(8,128)S(1)}, u32[]{:S(2)}, u32[]{:S(2)}) collective-permute-start(f32[2,4,16,256]{3,2,1,0:T(8,128)S(1)} %pad_maximum_fusion.refs_0_), channel_id=1, source_target_pairs={{0,3},{1,2},{2,1},{3,0},{4,7},{5,6},{6,5},{7,4},{8,11},{9,10},{10,... | collective-permute-start | bytes 393224 | tf_op jit(solution)/shard_map/ppermute | solution.py:20
  14.9 0.2 collective-permute-start.3
  15.2 0.2 collective-permute-start.2
  15.5 6.3 %inner_steps.1 = (f32[33,6,16,256]{3,2,1,0:T(8,128)S(1)}, f32[4,4,16,256]{3,2,1,0:T(8,128)S(1)}, f32[32,4,16,256]{3,2,1,0:T(8,128)S(1)}, f32[32,4,16,256]{3,2,1,...) custom-call(s32[2]{0:T(128)S(1)} %pad_add_fusion.place, ...), custom_call_target="tpu_custom_call" | custom-call | flops 1000 | bytes 1000 | tf_op jit(solution)/shard_map/inner_steps/pallas_call | solution.py:268
  21.8 1.1 %write_inner.1.refs_1_ = f32[4,16,32,256]{3,2,1,0:T(8,128)} custom-call(f32[4264,128]{1,0:T(8,128)S(1)} %get-tuple-element.21.final.refs_0_), custom_call_target="tpu_custom_call" | custom-call | flops 1000 | bytes 1000 | tf_op jit(solution)/shard_map/write_inner/pallas_call | solution.py:503
  22.9 0.0 collective-permute-done.4.refs_3_
  22.9 0.6 %outer_coefs.1.wide = f32[2,7,6,16,256]{4,3,2,1,0:T(8,128)S(1)} custom-call(s32[2]{0:T(128)S(1)} %pad_add_fusion.place, f32[33,6,16,256]{3,2,1,0:T(8,128)S(1)} %get-tuple-element.18.coef, f32[2,4,16,256]{3,2,1,0:T(8,128)S(1)} %pad_maximum_fusion.refs_0_, f32[2,4,16,256]{3,2,1,0:T(8,128)S(1)} %collective-permute-done.2.refs_1_, ...), custom_call_target="tpu_custom_call" | custom-call | flops 1000 | bytes 1000 | tf_op jit(solution)/shard_map/outer_coefs/pallas_call | solution.py:327
  23.6 1.3 %border_low_levels.1 = f32[32,256]{1,0:T(8,128)S(1)} custom-call(s32[2]{0:T(128)S(1)} %pad_add_fusion.place, s32[32,256]{1,0:T(8,128)S(1)} %copy-done.7, f32[33,6,16,256]{3,2,1,0:T(8,128)S(1)} %get-tuple-element.18.coef, f32[2,7,6,16,256]{4,3,2,1,0:T(8,128)S(1)} %outer_coefs.1.wide, f32[4,4,16,256]{3,2,1,0:T(8,128)S(1)} %get-tuple-element.23.l0, ...), custom_call_target="tpu_custom_call" | custom-call | flops 1000 | bytes 1000 | tf_op jit(solution)/shard_map/border_low_levels/pallas_call | solution.py:406
  24.9 0.6 %collective-permute-start.9 = (f32[32,256]{1,0:T(8,128)S(1)}, f32[32,256]{1,0:T(8,128)S(1)}, u32[]{:S(2)}, u32[]{:S(2)}) collective-permute-start(f32[32,256]{1,0:T(8,128)S(1)} %border_low_levels.1), channel_id=1, source_target_pairs={{0,3},{1,0},{2,1},{3,2},{4,7},{5,4},{6,5},{7,6},{8,11},{9,8},{10,9... | collective-permute-start | bytes 98312 | tf_op jit(solution)/shard_map/ppermute | solution.py:20
  25.5 1.3 %collective-permute-start.8 = (f32[32,256]{1,0:T(8,128)S(1)}, f32[32,256]{1,0:T(8,128)S(1)}, u32[]{:S(2)}, u32[]{:S(2)}) collective-permute-start(f32[32,256]{1,0:T(8,128)S(1)} %border_low_levels.1), channel_id=1, source_target_pairs={{0,2},{1,3},{2,0},{3,1},{4,6},{5,7},{6,4},{7,5},{8,10},{9,11},{10,... | collective-permute-start | bytes 98312 | tf_op jit(solution)/shard_map/ppermute | solution.py:20
  26.7 1.2 %collective-permute-start.7 = (f32[32,256]{1,0:T(8,128)S(1)}, f32[32,256]{1,0:T(8,128)S(1)}, u32[]{:S(2)}, u32[]{:S(2)}) collective-permute-start(f32[32,256]{1,0:T(8,128)S(1)} %border_low_levels.1), channel_id=1, source_target_pairs={{0,1},{1,2},{2,3},{3,0},{4,5},{5,6},{6,7},{7,4},{8,9},{9,10},{10,1... | collective-permute-start | bytes 98312 | tf_op jit(solution)/shard_map/ppermute | solution.py:20
  28.0 3.2 %border_all_levels.1 = (f32[4264,128]{1,0:T(8,128)S(1)}, f32[4,16,32,256]{3,2,1,0:T(8,128)}) custom-call(s32[2]{0:T(128)S(1)} %pad_add_fusion.place, f32[33,6,16,256]{3,2,1,0:T(8,128)S(1)} %get-tuple-element.18.coef, f32[2,7,6,16,256]{4,3,2,1,0:T(8,128)S(1)} %outer_coefs.1.wide, ...), custom_call_target="tpu_custom_call", output_to_operand_aliasing={{0}: (9, {}), {1}: (10, {})} | custom-call | flops 1000 | bytes 1000 | tf_op jit(solution)/shard_map/border_all_levels/pallas_call | solution.py:459
  31.2 0.6 %add_add_fusion = f32[32,256]{1,0:T(8,128)} fusion(f32[32,256]{1,0:T(8,128)S(1)} %collective-permute-done.9, f32[32,256]{1,0:T(8,128)S(1)} %collective-permute-done.8, f32[32,256]{1,0:T(8,128)S(1)} %border_low_levels.1, f32[32,256]{1,0:T(8,128)S(1)} %collective-permute-done.7), kind=kLoop, calls=%fused_computation.1 | loop fusion | flops 24576 | bytes 163840 | tf_op jit(solution)/shard_map/add | solution.py:545
  (21 shorter events, 0.1 us)
Async XLA Ops:
  0.7 14.7 %copy-start = (f32[4,16,32,256]{3,2,1,0:T(8,128)S(1)}, f32[4,16,32,256]{3,2,1,0:T(8,128)}, u32[]{:S(2)}) copy-start(f32[4,16,32,256]{3,2,1,0:T(8,128)} %lam.3) | copy-start | bytes 6291460
  0.7 14.7 %copy-start.1 = (f32[16,32,256]{2,1,0:T(8,128)S(1)}, f32[16,32,256]{2,1,0:T(8,128)}, u32[]{:S(2)}) copy-start(f32[16,32,256]{2,1,0:T(8,128)} %ew.3) | copy-start | bytes 1572868
  0.7 14.7 %copy-start.2 = (f32[16,32,256]{2,1,0:T(8,128)S(1)}, f32[16,32,256]{2,1,0:T(8,128)}, u32[]{:S(2)}) copy-start(f32[16,32,256]{2,1,0:T(8,128)} %ed.3) | copy-start | bytes 1572868
  0.7 14.7 %copy-start.3 = (f32[16,32,256]{2,1,0:T(8,128)S(1)}, f32[16,32,256]{2,1,0:T(8,128)}, u32[]{:S(2)}) copy-start(f32[16,32,256]{2,1,0:T(8,128)} %nw.3) | copy-start | bytes 1572868
  0.7 14.7 %copy-start.4 = (f32[16,32,256]{2,1,0:T(8,128)S(1)}, f32[16,32,256]{2,1,0:T(8,128)}, u32[]{:S(2)}) copy-start(f32[16,32,256]{2,1,0:T(8,128)} %nd.3) | copy-start | bytes 1572868
  0.7 14.7 %copy-start.5 = (f32[16,32,256]{2,1,0:T(8,128)S(1)}, f32[16,32,256]{2,1,0:T(8,128)}, u32[]{:S(2)}) copy-start(f32[16,32,256]{2,1,0:T(8,128)} %mf.3) | copy-start | bytes 1572868
  0.8 14.7 %copy-start.6 = (s32[32,256]{1,0:T(8,128)S(1)}, s32[32,256]{1,0:T(8,128)}, u32[]{:S(2)}) copy-start(s32[32,256]{1,0:T(8,128)} %top.3) | copy-start | bytes 98308
  0.8 14.7 %copy-start.7 = (s32[32,256]{1,0:T(8,128)S(1)}, s32[32,256]{1,0:T(8,128)}, u32[]{:S(2)}) copy-start(s32[32,256]{1,0:T(8,128)} %region.3) | copy-start | bytes 98308
  3.6 6.8 %collective-permute-start = (f32[4,16,256]{2,1,0:T(8,128)S(1)}, f32[4,16,256]{2,1,0:T(8,128)S(1)}, u32[]{:S(2)}, u32[]{:S(2)}) collective-permute-start(f32[4,16,256]{2,1,0:T(8,128)S(1)} %get-tuple-element.19), channel_id=1, source_target_pairs={{0,4},{4,0},{8,12},{12,8},{16,20},{20,16},{24,28},{28,24},{1,5},{5... | collective-permute-start | bytes 196616 | tf_op jit(solution)/shard_map/ppermute | solution.py:20
  5.7 5.8 %collective-permute-start.1 = (f32[4,16,256]{2,1,0:T(8,128)S(1)}, f32[4,16,256]{2,1,0:T(8,128)S(1)}, u32[]{:S(2)}, u32[]{:S(2)}) collective-permute-start(f32[4,16,256]{2,1,0:T(8,128)S(1)} %get-tuple-element.20), channel_id=1, source_target_pairs={{0,28},{4,8},{8,4},{12,16},{16,12},{20,24},{24,20},{28,0},{1,29},{... | collective-permute-start | bytes 196616 | tf_op jit(solution)/shard_map/ppermute | solution.py:20
  9.0 14.6 %collective-permute-start.5 = (f32[16,16,256]{2,1,0:T(8,128)S(1)}, f32[16,16,256]{2,1,0:T(8,128)S(1)}, u32[]{:S(2)}, u32[]{:S(2)}) collective-permute-start(f32[16,16,256]{2,1,0:T(8,128)S(1)} %get-tuple-element.27), channel_id=1, source_target_pairs={{0,4},{4,0},{8,12},{12,8},{16,20},{20,16},{24,28},{28,24},{1,5},{5... | collective-permute-start | bytes 786440 | tf_op jit(solution)/shard_map/ppermute | solution.py:20
  9.0 14.6 %collective-permute-start.6 = (f32[16,16,256]{2,1,0:T(8,128)S(1)}, f32[16,16,256]{2,1,0:T(8,128)S(1)}, u32[]{:S(2)}, u32[]{:S(2)}) collective-permute-start(f32[16,16,256]{2,1,0:T(8,128)S(1)} %get-tuple-element.28), channel_id=1, source_target_pairs={{0,28},{4,8},{8,4},{12,16},{16,12},{20,24},{24,20},{28,0},{1,29},{... | collective-permute-start | bytes 786440 | tf_op jit(solution)/shard_map/ppermute | solution.py:20
  11.6 11.4 %collective-permute-start.4 = (f32[2,4,16,256]{3,2,1,0:T(8,128)S(1)}, f32[2,4,16,256]{3,2,1,0:T(8,128)S(1)}, u32[]{:S(2)}, u32[]{:S(2)}) collective-permute-start(f32[2,4,16,256]{3,2,1,0:T(8,128)S(1)} %pad_maximum_fusion.refs_0_), channel_id=1, source_target_pairs={{0,3},{1,2},{2,1},{3,0},{4,7},{5,6},{6,5},{7,4},{8,11},{9,10},{10,... | collective-permute-start | bytes 393224 | tf_op jit(solution)/shard_map/ppermute | solution.py:20
  14.9 8.0 %collective-permute-start.3 = (f32[2,4,16,256]{3,2,1,0:T(8,128)S(1)}, f32[2,4,16,256]{3,2,1,0:T(8,128)S(1)}, u32[]{:S(2)}, u32[]{:S(2)}) collective-permute-start(f32[2,4,16,256]{3,2,1,0:T(8,128)S(1)} %pad_maximum_fusion.refs_0_), channel_id=1, source_target_pairs={{0,2},{1,3},{2,0},{3,1},{4,6},{5,7},{6,4},{7,5},{8,10},{9,11},{10,... | collective-permute-start | bytes 393224 | tf_op jit(solution)/shard_map/ppermute | solution.py:20
  15.2 7.8 %collective-permute-start.2 = (f32[2,4,16,256]{3,2,1,0:T(8,128)S(1)}, f32[2,4,16,256]{3,2,1,0:T(8,128)S(1)}, u32[]{:S(2)}, u32[]{:S(2)}) collective-permute-start(f32[2,4,16,256]{3,2,1,0:T(8,128)S(1)} %pad_maximum_fusion.refs_0_), channel_id=1, source_target_pairs={{0,1},{1,0},{2,3},{3,2},{4,5},{5,4},{6,7},{7,6},{8,9},{9,8},{10,11... | collective-permute-start | bytes 393224 | tf_op jit(solution)/shard_map/ppermute | solution.py:20
  24.9 6.3 %collective-permute-start.9 = (f32[32,256]{1,0:T(8,128)S(1)}, f32[32,256]{1,0:T(8,128)S(1)}, u32[]{:S(2)}, u32[]{:S(2)}) collective-permute-start(f32[32,256]{1,0:T(8,128)S(1)} %border_low_levels.1), channel_id=1, source_target_pairs={{0,3},{1,0},{2,1},{3,2},{4,7},{5,4},{6,5},{7,6},{8,11},{9,8},{10,9... | collective-permute-start | bytes 98312 | tf_op jit(solution)/shard_map/ppermute | solution.py:20
  25.5 5.7 %collective-permute-start.8 = (f32[32,256]{1,0:T(8,128)S(1)}, f32[32,256]{1,0:T(8,128)S(1)}, u32[]{:S(2)}, u32[]{:S(2)}) collective-permute-start(f32[32,256]{1,0:T(8,128)S(1)} %border_low_levels.1), channel_id=1, source_target_pairs={{0,2},{1,3},{2,0},{3,1},{4,6},{5,7},{6,4},{7,5},{8,10},{9,11},{10,... | collective-permute-start | bytes 98312 | tf_op jit(solution)/shard_map/ppermute | solution.py:20
  26.7 4.4 %collective-permute-start.7 = (f32[32,256]{1,0:T(8,128)S(1)}, f32[32,256]{1,0:T(8,128)S(1)}, u32[]{:S(2)}, u32[]{:S(2)}) collective-permute-start(f32[32,256]{1,0:T(8,128)S(1)} %border_low_levels.1), channel_id=1, source_target_pairs={{0,1},{1,2},{2,3},{3,0},{4,5},{5,6},{6,7},{7,4},{8,9},{9,10},{10,1... | collective-permute-start | bytes 98312 | tf_op jit(solution)/shard_map/ppermute | solution.py:20

commit v12 on v11

--- a/solution.py
+++ b/solution.py
@@ -336,7 +336,9 @@
     )(place, coef, *pieces)
 
 
-def border_steps(depth, place, region, coef, wide, kept, l0, halos, halo, work, store, rows):
+def border_steps(
+    depth, place, region, coef, wide, kept, l0, halos, halo, work, rows=None, store=None, finish=None
+):
     cols, tags, levels, lats = kept[1].shape
     first_tag = place[0] * tags
     part = slice(0, depth)
@@ -362,7 +364,7 @@
     def column(t, c):
         return [state(t, c, tag) for tag in range(tags)]
 
-    for t in range(ITERS):
+    for t in range(ITERS if store is None else ITERS - 1):
         reach = EDGE - 1 - t
         for run in (range(-reach, t + 1), range(cols - t - 1, cols + reach)):
             west, mid = column(t, run[0] - 1), column(t, run[0])
@@ -370,22 +372,26 @@
                 east = column(t, c + 1)
                 coefs = coefs_at(c)
                 new = [advance(coefs, mid[k], east[k], west[k]) for k in range(tags)]
-                for k in range(tags):
-                    if t < ITERS - 1:
+                if t < ITERS - 1:
+                    for k in range(tags):
                         work[t + 1, *slot(c, cols), k] = new[k]
-                    elif store is not None:
-                        store(c, k, new[k])
                 if rows is not None and 0 <= c < cols:
                     rows[t, c : c + 1, :] = chosen(region[c : c + 1, :], first_tag, new)
                 west, mid = mid, east
+    if store is None:
+        return
+    t = ITERS - 1
+    for k in range(tags):
+        for c in [*range(EDGE), *range(cols - EDGE, cols)]:
+            near = [state(t, at, k) for at in (c, c + 1, c - 1)]
+            store(c, k, advance(coefs_at(c), *near))
+        finish(k)
 
 
 def low_kernel(place, region, coef, wide, l0, l1, l2, l3, first, second, rows_in, grad, halo, work, rows):
     rows[...] = rows_in[...]
     kept = (None, l1, l2, l3)
-    border_steps(
-        8, place, region, coef, wide, kept, l0, (first, second), halo, work, None, rows
-    )
+    border_steps(8, place, region, coef, wide, kept, l0, (first, second), halo, work, rows)
     total = rows[0]
     for t in range(1, ITERS):
         total = total + rows[t]
@@ -424,28 +430,29 @@
     pitch = cols + 1
     store = storing_rows(final, tags, levels, pitch)
     kept = (None, l1, l2, l3)
-    border_steps(
-        levels, place, None, coef, wide, kept, l0, (first, second), halo, work, store, None
-    )
-    edges = (0, cols - 8)
-
-    @pl.loop(0, levels)
-    def _(level):
-        for tag in range(tags):
-            for k in range(2):
-                at = ((k * tags + tag) * levels + level) * pitch
-                for side, c in enumerate(edges):
-                    sides[side, tag, level, :, HALVES[k]] = final[pl.ds(at + c, 8), :]
-
     copies = []
-    for side, c in enumerate(edges):
-        for tag in range(tags):
+
+    def finish(tag):
+        @pl.loop(0, levels // 8)
+        def _(i):
+            for j in range(8):
+                level = i * 8 + j
+                for k in range(2):
+                    at = ((k * tags + tag) * levels + level) * pitch
+                    for side, c in enumerate((0, cols - 8)):
+                        sides[side, tag, level, :, HALVES[k]] = final[pl.ds(at + c, 8), :]
+
+        for side, c in enumerate((0, cols - 8)):
             copies.append(
                 pltpu.make_async_copy(
                     sides.at[side, tag], out.at[tag, :, pl.ds(c, 8)], sems.at[len(copies)]
                 )
             )
             copies[-1].start()
+
+    border_steps(
+        levels, place, None, coef, wide, kept, l0, (first, second), halo, work, None, store, finish
+    )
     for c in copies:
         c.wait()
 
@@ -542,7 +549,7 @@
     out = border(place, coef, wide, states, (first, second), final, out)
     share = grad
     for by in range(1, groups):
-        grad = grad + swapped(share, "grp", lambda i: (i + by) % groups)
+        grad = grad + swapped(share, "grp", lambda i: i ^ by)
     return out, grad
 
 

time: 32 us -> 31.2 us (0.975)
  the two profiles are of different devices: /device:TPU:1 before, /device:TPU:0 now
where the time goes in v12:
time: 31.2 us; the launch traced here: 31 us
  Pallas kernels  15.1 us (48%)
  starting transfers between devices  12.3 us (39%)
  waiting for transfers between devices  2.02 us (6%)
  between operations  0.8 us (3%)
  other arithmetic  0.71 us (2%)
    ppermute x10, starting transfers between devices, swapped(): lax.ppermute(value, axis, [(i, partner(i)) for i in range(lax.axis_size(a...  12.3 us
    pallas_call x1, Pallas kernels, inner(): pl.pallas_call(inner_kernel, in_specs=[pl.BlockSpec(memory_space=pltpu.SM...  6.29 us
    pallas_call x1, Pallas kernels, border(): pl.pallas_call(border_kernel, in_specs=[pl.BlockSpec(memory_space=pltpu.S...  2.93 us
    pallas_call x1, Pallas kernels, pack(): pl.pallas_call(functools.partial(pack_kernel, parts), in_specs=[pl.BlockS...  2.83 us
    ppermute x10, waiting for transfers between devices, swapped(): lax.ppermute(value, axis, [(i, partner(i)) for i in range(lax.axis_size(a...  2.02 us
    pallas_call x1, Pallas kernels, gradient(): pl.pallas_call(low_kernel, in_specs=[pl.BlockSpec(memory_space=pltpu.SMEM...  1.27 us
    pallas_call x1, Pallas kernels, write_inner(): pl.pallas_call(write_kernel, in_specs=[pl.BlockSpec(memory_space=pltpu.VM...  1.14 us
    pallas_call x1, Pallas kernels, outer_coefs(): pl.pallas_call(functools.partial(outer_kernel, parts, cols), in_specs=[pl...  0.63 us
  transfers between devices with their start and end apart: 10, of which 3 were waited for; matrix products, arithmetic and copies ran while one was open for 0% of the time, Pallas kernels for 35%

profile of v12, /device:TPU:0, one launch (start us, length us, event | category | flops | bytes accessed | tf_op | source)
XLA Modules:
  0.0 31.0 jit_solution(1058676497911372041)
XLA Ops:
  0.6 0.1 pad_add_fusion.place
  0.7 0.0 copy-start.4
  0.7 0.0 copy-start.5
  0.8 0.0 copy-start.6
  0.8 0.0 copy-start.7
  0.8 2.8 %pack_edges.1 = (f32[4,16,256]{2,1,0:T(8,128)S(1)}, f32[4,16,256]{2,1,0:T(8,128)S(1)}, f32[16,16,256]{2,1,0:T(8,128)S(1)}, f32[16,16,256]{2,1,0:T(8,128)S(1)}) custom-call(s32[2]{0:T(128)S(1)} %pad_add_fusion.place, f32[4,16,32,256]{3,2,1,0:T(8,128)} %lam.3, f32[16,32,256]{2,1,0:T(8,128)} %ew.3, f32[16,32,256]{2,1,0:T(8,128)} %ed.3, f32[16,32,256]{2,1,0:T(8,128)} %nw.3, ...), custom_call_target="tpu_custom_call" | custom-call | flops 1000 | bytes 1000 | tf_op jit(solution)/shard_map/pack_edges/pallas_call | solution.py:148
  3.6 3.0 %collective-permute-start = (f32[4,16,256]{2,1,0:T(8,128)S(1)}, f32[4,16,256]{2,1,0:T(8,128)S(1)}, u32[]{:S(2)}, u32[]{:S(2)}) collective-permute-start(f32[4,16,256]{2,1,0:T(8,128)S(1)} %get-tuple-element.19), channel_id=1, source_target_pairs={{0,4},{4,0},{8,12},{12,8},{16,20},{20,16},{24,28},{28,24},{1,5},{5... | collective-permute-start | bytes 196616 | tf_op jit(solution)/shard_map/ppermute | solution.py:20
  6.6 3.6 %collective-permute-start.1 = (f32[4,16,256]{2,1,0:T(8,128)S(1)}, f32[4,16,256]{2,1,0:T(8,128)S(1)}, u32[]{:S(2)}, u32[]{:S(2)}) collective-permute-start(f32[4,16,256]{2,1,0:T(8,128)S(1)} %get-tuple-element.20), channel_id=1, source_target_pairs={{0,28},{4,8},{8,4},{12,16},{16,12},{20,24},{24,20},{28,0},{1,29},{... | collective-permute-start | bytes 196616 | tf_op jit(solution)/shard_map/ppermute | solution.py:20
  10.2 1.9 %collective-permute-start.6 = (f32[16,16,256]{2,1,0:T(8,128)S(1)}, f32[16,16,256]{2,1,0:T(8,128)S(1)}, u32[]{:S(2)}, u32[]{:S(2)}) collective-permute-start(f32[16,16,256]{2,1,0:T(8,128)S(1)} %get-tuple-element.28), channel_id=1, source_target_pairs={{0,28},{4,8},{8,4},{12,16},{16,12},{20,24},{24,20},{28,0},{1,29},{... | collective-permute-start | bytes 786440 | tf_op jit(solution)/shard_map/ppermute | solution.py:20
  12.1 1.6 %collective-permute-done.1 = f32[4,16,256]{2,1,0:T(8,128)S(1)} collective-permute-done((f32[4,16,256]{2,1,0:T(8,128)S(1)}, f32[4,16,256]{2,1,0:T(8,128)S(1)}, u32[]{:S(2)}, u32[]{:S(2)}) %collective-permute-start.1) | collective-permute-done | bytes 65568 | tf_op jit(solution)/shard_map/ppermute | solution.py:20
  13.7 0.1 collective-permute-start.4
  13.8 1.6 %collective-permute-start.3 = (f32[2,4,16,256]{3,2,1,0:T(8,128)S(1)}, f32[2,4,16,256]{3,2,1,0:T(8,128)S(1)}, u32[]{:S(2)}, u32[]{:S(2)}) collective-permute-start(f32[2,4,16,256]{3,2,1,0:T(8,128)S(1)} %pad_maximum_fusion.refs_0_), channel_id=1, source_target_pairs={{0,2},{1,3},{2,0},{3,1},{4,6},{5,7},{6,4},{7,5},{8,10},{9,11},{10,... | collective-permute-start | bytes 393224 | tf_op jit(solution)/shard_map/ppermute | solution.py:20
  15.4 0.3 collective-permute-start.2
  15.7 6.3 %inner_steps.1 = (f32[33,6,16,256]{3,2,1,0:T(8,128)S(1)}, f32[4,4,16,256]{3,2,1,0:T(8,128)S(1)}, f32[32,4,16,256]{3,2,1,0:T(8,128)S(1)}, f32[32,4,16,256]{3,2,1,...) custom-call(s32[2]{0:T(128)S(1)} %pad_add_fusion.place, ...), custom_call_target="tpu_custom_call" | custom-call | flops 1000 | bytes 1000 | tf_op jit(solution)/shard_map/inner_steps/pallas_call | solution.py:268
  22.0 1.1 %write_inner.1.refs_1_ = f32[4,16,32,256]{3,2,1,0:T(8,128)} custom-call(f32[4264,128]{1,0:T(8,128)S(1)} %get-tuple-element.21.final.refs_0_), custom_call_target="tpu_custom_call" | custom-call | flops 1000 | bytes 1000 | tf_op jit(solution)/shard_map/write_inner/pallas_call | solution.py:510
  23.2 0.6 %outer_coefs.1.wide = f32[2,7,6,16,256]{4,3,2,1,0:T(8,128)S(1)} custom-call(s32[2]{0:T(128)S(1)} %pad_add_fusion.place, f32[33,6,16,256]{3,2,1,0:T(8,128)S(1)} %get-tuple-element.18.coef, f32[2,4,16,256]{3,2,1,0:T(8,128)S(1)} %pad_maximum_fusion.refs_0_, f32[2,4,16,256]{3,2,1,0:T(8,128)S(1)} %collective-permute-done.2.refs_1_, ...), custom_call_target="tpu_custom_call" | custom-call | flops 1000 | bytes 1000 | tf_op jit(solution)/shard_map/outer_coefs/pallas_call | solution.py:327
  23.8 0.3 %collective-permute-done.5.first = f32[16,16,256]{2,1,0:T(8,128)S(1)} collective-permute-done((f32[16,16,256]{2,1,0:T(8,128)S(1)}, f32[16,16,256]{2,1,0:T(8,128)S(1)}, u32[]{:S(2)}, u32[]{:S(2)}) %collective-permute-start.5) | collective-permute-done | bytes 262176 | tf_op jit(solution)/shard_map/ppermute | solution.py:20
  24.1 1.3 %border_low_levels.1 = f32[32,256]{1,0:T(8,128)S(1)} custom-call(s32[2]{0:T(128)S(1)} %pad_add_fusion.place, s32[32,256]{1,0:T(8,128)S(1)} %copy-done.7, f32[33,6,16,256]{3,2,1,0:T(8,128)S(1)} %get-tuple-element.18.coef, f32[2,7,6,16,256]{4,3,2,1,0:T(8,128)S(1)} %outer_coefs.1.wide, f32[4,4,16,256]{3,2,1,0:T(8,128)S(1)} %get-tuple-element.23.l0, ...), custom_call_target="tpu_custom_call" | custom-call | flops 1000 | bytes 1000 | tf_op jit(solution)/shard_map/border_low_levels/pallas_call | solution.py:412
  25.4 0.9 %collective-permute-start.9 = (f32[32,256]{1,0:T(8,128)S(1)}, f32[32,256]{1,0:T(8,128)S(1)}, u32[]{:S(2)}, u32[]{:S(2)}) collective-permute-start(f32[32,256]{1,0:T(8,128)S(1)} %border_low_levels.1), channel_id=1, source_target_pairs={{0,3},{1,2},{2,1},{3,0},{4,7},{5,6},{6,5},{7,4},{8,11},{9,10},{10,... | collective-permute-start | bytes 98312 | tf_op jit(solution)/shard_map/ppermute | solution.py:20
  26.3 0.7 %collective-permute-start.8 = (f32[32,256]{1,0:T(8,128)S(1)}, f32[32,256]{1,0:T(8,128)S(1)}, u32[]{:S(2)}, u32[]{:S(2)}) collective-permute-start(f32[32,256]{1,0:T(8,128)S(1)} %border_low_levels.1), channel_id=1, source_target_pairs={{0,2},{1,3},{2,0},{3,1},{4,6},{5,7},{6,4},{7,5},{8,10},{9,11},{10,... | collective-permute-start | bytes 98312 | tf_op jit(solution)/shard_map/ppermute | solution.py:20
  27.0 0.3 collective-permute-start.7
  27.3 2.9 %border_all_levels.1 = (f32[4264,128]{1,0:T(8,128)S(1)}, f32[4,16,32,256]{3,2,1,0:T(8,128)}) custom-call(s32[2]{0:T(128)S(1)} %pad_add_fusion.place, f32[33,6,16,256]{3,2,1,0:T(8,128)S(1)} %get-tuple-element.18.coef, f32[2,7,6,16,256]{4,3,2,1,0:T(8,128)S(1)} %outer_coefs.1.wide, ...), custom_call_target="tpu_custom_call", output_to_operand_aliasing={{0}: (9, {}), {1}: (10, {})} | custom-call | flops 1000 | bytes 1000 | tf_op jit(solution)/shard_map/border_all_levels/pallas_call | solution.py:466
  30.3 0.1 collective-permute-done.8
  30.4 0.6 %add_add_fusion = f32[32,256]{1,0:T(8,128)} fusion(f32[32,256]{1,0:T(8,128)S(1)} %collective-permute-done.9, f32[32,256]{1,0:T(8,128)S(1)} %collective-permute-done.8, f32[32,256]{1,0:T(8,128)S(1)} %border_low_levels.1, f32[32,256]{1,0:T(8,128)S(1)} %collective-permute-done.7), kind=kLoop, calls=%fused_computation.1 | loop fusion | flops 24576 | bytes 163840 | tf_op jit(solution)/shard_map/add | solution.py:552
  (21 shorter events, 0.1 us)
Async XLA Ops:
  0.7 14.9 %copy-start = (f32[4,16,32,256]{3,2,1,0:T(8,128)S(1)}, f32[4,16,32,256]{3,2,1,0:T(8,128)}, u32[]{:S(2)}) copy-start(f32[4,16,32,256]{3,2,1,0:T(8,128)} %lam.3) | copy-start | bytes 6291460
  0.7 14.9 %copy-start.1 = (f32[16,32,256]{2,1,0:T(8,128)S(1)}, f32[16,32,256]{2,1,0:T(8,128)}, u32[]{:S(2)}) copy-start(f32[16,32,256]{2,1,0:T(8,128)} %ew.3) | copy-start | bytes 1572868
  0.7 14.9 %copy-start.2 = (f32[16,32,256]{2,1,0:T(8,128)S(1)}, f32[16,32,256]{2,1,0:T(8,128)}, u32[]{:S(2)}) copy-start(f32[16,32,256]{2,1,0:T(8,128)} %ed.3) | copy-start | bytes 1572868
  0.7 14.9 %copy-start.3 = (f32[16,32,256]{2,1,0:T(8,128)S(1)}, f32[16,32,256]{2,1,0:T(8,128)}, u32[]{:S(2)}) copy-start(f32[16,32,256]{2,1,0:T(8,128)} %nw.3) | copy-start | bytes 1572868
  0.7 14.9 %copy-start.4 = (f32[16,32,256]{2,1,0:T(8,128)S(1)}, f32[16,32,256]{2,1,0:T(8,128)}, u32[]{:S(2)}) copy-start(f32[16,32,256]{2,1,0:T(8,128)} %nd.3) | copy-start | bytes 1572868
  0.7 14.9 %copy-start.5 = (f32[16,32,256]{2,1,0:T(8,128)S(1)}, f32[16,32,256]{2,1,0:T(8,128)}, u32[]{:S(2)}) copy-start(f32[16,32,256]{2,1,0:T(8,128)} %mf.3) | copy-start | bytes 1572868
  0.8 14.9 %copy-start.6 = (s32[32,256]{1,0:T(8,128)S(1)}, s32[32,256]{1,0:T(8,128)}, u32[]{:S(2)}) copy-start(s32[32,256]{1,0:T(8,128)} %top.3) | copy-start | bytes 98308
  0.8 14.9 %copy-start.7 = (s32[32,256]{1,0:T(8,128)S(1)}, s32[32,256]{1,0:T(8,128)}, u32[]{:S(2)}) copy-start(s32[32,256]{1,0:T(8,128)} %region.3) | copy-start | bytes 98308
  3.6 8.5 %collective-permute-start = (f32[4,16,256]{2,1,0:T(8,128)S(1)}, f32[4,16,256]{2,1,0:T(8,128)S(1)}, u32[]{:S(2)}, u32[]{:S(2)}) collective-permute-start(f32[4,16,256]{2,1,0:T(8,128)S(1)} %get-tuple-element.19), channel_id=1, source_target_pairs={{0,4},{4,0},{8,12},{12,8},{16,20},{20,16},{24,28},{28,24},{1,5},{5... | collective-permute-start | bytes 196616 | tf_op jit(solution)/shard_map/ppermute | solution.py:20
  6.6 7.1 %collective-permute-start.1 = (f32[4,16,256]{2,1,0:T(8,128)S(1)}, f32[4,16,256]{2,1,0:T(8,128)S(1)}, u32[]{:S(2)}, u32[]{:S(2)}) collective-permute-start(f32[4,16,256]{2,1,0:T(8,128)S(1)} %get-tuple-element.20), channel_id=1, source_target_pairs={{0,28},{4,8},{8,4},{12,16},{16,12},{20,24},{24,20},{28,0},{1,29},{... | collective-permute-start | bytes 196616 | tf_op jit(solution)/shard_map/ppermute | solution.py:20
  10.2 13.9 %collective-permute-start.5 = (f32[16,16,256]{2,1,0:T(8,128)S(1)}, f32[16,16,256]{2,1,0:T(8,128)S(1)}, u32[]{:S(2)}, u32[]{:S(2)}) collective-permute-start(f32[16,16,256]{2,1,0:T(8,128)S(1)} %get-tuple-element.27), channel_id=1, source_target_pairs={{0,4},{4,0},{8,12},{12,8},{16,20},{20,16},{24,28},{28,24},{1,5},{5... | collective-permute-start | bytes 786440 | tf_op jit(solution)/shard_map/ppermute | solution.py:20
  10.2 13.9 %collective-permute-start.6 = (f32[16,16,256]{2,1,0:T(8,128)S(1)}, f32[16,16,256]{2,1,0:T(8,128)S(1)}, u32[]{:S(2)}, u32[]{:S(2)}) collective-permute-start(f32[16,16,256]{2,1,0:T(8,128)S(1)} %get-tuple-element.28), channel_id=1, source_target_pairs={{0,28},{4,8},{8,4},{12,16},{16,12},{20,24},{24,20},{28,0},{1,29},{... | collective-permute-start | bytes 786440 | tf_op jit(solution)/shard_map/ppermute | solution.py:20
  13.7 9.4 %collective-permute-start.4 = (f32[2,4,16,256]{3,2,1,0:T(8,128)S(1)}, f32[2,4,16,256]{3,2,1,0:T(8,128)S(1)}, u32[]{:S(2)}, u32[]{:S(2)}) collective-permute-start(f32[2,4,16,256]{3,2,1,0:T(8,128)S(1)} %pad_maximum_fusion.refs_0_), channel_id=1, source_target_pairs={{0,3},{1,2},{2,1},{3,0},{4,7},{5,6},{6,5},{7,4},{8,11},{9,10},{10,... | collective-permute-start | bytes 393224 | tf_op jit(solution)/shard_map/ppermute | solution.py:20
  13.8 9.4 %collective-permute-start.3 = (f32[2,4,16,256]{3,2,1,0:T(8,128)S(1)}, f32[2,4,16,256]{3,2,1,0:T(8,128)S(1)}, u32[]{:S(2)}, u32[]{:S(2)}) collective-permute-start(f32[2,4,16,256]{3,2,1,0:T(8,128)S(1)} %pad_maximum_fusion.refs_0_), channel_id=1, source_target_pairs={{0,2},{1,3},{2,0},{3,1},{4,6},{5,7},{6,4},{7,5},{8,10},{9,11},{10,... | collective-permute-start | bytes 393224 | tf_op jit(solution)/shard_map/ppermute | solution.py:20
  15.4 7.8 %collective-permute-start.2 = (f32[2,4,16,256]{3,2,1,0:T(8,128)S(1)}, f32[2,4,16,256]{3,2,1,0:T(8,128)S(1)}, u32[]{:S(2)}, u32[]{:S(2)}) collective-permute-start(f32[2,4,16,256]{3,2,1,0:T(8,128)S(1)} %pad_maximum_fusion.refs_0_), channel_id=1, source_target_pairs={{0,1},{1,0},{2,3},{3,2},{4,5},{5,4},{6,7},{7,6},{8,9},{9,8},{10,11... | collective-permute-start | bytes 393224 | tf_op jit(solution)/shard_map/ppermute | solution.py:20
  25.4 4.9 %collective-permute-start.9 = (f32[32,256]{1,0:T(8,128)S(1)}, f32[32,256]{1,0:T(8,128)S(1)}, u32[]{:S(2)}, u32[]{:S(2)}) collective-permute-start(f32[32,256]{1,0:T(8,128)S(1)} %border_low_levels.1), channel_id=1, source_target_pairs={{0,3},{1,2},{2,1},{3,0},{4,7},{5,6},{6,5},{7,4},{8,11},{9,10},{10,... | collective-permute-start | bytes 98312 | tf_op jit(solution)/shard_map/ppermute | solution.py:20
  26.3 4.1 %collective-permute-start.8 = (f32[32,256]{1,0:T(8,128)S(1)}, f32[32,256]{1,0:T(8,128)S(1)}, u32[]{:S(2)}, u32[]{:S(2)}) collective-permute-start(f32[32,256]{1,0:T(8,128)S(1)} %border_low_levels.1), channel_id=1, source_target_pairs={{0,2},{1,3},{2,0},{3,1},{4,6},{5,7},{6,4},{7,5},{8,10},{9,11},{10,... | collective-permute-start | bytes 98312 | tf_op jit(solution)/shard_map/ppermute | solution.py:20
  27.0 3.3 %collective-permute-start.7 = (f32[32,256]{1,0:T(8,128)S(1)}, f32[32,256]{1,0:T(8,128)S(1)}, u32[]{:S(2)}, u32[]{:S(2)}) collective-permute-start(f32[32,256]{1,0:T(8,128)S(1)} %border_low_levels.1), channel_id=1, source_target_pairs={{0,1},{1,0},{2,3},{3,2},{4,5},{5,4},{6,7},{7,6},{8,9},{9,8},{10,11... | collective-permute-start | bytes 98312 | tf_op jit(solution)/shard_map/ppermute | solution.py:20

commit v13 on v12

--- a/solution.py
+++ b/solution.py
@@ -69,8 +69,10 @@
 
 def pack_kernel(parts, place, lam, ew, ed, nw, nd, mf, top, *refs):
     coef_first, coef_second, lam_first, lam_second = refs[:4]
-    field_s, top_s, lam_s, entry, field_p, lam_p, sems = refs[4:]
+    field_s, top_s, lam_s, coef_p, lam_p, sems = refs[4:]
     tags, levels, cols, lats = lam.shape
+    per = levels // parts
+    base = lax.rem(place[0], parts) * per
     copies = []
 
     def copy(src, dst):
@@ -79,83 +81,77 @@
 
     for side, at in ((LOW, 0), (HIGH, cols - 8)):
         for f, field in enumerate((ew, ed, nw, nd, mf)):
-            copy(field.at[:, pl.ds(at, 8)], field_s.at[f, side])
+            copy(field.at[pl.ds(base, per), pl.ds(at, 8)], field_s.at[f, side])
         copy(top.at[pl.ds(at, 8)], top_s.at[side])
-    field_copies = len(copies)
     for side, at in ((LOW, 0), (HIGH, cols - 8)):
         for tag in range(tags):
             copy(lam.at[tag, :, pl.ds(at, 8)], lam_s.at[side, tag])
-    for c in copies[:field_copies]:
+    for c in copies[:12]:
         c.wait()
     pitch = 9
+    few = per * pitch
+
+    @pl.loop(0, per)
+    def _(i):
+        level = base + i
+        for side in (LOW, HIGH):
+            ew, ed, nw, nd, mf = (field_s[f, side, i] for f in range(5))
+            lift = jnp.where((level < top_s[side]) & (level < levels - 1), mf, 0.0)
+            for j, value in enumerate((*faces(ew, ed, nw, nd), lift)):
+                for k in range(2):
+                    at = ((j * 2 + side) * 2 + k) * few + i * pitch
+                    coef_p[pl.ds(at, 8), :] = value[:, HALVES[k]]
+
+    odd = place[1]
+    start = 8 - EDGE
+    for dest, side in ((coef_first, 1 - odd), (coef_second, odd)):
+
+        def column(j, c):
+            return column_at(coef_p, (j * 2 + side) * 2 * few + c, per, pitch, few)
+
+        c = side * (start + 1)
+        dest[0] = column(1, jnp.maximum(c - 1, 0))
+        for i in range(EDGE - 1):
+            for n, j in enumerate((0, 2, 3, 4, 1)):
+                dest[5 * i + 1 + n] = column(j, c + i)
+
+    for c in copies[12:]:
+        c.wait()
     slab = levels * pitch
 
     @pl.loop(0, levels)
     def _(level):
-        row = level * pitch
-        for f in range(5):
-            for side in range(2):
-                for k in range(2):
-                    at = ((f * 2 + side) * 2 + k) * slab
-                    field_p[pl.ds(at + row, 8), :] = field_s[f, side, level, :, HALVES[k]]
-
-    def field(f, side, c):
-        return column_at(field_p, (f * 2 + side) * 2 * slab + c, levels, pitch, slab)
-
-    for side in (LOW, HIGH):
-        slot = 0
-        for c in range(EDGE - 1) if side == LOW else range(8 - EDGE, 8):
-            east, west, north, south = faces(*(field(f, side, c) for f in range(4)))
-            lift = updraft(field(4, side, c), top_s[side, pl.ds(c, 1), :])
-            wanted = (east, west, north, south, lift)
-            if side == HIGH and c == 8 - EDGE:
-                wanted = (west,)
-            for value in wanted:
-                entry[side, slot] = value
-                slot += 1
-        for left in range(slot, ENTRIES):
-            entry[side, left] = jnp.zeros((levels, lats), jnp.float32)
-    per = ENTRIES // parts
-    mine = lax.rem(place[0], parts) * per
-    odd = place[1]
-    coef_first[...] = entry[1 - odd, pl.ds(mine, per)]
-    coef_second[...] = entry[odd, pl.ds(mine, per)]
-
-    for c in copies[field_copies:]:
-        c.wait()
-
-    @pl.loop(0, levels)
-    def _(level):
-        row = level * pitch
-        for side in range(2):
+        for side in (LOW, HIGH):
             for tag in range(tags):
                 for k in range(2):
-                    at = ((side * 2 + k) * tags + tag) * slab
-                    lam_p[pl.ds(at + row, 8), :] = lam_s[side, tag, level, :, HALVES[k]]
+                    at = ((side * 2 + k) * tags + tag) * slab + level * pitch
+                    lam_p[pl.ds(at, 8), :] = lam_s[side, tag, level, :, HALVES[k]]
 
     for dest, side in ((lam_first, 1 - odd), (lam_second, odd)):
-        start = side * (2 * tags * slab + 8 - EDGE)
+        at = side * (2 * tags * slab + start)
         for tag in range(tags):
             for c in range(EDGE):
-                dest[tag * EDGE + c] = column_at(lam_p, start + tag * slab + c, levels, pitch, tags * slab)
+                dest[tag * EDGE + c] = column_at(
+                    lam_p, at + tag * slab + c, levels, pitch, tags * slab
+                )
 
 
 def pack(parts, place, lam, fields, top):
     tags, levels, cols, lats = lam.shape
+    per = levels // parts
     hbm = pl.BlockSpec(memory_space=pltpu.HBM)
-    send = lambda slabs: pltpu.VMEM((slabs, levels, lats), jnp.float32)
-    few, many = ENTRIES // parts, tags * EDGE
+    coef_send = pltpu.VMEM((ENTRIES, per, lats), jnp.float32)
+    lam_send = pltpu.VMEM((tags * EDGE, levels, lats), jnp.float32)
     return pl.pallas_call(
         functools.partial(pack_kernel, parts),
         in_specs=[pl.BlockSpec(memory_space=pltpu.SMEM)] + [hbm] * 7,
         out_specs=[pl.BlockSpec(memory_space=pltpu.VMEM)] * 4,
-        out_shape=[send(few), send(few), send(many), send(many)],
+        out_shape=[coef_send, coef_send, lam_send, lam_send],
         scratch_shapes=[
-            pltpu.VMEM((5, 2, levels, 8, lats), jnp.float32),
+            pltpu.VMEM((5, 2, per, 8, lats), jnp.float32),
             pltpu.VMEM((2, 8, lats), jnp.int32),
             pltpu.VMEM((2, tags, levels, 8, lats), jnp.float32),
-            pltpu.VMEM((2, ENTRIES, levels, lats), jnp.float32),
-            pltpu.VMEM((pitched(20, levels, 8), LANES), jnp.float32),
+            pltpu.VMEM((pitched(20, per, 8), LANES), jnp.float32),
             pltpu.VMEM((pitched(4 * tags, levels, 8), LANES), jnp.float32),
             pltpu.SemaphoreType.DMA((12 + 2 * tags,)),
         ],
@@ -292,33 +288,36 @@
 
 def outer_kernel(parts, cols, place, coef, *refs):
     pieces, wide, entry = refs[:parts], refs[parts], refs[parts + 1]
-    per = ENTRIES // parts
+    levels = coef.shape[2]
+    per = levels // parts
     mine = lax.rem(place[0], parts)
     odd = place[1]
     for by in range(parts):
-        base = (mine ^ by) * per
-        entry[1 - odd, pl.ds(base, per)] = pieces[by][0]
-        entry[odd, pl.ds(base, per)] = pieces[by][1]
-
-    def outside(c):
-        if c < 0:
-            at = 1 + 5 * (c + EDGE - 1)
-            e, _, n, s, u = (entry[LOW, at + j] for j in range(5))
-            w = entry[LOW, at - 4] if c > 1 - EDGE else entry[LOW, 0]
-        else:
-            at = 5 * (c - cols)
-            e, _, n, s, u = (entry[HIGH, at + j] for j in range(5))
-            w = entry[HIGH, at - 4] if c > cols else coef[cols, 2]
-        return e, w, n, s, u
-
-    first_west = entry[LOW, 1 + 5 * (EDGE - 2) + 1]
-    for c in [*range(1 - EDGE, 1), *range(cols, cols + EDGE - 1)]:
-        if c == 0:
-            e, w, n, s, u = coef[0, 1], first_west, coef[0, 3], coef[0, 4], coef[0, 5]
-        else:
-            e, w, n, s, u = outside(c)
-        for j, value in enumerate((1.0 - e - w - n - s, e, w, n, s, u)):
-            wide[*slot(c, cols), j] = value
+        for half, side in enumerate((1 - odd, odd)):
+
+            @pl.loop(0, ENTRIES // 4)
+            def _(i):
+                for j in range(4):
+                    e = i * 4 + j
+                    for k in range(2):
+                        at = ((side * ENTRIES + e) * 2 + k) * levels + (mine ^ by) * per
+                        entry[pl.ds(at, per), :] = pieces[by][half, e, :, HALVES[k]]
+
+    def slab(side, e):
+        at = (side * ENTRIES + e) * 2 * levels
+        return jnp.concatenate([entry[at + k * levels : at + (k + 1) * levels] for k in (0, 1)], 1)
+
+    for side in (LOW, HIGH):
+        for i in range(EDGE - 1):
+            w, e, n, s, u = (slab(side, 5 * i + j) for j in range(5))
+            if side == HIGH and i == 0:
+                w = coef[cols, 2]
+            for j, value in enumerate((1.0 - e - w - n - s, e, w, n, s, u)):
+                wide[side, i + EDGE * side, j] = value
+    first_west = slab(LOW, ENTRIES - 1)
+    e, n, s, u = (coef[0, j] for j in (1, 3, 4, 5))
+    for j, value in enumerate((1.0 - e - first_west - n - s, e, first_west, n, s, u)):
+        wide[*slot(0, cols), j] = value
 
 
 def outer_coefs(parts, cols, place, coef, pieces):
@@ -329,7 +328,7 @@
         in_specs=[pl.BlockSpec(memory_space=pltpu.SMEM)] + [vmem] * (1 + parts),
         out_specs=vmem,
         out_shape=pltpu.VMEM((2, 2 * EDGE - 1, 6, levels, lats), jnp.float32),
-        scratch_shapes=[pltpu.VMEM((2, ENTRIES, levels, lats), jnp.float32)],
+        scratch_shapes=[pltpu.VMEM((2 * ENTRIES * 2 * levels, LANES), jnp.float32)],
         compiler_params=pltpu.CompilerParams(vmem_limit_bytes=24 << 20),
         cost_estimate=SHORT,
         name="outer_coefs",

time: 31.2 us -> 30.9 us (level)
  transfers between devices with their start and end apart: 10 -> 10, of which waited for: 3 -> 3; matrix products, arithmetic and copies ran while one was open for 0% -> 0% of each run, Pallas kernels for 35% -> 36%
where the time goes in v13:
time: 30.9 us; the launch traced here: 30.8 us
  Pallas kernels  15 us (49%)
  starting transfers between devices  12.3 us (40%)
  waiting for transfers between devices  1.86 us (6%)
  between operations  0.8 us (3%)
  other arithmetic  0.73 us (2%)
    ppermute x10, starting transfers between devices, swapped(): lax.ppermute(value, axis, [(i, partner(i)) for i in range(lax.axis_size(a...  12.3 us
    pallas_call x1, Pallas kernels, inner(): pl.pallas_call(inner_kernel, in_specs=[pl.BlockSpec(memory_space=pltpu.SM...  6.29 us
    pallas_call x1, Pallas kernels, border(): pl.pallas_call(border_kernel, in_specs=[pl.BlockSpec(memory_space=pltpu.S...  2.93 us
    pallas_call x1, Pallas kernels, pack(): pl.pallas_call(functools.partial(pack_kernel, parts), in_specs=[pl.BlockS...  2.55 us
    ppermute x10, waiting for transfers between devices, swapped(): lax.ppermute(value, axis, [(i, partner(i)) for i in range(lax.axis_size(a...  1.86 us
    pallas_call x1, Pallas kernels, gradient(): pl.pallas_call(low_kernel, in_specs=[pl.BlockSpec(memory_space=pltpu.SMEM...  1.27 us
    pallas_call x1, Pallas kernels, write_inner(): pl.pallas_call(write_kernel, in_specs=[pl.BlockSpec(memory_space=pltpu.VM...  1.14 us
    pallas_call x1, Pallas kernels, outer_coefs(): pl.pallas_call(functools.partial(outer_kernel, parts, cols), in_specs=[pl...  0.83 us
  transfers between devices with their start and end apart: 10, of which 3 were waited for; matrix products, arithmetic and copies ran while one was open for 0% of the time, Pallas kernels for 36%

profile of v13, /device:TPU:0, one launch (start us, length us, event | category | flops | bytes accessed | tf_op | source)
XLA Modules:
  0.0 30.8 jit_solution(8646798925880017365)
XLA Ops:
  0.6 0.1 pad_add_fusion.place
  0.7 0.0 copy-start.4
  0.7 0.0 copy-start.5
  0.8 0.0 copy-start.6
  0.8 0.0 copy-start.7
  0.8 2.5 %pack_edges.1 = (f32[16,4,256]{2,1,0:T(4,128)S(1)}, f32[16,4,256]{2,1,0:T(4,128)S(1)}, f32[16,16,256]{2,1,0:T(8,128)S(1)}, f32[16,16,256]{2,1,0:T(8,128)S(1)}) custom-call(s32[2]{0:T(128)S(1)} %pad_add_fusion.place, f32[4,16,32,256]{3,2,1,0:T(8,128)} %lam.3, f32[16,32,256]{2,1,0:T(8,128)} %ew.3, f32[16,32,256]{2,1,0:T(8,128)} %ed.3, f32[16,32,256]{2,1,0:T(8,128)} %nw.3, ...), custom_call_target="tpu_custom_call" | custom-call | flops 1000 | bytes 1000 | tf_op jit(solution)/shard_map/pack_edges/pallas_call | solution.py:145
  3.3 3.0 %collective-permute-start = (f32[16,4,256]{2,1,0:T(4,128)S(1)}, f32[16,4,256]{2,1,0:T(4,128)S(1)}, u32[]{:S(2)}, u32[]{:S(2)}) collective-permute-start(f32[16,4,256]{2,1,0:T(4,128)S(1)} %get-tuple-element.19), channel_id=1, source_target_pairs={{0,4},{4,0},{8,12},{12,8},{16,20},{20,16},{24,28},{28,24},{1,5},{5... | collective-permute-start | bytes 196616 | tf_op jit(solution)/shard_map/ppermute | solution.py:20
  6.3 3.6 %collective-permute-start.1 = (f32[16,4,256]{2,1,0:T(4,128)S(1)}, f32[16,4,256]{2,1,0:T(4,128)S(1)}, u32[]{:S(2)}, u32[]{:S(2)}) collective-permute-start(f32[16,4,256]{2,1,0:T(4,128)S(1)} %get-tuple-element.20), channel_id=1, source_target_pairs={{0,28},{4,8},{8,4},{12,16},{16,12},{20,24},{24,20},{28,0},{1,29},{... | collective-permute-start | bytes 196616 | tf_op jit(solution)/shard_map/ppermute | solution.py:20
  9.9 1.9 %collective-permute-start.6 = (f32[16,16,256]{2,1,0:T(8,128)S(1)}, f32[16,16,256]{2,1,0:T(8,128)S(1)}, u32[]{:S(2)}, u32[]{:S(2)}) collective-permute-start(f32[16,16,256]{2,1,0:T(8,128)S(1)} %get-tuple-element.28), channel_id=1, source_target_pairs={{0,28},{4,8},{8,4},{12,16},{16,12},{20,24},{24,20},{28,0},{1,29},{... | collective-permute-start | bytes 786440 | tf_op jit(solution)/shard_map/ppermute | solution.py:20
  11.8 1.6 %collective-permute-done.1 = f32[16,4,256]{2,1,0:T(4,128)S(1)} collective-permute-done((f32[16,4,256]{2,1,0:T(4,128)S(1)}, f32[16,4,256]{2,1,0:T(4,128)S(1)}, u32[]{:S(2)}, u32[]{:S(2)}) %collective-permute-start.1) | collective-permute-done | bytes 65568 | tf_op jit(solution)/shard_map/ppermute | solution.py:20
  13.4 0.1 collective-permute-start.4
  13.5 1.6 %collective-permute-start.3 = (f32[2,16,4,256]{3,2,1,0:T(4,128)S(1)}, f32[2,16,4,256]{3,2,1,0:T(4,128)S(1)}, u32[]{:S(2)}, u32[]{:S(2)}) collective-permute-start(f32[2,16,4,256]{3,2,1,0:T(4,128)S(1)} %pad_maximum_fusion.refs_0_), channel_id=1, source_target_pairs={{0,2},{1,3},{2,0},{3,1},{4,6},{5,7},{6,4},{7,5},{8,10},{9,11},{10,... | collective-permute-start | bytes 393224 | tf_op jit(solution)/shard_map/ppermute | solution.py:20
  15.1 0.3 collective-permute-start.2
  15.4 6.3 %inner_steps.1 = (f32[33,6,16,256]{3,2,1,0:T(8,128)S(1)}, f32[4,4,16,256]{3,2,1,0:T(8,128)S(1)}, f32[32,4,16,256]{3,2,1,0:T(8,128)S(1)}, f32[32,4,16,256]{3,2,1,...) custom-call(s32[2]{0:T(128)S(1)} %pad_add_fusion.place, ...), custom_call_target="tpu_custom_call" | custom-call | flops 1000 | bytes 1000 | tf_op jit(solution)/shard_map/inner_steps/pallas_call | solution.py:264
  21.7 1.1 %write_inner.1.refs_1_ = f32[4,16,32,256]{3,2,1,0:T(8,128)} custom-call(f32[4264,128]{1,0:T(8,128)S(1)} %get-tuple-element.21.final.refs_0_), custom_call_target="tpu_custom_call" | custom-call | flops 1000 | bytes 1000 | tf_op jit(solution)/shard_map/write_inner/pallas_call | solution.py:509
  22.9 0.8 %outer_coefs.1.wide = f32[2,7,6,16,256]{4,3,2,1,0:T(8,128)S(1)} custom-call(s32[2]{0:T(128)S(1)} %pad_add_fusion.place, f32[33,6,16,256]{3,2,1,0:T(8,128)S(1)} %get-tuple-element.18.coef, f32[2,16,4,256]{3,2,1,0:T(4,128)S(1)} %pad_maximum_fusion.refs_0_, f32[2,16,4,256]{3,2,1,0:T(4,128)S(1)} %collective-permute-done.2.refs_1_, ...), custom_call_target="tpu_custom_call" | custom-call | flops 1000 | bytes 1000 | tf_op jit(solution)/shard_map/outer_coefs/pallas_call | solution.py:326
  23.7 0.1 collective-permute-done.5.first
  23.8 1.3 %border_low_levels.1 = f32[32,256]{1,0:T(8,128)S(1)} custom-call(s32[2]{0:T(128)S(1)} %pad_add_fusion.place, s32[32,256]{1,0:T(8,128)S(1)} %copy-done.7, f32[33,6,16,256]{3,2,1,0:T(8,128)S(1)} %get-tuple-element.18.coef, f32[2,7,6,16,256]{4,3,2,1,0:T(8,128)S(1)} %outer_coefs.1.wide, f32[4,4,16,256]{3,2,1,0:T(8,128)S(1)} %get-tuple-element.23.l0, ...), custom_call_target="tpu_custom_call" | custom-call | flops 1000 | bytes 1000 | tf_op jit(solution)/shard_map/border_low_levels/pallas_call | solution.py:411
  25.1 1.1 %collective-permute-start.9 = (f32[32,256]{1,0:T(8,128)S(1)}, f32[32,256]{1,0:T(8,128)S(1)}, u32[]{:S(2)}, u32[]{:S(2)}) collective-permute-start(f32[32,256]{1,0:T(8,128)S(1)} %border_low_levels.1), channel_id=1, source_target_pairs={{0,3},{1,2},{2,1},{3,0},{4,7},{5,6},{6,5},{7,4},{8,11},{9,10},{10,... | collective-permute-start | bytes 98312 | tf_op jit(solution)/shard_map/ppermute | solution.py:20
  26.2 0.7 %collective-permute-start.8 = (f32[32,256]{1,0:T(8,128)S(1)}, f32[32,256]{1,0:T(8,128)S(1)}, u32[]{:S(2)}, u32[]{:S(2)}) collective-permute-start(f32[32,256]{1,0:T(8,128)S(1)} %border_low_levels.1), channel_id=1, source_target_pairs={{0,2},{1,3},{2,0},{3,1},{4,6},{5,7},{6,4},{7,5},{8,10},{9,11},{10,... | collective-permute-start | bytes 98312 | tf_op jit(solution)/shard_map/ppermute | solution.py:20
  27.0 0.1 collective-permute-start.7
  27.0 2.9 %border_all_levels.1 = (f32[4264,128]{1,0:T(8,128)S(1)}, f32[4,16,32,256]{3,2,1,0:T(8,128)}) custom-call(s32[2]{0:T(128)S(1)} %pad_add_fusion.place, f32[33,6,16,256]{3,2,1,0:T(8,128)S(1)} %get-tuple-element.18.coef, f32[2,7,6,16,256]{4,3,2,1,0:T(8,128)S(1)} %outer_coefs.1.wide, ...), custom_call_target="tpu_custom_call", output_to_operand_aliasing={{0}: (9, {}), {1}: (10, {})} | custom-call | flops 1000 | bytes 1000 | tf_op jit(solution)/shard_map/border_all_levels/pallas_call | solution.py:465
  30.0 0.2 collective-permute-done.8
  30.1 0.6 %add_add_fusion = f32[32,256]{1,0:T(8,128)} fusion(f32[32,256]{1,0:T(8,128)S(1)} %collective-permute-done.9, f32[32,256]{1,0:T(8,128)S(1)} %collective-permute-done.8, f32[32,256]{1,0:T(8,128)S(1)} %border_low_levels.1, f32[32,256]{1,0:T(8,128)S(1)} %collective-permute-done.7), kind=kLoop, calls=%fused_computation.1 | loop fusion | flops 24576 | bytes 163840 | tf_op jit(solution)/shard_map/add | solution.py:551
  (21 shorter events, 0.1 us)
Async XLA Ops:
  0.7 14.7 %copy-start = (f32[4,16,32,256]{3,2,1,0:T(8,128)S(1)}, f32[4,16,32,256]{3,2,1,0:T(8,128)}, u32[]{:S(2)}) copy-start(f32[4,16,32,256]{3,2,1,0:T(8,128)} %lam.3) | copy-start | bytes 6291460
  0.7 14.7 %copy-start.1 = (f32[16,32,256]{2,1,0:T(8,128)S(1)}, f32[16,32,256]{2,1,0:T(8,128)}, u32[]{:S(2)}) copy-start(f32[16,32,256]{2,1,0:T(8,128)} %ew.3) | copy-start | bytes 1572868
  0.7 14.7 %copy-start.2 = (f32[16,32,256]{2,1,0:T(8,128)S(1)}, f32[16,32,256]{2,1,0:T(8,128)}, u32[]{:S(2)}) copy-start(f32[16,32,256]{2,1,0:T(8,128)} %ed.3) | copy-start | bytes 1572868
  0.7 14.7 %copy-start.3 = (f32[16,32,256]{2,1,0:T(8,128)S(1)}, f32[16,32,256]{2,1,0:T(8,128)}, u32[]{:S(2)}) copy-start(f32[16,32,256]{2,1,0:T(8,128)} %nw.3) | copy-start | bytes 1572868
  0.7 14.7 %copy-start.4 = (f32[16,32,256]{2,1,0:T(8,128)S(1)}, f32[16,32,256]{2,1,0:T(8,128)}, u32[]{:S(2)}) copy-start(f32[16,32,256]{2,1,0:T(8,128)} %nd.3) | copy-start | bytes 1572868
  0.7 14.7 %copy-start.5 = (f32[16,32,256]{2,1,0:T(8,128)S(1)}, f32[16,32,256]{2,1,0:T(8,128)}, u32[]{:S(2)}) copy-start(f32[16,32,256]{2,1,0:T(8,128)} %mf.3) | copy-start | bytes 1572868
  0.8 14.6 %copy-start.6 = (s32[32,256]{1,0:T(8,128)S(1)}, s32[32,256]{1,0:T(8,128)}, u32[]{:S(2)}) copy-start(s32[32,256]{1,0:T(8,128)} %top.3) | copy-start | bytes 98308
  0.8 14.6 %copy-start.7 = (s32[32,256]{1,0:T(8,128)S(1)}, s32[32,256]{1,0:T(8,128)}, u32[]{:S(2)}) copy-start(s32[32,256]{1,0:T(8,128)} %region.3) | copy-start | bytes 98308
  3.3 8.5 %collective-permute-start = (f32[16,4,256]{2,1,0:T(4,128)S(1)}, f32[16,4,256]{2,1,0:T(4,128)S(1)}, u32[]{:S(2)}, u32[]{:S(2)}) collective-permute-start(f32[16,4,256]{2,1,0:T(4,128)S(1)} %get-tuple-element.19), channel_id=1, source_target_pairs={{0,4},{4,0},{8,12},{12,8},{16,20},{20,16},{24,28},{28,24},{1,5},{5... | collective-permute-start | bytes 196616 | tf_op jit(solution)/shard_map/ppermute | solution.py:20
  6.3 7.1 %collective-permute-start.1 = (f32[16,4,256]{2,1,0:T(4,128)S(1)}, f32[16,4,256]{2,1,0:T(4,128)S(1)}, u32[]{:S(2)}, u32[]{:S(2)}) collective-permute-start(f32[16,4,256]{2,1,0:T(4,128)S(1)} %get-tuple-element.20), channel_id=1, source_target_pairs={{0,28},{4,8},{8,4},{12,16},{16,12},{20,24},{24,20},{28,0},{1,29},{... | collective-permute-start | bytes 196616 | tf_op jit(solution)/shard_map/ppermute | solution.py:20
  9.9 13.9 %collective-permute-start.5 = (f32[16,16,256]{2,1,0:T(8,128)S(1)}, f32[16,16,256]{2,1,0:T(8,128)S(1)}, u32[]{:S(2)}, u32[]{:S(2)}) collective-permute-start(f32[16,16,256]{2,1,0:T(8,128)S(1)} %get-tuple-element.27), channel_id=1, source_target_pairs={{0,4},{4,0},{8,12},{12,8},{16,20},{20,16},{24,28},{28,24},{1,5},{5... | collective-permute-start | bytes 786440 | tf_op jit(solution)/shard_map/ppermute | solution.py:20
  9.9 13.9 %collective-permute-start.6 = (f32[16,16,256]{2,1,0:T(8,128)S(1)}, f32[16,16,256]{2,1,0:T(8,128)S(1)}, u32[]{:S(2)}, u32[]{:S(2)}) collective-permute-start(f32[16,16,256]{2,1,0:T(8,128)S(1)} %get-tuple-element.28), channel_id=1, source_target_pairs={{0,28},{4,8},{8,4},{12,16},{16,12},{20,24},{24,20},{28,0},{1,29},{... | collective-permute-start | bytes 786440 | tf_op jit(solution)/shard_map/ppermute | solution.py:20
  13.4 9.4 %collective-permute-start.4 = (f32[2,16,4,256]{3,2,1,0:T(4,128)S(1)}, f32[2,16,4,256]{3,2,1,0:T(4,128)S(1)}, u32[]{:S(2)}, u32[]{:S(2)}) collective-permute-start(f32[2,16,4,256]{3,2,1,0:T(4,128)S(1)} %pad_maximum_fusion.refs_0_), channel_id=1, source_target_pairs={{0,3},{1,2},{2,1},{3,0},{4,7},{5,6},{6,5},{7,4},{8,11},{9,10},{10,... | collective-permute-start | bytes 393224 | tf_op jit(solution)/shard_map/ppermute | solution.py:20
  13.5 9.4 %collective-permute-start.3 = (f32[2,16,4,256]{3,2,1,0:T(4,128)S(1)}, f32[2,16,4,256]{3,2,1,0:T(4,128)S(1)}, u32[]{:S(2)}, u32[]{:S(2)}) collective-permute-start(f32[2,16,4,256]{3,2,1,0:T(4,128)S(1)} %pad_maximum_fusion.refs_0_), channel_id=1, source_target_pairs={{0,2},{1,3},{2,0},{3,1},{4,6},{5,7},{6,4},{7,5},{8,10},{9,11},{10,... | collective-permute-start | bytes 393224 | tf_op jit(solution)/shard_map/ppermute | solution.py:20
  15.1 7.8 %collective-permute-start.2 = (f32[2,16,4,256]{3,2,1,0:T(4,128)S(1)}, f32[2,16,4,256]{3,2,1,0:T(4,128)S(1)}, u32[]{:S(2)}, u32[]{:S(2)}) collective-permute-start(f32[2,16,4,256]{3,2,1,0:T(4,128)S(1)} %pad_maximum_fusion.refs_0_), channel_id=1, source_target_pairs={{0,1},{1,0},{2,3},{3,2},{4,5},{5,4},{6,7},{7,6},{8,9},{9,8},{10,11... | collective-permute-start | bytes 393224 | tf_op jit(solution)/shard_map/ppermute | solution.py:20
  25.1 4.9 %collective-permute-start.9 = (f32[32,256]{1,0:T(8,128)S(1)}, f32[32,256]{1,0:T(8,128)S(1)}, u32[]{:S(2)}, u32[]{:S(2)}) collective-permute-start(f32[32,256]{1,0:T(8,128)S(1)} %border_low_levels.1), channel_id=1, source_target_pairs={{0,3},{1,2},{2,1},{3,0},{4,7},{5,6},{6,5},{7,4},{8,11},{9,10},{10,... | collective-permute-start | bytes 98312 | tf_op jit(solution)/shard_map/ppermute | solution.py:20
  26.2 3.9 %collective-permute-start.8 = (f32[32,256]{1,0:T(8,128)S(1)}, f32[32,256]{1,0:T(8,128)S(1)}, u32[]{:S(2)}, u32[]{:S(2)}) collective-permute-start(f32[32,256]{1,0:T(8,128)S(1)} %border_low_levels.1), channel_id=1, source_target_pairs={{0,2},{1,3},{2,0},{3,1},{4,6},{5,7},{6,4},{7,5},{8,10},{9,11},{10,... | collective-permute-start | bytes 98312 | tf_op jit(solution)/shard_map/ppermute | solution.py:20
  27.0 3.2 %collective-permute-start.7 = (f32[32,256]{1,0:T(8,128)S(1)}, f32[32,256]{1,0:T(8,128)S(1)}, u32[]{:S(2)}, u32[]{:S(2)}) collective-permute-start(f32[32,256]{1,0:T(8,128)S(1)} %border_low_levels.1), channel_id=1, source_target_pairs={{0,1},{1,0},{2,3},{3,2},{4,5},{5,4},{6,7},{7,6},{8,9},{9,8},{10,11... | collective-permute-start | bytes 98312 | tf_op jit(solution)/shard_map/ppermute | solution.py:20

commit v14 on v13

--- a/solution.py
+++ b/solution.py
@@ -210,7 +210,8 @@
 
 
 def inner_kernel(place, lam, ew, ed, nw, nd, mf, top, region, *refs):
-    coef, l0, l1, l2, l3, final, rows, lam_p, field_p = refs
+    coef, l0, l1, l2, l3, final, grad, lam_p, field_p, rows = refs
+    rows[...] = jnp.zeros_like(rows)
     tags, levels, cols, lats = lam.shape
     pitch = cols + 1
     slab = levels * pitch
@@ -255,6 +256,10 @@
     stores = (storing(l1), storing(l2), storing(l3), last)
     for t in range(ITERS):
         sweep(t, lam.shape, place[0] * tags, region, coef, loads[t], stores[t], rows)
+    total = rows[0]
+    for t in range(1, ITERS):
+        total = total + rows[t]
+    grad[...] = total
 
 
 def inner(place, lam, fields, top, region):
@@ -270,11 +275,12 @@
             pltpu.VMEM((4, tags, levels, lats), jnp.float32),
             *[state] * 3,
             pltpu.VMEM((pitched(2 * tags, levels, cols), LANES), jnp.float32),
-            pltpu.VMEM((ITERS, cols, lats), jnp.float32),
+            pltpu.VMEM((cols, lats), jnp.float32),
         ],
         scratch_shapes=[
             pltpu.VMEM((pitched(2 * tags, levels, cols), LANES), jnp.float32),
             pltpu.VMEM((pitched(10, levels, cols), LANES), jnp.float32),
+            pltpu.VMEM((ITERS, cols, lats), jnp.float32),
         ],
         compiler_params=pltpu.CompilerParams(vmem_limit_bytes=32 << 20),
         cost_estimate=SHORT,
@@ -336,7 +342,7 @@
 
 
 def border_steps(
-    depth, place, region, coef, wide, kept, l0, halos, halo, work, rows=None, store=None, finish=None
+    depth, place, region, coef, wide, kept, l0, halos, halo, work, grad=None, store=None, finish=None
 ):
     cols, tags, levels, lats = kept[1].shape
     first_tag = place[0] * tags
@@ -374,8 +380,8 @@
                 if t < ITERS - 1:
                     for k in range(tags):
                         work[t + 1, *slot(c, cols), k] = new[k]
-                if rows is not None and 0 <= c < cols:
-                    rows[t, c : c + 1, :] = chosen(region[c : c + 1, :], first_tag, new)
+                if grad is not None and 0 <= c < cols:
+                    grad[c : c + 1] += chosen(region[c : c + 1, :], first_tag, new)
                 west, mid = mid, east
     if store is None:
         return
@@ -387,14 +393,10 @@
         finish(k)
 
 
-def low_kernel(place, region, coef, wide, l0, l1, l2, l3, first, second, rows_in, grad, halo, work, rows):
-    rows[...] = rows_in[...]
+def low_kernel(place, region, coef, wide, l0, l1, l2, l3, second, first, inner_grad, grad, halo, work):
+    grad[...] = inner_grad[...]
     kept = (None, l1, l2, l3)
-    border_steps(8, place, region, coef, wide, kept, l0, (first, second), halo, work, rows)
-    total = rows[0]
-    for t in range(1, ITERS):
-        total = total + rows[t]
-    grad[...] = total
+    border_steps(8, place, region, coef, wide, kept, l0, (first, second), halo, work, grad)
 
 
 def border_scratch(tags, depth, lats):
@@ -404,26 +406,23 @@
     ]
 
 
-def gradient(place, region, coef, wide, states, halos, rows):
+def gradient(place, region, coef, wide, states, halos, inner_grad):
     cols, tags, levels, lats = states[1].shape
     vmem = pl.BlockSpec(memory_space=pltpu.VMEM)
-    operands = [region, coef, wide, *states, *halos, rows]
+    operands = [region, coef, wide, *states, *halos, inner_grad]
     return pl.pallas_call(
         low_kernel,
         in_specs=[pl.BlockSpec(memory_space=pltpu.SMEM)] + [vmem] * len(operands),
         out_specs=vmem,
         out_shape=pltpu.VMEM((cols, lats), jnp.float32),
-        scratch_shapes=[
-            *border_scratch(tags, 8, lats),
-            pltpu.VMEM((ITERS, cols, lats), jnp.float32),
-        ],
+        scratch_shapes=border_scratch(tags, 8, lats),
         compiler_params=pltpu.CompilerParams(vmem_limit_bytes=32 << 20),
         cost_estimate=SHORT,
         name="border_low_levels",
     )(place, *operands)
 
 
-def border_kernel(place, coef, wide, l0, l1, l2, l3, first, second, *refs):
+def border_kernel(place, coef, wide, l0, l1, l2, l3, second, first, *refs):
     final_in, out_in, final, out, halo, work, sides, sems = refs
     cols, tags, levels, lats = l1.shape
     pitch = cols + 1
@@ -534,18 +533,18 @@
     coef_first, coef_second, first, second = pack(parts, place, far[0], far[1:6], far[6])
     coef_first = swapped(coef_first, "dom", pairs)
     coef_second = swapped(coef_second, "dom", turn)
+    second = swapped(second, "dom", turn)
     first = swapped(first, "dom", pairs)
-    second = swapped(second, "dom", turn)
     pieces = [jnp.stack([coef_first, coef_second])]
     for by in range(1, parts):
         pieces.append(swapped(pieces[0], "grp", lambda i: i ^ by))
-    coef, *states, final, rows = inner(place, own[0], own[1:], top, region)
+    coef, *states, final, inner_grad = inner(place, own[0], own[1:], top, region)
     wide = outer_coefs(parts, lam.shape[2], place, coef, pieces)
     out = write_inner(final, lam.shape)
     wide, out = lax.optimization_barrier((wide, out))
-    grad = gradient(place, region, coef, wide, states, (first, second), rows)
+    grad = gradient(place, region, coef, wide, states, (second, first), inner_grad)
     grad, wide = lax.optimization_barrier((grad, wide))
-    out = border(place, coef, wide, states, (first, second), final, out)
+    out = border(place, coef, wide, states, (second, first), final, out)
     share = grad
     for by in range(1, groups):
         grad = grad + swapped(share, "grp", lambda i: i ^ by)

time: 30.9 us -> 31.5 us (1.019)
  waiting for transfers between devices: 1.86 us -> 3.15 us
  starting transfers between devices: 12.3 us -> 11.6 us
    ppermute x10, waiting for transfers between devices: 1.86 us -> 3.15 us  [swapped(): lax.ppermute(value, axis, [(i, partner(i)) for i in range(lax.axis_size(a...]
    ppermute x10, starting transfers between devices: 12.3 us -> 11.6 us  [swapped(): lax.ppermute(value, axis, [(i, partner(i)) for i in range(lax.axis_size(a...]
  transfers between devices with their start and end apart: 10 -> 10, of which waited for: 3 -> 2; matrix products, arithmetic and copies ran while one was open for 0% -> 0% of each run, Pallas kernels for 36% -> 36%
where the time goes in v14:
time: 31.5 us; the launch traced here: 31.3 us
  Pallas kernels  15 us (48%)
  starting transfers between devices  11.6 us (37%)
  waiting for transfers between devices  3.15 us (10%)
  between operations  0.83 us (3%)
  other arithmetic  0.73 us (2%)
    ppermute x10, starting transfers between devices, swapped(): lax.ppermute(value, axis, [(i, partner(i)) for i in range(lax.axis_size(a...  11.6 us
    pallas_call x1, Pallas kernels, inner(): pl.pallas_call(inner_kernel, in_specs=[pl.BlockSpec(memory_space=pltpu.SM...  6.3 us
    ppermute x10, waiting for transfers between devices, swapped(): lax.ppermute(value, axis, [(i, partner(i)) for i in range(lax.axis_size(a...  3.15 us
    pallas_call x1, Pallas kernels, border(): pl.pallas_call(border_kernel, in_specs=[pl.BlockSpec(memory_space=pltpu.S...  2.93 us
    pallas_call x1, Pallas kernels, pack(): pl.pallas_call(functools.partial(pack_kernel, parts), in_specs=[pl.BlockS...  2.55 us
    pallas_call x1, Pallas kernels, gradient(): pl.pallas_call(low_kernel, in_specs=[pl.BlockSpec(memory_space=pltpu.SMEM...  1.27 us
    pallas_call x1, Pallas kernels, write_inner(): pl.pallas_call(write_kernel, in_specs=[pl.BlockSpec(memory_space=pltpu.VM...  1.14 us
    pallas_call x1, Pallas kernels, outer_coefs(): pl.pallas_call(functools.partial(outer_kernel, parts, cols), in_specs=[pl...  0.83 us
  transfers between devices with their start and end apart: 10, of which 2 were waited for; matrix products, arithmetic and copies ran while one was open for 0% of the time, Pallas kernels for 36%

profile of v14, /device:TPU:0, one launch (start us, length us, event | category | flops | bytes accessed | tf_op | source)
XLA Modules:
  0.0 31.3 jit_solution(7929767961407742974)
XLA Ops:
  0.6 0.1 pad_add_fusion.place
  0.7 0.0 copy-start.4
  0.7 0.0 copy-start.5
  0.8 0.0 copy-start.6
  0.8 0.0 copy-start.7
  0.8 2.5 %pack_edges.1 = (f32[16,4,256]{2,1,0:T(4,128)S(1)}, f32[16,4,256]{2,1,0:T(4,128)S(1)}, f32[16,16,256]{2,1,0:T(8,128)S(1)}, f32[16,16,256]{2,1,0:T(8,128)S(1)}) custom-call(s32[2]{0:T(128)S(1)} %pad_add_fusion.place, f32[4,16,32,256]{3,2,1,0:T(8,128)} %lam.3, f32[16,32,256]{2,1,0:T(8,128)} %ew.3, f32[16,32,256]{2,1,0:T(8,128)} %ed.3, f32[16,32,256]{2,1,0:T(8,128)} %nw.3, ...), custom_call_target="tpu_custom_call" | custom-call | flops 1000 | bytes 1000 | tf_op jit(solution)/shard_map/pack_edges/pallas_call | solution.py:145
  3.3 3.0 %collective-permute-start = (f32[16,4,256]{2,1,0:T(4,128)S(1)}, f32[16,4,256]{2,1,0:T(4,128)S(1)}, u32[]{:S(2)}, u32[]{:S(2)}) collective-permute-start(f32[16,4,256]{2,1,0:T(4,128)S(1)} %get-tuple-element.19), channel_id=1, source_target_pairs={{0,4},{4,0},{8,12},{12,8},{16,20},{20,16},{24,28},{28,24},{1,5},{5... | collective-permute-start | bytes 196616 | tf_op jit(solution)/shard_map/ppermute | solution.py:20
  6.3 3.6 %collective-permute-start.1 = (f32[16,4,256]{2,1,0:T(4,128)S(1)}, f32[16,4,256]{2,1,0:T(4,128)S(1)}, u32[]{:S(2)}, u32[]{:S(2)}) collective-permute-start(f32[16,4,256]{2,1,0:T(4,128)S(1)} %get-tuple-element.20), channel_id=1, source_target_pairs={{0,28},{4,8},{8,4},{12,16},{16,12},{20,24},{24,20},{28,0},{1,29},{... | collective-permute-start | bytes 196616 | tf_op jit(solution)/shard_map/ppermute | solution.py:20
  9.9 1.1 %collective-permute-start.5 = (f32[16,16,256]{2,1,0:T(8,128)S(1)}, f32[16,16,256]{2,1,0:T(8,128)S(1)}, u32[]{:S(2)}, u32[]{:S(2)}) collective-permute-start(f32[16,16,256]{2,1,0:T(8,128)S(1)} %get-tuple-element.27), channel_id=1, source_target_pairs={{0,28},{4,8},{8,4},{12,16},{16,12},{20,24},{24,20},{28,0},{1,29},{... | collective-permute-start | bytes 786440 | tf_op jit(solution)/shard_map/ppermute | solution.py:20
  11.1 2.3 %collective-permute-done.1 = f32[16,4,256]{2,1,0:T(4,128)S(1)} collective-permute-done((f32[16,4,256]{2,1,0:T(4,128)S(1)}, f32[16,4,256]{2,1,0:T(4,128)S(1)}, u32[]{:S(2)}, u32[]{:S(2)}) %collective-permute-start.1) | collective-permute-done | bytes 65568 | tf_op jit(solution)/shard_map/ppermute | solution.py:20
  13.4 0.1 collective-permute-start.4
  13.5 1.6 %collective-permute-start.3 = (f32[2,16,4,256]{3,2,1,0:T(4,128)S(1)}, f32[2,16,4,256]{3,2,1,0:T(4,128)S(1)}, u32[]{:S(2)}, u32[]{:S(2)}) collective-permute-start(f32[2,16,4,256]{3,2,1,0:T(4,128)S(1)} %pad_maximum_fusion.refs_0_), channel_id=1, source_target_pairs={{0,2},{1,3},{2,0},{3,1},{4,6},{5,7},{6,4},{7,5},{8,10},{9,11},{10,... | collective-permute-start | bytes 393224 | tf_op jit(solution)/shard_map/ppermute | solution.py:20
  15.1 0.3 collective-permute-start.2
  15.4 6.3 %inner_steps.1 = (f32[33,6,16,256]{3,2,1,0:T(8,128)S(1)}, f32[4,4,16,256]{3,2,1,0:T(8,128)S(1)}, f32[32,4,16,256]{3,2,1,0:T(8,128)S(1)}, f32[32,4,16,256]{3,2,1,...) custom-call(s32[2]{0:T(128)S(1)} %pad_add_fusion.place, ...), custom_call_target="tpu_custom_call" | custom-call | flops 1000 | bytes 1000 | tf_op jit(solution)/shard_map/inner_steps/pallas_call | solution.py:269
  21.7 1.1 %write_inner.1.refs_1_ = f32[4,16,32,256]{3,2,1,0:T(8,128)} custom-call(f32[4264,128]{1,0:T(8,128)S(1)} %get-tuple-element.21.final.refs_0_), custom_call_target="tpu_custom_call" | custom-call | flops 1000 | bytes 1000 | tf_op jit(solution)/shard_map/write_inner/pallas_call | solution.py:508
  22.8 0.0 collective-permute-done.2.refs_1_
  22.9 0.8 %outer_coefs.1.wide = f32[2,7,6,16,256]{4,3,2,1,0:T(8,128)S(1)} custom-call(s32[2]{0:T(128)S(1)} %pad_add_fusion.place, f32[33,6,16,256]{3,2,1,0:T(8,128)S(1)} %get-tuple-element.18.coef, f32[2,16,4,256]{3,2,1,0:T(4,128)S(1)} %pad_maximum_fusion.refs_0_, f32[2,16,4,256]{3,2,1,0:T(4,128)S(1)} %collective-permute-done.2.refs_1_, ...), custom_call_target="tpu_custom_call" | custom-call | flops 1000 | bytes 1000 | tf_op jit(solution)/shard_map/outer_coefs/pallas_call | solution.py:332
  23.7 0.8 %collective-permute-done.6.first = f32[16,16,256]{2,1,0:T(8,128)S(1)} collective-permute-done((f32[16,16,256]{2,1,0:T(8,128)S(1)}, f32[16,16,256]{2,1,0:T(8,128)S(1)}, u32[]{:S(2)}, u32[]{:S(2)}) %collective-permute-start.6) | collective-permute-done | bytes 262176 | tf_op jit(solution)/shard_map/ppermute | solution.py:20
  24.5 1.3 %border_low_levels.1 = f32[32,256]{1,0:T(8,128)S(1)} custom-call(s32[2]{0:T(128)S(1)} %pad_add_fusion.place, s32[32,256]{1,0:T(8,128)S(1)} %copy-done.7, f32[33,6,16,256]{3,2,1,0:T(8,128)S(1)} %get-tuple-element.18.coef, f32[2,7,6,16,256]{4,3,2,1,0:T(8,128)S(1)} %outer_coefs.1.wide, f32[4,4,16,256]{3,2,1,0:T(8,128)S(1)} %get-tuple-element.23.l0, ...), custom_call_target="tpu_custom_call" | custom-call | flops 1000 | bytes 1000 | tf_op jit(solution)/shard_map/border_low_levels/pallas_call | solution.py:413
  25.8 0.4 %collective-permute-start.9 = (f32[32,256]{1,0:T(8,128)S(1)}, f32[32,256]{1,0:T(8,128)S(1)}, u32[]{:S(2)}, u32[]{:S(2)}) collective-permute-start(f32[32,256]{1,0:T(8,128)S(1)} %border_low_levels.1), channel_id=1, source_target_pairs={{0,3},{1,2},{2,1},{3,0},{4,7},{5,6},{6,5},{7,4},{8,11},{9,10},{10,... | collective-permute-start | bytes 98312 | tf_op jit(solution)/shard_map/ppermute | solution.py:20
  26.2 1.3 %collective-permute-start.8 = (f32[32,256]{1,0:T(8,128)S(1)}, f32[32,256]{1,0:T(8,128)S(1)}, u32[]{:S(2)}, u32[]{:S(2)}) collective-permute-start(f32[32,256]{1,0:T(8,128)S(1)} %border_low_levels.1), channel_id=1, source_target_pairs={{0,2},{1,3},{2,0},{3,1},{4,6},{5,7},{6,4},{7,5},{8,10},{9,11},{10,... | collective-permute-start | bytes 98312 | tf_op jit(solution)/shard_map/ppermute | solution.py:20
  27.5 0.3 collective-permute-start.7
  27.7 2.9 %border_all_levels.1 = (f32[4264,128]{1,0:T(8,128)S(1)}, f32[4,16,32,256]{3,2,1,0:T(8,128)}) custom-call(s32[2]{0:T(128)S(1)} %pad_add_fusion.place, f32[33,6,16,256]{3,2,1,0:T(8,128)S(1)} %get-tuple-element.18.coef, f32[2,7,6,16,256]{4,3,2,1,0:T(8,128)S(1)} %outer_coefs.1.wide, ...), custom_call_target="tpu_custom_call", output_to_operand_aliasing={{0}: (9, {}), {1}: (10, {})} | custom-call | flops 1000 | bytes 1000 | tf_op jit(solution)/shard_map/border_all_levels/pallas_call | solution.py:464
  30.7 0.6 %add_add_fusion = f32[32,256]{1,0:T(8,128)} fusion(f32[32,256]{1,0:T(8,128)S(1)} %collective-permute-done.9, f32[32,256]{1,0:T(8,128)S(1)} %collective-permute-done.8, f32[32,256]{1,0:T(8,128)S(1)} %border_low_levels.1, f32[32,256]{1,0:T(8,128)S(1)} %collective-permute-done.7), kind=kLoop, calls=%fused_computation.1 | loop fusion | flops 24576 | bytes 163840 | tf_op jit(solution)/shard_map/add | solution.py:550
  (21 shorter events, 0.1 us)
Async XLA Ops:
  0.7 14.6 %copy-start = (f32[4,16,32,256]{3,2,1,0:T(8,128)S(1)}, f32[4,16,32,256]{3,2,1,0:T(8,128)}, u32[]{:S(2)}) copy-start(f32[4,16,32,256]{3,2,1,0:T(8,128)} %lam.3) | copy-start | bytes 6291460
  0.7 14.6 %copy-start.1 = (f32[16,32,256]{2,1,0:T(8,128)S(1)}, f32[16,32,256]{2,1,0:T(8,128)}, u32[]{:S(2)}) copy-start(f32[16,32,256]{2,1,0:T(8,128)} %ew.3) | copy-start | bytes 1572868
  0.7 14.6 %copy-start.2 = (f32[16,32,256]{2,1,0:T(8,128)S(1)}, f32[16,32,256]{2,1,0:T(8,128)}, u32[]{:S(2)}) copy-start(f32[16,32,256]{2,1,0:T(8,128)} %ed.3) | copy-start | bytes 1572868
  0.7 14.6 %copy-start.3 = (f32[16,32,256]{2,1,0:T(8,128)S(1)}, f32[16,32,256]{2,1,0:T(8,128)}, u32[]{:S(2)}) copy-start(f32[16,32,256]{2,1,0:T(8,128)} %nw.3) | copy-start | bytes 1572868
  0.7 14.6 %copy-start.4 = (f32[16,32,256]{2,1,0:T(8,128)S(1)}, f32[16,32,256]{2,1,0:T(8,128)}, u32[]{:S(2)}) copy-start(f32[16,32,256]{2,1,0:T(8,128)} %nd.3) | copy-start | bytes 1572868
  0.7 14.6 %copy-start.5 = (f32[16,32,256]{2,1,0:T(8,128)S(1)}, f32[16,32,256]{2,1,0:T(8,128)}, u32[]{:S(2)}) copy-start(f32[16,32,256]{2,1,0:T(8,128)} %mf.3) | copy-start | bytes 1572868
  0.8 14.6 %copy-start.6 = (s32[32,256]{1,0:T(8,128)S(1)}, s32[32,256]{1,0:T(8,128)}, u32[]{:S(2)}) copy-start(s32[32,256]{1,0:T(8,128)} %top.3) | copy-start | bytes 98308
  0.8 14.6 %copy-start.7 = (s32[32,256]{1,0:T(8,128)S(1)}, s32[32,256]{1,0:T(8,128)}, u32[]{:S(2)}) copy-start(s32[32,256]{1,0:T(8,128)} %region.3) | copy-start | bytes 98308
  3.3 7.7 %collective-permute-start = (f32[16,4,256]{2,1,0:T(4,128)S(1)}, f32[16,4,256]{2,1,0:T(4,128)S(1)}, u32[]{:S(2)}, u32[]{:S(2)}) collective-permute-start(f32[16,4,256]{2,1,0:T(4,128)S(1)} %get-tuple-element.19), channel_id=1, source_target_pairs={{0,4},{4,0},{8,12},{12,8},{16,20},{20,16},{24,28},{28,24},{1,5},{5... | collective-permute-start | bytes 196616 | tf_op jit(solution)/shard_map/ppermute | solution.py:20
  6.3 7.0 %collective-permute-start.1 = (f32[16,4,256]{2,1,0:T(4,128)S(1)}, f32[16,4,256]{2,1,0:T(4,128)S(1)}, u32[]{:S(2)}, u32[]{:S(2)}) collective-permute-start(f32[16,4,256]{2,1,0:T(4,128)S(1)} %get-tuple-element.20), channel_id=1, source_target_pairs={{0,28},{4,8},{8,4},{12,16},{16,12},{20,24},{24,20},{28,0},{1,29},{... | collective-permute-start | bytes 196616 | tf_op jit(solution)/shard_map/ppermute | solution.py:20
  9.9 13.8 %collective-permute-start.5 = (f32[16,16,256]{2,1,0:T(8,128)S(1)}, f32[16,16,256]{2,1,0:T(8,128)S(1)}, u32[]{:S(2)}, u32[]{:S(2)}) collective-permute-start(f32[16,16,256]{2,1,0:T(8,128)S(1)} %get-tuple-element.27), channel_id=1, source_target_pairs={{0,28},{4,8},{8,4},{12,16},{16,12},{20,24},{24,20},{28,0},{1,29},{... | collective-permute-start | bytes 786440 | tf_op jit(solution)/shard_map/ppermute | solution.py:20
  11.1 13.5 %collective-permute-start.6 = (f32[16,16,256]{2,1,0:T(8,128)S(1)}, f32[16,16,256]{2,1,0:T(8,128)S(1)}, u32[]{:S(2)}, u32[]{:S(2)}) collective-permute-start(f32[16,16,256]{2,1,0:T(8,128)S(1)} %get-tuple-element.28), channel_id=1, source_target_pairs={{0,4},{4,0},{8,12},{12,8},{16,20},{20,16},{24,28},{28,24},{1,5},{5... | collective-permute-start | bytes 786440 | tf_op jit(solution)/shard_map/ppermute | solution.py:20
  13.4 9.4 %collective-permute-start.4 = (f32[2,16,4,256]{3,2,1,0:T(4,128)S(1)}, f32[2,16,4,256]{3,2,1,0:T(4,128)S(1)}, u32[]{:S(2)}, u32[]{:S(2)}) collective-permute-start(f32[2,16,4,256]{3,2,1,0:T(4,128)S(1)} %pad_maximum_fusion.refs_0_), channel_id=1, source_target_pairs={{0,3},{1,2},{2,1},{3,0},{4,7},{5,6},{6,5},{7,4},{8,11},{9,10},{10,... | collective-permute-start | bytes 393224 | tf_op jit(solution)/shard_map/ppermute | solution.py:20
  13.5 9.4 %collective-permute-start.3 = (f32[2,16,4,256]{3,2,1,0:T(4,128)S(1)}, f32[2,16,4,256]{3,2,1,0:T(4,128)S(1)}, u32[]{:S(2)}, u32[]{:S(2)}) collective-permute-start(f32[2,16,4,256]{3,2,1,0:T(4,128)S(1)} %pad_maximum_fusion.refs_0_), channel_id=1, source_target_pairs={{0,2},{1,3},{2,0},{3,1},{4,6},{5,7},{6,4},{7,5},{8,10},{9,11},{10,... | collective-permute-start | bytes 393224 | tf_op jit(solution)/shard_map/ppermute | solution.py:20
  15.1 7.8 %collective-permute-start.2 = (f32[2,16,4,256]{3,2,1,0:T(4,128)S(1)}, f32[2,16,4,256]{3,2,1,0:T(4,128)S(1)}, u32[]{:S(2)}, u32[]{:S(2)}) collective-permute-start(f32[2,16,4,256]{3,2,1,0:T(4,128)S(1)} %pad_maximum_fusion.refs_0_), channel_id=1, source_target_pairs={{0,1},{1,0},{2,3},{3,2},{4,5},{5,4},{6,7},{7,6},{8,9},{9,8},{10,11... | collective-permute-start | bytes 393224 | tf_op jit(solution)/shard_map/ppermute | solution.py:20
  25.8 4.9 %collective-permute-start.9 = (f32[32,256]{1,0:T(8,128)S(1)}, f32[32,256]{1,0:T(8,128)S(1)}, u32[]{:S(2)}, u32[]{:S(2)}) collective-permute-start(f32[32,256]{1,0:T(8,128)S(1)} %border_low_levels.1), channel_id=1, source_target_pairs={{0,3},{1,2},{2,1},{3,0},{4,7},{5,6},{6,5},{7,4},{8,11},{9,10},{10,... | collective-permute-start | bytes 98312 | tf_op jit(solution)/shard_map/ppermute | solution.py:20
  26.2 4.5 %collective-permute-start.8 = (f32[32,256]{1,0:T(8,128)S(1)}, f32[32,256]{1,0:T(8,128)S(1)}, u32[]{:S(2)}, u32[]{:S(2)}) collective-permute-start(f32[32,256]{1,0:T(8,128)S(1)} %border_low_levels.1), channel_id=1, source_target_pairs={{0,2},{1,3},{2,0},{3,1},{4,6},{5,7},{6,4},{7,5},{8,10},{9,11},{10,... | collective-permute-start | bytes 98312 | tf_op jit(solution)/shard_map/ppermute | solution.py:20
  27.5 3.2 %collective-permute-start.7 = (f32[32,256]{1,0:T(8,128)S(1)}, f32[32,256]{1,0:T(8,128)S(1)}, u32[]{:S(2)}, u32[]{:S(2)}) collective-permute-start(f32[32,256]{1,0:T(8,128)S(1)} %border_low_levels.1), channel_id=1, source_target_pairs={{0,1},{1,0},{2,3},{3,2},{4,5},{5,4},{6,7},{7,6},{8,9},{9,8},{10,11... | collective-permute-start | bytes 98312 | tf_op jit(solution)/shard_map/ppermute | solution.py:20

commit v15 on v13

--- a/solution.py
+++ b/solution.py
@@ -35,6 +35,10 @@
     levels = mf.shape[0]
     level = lax.broadcasted_iota(jnp.int32, mf.shape, 0)
     return jnp.where((level < top_row) & (level < levels - 1), mf, 0.0)
+
+
+def parity():
+    return lax.rem(lax.axis_index("dom"), 2)
 
 
 def level_above(h):
@@ -67,12 +71,12 @@
     return jnp.concatenate(parts, axis=1)
 
 
-def pack_kernel(parts, place, lam, ew, ed, nw, nd, mf, top, *refs):
+def pack_kernel(parts, lam, ew, ed, nw, nd, mf, top, *refs):
     coef_first, coef_second, lam_first, lam_second = refs[:4]
     field_s, top_s, lam_s, coef_p, lam_p, sems = refs[4:]
     tags, levels, cols, lats = lam.shape
     per = levels // parts
-    base = lax.rem(place[0], parts) * per
+    base = lax.rem(lax.axis_index("grp"), parts) * per
     copies = []
 
     def copy(src, dst):
@@ -102,7 +106,7 @@
                     at = ((j * 2 + side) * 2 + k) * few + i * pitch
                     coef_p[pl.ds(at, 8), :] = value[:, HALVES[k]]
 
-    odd = place[1]
+    odd = parity()
     start = 8 - EDGE
     for dest, side in ((coef_first, 1 - odd), (coef_second, odd)):
 
@@ -136,7 +140,7 @@
                 )
 
 
-def pack(parts, place, lam, fields, top):
+def pack(parts, lam, fields, top):
     tags, levels, cols, lats = lam.shape
     per = levels // parts
     hbm = pl.BlockSpec(memory_space=pltpu.HBM)
@@ -144,7 +148,7 @@
     lam_send = pltpu.VMEM((tags * EDGE, levels, lats), jnp.float32)
     return pl.pallas_call(
         functools.partial(pack_kernel, parts),
-        in_specs=[pl.BlockSpec(memory_space=pltpu.SMEM)] + [hbm] * 7,
+        in_specs=[hbm] * 7,
         out_specs=[pl.BlockSpec(memory_space=pltpu.VMEM)] * 4,
         out_shape=[coef_send, coef_send, lam_send, lam_send],
         scratch_shapes=[
@@ -158,7 +162,7 @@
         compiler_params=pltpu.CompilerParams(vmem_limit_bytes=24 << 20),
         cost_estimate=SHORT,
         name="pack_edges",
-    )(place, lam, *fields, top)
+    )(lam, *fields, top)
 
 
 def chosen(region_row, first_tag, values):
@@ -209,7 +213,7 @@
     return store
 
 
-def inner_kernel(place, lam, ew, ed, nw, nd, mf, top, region, *refs):
+def inner_kernel(lam, ew, ed, nw, nd, mf, top, region, *refs):
     coef, l0, l1, l2, l3, final, rows, lam_p, field_p = refs
     tags, levels, cols, lats = lam.shape
     pitch = cols + 1
@@ -254,16 +258,16 @@
     loads = (given, loading(l1), loading(l2), loading(l3))
     stores = (storing(l1), storing(l2), storing(l3), last)
     for t in range(ITERS):
-        sweep(t, lam.shape, place[0] * tags, region, coef, loads[t], stores[t], rows)
-
-
-def inner(place, lam, fields, top, region):
+        sweep(t, lam.shape, lax.axis_index("grp") * tags, region, coef, loads[t], stores[t], rows)
+
+
+def inner(lam, fields, top, region):
     tags, levels, cols, lats = lam.shape
     vmem = pl.BlockSpec(memory_space=pltpu.VMEM)
     state = pltpu.VMEM((cols, tags, levels, lats), jnp.float32)
     return pl.pallas_call(
         inner_kernel,
-        in_specs=[pl.BlockSpec(memory_space=pltpu.SMEM)] + [vmem] * 8,
+        in_specs=[vmem] * 8,
         out_specs=[vmem] * 7,
         out_shape=[
             pltpu.VMEM((cols + 1, 6, levels, lats), jnp.float32),
@@ -279,19 +283,19 @@
         compiler_params=pltpu.CompilerParams(vmem_limit_bytes=32 << 20),
         cost_estimate=SHORT,
         name="inner_steps",
-    )(place, lam, *fields, top, region)
+    )(lam, *fields, top, region)
 
 
 def slot(c, cols):
     return (LOW, c + EDGE - 1) if c < EDGE else (HIGH, c - (cols - EDGE))
 
 
-def outer_kernel(parts, cols, place, coef, *refs):
+def outer_kernel(parts, cols, coef, *refs):
     pieces, wide, entry = refs[:parts], refs[parts], refs[parts + 1]
     levels = coef.shape[2]
     per = levels // parts
-    mine = lax.rem(place[0], parts)
-    odd = place[1]
+    mine = lax.rem(lax.axis_index("grp"), parts)
+    odd = parity()
     for by in range(parts):
         for half, side in enumerate((1 - odd, odd)):
 
@@ -320,29 +324,29 @@
         wide[*slot(0, cols), j] = value
 
 
-def outer_coefs(parts, cols, place, coef, pieces):
+def outer_coefs(parts, cols, coef, pieces):
     _, _, levels, lats = coef.shape
     vmem = pl.BlockSpec(memory_space=pltpu.VMEM)
     return pl.pallas_call(
         functools.partial(outer_kernel, parts, cols),
-        in_specs=[pl.BlockSpec(memory_space=pltpu.SMEM)] + [vmem] * (1 + parts),
+        in_specs=[vmem] * (1 + parts),
         out_specs=vmem,
         out_shape=pltpu.VMEM((2, 2 * EDGE - 1, 6, levels, lats), jnp.float32),
         scratch_shapes=[pltpu.VMEM((2 * ENTRIES * 2 * levels, LANES), jnp.float32)],
         compiler_params=pltpu.CompilerParams(vmem_limit_bytes=24 << 20),
         cost_estimate=SHORT,
         name="outer_coefs",
-    )(place, coef, *pieces)
+    )(coef, *pieces)
 
 
 def border_steps(
-    depth, place, region, coef, wide, kept, l0, halos, halo, work, rows=None, store=None, finish=None
+    depth, region, coef, wide, kept, l0, halos, halo, work, rows=None, store=None, finish=None
 ):
     cols, tags, levels, lats = kept[1].shape
-    first_tag = place[0] * tags
+    first_tag = lax.axis_index("grp") * tags
     part = slice(0, depth)
-    halo[1 - place[1]] = halos[0][:, part]
-    halo[place[1]] = halos[1][:, part]
+    halo[1 - parity()] = halos[0][:, part]
+    halo[parity()] = halos[1][:, part]
 
     def coefs_at(c):
         if 0 < c < cols:
@@ -387,10 +391,10 @@
         finish(k)
 
 
-def low_kernel(place, region, coef, wide, l0, l1, l2, l3, first, second, rows_in, grad, halo, work, rows):
+def low_kernel(region, coef, wide, l0, l1, l2, l3, first, second, rows_in, grad, halo, work, rows):
     rows[...] = rows_in[...]
     kept = (None, l1, l2, l3)
-    border_steps(8, place, region, coef, wide, kept, l0, (first, second), halo, work, rows)
+    border_steps(8, region, coef, wide, kept, l0, (first, second), halo, work, rows)
     total = rows[0]
     for t in range(1, ITERS):
         total = total + rows[t]
@@ -404,13 +408,13 @@
     ]
 
 
-def gradient(place, region, coef, wide, states, halos, rows):
+def gradient(region, coef, wide, states, halos, rows):
     cols, tags, levels, lats = states[1].shape
     vmem = pl.BlockSpec(memory_space=pltpu.VMEM)
     operands = [region, coef, wide, *states, *halos, rows]
     return pl.pallas_call(
         low_kernel,
-        in_specs=[pl.BlockSpec(memory_space=pltpu.SMEM)] + [vmem] * len(operands),
+        in_specs=[vmem] * len(operands),
         out_specs=vmem,
         out_shape=pltpu.VMEM((cols, lats), jnp.float32),
         scratch_shapes=[
@@ -420,10 +424,10 @@
         compiler_params=pltpu.CompilerParams(vmem_limit_bytes=32 << 20),
         cost_estimate=SHORT,
         name="border_low_levels",
-    )(place, *operands)
-
-
-def border_kernel(place, coef, wide, l0, l1, l2, l3, first, second, *refs):
+    )(*operands)
+
+
+def border_kernel(coef, wide, l0, l1, l2, l3, first, second, *refs):
     final_in, out_in, final, out, halo, work, sides, sems = refs
     cols, tags, levels, lats = l1.shape
     pitch = cols + 1
@@ -450,21 +454,21 @@
             copies[-1].start()
 
     border_steps(
-        levels, place, None, coef, wide, kept, l0, (first, second), halo, work, None, store, finish
+        levels, None, coef, wide, kept, l0, (first, second), halo, work, None, store, finish
     )
     for c in copies:
         c.wait()
 
 
-def border(place, coef, wide, states, halos, final, out):
+def border(coef, wide, states, halos, final, out):
     cols, tags, levels, lats = states[1].shape
     vmem = pl.BlockSpec(memory_space=pltpu.VMEM)
     hbm = pl.BlockSpec(memory_space=pltpu.HBM)
     operands = [coef, wide, *states, *halos]
-    n = len(operands) + 1
+    n = len(operands)
     return pl.pallas_call(
         border_kernel,
-        in_specs=[pl.BlockSpec(memory_space=pltpu.SMEM)] + [vmem] * n + [hbm],
+        in_specs=[vmem] * (n + 1) + [hbm],
         out_specs=[vmem, hbm],
         out_shape=[
             pltpu.VMEM(final.shape, jnp.float32),
@@ -479,7 +483,7 @@
         compiler_params=pltpu.CompilerParams(vmem_limit_bytes=32 << 20),
         cost_estimate=SHORT,
         name="border_all_levels",
-    )(place, *operands, final, out)[1]
+    )(*operands, final, out)[1]
 
 
 def write_kernel(final, out, block, sems):
@@ -524,14 +528,12 @@
 def local(lam, east_wind, north_wind, east_diff, north_diff, mass_flux, region, top):
     groups, tiles = lax.axis_size("grp"), lax.axis_size("dom")
     parts = 4 if groups % 4 == 0 else 1
-    grp, dom = lax.axis_index("grp"), lax.axis_index("dom")
-    place = jnp.stack([grp, dom % 2]).astype(jnp.int32)
     own = (lam, east_wind, east_diff, north_wind, north_diff, mass_flux)
     far = [pltpu.with_memory_space_constraint(value, pltpu.HBM) for value in (*own, top)]
 
     pairs = lambda i: i ^ 1
     turn = lambda i: (((i - 1) % tiles ^ 1) + 1) % tiles
-    coef_first, coef_second, first, second = pack(parts, place, far[0], far[1:6], far[6])
+    coef_first, coef_second, first, second = pack(parts, far[0], far[1:6], far[6])
     coef_first = swapped(coef_first, "dom", pairs)
     coef_second = swapped(coef_second, "dom", turn)
     first = swapped(first, "dom", pairs)
@@ -539,13 +541,13 @@
     pieces = [jnp.stack([coef_first, coef_second])]
     for by in range(1, parts):
         pieces.append(swapped(pieces[0], "grp", lambda i: i ^ by))
-    coef, *states, final, rows = inner(place, own[0], own[1:], top, region)
-    wide = outer_coefs(parts, lam.shape[2], place, coef, pieces)
+    coef, *states, final, rows = inner(own[0], own[1:], top, region)
+    wide = outer_coefs(parts, lam.shape[2], coef, pieces)
     out = write_inner(final, lam.shape)
     wide, out = lax.optimization_barrier((wide, out))
-    grad = gradient(place, region, coef, wide, states, (first, second), rows)
+    grad = gradient(region, coef, wide, states, (first, second), rows)
     grad, wide = lax.optimization_barrier((grad, wide))
-    out = border(place, coef, wide, states, (first, second), final, out)
+    out = border(coef, wide, states, (first, second), final, out)
     share = grad
     for by in range(1, groups):
         grad = grad + swapped(share, "grp", lambda i: i ^ by)

time: 30.9 us -> 28.9 us (0.935)
  Pallas kernels: 15 us -> 12.1 us
  waiting for transfers between devices: 1.86 us -> 2.86 us
    pallas_call x5, Pallas kernels: 13.9 us -> 10.9 us  [the longest x1 5.65 us: inner(): pl.pallas_call(inner_kernel, in_specs=[vmem] * 8, out_specs=[vmem] * 7, o...]
    ppermute x10, waiting for transfers between devices: 1.86 us -> 2.86 us  [swapped(): lax.ppermute(value, axis, [(i, partner(i)) for i in range(lax.axis_size(a...]
  transfers between devices with their start and end apart: 10 -> 10, of which waited for: 3 -> 2; matrix products, arithmetic and copies ran while one was open for 0% -> 0% of each run, Pallas kernels for 36% -> 33%
where the time goes in v15:
time: 28.9 us; the launch traced here: 28.8 us
  starting transfers between devices  12.3 us (43%)
  Pallas kernels  12.1 us (42%)
  waiting for transfers between devices  2.86 us (10%)
  between operations  0.84 us (3%)
  other arithmetic  0.66 us (2%)
    ppermute x10, starting transfers between devices, swapped(): lax.ppermute(value, axis, [(i, partner(i)) for i in range(lax.axis_size(a...  12.3 us
    pallas_call x1, Pallas kernels, inner(): pl.pallas_call(inner_kernel, in_specs=[vmem] * 8, out_specs=[vmem] * 7, o...  5.65 us
    ppermute x10, waiting for transfers between devices, swapped(): lax.ppermute(value, axis, [(i, partner(i)) for i in range(lax.axis_size(a...  2.86 us
    pallas_call x1, Pallas kernels, border(): pl.pallas_call(border_kernel, in_specs=[vmem] * (n + 1) + [hbm], out_spec...  2.38 us
    pallas_call x1, Pallas kernels, pack(): pl.pallas_call(functools.partial(pack_kernel, parts), in_specs=[hbm] * 7,...  1.87 us
    pallas_call x1, Pallas kernels, write_inner(): pl.pallas_call(write_kernel, in_specs=[pl.BlockSpec(memory_space=pltpu.VM...  1.14 us
    pallas_call x1, Pallas kernels, gradient(): pl.pallas_call(low_kernel, in_specs=[vmem] * len(operands), out_specs=vme...  0.75 us
    add x1, other arithmetic, local(): grad = grad + swapped(share, 'grp', lambda i: i ^ by)  0.63 us
  transfers between devices with their start and end apart: 10, of which 2 were waited for; matrix products, arithmetic and copies ran while one was open for 0% of the time, Pallas kernels for 33%

profile of v15, /device:TPU:0, one launch (start us, length us, event | category | flops | bytes accessed | tf_op | source)
XLA Modules:
  0.0 28.8 jit_solution(3062053855464112407)
XLA Ops:
  0.7 1.9 %pack_edges.1 = (f32[16,4,256]{2,1,0:T(4,128)S(1)}, f32[16,4,256]{2,1,0:T(4,128)S(1)}, f32[16,16,256]{2,1,0:T(8,128)S(1)}, f32[16,16,256]{2,1,0:T(8,128)S(1)}) custom-call(f32[4,16,32,256]{3,2,1,0:T(8,128)} %lam.3, f32[16,32,256]{2,1,0:T(8,128)} %ew.3, f32[16,32,256]{2,1,0:T(8,128)} %ed.3, f32[16,32,256]{2,1,0:T(8,128)} %nw.3, f32[16,32,256]{2,1,0:T(8,128)} %nd.3, ...), custom_call_target="tpu_custom_call" | custom-call | flops 1000 | bytes 1000 | tf_op jit(solution)/shard_map/pack_edges/pallas_call | solution.py:149
  2.6 3.0 %collective-permute-start = (f32[16,4,256]{2,1,0:T(4,128)S(1)}, f32[16,4,256]{2,1,0:T(4,128)S(1)}, u32[]{:S(2)}, u32[]{:S(2)}) collective-permute-start(f32[16,4,256]{2,1,0:T(4,128)S(1)} %get-tuple-element.19), channel_id=1, source_target_pairs={{0,4},{4,0},{8,12},{12,8},{16,20},{20,16},{24,28},{28,24},{1,5},{5... | collective-permute-start | bytes 196616 | tf_op jit(solution)/shard_map/ppermute | solution.py:20
  5.6 3.6 %collective-permute-start.1 = (f32[16,4,256]{2,1,0:T(4,128)S(1)}, f32[16,4,256]{2,1,0:T(4,128)S(1)}, u32[]{:S(2)}, u32[]{:S(2)}) collective-permute-start(f32[16,4,256]{2,1,0:T(4,128)S(1)} %get-tuple-element.20), channel_id=1, source_target_pairs={{0,28},{4,8},{8,4},{12,16},{16,12},{20,24},{24,20},{28,0},{1,29},{... | collective-permute-start | bytes 196616 | tf_op jit(solution)/shard_map/ppermute | solution.py:20
  9.2 0.0 collective-permute-start.5
  9.2 1.9 %collective-permute-start.6 = (f32[16,16,256]{2,1,0:T(8,128)S(1)}, f32[16,16,256]{2,1,0:T(8,128)S(1)}, u32[]{:S(2)}, u32[]{:S(2)}) collective-permute-start(f32[16,16,256]{2,1,0:T(8,128)S(1)} %get-tuple-element.28), channel_id=1, source_target_pairs={{0,28},{4,8},{8,4},{12,16},{16,12},{20,24},{24,20},{28,0},{1,29},{... | collective-permute-start | bytes 786440 | tf_op jit(solution)/shard_map/ppermute | solution.py:20
  11.1 0.0 collective-permute-done
  11.1 1.6 %collective-permute-done.1 = f32[16,4,256]{2,1,0:T(4,128)S(1)} collective-permute-done((f32[16,4,256]{2,1,0:T(4,128)S(1)}, f32[16,4,256]{2,1,0:T(4,128)S(1)}, u32[]{:S(2)}, u32[]{:S(2)}) %collective-permute-start.1) | collective-permute-done | bytes 65568 | tf_op jit(solution)/shard_map/ppermute | solution.py:20
  12.7 0.1 collective-permute-start.4
  12.8 1.6 %collective-permute-start.3 = (f32[2,16,4,256]{3,2,1,0:T(4,128)S(1)}, f32[2,16,4,256]{3,2,1,0:T(4,128)S(1)}, u32[]{:S(2)}, u32[]{:S(2)}) collective-permute-start(f32[2,16,4,256]{3,2,1,0:T(4,128)S(1)} %pad_maximum_fusion.refs_0_), channel_id=1, source_target_pairs={{0,2},{1,3},{2,0},{3,1},{4,6},{5,7},{6,4},{7,5},{8,10},{9,11},{10,... | collective-permute-start | bytes 393224 | tf_op jit(solution)/shard_map/ppermute | solution.py:20
  14.4 0.3 collective-permute-start.2
  14.7 5.7 %inner_steps.1 = (f32[33,6,16,256]{3,2,1,0:T(8,128)S(1)}, f32[4,4,16,256]{3,2,1,0:T(8,128)S(1)}, f32[32,4,16,256]{3,2,1,0:T(8,128)S(1)}, f32[32,4,16,256]{3,2,1,...) custom-call(f32[4,16,32,256]{3,2,1,0:T(8,128)S(1)} %copy-done, ...), custom_call_target="tpu_custom_call" | custom-call | flops 1000 | bytes 1000 | tf_op jit(solution)/shard_map/inner_steps/pallas_call | solution.py:268
  20.3 1.1 %write_inner.1.refs_1_ = f32[4,16,32,256]{3,2,1,0:T(8,128)} custom-call(f32[4264,128]{1,0:T(8,128)S(1)} %get-tuple-element.21.final.refs_0_), custom_call_target="tpu_custom_call" | custom-call | flops 1000 | bytes 1000 | tf_op jit(solution)/shard_map/write_inner/pallas_call | solution.py:513
  21.5 0.0 collective-permute-done.3.refs_2_
  21.5 0.3 %outer_coefs.1.wide = f32[2,7,6,16,256]{4,3,2,1,0:T(8,128)S(1)} custom-call(f32[33,6,16,256]{3,2,1,0:T(8,128)S(1)} %get-tuple-element.18.coef, f32[2,16,4,256]{3,2,1,0:T(4,128)S(1)} %pad_maximum_fusion.refs_0_, f32[2,16,4,256]{3,2,1,0:T(4,128)S(1)} %collective-permute-done.2.refs_1_, f32[2,16,4,256]{3,2,1,0:T(4,128)S(1)} %collective-permute-done.3.refs_2_, ...), custom_call_target="tpu_custom_call" | custom-call | flops 1000 | bytes 1000 | tf_op jit(solution)/shard_map/outer_coefs/pallas_call | solution.py:330
  21.8 1.3 %collective-permute-done.5.first = f32[16,16,256]{2,1,0:T(8,128)S(1)} collective-permute-done((f32[16,16,256]{2,1,0:T(8,128)S(1)}, f32[16,16,256]{2,1,0:T(8,128)S(1)}, u32[]{:S(2)}, u32[]{:S(2)}) %collective-permute-start.5) | collective-permute-done | bytes 262176 | tf_op jit(solution)/shard_map/ppermute | solution.py:20
  23.1 0.0 collective-permute-done.6.second
  23.1 0.7 %border_low_levels.1 = f32[32,256]{1,0:T(8,128)S(1)} custom-call(s32[32,256]{1,0:T(8,128)S(1)} %copy-done.7, f32[33,6,16,256]{3,2,1,0:T(8,128)S(1)} %get-tuple-element.18.coef, f32[2,7,6,16,256]{4,3,2,1,0:T(8,128)S(1)} %outer_coefs.1.wide, f32[4,4,16,256]{3,2,1,0:T(8,128)S(1)} %get-tuple-element.23.l0, f32[32,4,16,256]{3,2,1,0:T(8,128)S(1)} %get-tuple-element.24.l1, ...), custom_call_target="tpu_custom_call" | custom-call | flops 1000 | bytes 1000 | tf_op jit(solution)/shard_map/border_low_levels/pallas_call | solution.py:415
  23.8 0.3 %collective-permute-start.9 = (f32[32,256]{1,0:T(8,128)S(1)}, f32[32,256]{1,0:T(8,128)S(1)}, u32[]{:S(2)}, u32[]{:S(2)}) collective-permute-start(f32[32,256]{1,0:T(8,128)S(1)} %border_low_levels.1), channel_id=1, source_target_pairs={{0,3},{1,2},{2,1},{3,0},{4,7},{5,6},{6,5},{7,4},{8,11},{9,10},{10,... | collective-permute-start | bytes 98312 | tf_op jit(solution)/shard_map/ppermute | solution.py:20
  24.2 1.3 %collective-permute-start.8 = (f32[32,256]{1,0:T(8,128)S(1)}, f32[32,256]{1,0:T(8,128)S(1)}, u32[]{:S(2)}, u32[]{:S(2)}) collective-permute-start(f32[32,256]{1,0:T(8,128)S(1)} %border_low_levels.1), channel_id=1, source_target_pairs={{0,2},{1,3},{2,0},{3,1},{4,6},{5,7},{6,4},{7,5},{8,10},{9,11},{10,... | collective-permute-start | bytes 98312 | tf_op jit(solution)/shard_map/ppermute | solution.py:20
  25.5 0.3 collective-permute-start.7
  25.8 2.4 %border_all_levels.1 = (f32[4264,128]{1,0:T(8,128)S(1)}, f32[4,16,32,256]{3,2,1,0:T(8,128)}) custom-call(f32[33,6,16,256]{3,2,1,0:T(8,128)S(1)} %get-tuple-element.18.coef, f32[2,7,6,16,256]{4,3,2,1,0:T(8,128)S(1)} %outer_coefs.1.wide, f32[4,4,16,256]{3,2,1,0:T(8,128)S(1)} %get-tuple-element.23.l0, ...), custom_call_target="tpu_custom_call", output_to_operand_aliasing={{0}: (8, {}), {1}: (9, {})} | custom-call | flops 1000 | bytes 1000 | tf_op jit(solution)/shard_map/border_all_levels/pallas_call | solution.py:469
  28.1 0.0 collective-permute-done.8
  28.2 0.0 collective-permute-done.7
  28.2 0.6 %add_add_fusion = f32[32,256]{1,0:T(8,128)} fusion(f32[32,256]{1,0:T(8,128)S(1)} %collective-permute-done.9, f32[32,256]{1,0:T(8,128)S(1)} %collective-permute-done.8, f32[32,256]{1,0:T(8,128)S(1)} %border_low_levels.1, f32[32,256]{1,0:T(8,128)S(1)} %collective-permute-done.7), kind=kLoop, calls=%fused_computation.1 | loop fusion | flops 24576 | bytes 163840 | tf_op jit(solution)/shard_map/add | solution.py:553
  (20 shorter events, 0.1 us)
Async XLA Ops:
  0.6 14.0 %copy-start.6 = (s32[32,256]{1,0:T(8,128)S(1)}, s32[32,256]{1,0:T(8,128)}, u32[]{:S(2)}) copy-start(s32[32,256]{1,0:T(8,128)} %top.3) | copy-start | bytes 98308
  0.6 14.0 %copy-start.5 = (f32[16,32,256]{2,1,0:T(8,128)S(1)}, f32[16,32,256]{2,1,0:T(8,128)}, u32[]{:S(2)}) copy-start(f32[16,32,256]{2,1,0:T(8,128)} %mf.3) | copy-start | bytes 1572868
  0.7 14.0 %copy-start.4 = (f32[16,32,256]{2,1,0:T(8,128)S(1)}, f32[16,32,256]{2,1,0:T(8,128)}, u32[]{:S(2)}) copy-start(f32[16,32,256]{2,1,0:T(8,128)} %nd.3) | copy-start | bytes 1572868
  0.7 14.0 %copy-start.2 = (f32[16,32,256]{2,1,0:T(8,128)S(1)}, f32[16,32,256]{2,1,0:T(8,128)}, u32[]{:S(2)}) copy-start(f32[16,32,256]{2,1,0:T(8,128)} %ed.3) | copy-start | bytes 1572868
  0.7 14.0 %copy-start.3 = (f32[16,32,256]{2,1,0:T(8,128)S(1)}, f32[16,32,256]{2,1,0:T(8,128)}, u32[]{:S(2)}) copy-start(f32[16,32,256]{2,1,0:T(8,128)} %nw.3) | copy-start | bytes 1572868
  0.7 14.0 %copy-start.1 = (f32[16,32,256]{2,1,0:T(8,128)S(1)}, f32[16,32,256]{2,1,0:T(8,128)}, u32[]{:S(2)}) copy-start(f32[16,32,256]{2,1,0:T(8,128)} %ew.3) | copy-start | bytes 1572868
  0.7 14.0 %copy-start = (f32[4,16,32,256]{3,2,1,0:T(8,128)S(1)}, f32[4,16,32,256]{3,2,1,0:T(8,128)}, u32[]{:S(2)}) copy-start(f32[4,16,32,256]{3,2,1,0:T(8,128)} %lam.3) | copy-start | bytes 6291460
  0.7 14.0 %copy-start.7 = (s32[32,256]{1,0:T(8,128)S(1)}, s32[32,256]{1,0:T(8,128)}, u32[]{:S(2)}) copy-start(s32[32,256]{1,0:T(8,128)} %region.3) | copy-start | bytes 98308
  2.6 8.5 %collective-permute-start = (f32[16,4,256]{2,1,0:T(4,128)S(1)}, f32[16,4,256]{2,1,0:T(4,128)S(1)}, u32[]{:S(2)}, u32[]{:S(2)}) collective-permute-start(f32[16,4,256]{2,1,0:T(4,128)S(1)} %get-tuple-element.19), channel_id=1, source_target_pairs={{0,4},{4,0},{8,12},{12,8},{16,20},{20,16},{24,28},{28,24},{1,5},{5... | collective-permute-start | bytes 196616 | tf_op jit(solution)/shard_map/ppermute | solution.py:20
  5.6 7.1 %collective-permute-start.1 = (f32[16,4,256]{2,1,0:T(4,128)S(1)}, f32[16,4,256]{2,1,0:T(4,128)S(1)}, u32[]{:S(2)}, u32[]{:S(2)}) collective-permute-start(f32[16,4,256]{2,1,0:T(4,128)S(1)} %get-tuple-element.20), channel_id=1, source_target_pairs={{0,28},{4,8},{8,4},{12,16},{16,12},{20,24},{24,20},{28,0},{1,29},{... | collective-permute-start | bytes 196616 | tf_op jit(solution)/shard_map/ppermute | solution.py:20
  9.2 13.9 %collective-permute-start.5 = (f32[16,16,256]{2,1,0:T(8,128)S(1)}, f32[16,16,256]{2,1,0:T(8,128)S(1)}, u32[]{:S(2)}, u32[]{:S(2)}) collective-permute-start(f32[16,16,256]{2,1,0:T(8,128)S(1)} %get-tuple-element.27), channel_id=1, source_target_pairs={{0,4},{4,0},{8,12},{12,8},{16,20},{20,16},{24,28},{28,24},{1,5},{5... | collective-permute-start | bytes 786440 | tf_op jit(solution)/shard_map/ppermute | solution.py:20
  9.2 13.9 %collective-permute-start.6 = (f32[16,16,256]{2,1,0:T(8,128)S(1)}, f32[16,16,256]{2,1,0:T(8,128)S(1)}, u32[]{:S(2)}, u32[]{:S(2)}) collective-permute-start(f32[16,16,256]{2,1,0:T(8,128)S(1)} %get-tuple-element.28), channel_id=1, source_target_pairs={{0,28},{4,8},{8,4},{12,16},{16,12},{20,24},{24,20},{28,0},{1,29},{... | collective-permute-start | bytes 786440 | tf_op jit(solution)/shard_map/ppermute | solution.py:20
  12.7 8.8 %collective-permute-start.4 = (f32[2,16,4,256]{3,2,1,0:T(4,128)S(1)}, f32[2,16,4,256]{3,2,1,0:T(4,128)S(1)}, u32[]{:S(2)}, u32[]{:S(2)}) collective-permute-start(f32[2,16,4,256]{3,2,1,0:T(4,128)S(1)} %pad_maximum_fusion.refs_0_), channel_id=1, source_target_pairs={{0,3},{1,2},{2,1},{3,0},{4,7},{5,6},{6,5},{7,4},{8,11},{9,10},{10,... | collective-permute-start | bytes 393224 | tf_op jit(solution)/shard_map/ppermute | solution.py:20
  12.8 8.7 %collective-permute-start.3 = (f32[2,16,4,256]{3,2,1,0:T(4,128)S(1)}, f32[2,16,4,256]{3,2,1,0:T(4,128)S(1)}, u32[]{:S(2)}, u32[]{:S(2)}) collective-permute-start(f32[2,16,4,256]{3,2,1,0:T(4,128)S(1)} %pad_maximum_fusion.refs_0_), channel_id=1, source_target_pairs={{0,2},{1,3},{2,0},{3,1},{4,6},{5,7},{6,4},{7,5},{8,10},{9,11},{10,... | collective-permute-start | bytes 393224 | tf_op jit(solution)/shard_map/ppermute | solution.py:20
  14.4 7.1 %collective-permute-start.2 = (f32[2,16,4,256]{3,2,1,0:T(4,128)S(1)}, f32[2,16,4,256]{3,2,1,0:T(4,128)S(1)}, u32[]{:S(2)}, u32[]{:S(2)}) collective-permute-start(f32[2,16,4,256]{3,2,1,0:T(4,128)S(1)} %pad_maximum_fusion.refs_0_), channel_id=1, source_target_pairs={{0,1},{1,0},{2,3},{3,2},{4,5},{5,4},{6,7},{7,6},{8,9},{9,8},{10,11... | collective-permute-start | bytes 393224 | tf_op jit(solution)/shard_map/ppermute | solution.py:20
  23.8 4.3 %collective-permute-start.9 = (f32[32,256]{1,0:T(8,128)S(1)}, f32[32,256]{1,0:T(8,128)S(1)}, u32[]{:S(2)}, u32[]{:S(2)}) collective-permute-start(f32[32,256]{1,0:T(8,128)S(1)} %border_low_levels.1), channel_id=1, source_target_pairs={{0,3},{1,2},{2,1},{3,0},{4,7},{5,6},{6,5},{7,4},{8,11},{9,10},{10,... | collective-permute-start | bytes 98312 | tf_op jit(solution)/shard_map/ppermute | solution.py:20
  24.2 4.0 %collective-permute-start.8 = (f32[32,256]{1,0:T(8,128)S(1)}, f32[32,256]{1,0:T(8,128)S(1)}, u32[]{:S(2)}, u32[]{:S(2)}) collective-permute-start(f32[32,256]{1,0:T(8,128)S(1)} %border_low_levels.1), channel_id=1, source_target_pairs={{0,2},{1,3},{2,0},{3,1},{4,6},{5,7},{6,4},{7,5},{8,10},{9,11},{10,... | collective-permute-start | bytes 98312 | tf_op jit(solution)/shard_map/ppermute | solution.py:20
  25.5 2.7 %collective-permute-start.7 = (f32[32,256]{1,0:T(8,128)S(1)}, f32[32,256]{1,0:T(8,128)S(1)}, u32[]{:S(2)}, u32[]{:S(2)}) collective-permute-start(f32[32,256]{1,0:T(8,128)S(1)} %border_low_levels.1), channel_id=1, source_target_pairs={{0,1},{1,0},{2,3},{3,2},{4,5},{5,4},{6,7},{7,6},{8,9},{9,8},{10,11... | collective-permute-start | bytes 98312 | tf_op jit(solution)/shard_map/ppermute | solution.py:20

commit v16 on v15

--- a/solution.py
+++ b/solution.py
@@ -10,6 +10,7 @@
 ITERS = 4
 EDGE = ITERS
 ENTRIES = 16
+BLOCK = 4
 CHUNKS = 2
 LANES = 128
 HALVES = (slice(0, LANES), slice(LANES, 2 * LANES))
@@ -71,55 +72,64 @@
     return jnp.concatenate(parts, axis=1)
 
 
-def pack_kernel(parts, lam, ew, ed, nw, nd, mf, top, *refs):
-    coef_first, coef_second, lam_first, lam_second = refs[:4]
-    field_s, top_s, lam_s, coef_p, lam_p, sems = refs[4:]
+def coef_side(rank):
+    return lax.rem(1 - parity() + rank, 2)
+
+
+def coef_half(rank):
+    return lax.rem(lax.div(rank, 2), 2)
+
+
+def pack_kernel(lam, ew, ed, nw, nd, mf, top, *refs):
+    coef_send, lam_first, lam_second = refs[:3]
+    field_s, top_s, lam_s, coef_p, lam_p, sems = refs[3:]
     tags, levels, cols, lats = lam.shape
-    per = levels // parts
-    base = lax.rem(lax.axis_index("grp"), parts) * per
+    per = levels // 2
+    rank = lax.axis_index("grp")
+    base = coef_half(rank) * per
+    high = coef_side(rank)
+    edge = pl.ds(pl.multiple_of(high * (cols - 8), 8), 8)
     copies = []
 
     def copy(src, dst):
         copies.append(pltpu.make_async_copy(src, dst, sems.at[len(copies)]))
         copies[-1].start()
 
-    for side, at in ((LOW, 0), (HIGH, cols - 8)):
-        for f, field in enumerate((ew, ed, nw, nd, mf)):
-            copy(field.at[pl.ds(base, per), pl.ds(at, 8)], field_s.at[f, side])
-        copy(top.at[pl.ds(at, 8)], top_s.at[side])
+    for f, field in enumerate((ew, ed, nw, nd, mf)):
+        copy(field.at[pl.ds(base, per), edge], field_s.at[f])
+    copy(top.at[edge], top_s)
     for side, at in ((LOW, 0), (HIGH, cols - 8)):
         for tag in range(tags):
             copy(lam.at[tag, :, pl.ds(at, 8)], lam_s.at[side, tag])
-    for c in copies[:12]:
+    for c in copies[:6]:
         c.wait()
     pitch = 9
     few = per * pitch
 
-    @pl.loop(0, per)
-    def _(i):
-        level = base + i
-        for side in (LOW, HIGH):
-            ew, ed, nw, nd, mf = (field_s[f, side, i] for f in range(5))
-            lift = jnp.where((level < top_s[side]) & (level < levels - 1), mf, 0.0)
+    @pl.loop(0, per // 2)
+    def _(pair):
+        for half in range(2):
+            i = pair * 2 + half
+            level = base + i
+            ew, ed, nw, nd, mf = (field_s[f, i] for f in range(5))
+            lift = jnp.where((level < top_s[...]) & (level < levels - 1), mf, 0.0)
             for j, value in enumerate((*faces(ew, ed, nw, nd), lift)):
                 for k in range(2):
-                    at = ((j * 2 + side) * 2 + k) * few + i * pitch
+                    at = (j * 2 + k) * few + i * pitch
                     coef_p[pl.ds(at, 8), :] = value[:, HALVES[k]]
 
+    def coef_column(j, c):
+        return column_at(coef_p, j * 2 * few + c, per, pitch, few)
+
+    start = 8 - EDGE
+    c = high * (start + 1)
+    coef_send[0] = coef_column(1, jnp.maximum(c - 1, 0))
+    for i in range(EDGE - 1):
+        for n, j in enumerate((0, 2, 3, 4, 1)):
+            coef_send[5 * i + 1 + n] = coef_column(j, c + i)
+
     odd = parity()
-    start = 8 - EDGE
-    for dest, side in ((coef_first, 1 - odd), (coef_second, odd)):
-
-        def column(j, c):
-            return column_at(coef_p, (j * 2 + side) * 2 * few + c, per, pitch, few)
-
-        c = side * (start + 1)
-        dest[0] = column(1, jnp.maximum(c - 1, 0))
-        for i in range(EDGE - 1):
-            for n, j in enumerate((0, 2, 3, 4, 1)):
-                dest[5 * i + 1 + n] = column(j, c + i)
-
-    for c in copies[12:]:
+    for c in copies[6:]:
         c.wait()
     slab = levels * pitch
 
@@ -140,24 +150,24 @@
                 )
 
 
-def pack(parts, lam, fields, top):
+def pack(lam, fields, top):
     tags, levels, cols, lats = lam.shape
-    per = levels // parts
+    per = levels // 2
     hbm = pl.BlockSpec(memory_space=pltpu.HBM)
     coef_send = pltpu.VMEM((ENTRIES, per, lats), jnp.float32)
     lam_send = pltpu.VMEM((tags * EDGE, levels, lats), jnp.float32)
     return pl.pallas_call(
-        functools.partial(pack_kernel, parts),
+        pack_kernel,
         in_specs=[hbm] * 7,
-        out_specs=[pl.BlockSpec(memory_space=pltpu.VMEM)] * 4,
-        out_shape=[coef_send, coef_send, lam_send, lam_send],
+        out_specs=[pl.BlockSpec(memory_space=pltpu.VMEM)] * 3,
+        out_shape=[coef_send, lam_send, lam_send],
         scratch_shapes=[
-            pltpu.VMEM((5, 2, per, 8, lats), jnp.float32),
-            pltpu.VMEM((2, 8, lats), jnp.int32),
+            pltpu.VMEM((5, per, 8, lats), jnp.float32),
+            pltpu.VMEM((8, lats), jnp.int32),
             pltpu.VMEM((2, tags, levels, 8, lats), jnp.float32),
-            pltpu.VMEM((pitched(20, per, 8), LANES), jnp.float32),
+            pltpu.VMEM((pitched(10, per, 8), LANES), jnp.float32),
             pltpu.VMEM((pitched(4 * tags, levels, 8), LANES), jnp.float32),
-            pltpu.SemaphoreType.DMA((12 + 2 * tags,)),
+            pltpu.SemaphoreType.DMA((6 + 2 * tags,)),
         ],
         compiler_params=pltpu.CompilerParams(vmem_limit_bytes=24 << 20),
         cost_estimate=SHORT,
@@ -290,26 +300,16 @@
     return (LOW, c + EDGE - 1) if c < EDGE else (HIGH, c - (cols - EDGE))
 
 
-def outer_kernel(parts, cols, coef, *refs):
-    pieces, wide, entry = refs[:parts], refs[parts], refs[parts + 1]
-    levels = coef.shape[2]
-    per = levels // parts
-    mine = lax.rem(lax.axis_index("grp"), parts)
-    odd = parity()
-    for by in range(parts):
-        for half, side in enumerate((1 - odd, odd)):
-
-            @pl.loop(0, ENTRIES // 4)
-            def _(i):
-                for j in range(4):
-                    e = i * 4 + j
-                    for k in range(2):
-                        at = ((side * ENTRIES + e) * 2 + k) * levels + (mine ^ by) * per
-                        entry[pl.ds(at, per), :] = pieces[by][half, e, :, HALVES[k]]
+def outer_kernel(cols, coef, *refs):
+    pieces, wide, entry = refs[:BLOCK], refs[BLOCK], refs[BLOCK + 1]
+    per = coef.shape[2] // 2
+    for by in range(BLOCK):
+        rank = lax.axis_index("grp") ^ by
+        rows = pl.ds(pl.multiple_of(coef_half(rank) * per, 8), per)
+        entry[coef_side(rank), :, rows] = pieces[by][...]
 
     def slab(side, e):
-        at = (side * ENTRIES + e) * 2 * levels
-        return jnp.concatenate([entry[at + k * levels : at + (k + 1) * levels] for k in (0, 1)], 1)
+        return entry[side, e]
 
     for side in (LOW, HIGH):
         for i in range(EDGE - 1):
@@ -324,15 +324,15 @@
         wide[*slot(0, cols), j] = value
 
 
-def outer_coefs(parts, cols, coef, pieces):
+def outer_coefs(cols, coef, pieces):
     _, _, levels, lats = coef.shape
     vmem = pl.BlockSpec(memory_space=pltpu.VMEM)
     return pl.pallas_call(
-        functools.partial(outer_kernel, parts, cols),
-        in_specs=[vmem] * (1 + parts),
+        functools.partial(outer_kernel, cols),
+        in_specs=[vmem] * (1 + BLOCK),
         out_specs=vmem,
         out_shape=pltpu.VMEM((2, 2 * EDGE - 1, 6, levels, lats), jnp.float32),
-        scratch_shapes=[pltpu.VMEM((2 * ENTRIES * 2 * levels, LANES), jnp.float32)],
+        scratch_shapes=[pltpu.VMEM((2, ENTRIES, levels, lats), jnp.float32)],
         compiler_params=pltpu.CompilerParams(vmem_limit_bytes=24 << 20),
         cost_estimate=SHORT,
         name="outer_coefs",
@@ -527,22 +527,25 @@
 
 def local(lam, east_wind, north_wind, east_diff, north_diff, mass_flux, region, top):
     groups, tiles = lax.axis_size("grp"), lax.axis_size("dom")
-    parts = 4 if groups % 4 == 0 else 1
     own = (lam, east_wind, east_diff, north_wind, north_diff, mass_flux)
     far = [pltpu.with_memory_space_constraint(value, pltpu.HBM) for value in (*own, top)]
 
     pairs = lambda i: i ^ 1
     turn = lambda i: (((i - 1) % tiles ^ 1) + 1) % tiles
-    coef_first, coef_second, first, second = pack(parts, far[0], far[1:6], far[6])
-    coef_first = swapped(coef_first, "dom", pairs)
-    coef_second = swapped(coef_second, "dom", turn)
+    coefs, first, second = pack(far[0], far[1:6], far[6])
+
+    def partner(i):
+        tile, rank = divmod(i, groups)
+        return (turn if rank % 2 else pairs)(tile) * groups + rank
+
+    coefs = swapped(coefs, ("dom", "grp"), partner)
     first = swapped(first, "dom", pairs)
     second = swapped(second, "dom", turn)
-    pieces = [jnp.stack([coef_first, coef_second])]
-    for by in range(1, parts):
-        pieces.append(swapped(pieces[0], "grp", lambda i: i ^ by))
+    pieces = [coefs]
+    for by in range(1, BLOCK):
+        pieces.append(swapped(coefs, "grp", lambda i: i ^ by))
     coef, *states, final, rows = inner(own[0], own[1:], top, region)
-    wide = outer_coefs(parts, lam.shape[2], coef, pieces)
+    wide = outer_coefs(lam.shape[2], coef, pieces)
     out = write_inner(final, lam.shape)
     wide, out = lax.optimization_barrier((wide, out))
     grad = gradient(region, coef, wide, states, (first, second), rows)

time: 28.9 us -> 32.3 us (1.12)
  the two profiles are of different devices: /device:TPU:0 before, /device:TPU:26 now
where the time goes in v16:
time: 32.3 us; the launch traced here: 32.1 us
  waiting for transfers between devices  12.2 us (38%)
  Pallas kernels  11.8 us (37%)
  starting transfers between devices  5.88 us (18%)
  between operations  0.82 us (3%)
  local copies, waits for them, and re-layouts  0.78 us (2%)
  other arithmetic  0.63 us (2%)
    ppermute x9, waiting for transfers between devices, swapped(): lax.ppermute(value, axis, [(i, partner(i)) for i in range(lax.axis_size(a...  12.2 us
    ppermute x9, starting transfers between devices, swapped(): lax.ppermute(value, axis, [(i, partner(i)) for i in range(lax.axis_size(a...  5.88 us
    pallas_call x1, Pallas kernels, inner(): pl.pallas_call(inner_kernel, in_specs=[vmem] * 8, out_specs=[vmem] * 7, o...  5.64 us
    pallas_call x1, Pallas kernels, border(): pl.pallas_call(border_kernel, in_specs=[vmem] * (n + 1) + [hbm], out_spec...  2.38 us
    pallas_call x1, Pallas kernels, pack(): pl.pallas_call(pack_kernel, in_specs=[hbm] * 7, out_specs=[pl.BlockSpec(m...  1.82 us
    pallas_call x1, Pallas kernels, write_inner(): pl.pallas_call(write_kernel, in_specs=[pl.BlockSpec(memory_space=pltpu.VM...  1.14 us
    unnamed x16, local copies, waits for them, and re-layouts  0.78 us
    pallas_call x1, Pallas kernels, gradient(): pl.pallas_call(low_kernel, in_specs=[vmem] * len(operands), out_specs=vme...  0.75 us
  transfers between devices with their start and end apart: 9, of which 2 were waited for; matrix products, arithmetic and copies ran while one was open for 0% of the time, Pallas kernels for 29%

profile of v16, /device:TPU:26, one launch (start us, length us, event | category | flops | bytes accessed | tf_op | source)
XLA Modules:
  0.0 32.1 jit_solution(18402796667716331974)
XLA Ops:
  0.7 1.8 %pack_edges.1 = (f32[16,8,256]{2,1,0:T(8,128)S(1)}, f32[16,16,256]{2,1,0:T(8,128)S(1)}, f32[16,16,256]{2,1,0:T(8,128)S(1)}) custom-call(f32[4,16,32,256]{3,2,1,0:T(8,128)} %lam.3, f32[16,32,256]{2,1,0:T(8,128)} %ew.3, f32[16,32,256]{2,1,0:T(8,128)} %ed.3, f32[16,32,256]{2,1,0:T(8,128)} %nw.3, f32[16,32,256]{2,1,0:T(8,128)} %nd.3, f32[16,32,256]{2,1,0:T(8,128)} %mf.3, ...), custom_call_target="tpu_custom_call" | custom-call | flops 1000 | bytes 1000 | tf_op jit(solution)/shard_map/pack_edges/pallas_call | solution.py:159
  2.5 0.6 %collective-permute-start = (f32[16,8,256]{2,1,0:T(8,128)S(1)}, f32[16,8,256]{2,1,0:T(8,128)S(1)}, u32[]{:S(2)}, u32[]{:S(2)}) collective-permute-start(f32[16,8,256]{2,1,0:T(8,128)S(1)} %get-tuple-element.18), channel_id=1, source_target_pairs={{0,4},{1,29},{2,6},{3,31},{4,0},{5,9},{6,2},{7,11},{8,12},{9,5},{1... | collective-permute-start | bytes 393224 | tf_op jit(solution)/shard_map/ppermute | solution.py:21
  3.1 1.5 %collective-permute-start.4 = (f32[16,16,256]{2,1,0:T(8,128)S(1)}, f32[16,16,256]{2,1,0:T(8,128)S(1)}, u32[]{:S(2)}, u32[]{:S(2)}) collective-permute-start(f32[16,16,256]{2,1,0:T(8,128)S(1)} %get-tuple-element.25), channel_id=1, source_target_pairs={{0,4},{4,0},{8,12},{12,8},{16,20},{20,16},{24,28},{28,24},{1,5},{5... | collective-permute-start | bytes 786440 | tf_op jit(solution)/shard_map/ppermute | solution.py:21
  4.6 0.0 collective-permute-start.5
  4.6 11.4 %collective-permute-done.refs_0_ = f32[16,8,256]{2,1,0:T(8,128)S(1)} collective-permute-done((f32[16,8,256]{2,1,0:T(8,128)S(1)}, f32[16,8,256]{2,1,0:T(8,128)S(1)}, u32[]{:S(2)}, u32[]{:S(2)}) %collective-permute-start) | collective-permute-done | bytes 131104 | tf_op jit(solution)/shard_map/ppermute | solution.py:21
  16.0 0.0 collective-permute-start.3
  16.0 1.6 %collective-permute-start.2 = (f32[16,8,256]{2,1,0:T(8,128)S(1)}, f32[16,8,256]{2,1,0:T(8,128)S(1)}, u32[]{:S(2)}, u32[]{:S(2)}) collective-permute-start(f32[16,8,256]{2,1,0:T(8,128)S(1)} %collective-permute-done.refs_0_), channel_id=1, source_target_pairs={{0,2},{1,3},{2,0},{3,1},{4,6},{5,7},{6,4},{7,5},{8,10},{9,11},{10,... | collective-permute-start | bytes 393224 | tf_op jit(solution)/shard_map/ppermute | solution.py:21
  17.5 0.3 collective-permute-start.1
  17.9 0.0 copy-start.7
  17.9 0.7 %copy-done.7 = s32[32,256]{1,0:T(8,128)S(1)} copy-done((s32[32,256]{1,0:T(8,128)S(1)}, s32[32,256]{1,0:T(8,128)}, u32[]{:S(2)}) %copy-start.7) | copy-done | bytes 32792
  18.7 5.6 %inner_steps.1 = (f32[33,6,16,256]{3,2,1,0:T(8,128)S(1)}, f32[4,4,16,256]{3,2,1,0:T(8,128)S(1)}, f32[32,4,16,256]{3,2,1,0:T(8,128)S(1)}, f32[32,4,16,256]{3,2,1,...) custom-call(f32[4,16,32,256]{3,2,1,0:T(8,128)S(1)} %copy-done, ...), custom_call_target="tpu_custom_call" | custom-call | flops 1000 | bytes 1000 | tf_op jit(solution)/shard_map/inner_steps/pallas_call | solution.py:278
  24.3 1.1 %write_inner.1.refs_1_ = f32[4,16,32,256]{3,2,1,0:T(8,128)} custom-call(f32[4264,128]{1,0:T(8,128)S(1)} %get-tuple-element.19.final.refs_0_), custom_call_target="tpu_custom_call" | custom-call | flops 1000 | bytes 1000 | tf_op jit(solution)/shard_map/write_inner/pallas_call | solution.py:513
  25.5 0.0 collective-permute-done.3.refs_3_
  25.5 0.0 collective-permute-done.2.refs_2_
  25.5 0.0 collective-permute-done.1.refs_1_
  25.5 0.1 outer_coefs.1.wide
  25.6 0.7 %border_low_levels.1 = f32[32,256]{1,0:T(8,128)S(1)} custom-call(s32[32,256]{1,0:T(8,128)S(1)} %copy-done.7, f32[33,6,16,256]{3,2,1,0:T(8,128)S(1)} %get-tuple-element.17.coef, f32[2,7,6,16,256]{4,3,2,1,0:T(8,128)S(1)} %outer_coefs.1.wide, f32[4,4,16,256]{3,2,1,0:T(8,128)S(1)} %get-tuple-element.21.l0, f32[32,4,16,256]{3,2,1,0:T(8,128)S(1)} %get-tuple-element.22.l1, ...), custom_call_target="tpu_custom_call" | custom-call | flops 1000 | bytes 1000 | tf_op jit(solution)/shard_map/border_low_levels/pallas_call | solution.py:415
  26.4 1.2 %collective-permute-start.8 = (f32[32,256]{1,0:T(8,128)S(1)}, f32[32,256]{1,0:T(8,128)S(1)}, u32[]{:S(2)}, u32[]{:S(2)}) collective-permute-start(f32[32,256]{1,0:T(8,128)S(1)} %border_low_levels.1), channel_id=1, source_target_pairs={{0,3},{1,2},{2,1},{3,0},{4,7},{5,6},{6,5},{7,4},{8,11},{9,10},{10,... | collective-permute-start | bytes 98312 | tf_op jit(solution)/shard_map/ppermute | solution.py:21
  27.6 0.7 %collective-permute-start.7 = (f32[32,256]{1,0:T(8,128)S(1)}, f32[32,256]{1,0:T(8,128)S(1)}, u32[]{:S(2)}, u32[]{:S(2)}) collective-permute-start(f32[32,256]{1,0:T(8,128)S(1)} %border_low_levels.1), channel_id=1, source_target_pairs={{0,2},{1,3},{2,0},{3,1},{4,6},{5,7},{6,4},{7,5},{8,10},{9,11},{10,... | collective-permute-start | bytes 98312 | tf_op jit(solution)/shard_map/ppermute | solution.py:21
  28.3 0.0 collective-permute-start.6
  28.3 2.4 %border_all_levels.1 = (f32[4264,128]{1,0:T(8,128)S(1)}, f32[4,16,32,256]{3,2,1,0:T(8,128)}) custom-call(f32[33,6,16,256]{3,2,1,0:T(8,128)S(1)} %get-tuple-element.17.coef, f32[2,7,6,16,256]{4,3,2,1,0:T(8,128)S(1)} %outer_coefs.1.wide, f32[4,4,16,256]{3,2,1,0:T(8,128)S(1)} %get-tuple-element.21.l0, ...), custom_call_target="tpu_custom_call", output_to_operand_aliasing={{0}: (8, {}), {1}: (9, {})} | custom-call | flops 1000 | bytes 1000 | tf_op jit(solution)/shard_map/border_all_levels/pallas_call | solution.py:469
  30.7 0.8 %collective-permute-done.7 = f32[32,256]{1,0:T(8,128)S(1)} collective-permute-done((f32[32,256]{1,0:T(8,128)S(1)}, f32[32,256]{1,0:T(8,128)S(1)}, u32[]{:S(2)}, u32[]{:S(2)}) %collective-permute-start.7) | collective-permute-done | bytes 32800 | tf_op jit(solution)/shard_map/ppermute | solution.py:21
  31.5 0.0 collective-permute-done.6
  31.5 0.6 %add_add_fusion = f32[32,256]{1,0:T(8,128)} fusion(f32[32,256]{1,0:T(8,128)S(1)} %collective-permute-done.8, f32[32,256]{1,0:T(8,128)S(1)} %collective-permute-done.7, f32[32,256]{1,0:T(8,128)S(1)} %border_low_levels.1, f32[32,256]{1,0:T(8,128)S(1)} %collective-permute-done.6), kind=kLoop, calls=%fused_computation | loop fusion | flops 24576 | bytes 163840 | tf_op jit(solution)/shard_map/add | solution.py:556
  (17 shorter events, 0.0 us)
Async XLA Ops:
  0.6 17.2 %copy-start.6 = (s32[32,256]{1,0:T(8,128)S(1)}, s32[32,256]{1,0:T(8,128)}, u32[]{:S(2)}) copy-start(s32[32,256]{1,0:T(8,128)} %top.3) | copy-start | bytes 98308
  0.6 17.2 %copy-start.5 = (f32[16,32,256]{2,1,0:T(8,128)S(1)}, f32[16,32,256]{2,1,0:T(8,128)}, u32[]{:S(2)}) copy-start(f32[16,32,256]{2,1,0:T(8,128)} %mf.3) | copy-start | bytes 1572868
  0.7 17.2 %copy-start.4 = (f32[16,32,256]{2,1,0:T(8,128)S(1)}, f32[16,32,256]{2,1,0:T(8,128)}, u32[]{:S(2)}) copy-start(f32[16,32,256]{2,1,0:T(8,128)} %nd.3) | copy-start | bytes 1572868
  0.7 17.2 %copy-start.2 = (f32[16,32,256]{2,1,0:T(8,128)S(1)}, f32[16,32,256]{2,1,0:T(8,128)}, u32[]{:S(2)}) copy-start(f32[16,32,256]{2,1,0:T(8,128)} %ed.3) | copy-start | bytes 1572868
  0.7 17.2 %copy-start.3 = (f32[16,32,256]{2,1,0:T(8,128)S(1)}, f32[16,32,256]{2,1,0:T(8,128)}, u32[]{:S(2)}) copy-start(f32[16,32,256]{2,1,0:T(8,128)} %nw.3) | copy-start | bytes 1572868
  0.7 17.2 %copy-start.1 = (f32[16,32,256]{2,1,0:T(8,128)S(1)}, f32[16,32,256]{2,1,0:T(8,128)}, u32[]{:S(2)}) copy-start(f32[16,32,256]{2,1,0:T(8,128)} %ew.3) | copy-start | bytes 1572868
  0.7 17.2 %copy-start = (f32[4,16,32,256]{3,2,1,0:T(8,128)S(1)}, f32[4,16,32,256]{3,2,1,0:T(8,128)}, u32[]{:S(2)}) copy-start(f32[4,16,32,256]{3,2,1,0:T(8,128)} %lam.3) | copy-start | bytes 6291460
  2.5 13.5 %collective-permute-start = (f32[16,8,256]{2,1,0:T(8,128)S(1)}, f32[16,8,256]{2,1,0:T(8,128)S(1)}, u32[]{:S(2)}, u32[]{:S(2)}) collective-permute-start(f32[16,8,256]{2,1,0:T(8,128)S(1)} %get-tuple-element.18), channel_id=1, source_target_pairs={{0,4},{1,29},{2,6},{3,31},{4,0},{5,9},{6,2},{7,11},{8,12},{9,5},{1... | collective-permute-start | bytes 393224 | tf_op jit(solution)/shard_map/ppermute | solution.py:21
  3.1 22.5 %collective-permute-start.4 = (f32[16,16,256]{2,1,0:T(8,128)S(1)}, f32[16,16,256]{2,1,0:T(8,128)S(1)}, u32[]{:S(2)}, u32[]{:S(2)}) collective-permute-start(f32[16,16,256]{2,1,0:T(8,128)S(1)} %get-tuple-element.25), channel_id=1, source_target_pairs={{0,4},{4,0},{8,12},{12,8},{16,20},{20,16},{24,28},{28,24},{1,5},{5... | collective-permute-start | bytes 786440 | tf_op jit(solution)/shard_map/ppermute | solution.py:21
  4.6 21.0 %collective-permute-start.5 = (f32[16,16,256]{2,1,0:T(8,128)S(1)}, f32[16,16,256]{2,1,0:T(8,128)S(1)}, u32[]{:S(2)}, u32[]{:S(2)}) collective-permute-start(f32[16,16,256]{2,1,0:T(8,128)S(1)} %get-tuple-element.26), channel_id=1, source_target_pairs={{0,28},{4,8},{8,4},{12,16},{16,12},{20,24},{24,20},{28,0},{1,29},{... | collective-permute-start | bytes 786440 | tf_op jit(solution)/shard_map/ppermute | solution.py:21
  16.0 9.5 %collective-permute-start.3 = (f32[16,8,256]{2,1,0:T(8,128)S(1)}, f32[16,8,256]{2,1,0:T(8,128)S(1)}, u32[]{:S(2)}, u32[]{:S(2)}) collective-permute-start(f32[16,8,256]{2,1,0:T(8,128)S(1)} %collective-permute-done.refs_0_), channel_id=1, source_target_pairs={{0,3},{1,2},{2,1},{3,0},{4,7},{5,6},{6,5},{7,4},{8,11},{9,10},{10,... | collective-permute-start | bytes 393224 | tf_op jit(solution)/shard_map/ppermute | solution.py:21
  16.0 9.5 %collective-permute-start.2 = (f32[16,8,256]{2,1,0:T(8,128)S(1)}, f32[16,8,256]{2,1,0:T(8,128)S(1)}, u32[]{:S(2)}, u32[]{:S(2)}) collective-permute-start(f32[16,8,256]{2,1,0:T(8,128)S(1)} %collective-permute-done.refs_0_), channel_id=1, source_target_pairs={{0,2},{1,3},{2,0},{3,1},{4,6},{5,7},{6,4},{7,5},{8,10},{9,11},{10,... | collective-permute-start | bytes 393224 | tf_op jit(solution)/shard_map/ppermute | solution.py:21
  17.5 7.9 %collective-permute-start.1 = (f32[16,8,256]{2,1,0:T(8,128)S(1)}, f32[16,8,256]{2,1,0:T(8,128)S(1)}, u32[]{:S(2)}, u32[]{:S(2)}) collective-permute-start(f32[16,8,256]{2,1,0:T(8,128)S(1)} %collective-permute-done.refs_0_), channel_id=1, source_target_pairs={{0,1},{1,0},{2,3},{3,2},{4,5},{5,4},{6,7},{7,6},{8,9},{9,8},{10,11... | collective-permute-start | bytes 393224 | tf_op jit(solution)/shard_map/ppermute | solution.py:21
  17.9 0.8 %copy-start.7 = (s32[32,256]{1,0:T(8,128)S(1)}, s32[32,256]{1,0:T(8,128)}, u32[]{:S(2)}) copy-start(s32[32,256]{1,0:T(8,128)} %region.3) | copy-start | bytes 98308
  26.4 4.3 %collective-permute-start.8 = (f32[32,256]{1,0:T(8,128)S(1)}, f32[32,256]{1,0:T(8,128)S(1)}, u32[]{:S(2)}, u32[]{:S(2)}) collective-permute-start(f32[32,256]{1,0:T(8,128)S(1)} %border_low_levels.1), channel_id=1, source_target_pairs={{0,3},{1,2},{2,1},{3,0},{4,7},{5,6},{6,5},{7,4},{8,11},{9,10},{10,... | collective-permute-start | bytes 98312 | tf_op jit(solution)/shard_map/ppermute | solution.py:21
  27.6 3.9 %collective-permute-start.7 = (f32[32,256]{1,0:T(8,128)S(1)}, f32[32,256]{1,0:T(8,128)S(1)}, u32[]{:S(2)}, u32[]{:S(2)}) collective-permute-start(f32[32,256]{1,0:T(8,128)S(1)} %border_low_levels.1), channel_id=1, source_target_pairs={{0,2},{1,3},{2,0},{3,1},{4,6},{5,7},{6,4},{7,5},{8,10},{9,11},{10,... | collective-permute-start | bytes 98312 | tf_op jit(solution)/shard_map/ppermute | solution.py:21
  28.3 3.2 %collective-permute-start.6 = (f32[32,256]{1,0:T(8,128)S(1)}, f32[32,256]{1,0:T(8,128)S(1)}, u32[]{:S(2)}, u32[]{:S(2)}) collective-permute-start(f32[32,256]{1,0:T(8,128)S(1)} %border_low_levels.1), channel_id=1, source_target_pairs={{0,1},{1,0},{2,3},{3,2},{4,5},{5,4},{6,7},{7,6},{8,9},{9,8},{10,11... | collective-permute-start | bytes 98312 | tf_op jit(solution)/shard_map/ppermute | solution.py:21

commit v17 on v16

--- a/solution.py
+++ b/solution.py
@@ -223,8 +223,7 @@
     return store
 
 
-def inner_kernel(lam, ew, ed, nw, nd, mf, top, region, *refs):
-    coef, l0, l1, l2, l3, final, rows, lam_p, field_p = refs
+def prepare_kernel(lam, ew, ed, nw, nd, mf, top, coef, l0, lam_p, field_p):
     tags, levels, cols, lats = lam.shape
     pitch = cols + 1
     slab = levels * pitch
@@ -257,43 +256,63 @@
 
     west = lax.fori_loop(0, cols // 8, some, jnp.zeros((levels, lats), jnp.float32))
     coef[cols, 2] = west
+    for at, c in enumerate((0, 1, cols - 2, cols - 1)):
+        for tag in range(tags):
+            l0[at, tag] = column_at(lam_p, tag * slab + c, levels, pitch, tags * slab)
+
+
+def prepare(lam, fields, top):
+    tags, levels, cols, lats = lam.shape
+    vmem = pl.BlockSpec(memory_space=pltpu.VMEM)
+    return pl.pallas_call(
+        prepare_kernel,
+        in_specs=[vmem] * 7,
+        out_specs=[vmem] * 3,
+        out_shape=[
+            pltpu.VMEM((cols + 1, 6, levels, lats), jnp.float32),
+            pltpu.VMEM((4, tags, levels, lats), jnp.float32),
+            pltpu.VMEM((pitched(2 * tags, levels, cols), LANES), jnp.float32),
+        ],
+        scratch_shapes=[pltpu.VMEM((pitched(10, levels, cols), LANES), jnp.float32)],
+        compiler_params=pltpu.CompilerParams(vmem_limit_bytes=32 << 20),
+        cost_estimate=SHORT,
+        name="prepare",
+    )(lam, *fields, top)
+
+
+def inner_kernel(coef, lam_p, region, l1, l2, l3, final, rows):
+    cols, tags, levels, lats = l1.shape
+    pitch = cols + 1
+    slab = levels * pitch
 
     def given(c, tag):
         return column_at(lam_p, tag * slab + c, levels, pitch, tags * slab)
 
-    for at, c in enumerate((0, 1, cols - 2, cols - 1)):
-        for tag in range(tags):
-            l0[at, tag] = given(c, tag)
     last = storing_rows(final, tags, levels, pitch)
     loads = (given, loading(l1), loading(l2), loading(l3))
     stores = (storing(l1), storing(l2), storing(l3), last)
+    shape = (tags, levels, cols, lats)
     for t in range(ITERS):
-        sweep(t, lam.shape, lax.axis_index("grp") * tags, region, coef, loads[t], stores[t], rows)
-
-
-def inner(lam, fields, top, region):
-    tags, levels, cols, lats = lam.shape
+        sweep(t, shape, lax.axis_index("grp") * tags, region, coef, loads[t], stores[t], rows)
+
+
+def inner(shape, coef, lam_p, region):
+    tags, levels, cols, lats = shape
     vmem = pl.BlockSpec(memory_space=pltpu.VMEM)
     state = pltpu.VMEM((cols, tags, levels, lats), jnp.float32)
     return pl.pallas_call(
         inner_kernel,
-        in_specs=[vmem] * 8,
-        out_specs=[vmem] * 7,
+        in_specs=[vmem] * 3,
+        out_specs=[vmem] * 5,
         out_shape=[
-            pltpu.VMEM((cols + 1, 6, levels, lats), jnp.float32),
-            pltpu.VMEM((4, tags, levels, lats), jnp.float32),
             *[state] * 3,
-            pltpu.VMEM((pitched(2 * tags, levels, cols), LANES), jnp.float32),
+            pltpu.VMEM(lam_p.shape, jnp.float32),
             pltpu.VMEM((ITERS, cols, lats), jnp.float32),
         ],
-        scratch_shapes=[
-            pltpu.VMEM((pitched(2 * tags, levels, cols), LANES), jnp.float32),
-            pltpu.VMEM((pitched(10, levels, cols), LANES), jnp.float32),
-        ],
         compiler_params=pltpu.CompilerParams(vmem_limit_bytes=32 << 20),
         cost_estimate=SHORT,
         name="inner_steps",
-    )(lam, *fields, top, region)
+    )(coef, lam_p, region)
 
 
 def slot(c, cols):
@@ -539,12 +558,15 @@
         return (turn if rank % 2 else pairs)(tile) * groups + rank
 
     coefs = swapped(coefs, ("dom", "grp"), partner)
+    coef, l0, lam_p = prepare(own[0], own[1:], top)
+    first, second, coef = lax.optimization_barrier((first, second, coef))
     first = swapped(first, "dom", pairs)
     second = swapped(second, "dom", turn)
     pieces = [coefs]
     for by in range(1, BLOCK):
         pieces.append(swapped(coefs, "grp", lambda i: i ^ by))
-    coef, *states, final, rows = inner(own[0], own[1:], top, region)
+    *states, final, rows = inner(lam.shape, coef, lam_p, region)
+    states = [l0, *states]
     wide = outer_coefs(lam.shape[2], coef, pieces)
     out = write_inner(final, lam.shape)
     wide, out = lax.optimization_barrier((wide, out))

time: 32.3 us -> 30.7 us (0.950)
  the two profiles are of different devices: /device:TPU:26 before, /device:TPU:17 now
where the time goes in v17:
time: 30.7 us; the launch traced here: 30.6 us
  starting transfers between devices  15.3 us (50%)
  Pallas kernels  11.8 us (38%)
  waiting for transfers between devices  1.96 us (6%)
  between operations  0.82 us (3%)
  other arithmetic  0.63 us (2%)
    ppermute x9, starting transfers between devices, swapped(): lax.ppermute(value, axis, [(i, partner(i)) for i in range(lax.axis_size(a...  15.3 us
    pallas_call x1, Pallas kernels, inner(): pl.pallas_call(inner_kernel, in_specs=[vmem] * 3, out_specs=[vmem] * 5, o...  4.85 us
    pallas_call x1, Pallas kernels, border(): pl.pallas_call(border_kernel, in_specs=[vmem] * (n + 1) + [hbm], out_spec...  2.36 us
    ppermute x9, waiting for transfers between devices, swapped(): lax.ppermute(value, axis, [(i, partner(i)) for i in range(lax.axis_size(a...  1.96 us
    pallas_call x1, Pallas kernels, pack(): pl.pallas_call(pack_kernel, in_specs=[hbm] * 7, out_specs=[pl.BlockSpec(m...  1.82 us
    pallas_call x1, Pallas kernels, write_inner(): pl.pallas_call(write_kernel, in_specs=[pl.BlockSpec(memory_space=pltpu.VM...  1.14 us
    pallas_call x1, Pallas kernels, prepare(): pl.pallas_call(prepare_kernel, in_specs=[vmem] * 7, out_specs=[vmem] * 3,...  0.85 us
    pallas_call x1, Pallas kernels, gradient(): pl.pallas_call(low_kernel, in_specs=[vmem] * len(operands), out_specs=vme...  0.73 us
  transfers between devices with their start and end apart: 9, of which 2 were waited for; matrix products, arithmetic and copies ran while one was open for 0% of the time, Pallas kernels for 30%

profile of v17, /device:TPU:17, one launch (start us, length us, event | category | flops | bytes accessed | tf_op | source)
XLA Modules:
  0.0 30.6 jit_solution(18189345801262249663)
XLA Ops:
  0.7 1.8 %pack_edges.1 = (f32[16,8,256]{2,1,0:T(8,128)S(1)}, f32[16,16,256]{2,1,0:T(8,128)S(1)}, f32[16,16,256]{2,1,0:T(8,128)S(1)}) custom-call(f32[4,16,32,256]{3,2,1,0:T(8,128)} %lam.3, f32[16,32,256]{2,1,0:T(8,128)} %ew.3, f32[16,32,256]{2,1,0:T(8,128)} %ed.3, f32[16,32,256]{2,1,0:T(8,128)} %nw.3, f32[16,32,256]{2,1,0:T(8,128)} %nd.3, f32[16,32,256]{2,1,0:T(8,128)} %mf.3, ...), custom_call_target="tpu_custom_call" | custom-call | flops 1000 | bytes 1000 | tf_op jit(solution)/shard_map/pack_edges/pallas_call | solution.py:159
  2.5 0.0 copy-start.7
  2.5 1.2 %collective-permute-start = (f32[16,8,256]{2,1,0:T(8,128)S(1)}, f32[16,8,256]{2,1,0:T(8,128)S(1)}, u32[]{:S(2)}, u32[]{:S(2)}) collective-permute-start(f32[16,8,256]{2,1,0:T(8,128)S(1)} %get-tuple-element.25), channel_id=1, source_target_pairs={{0,4},{1,29},{2,6},{3,31},{4,0},{5,9},{6,2},{7,11},{8,12},{9,5},{1... | collective-permute-start | bytes 393224 | tf_op jit(solution)/shard_map/ppermute | solution.py:21
  3.8 0.9 %prepare.1 = (f32[33,6,16,256]{3,2,1,0:T(8,128)S(1)}, f32[4,4,16,256]{3,2,1,0:T(8,128)S(1)}, f32[4264,128]{1,0:T(8,128)S(1)}) custom-call(f32[4,16,32,256]{3,2,1,0:T(8,128)S(1)} %copy-done, f32[16,32,256]{2,1,0:T(8,128)S(1)} %copy-done.1, f32[16,32,256]{2,1,0:T(8,128)S(1)} %copy-done.2, f32[16,32,256]{2,1,0:T(8,128)S(1)} %copy-done.3, ...), custom_call_target="tpu_custom_call" | custom-call | flops 1000 | bytes 1000 | tf_op jit(solution)/shard_map/prepare/pallas_call | solution.py:267
  4.6 1.4 %collective-permute-start.4 = (f32[16,16,256]{2,1,0:T(8,128)S(1)}, f32[16,16,256]{2,1,0:T(8,128)S(1)}, u32[]{:S(2)}, u32[]{:S(2)}) collective-permute-start(f32[16,16,256]{2,1,0:T(8,128)S(1)} %get-tuple-element.33), channel_id=1, source_target_pairs={{0,4},{4,0},{8,12},{12,8},{16,20},{20,16},{24,28},{28,24},{1,5},{5... | collective-permute-start | bytes 786440 | tf_op jit(solution)/shard_map/ppermute | solution.py:21
  6.1 0.0 collective-permute-start.5
  6.1 1.4 %collective-permute-done.refs_0_ = f32[16,8,256]{2,1,0:T(8,128)S(1)} collective-permute-done((f32[16,8,256]{2,1,0:T(8,128)S(1)}, f32[16,8,256]{2,1,0:T(8,128)S(1)}, u32[]{:S(2)}, u32[]{:S(2)}) %collective-permute-start) | collective-permute-done | bytes 131104 | tf_op jit(solution)/shard_map/ppermute | solution.py:21
  7.4 10.0 %collective-permute-start.3 = (f32[16,8,256]{2,1,0:T(8,128)S(1)}, f32[16,8,256]{2,1,0:T(8,128)S(1)}, u32[]{:S(2)}, u32[]{:S(2)}) collective-permute-start(f32[16,8,256]{2,1,0:T(8,128)S(1)} %collective-permute-done.refs_0_), channel_id=1, source_target_pairs={{0,3},{1,2},{2,1},{3,0},{4,7},{5,6},{6,5},{7,4},{8,11},{9,10},{10,... | collective-permute-start | bytes 393224 | tf_op jit(solution)/shard_map/ppermute | solution.py:21
  17.5 0.2 collective-permute-start.2
  17.7 0.2 collective-permute-start.1
  17.9 4.9 %inner_steps.1 = (f32[32,4,16,256]{3,2,1,0:T(8,128)S(1)}, f32[32,4,16,256]{3,2,1,0:T(8,128)S(1)}, f32[32,4,16,256]{3,2,1,0:T(8,128)S(1)}, f32[4264,128]{1,0:T(8,128)S(1)}, f32[4,32,256]{2,1,0:T(8,128)S(1)}) custom-call(f32[33,6,16,256]{3,2,1,0:T(8,128)S(1)} %get-tuple-element.24.coef, f32[4264,128]{1,0:T(8,128)S(1)} %get-tuple-element.26.lam_p, ...), custom_call_target="tpu_custom_call" | custom-call | flops 1000 | bytes 1000 | tf_op jit(solution)/shard_map/inner_steps/pallas_call | solution.py:303
  22.8 1.1 %write_inner.1.refs_1_ = f32[4,16,32,256]{3,2,1,0:T(8,128)} custom-call(f32[4264,128]{1,0:T(8,128)S(1)} %get-tuple-element.27.final.refs_0_), custom_call_target="tpu_custom_call" | custom-call | flops 1000 | bytes 1000 | tf_op jit(solution)/shard_map/write_inner/pallas_call | solution.py:532
  23.9 0.6 %collective-permute-done.2.refs_2_ = f32[16,8,256]{2,1,0:T(8,128)S(1)} collective-permute-done((f32[16,8,256]{2,1,0:T(8,128)S(1)}, f32[16,8,256]{2,1,0:T(8,128)S(1)}, u32[]{:S(2)}, u32[]{:S(2)}) %collective-permute-start.2) | collective-permute-done | bytes 131104 | tf_op jit(solution)/shard_map/ppermute | solution.py:21
  24.5 0.0 collective-permute-done.1.refs_1_
  24.5 0.1 outer_coefs.1.wide
  24.6 0.0 collective-permute-done.5.second
  24.6 0.7 %border_low_levels.1 = f32[32,256]{1,0:T(8,128)S(1)} custom-call(s32[32,256]{1,0:T(8,128)S(1)} %copy-done.7, f32[33,6,16,256]{3,2,1,0:T(8,128)S(1)} %get-tuple-element.24.coef, f32[2,7,6,16,256]{4,3,2,1,0:T(8,128)S(1)} %outer_coefs.1.wide, f32[4,4,16,256]{3,2,1,0:T(8,128)S(1)} %get-tuple-element.29.l0, f32[32,4,16,256]{3,2,1,0:T(8,128)S(1)} %get-tuple-element.30.l1, ...), custom_call_target="tpu_custom_call" | custom-call | flops 1000 | bytes 1000 | tf_op jit(solution)/shard_map/border_low_levels/pallas_call | solution.py:434
  25.3 1.0 %collective-permute-start.8 = (f32[32,256]{1,0:T(8,128)S(1)}, f32[32,256]{1,0:T(8,128)S(1)}, u32[]{:S(2)}, u32[]{:S(2)}) collective-permute-start(f32[32,256]{1,0:T(8,128)S(1)} %border_low_levels.1), channel_id=1, source_target_pairs={{0,3},{1,2},{2,1},{3,0},{4,7},{5,6},{6,5},{7,4},{8,11},{9,10},{10,... | collective-permute-start | bytes 98312 | tf_op jit(solution)/shard_map/ppermute | solution.py:21
  26.3 0.9 %collective-permute-start.7 = (f32[32,256]{1,0:T(8,128)S(1)}, f32[32,256]{1,0:T(8,128)S(1)}, u32[]{:S(2)}, u32[]{:S(2)}) collective-permute-start(f32[32,256]{1,0:T(8,128)S(1)} %border_low_levels.1), channel_id=1, source_target_pairs={{0,2},{1,3},{2,0},{3,1},{4,6},{5,7},{6,4},{7,5},{8,10},{9,11},{10,... | collective-permute-start | bytes 98312 | tf_op jit(solution)/shard_map/ppermute | solution.py:21
  27.2 0.3 %collective-permute-start.6 = (f32[32,256]{1,0:T(8,128)S(1)}, f32[32,256]{1,0:T(8,128)S(1)}, u32[]{:S(2)}, u32[]{:S(2)}) collective-permute-start(f32[32,256]{1,0:T(8,128)S(1)} %border_low_levels.1), channel_id=1, source_target_pairs={{0,1},{1,0},{2,3},{3,2},{4,5},{5,4},{6,7},{7,6},{8,9},{9,8},{10,11... | collective-permute-start | bytes 98312 | tf_op jit(solution)/shard_map/ppermute | solution.py:21
  27.6 2.4 %border_all_levels.1 = (f32[4264,128]{1,0:T(8,128)S(1)}, f32[4,16,32,256]{3,2,1,0:T(8,128)}) custom-call(f32[33,6,16,256]{3,2,1,0:T(8,128)S(1)} %get-tuple-element.24.coef, f32[2,7,6,16,256]{4,3,2,1,0:T(8,128)S(1)} %outer_coefs.1.wide, f32[4,4,16,256]{3,2,1,0:T(8,128)S(1)} %get-tuple-element.29.l0, ...), custom_call_target="tpu_custom_call", output_to_operand_aliasing={{0}: (8, {}), {1}: (9, {})} | custom-call | flops 1000 | bytes 1000 | tf_op jit(solution)/shard_map/border_all_levels/pallas_call | solution.py:488
  29.9 0.0 collective-permute-done.8
  29.9 0.0 collective-permute-done.7
  29.9 0.6 %add_add_fusion = f32[32,256]{1,0:T(8,128)} fusion(f32[32,256]{1,0:T(8,128)S(1)} %collective-permute-done.8, f32[32,256]{1,0:T(8,128)S(1)} %collective-permute-done.7, f32[32,256]{1,0:T(8,128)S(1)} %border_low_levels.1, f32[32,256]{1,0:T(8,128)S(1)} %collective-permute-done.6), kind=kLoop, calls=%fused_computation | loop fusion | flops 24576 | bytes 163840 | tf_op jit(solution)/shard_map/add | solution.py:578
  (18 shorter events, 0.0 us)
Async XLA Ops:
  0.6 3.1 %copy-start.6 = (s32[32,256]{1,0:T(8,128)S(1)}, s32[32,256]{1,0:T(8,128)}, u32[]{:S(2)}) copy-start(s32[32,256]{1,0:T(8,128)} %top.3) | copy-start | bytes 98308
  0.6 3.1 %copy-start.5 = (f32[16,32,256]{2,1,0:T(8,128)S(1)}, f32[16,32,256]{2,1,0:T(8,128)}, u32[]{:S(2)}) copy-start(f32[16,32,256]{2,1,0:T(8,128)} %mf.3) | copy-start | bytes 1572868
  0.7 3.1 %copy-start.4 = (f32[16,32,256]{2,1,0:T(8,128)S(1)}, f32[16,32,256]{2,1,0:T(8,128)}, u32[]{:S(2)}) copy-start(f32[16,32,256]{2,1,0:T(8,128)} %nd.3) | copy-start | bytes 1572868
  0.7 3.1 %copy-start.2 = (f32[16,32,256]{2,1,0:T(8,128)S(1)}, f32[16,32,256]{2,1,0:T(8,128)}, u32[]{:S(2)}) copy-start(f32[16,32,256]{2,1,0:T(8,128)} %ed.3) | copy-start | bytes 1572868
  0.7 3.1 %copy-start.3 = (f32[16,32,256]{2,1,0:T(8,128)S(1)}, f32[16,32,256]{2,1,0:T(8,128)}, u32[]{:S(2)}) copy-start(f32[16,32,256]{2,1,0:T(8,128)} %nw.3) | copy-start | bytes 1572868
  0.7 3.1 %copy-start.1 = (f32[16,32,256]{2,1,0:T(8,128)S(1)}, f32[16,32,256]{2,1,0:T(8,128)}, u32[]{:S(2)}) copy-start(f32[16,32,256]{2,1,0:T(8,128)} %ew.3) | copy-start | bytes 1572868
  0.7 3.1 %copy-start = (f32[4,16,32,256]{3,2,1,0:T(8,128)S(1)}, f32[4,16,32,256]{3,2,1,0:T(8,128)}, u32[]{:S(2)}) copy-start(f32[4,16,32,256]{3,2,1,0:T(8,128)} %lam.3) | copy-start | bytes 6291460
  2.5 15.4 %copy-start.7 = (s32[32,256]{1,0:T(8,128)S(1)}, s32[32,256]{1,0:T(8,128)}, u32[]{:S(2)}) copy-start(s32[32,256]{1,0:T(8,128)} %region.3) | copy-start | bytes 98308
  2.5 4.9 %collective-permute-start = (f32[16,8,256]{2,1,0:T(8,128)S(1)}, f32[16,8,256]{2,1,0:T(8,128)S(1)}, u32[]{:S(2)}, u32[]{:S(2)}) collective-permute-start(f32[16,8,256]{2,1,0:T(8,128)S(1)} %get-tuple-element.25), channel_id=1, source_target_pairs={{0,4},{1,29},{2,6},{3,31},{4,0},{5,9},{6,2},{7,11},{8,12},{9,5},{1... | collective-permute-start | bytes 393224 | tf_op jit(solution)/shard_map/ppermute | solution.py:21
  4.6 20.0 %collective-permute-start.4 = (f32[16,16,256]{2,1,0:T(8,128)S(1)}, f32[16,16,256]{2,1,0:T(8,128)S(1)}, u32[]{:S(2)}, u32[]{:S(2)}) collective-permute-start(f32[16,16,256]{2,1,0:T(8,128)S(1)} %get-tuple-element.33), channel_id=1, source_target_pairs={{0,4},{4,0},{8,12},{12,8},{16,20},{20,16},{24,28},{28,24},{1,5},{5... | collective-permute-start | bytes 786440 | tf_op jit(solution)/shard_map/ppermute | solution.py:21
  6.1 18.6 %collective-permute-start.5 = (f32[16,16,256]{2,1,0:T(8,128)S(1)}, f32[16,16,256]{2,1,0:T(8,128)S(1)}, u32[]{:S(2)}, u32[]{:S(2)}) collective-permute-start(f32[16,16,256]{2,1,0:T(8,128)S(1)} %get-tuple-element.34), channel_id=1, source_target_pairs={{0,28},{4,8},{8,4},{12,16},{16,12},{20,24},{24,20},{28,0},{1,29},{... | collective-permute-start | bytes 786440 | tf_op jit(solution)/shard_map/ppermute | solution.py:21
  7.4 16.5 %collective-permute-start.3 = (f32[16,8,256]{2,1,0:T(8,128)S(1)}, f32[16,8,256]{2,1,0:T(8,128)S(1)}, u32[]{:S(2)}, u32[]{:S(2)}) collective-permute-start(f32[16,8,256]{2,1,0:T(8,128)S(1)} %collective-permute-done.refs_0_), channel_id=1, source_target_pairs={{0,3},{1,2},{2,1},{3,0},{4,7},{5,6},{6,5},{7,4},{8,11},{9,10},{10,... | collective-permute-start | bytes 393224 | tf_op jit(solution)/shard_map/ppermute | solution.py:21
  17.5 7.0 %collective-permute-start.2 = (f32[16,8,256]{2,1,0:T(8,128)S(1)}, f32[16,8,256]{2,1,0:T(8,128)S(1)}, u32[]{:S(2)}, u32[]{:S(2)}) collective-permute-start(f32[16,8,256]{2,1,0:T(8,128)S(1)} %collective-permute-done.refs_0_), channel_id=1, source_target_pairs={{0,2},{1,3},{2,0},{3,1},{4,6},{5,7},{6,4},{7,5},{8,10},{9,11},{10,... | collective-permute-start | bytes 393224 | tf_op jit(solution)/shard_map/ppermute | solution.py:21
  17.7 6.8 %collective-permute-start.1 = (f32[16,8,256]{2,1,0:T(8,128)S(1)}, f32[16,8,256]{2,1,0:T(8,128)S(1)}, u32[]{:S(2)}, u32[]{:S(2)}) collective-permute-start(f32[16,8,256]{2,1,0:T(8,128)S(1)} %collective-permute-done.refs_0_), channel_id=1, source_target_pairs={{0,1},{1,0},{2,3},{3,2},{4,5},{5,4},{6,7},{7,6},{8,9},{9,8},{10,11... | collective-permute-start | bytes 393224 | tf_op jit(solution)/shard_map/ppermute | solution.py:21
  25.3 4.6 %collective-permute-start.8 = (f32[32,256]{1,0:T(8,128)S(1)}, f32[32,256]{1,0:T(8,128)S(1)}, u32[]{:S(2)}, u32[]{:S(2)}) collective-permute-start(f32[32,256]{1,0:T(8,128)S(1)} %border_low_levels.1), channel_id=1, source_target_pairs={{0,3},{1,2},{2,1},{3,0},{4,7},{5,6},{6,5},{7,4},{8,11},{9,10},{10,... | collective-permute-start | bytes 98312 | tf_op jit(solution)/shard_map/ppermute | solution.py:21
  26.3 3.6 %collective-permute-start.7 = (f32[32,256]{1,0:T(8,128)S(1)}, f32[32,256]{1,0:T(8,128)S(1)}, u32[]{:S(2)}, u32[]{:S(2)}) collective-permute-start(f32[32,256]{1,0:T(8,128)S(1)} %border_low_levels.1), channel_id=1, source_target_pairs={{0,2},{1,3},{2,0},{3,1},{4,6},{5,7},{6,4},{7,5},{8,10},{9,11},{10,... | collective-permute-start | bytes 98312 | tf_op jit(solution)/shard_map/ppermute | solution.py:21
  27.2 2.7 %collective-permute-start.6 = (f32[32,256]{1,0:T(8,128)S(1)}, f32[32,256]{1,0:T(8,128)S(1)}, u32[]{:S(2)}, u32[]{:S(2)}) collective-permute-start(f32[32,256]{1,0:T(8,128)S(1)} %border_low_levels.1), channel_id=1, source_target_pairs={{0,1},{1,0},{2,3},{3,2},{4,5},{5,4},{6,7},{7,6},{8,9},{9,8},{10,11... | collective-permute-start | bytes 98312 | tf_op jit(solution)/shard_map/ppermute | solution.py:21

commit v18 on v16

--- a/solution.py
+++ b/solution.py
@@ -10,7 +10,6 @@
 ITERS = 4
 EDGE = ITERS
 ENTRIES = 16
-BLOCK = 4
 CHUNKS = 2
 LANES = 128
 HALVES = (slice(0, LANES), slice(LANES, 2 * LANES))
@@ -72,22 +71,19 @@
     return jnp.concatenate(parts, axis=1)
 
 
-def coef_side(rank):
-    return lax.rem(1 - parity() + rank, 2)
-
-
-def coef_half(rank):
-    return lax.rem(lax.div(rank, 2), 2)
+def coef_side(half):
+    return lax.rem(1 - parity() + half, 2)
+
+
+def coef_half():
+    return lax.rem(lax.div(lax.axis_index("grp"), 2), 2)
 
 
 def pack_kernel(lam, ew, ed, nw, nd, mf, top, *refs):
     coef_send, lam_first, lam_second = refs[:3]
     field_s, top_s, lam_s, coef_p, lam_p, sems = refs[3:]
     tags, levels, cols, lats = lam.shape
-    per = levels // 2
-    rank = lax.axis_index("grp")
-    base = coef_half(rank) * per
-    high = coef_side(rank)
+    high = coef_side(coef_half())
     edge = pl.ds(pl.multiple_of(high * (cols - 8), 8), 8)
     copies = []
 
@@ -96,7 +92,7 @@
         copies[-1].start()
 
     for f, field in enumerate((ew, ed, nw, nd, mf)):
-        copy(field.at[pl.ds(base, per), edge], field_s.at[f])
+        copy(field.at[:, edge], field_s.at[f])
     copy(top.at[edge], top_s)
     for side, at in ((LOW, 0), (HIGH, cols - 8)):
         for tag in range(tags):
@@ -104,22 +100,21 @@
     for c in copies[:6]:
         c.wait()
     pitch = 9
-    few = per * pitch
-
-    @pl.loop(0, per // 2)
-    def _(pair):
-        for half in range(2):
-            i = pair * 2 + half
-            level = base + i
-            ew, ed, nw, nd, mf = (field_s[f, i] for f in range(5))
+    few = levels * pitch
+
+    @pl.loop(0, levels // 4)
+    def _(i):
+        for step in range(4):
+            level = i * 4 + step
+            ew, ed, nw, nd, mf = (field_s[f, level] for f in range(5))
             lift = jnp.where((level < top_s[...]) & (level < levels - 1), mf, 0.0)
             for j, value in enumerate((*faces(ew, ed, nw, nd), lift)):
                 for k in range(2):
-                    at = (j * 2 + k) * few + i * pitch
+                    at = (j * 2 + k) * few + level * pitch
                     coef_p[pl.ds(at, 8), :] = value[:, HALVES[k]]
 
     def coef_column(j, c):
-        return column_at(coef_p, j * 2 * few + c, per, pitch, few)
+        return column_at(coef_p, j * 2 * few + c, levels, pitch, few)
 
     start = 8 - EDGE
     c = high * (start + 1)
@@ -152,9 +147,8 @@
 
 def pack(lam, fields, top):
     tags, levels, cols, lats = lam.shape
-    per = levels // 2
     hbm = pl.BlockSpec(memory_space=pltpu.HBM)
-    coef_send = pltpu.VMEM((ENTRIES, per, lats), jnp.float32)
+    coef_send = pltpu.VMEM((ENTRIES, levels, lats), jnp.float32)
     lam_send = pltpu.VMEM((tags * EDGE, levels, lats), jnp.float32)
     return pl.pallas_call(
         pack_kernel,
@@ -162,10 +156,10 @@
         out_specs=[pl.BlockSpec(memory_space=pltpu.VMEM)] * 3,
         out_shape=[coef_send, lam_send, lam_send],
         scratch_shapes=[
-            pltpu.VMEM((5, per, 8, lats), jnp.float32),
+            pltpu.VMEM((5, levels, 8, lats), jnp.float32),
             pltpu.VMEM((8, lats), jnp.int32),
             pltpu.VMEM((2, tags, levels, 8, lats), jnp.float32),
-            pltpu.VMEM((pitched(10, per, 8), LANES), jnp.float32),
+            pltpu.VMEM((pitched(10, levels, 8), LANES), jnp.float32),
             pltpu.VMEM((pitched(4 * tags, levels, 8), LANES), jnp.float32),
             pltpu.SemaphoreType.DMA((6 + 2 * tags,)),
         ],
@@ -300,13 +294,17 @@
     return (LOW, c + EDGE - 1) if c < EDGE else (HIGH, c - (cols - EDGE))
 
 
-def outer_kernel(cols, coef, *refs):
-    pieces, wide, entry = refs[:BLOCK], refs[BLOCK], refs[BLOCK + 1]
-    per = coef.shape[2] // 2
-    for by in range(BLOCK):
-        rank = lax.axis_index("grp") ^ by
-        rows = pl.ds(pl.multiple_of(coef_half(rank) * per, 8), per)
-        entry[coef_side(rank), :, rows] = pieces[by][...]
+def outer_kernel(cols, first, second, coef, own, mate, across, aslant, wide, halo, entry):
+    halo[1 - parity()] = first[...]
+    halo[parity()] = second[...]
+    half = coef_half()
+    odd_rank = lax.rem(lax.axis_index("grp"), 2)
+    for rank, near, far in ((0, mate, aslant), (1, own, across)):
+
+        @pl.when(odd_rank == rank)
+        def _():
+            entry[coef_side(half)] = near[...]
+            entry[coef_side(1 - half)] = far[...]
 
     def slab(side, e):
         return entry[side, e]
@@ -324,29 +322,30 @@
         wide[*slot(0, cols), j] = value
 
 
-def outer_coefs(cols, coef, pieces):
-    _, _, levels, lats = coef.shape
+def outer_parts(first, second, coef, pieces):
+    levels, lats = coef.shape[2:]
     vmem = pl.BlockSpec(memory_space=pltpu.VMEM)
     return pl.pallas_call(
-        functools.partial(outer_kernel, cols),
-        in_specs=[vmem] * (1 + BLOCK),
-        out_specs=vmem,
-        out_shape=pltpu.VMEM((2, 2 * EDGE - 1, 6, levels, lats), jnp.float32),
+        functools.partial(outer_kernel, coef.shape[0] - 1),
+        in_specs=[vmem] * 7,
+        out_specs=[vmem] * 2,
+        out_shape=[
+            pltpu.VMEM((2, 2 * EDGE - 1, 6, levels, lats), jnp.float32),
+            pltpu.VMEM((2, *first.shape), jnp.float32),
+        ],
         scratch_shapes=[pltpu.VMEM((2, ENTRIES, levels, lats), jnp.float32)],
         compiler_params=pltpu.CompilerParams(vmem_limit_bytes=24 << 20),
         cost_estimate=SHORT,
-        name="outer_coefs",
-    )(coef, *pieces)
+        name="outer_parts",
+    )(first, second, coef, *pieces)
 
 
 def border_steps(
-    depth, region, coef, wide, kept, l0, halos, halo, work, rows=None, store=None, finish=None
+    depth, region, coef, wide, kept, l0, halo, work, rows=None, store=None, finish=None
 ):
     cols, tags, levels, lats = kept[1].shape
     first_tag = lax.axis_index("grp") * tags
     part = slice(0, depth)
-    halo[1 - parity()] = halos[0][:, part]
-    halo[parity()] = halos[1][:, part]
 
     def coefs_at(c):
         if 0 < c < cols:
@@ -356,9 +355,9 @@
     def state(t, c, tag):
         if t == 0:
             if c < 0:
-                return halo[LOW, tag * EDGE + c + EDGE]
+                return halo[LOW, tag * EDGE + c + EDGE, part]
             if c >= cols:
-                return halo[HIGH, tag * EDGE + c - cols]
+                return halo[HIGH, tag * EDGE + c - cols, part]
             return l0[c if c < 2 else c - (cols - 4), tag, part]
         if t <= c < cols - t:
             return kept[t][c, tag, part]
@@ -391,10 +390,10 @@
         finish(k)
 
 
-def low_kernel(region, coef, wide, l0, l1, l2, l3, first, second, rows_in, grad, halo, work, rows):
+def low_kernel(region, coef, wide, halo, l0, l1, l2, l3, rows_in, grad, work, rows):
     rows[...] = rows_in[...]
     kept = (None, l1, l2, l3)
-    border_steps(8, region, coef, wide, kept, l0, (first, second), halo, work, rows)
+    border_steps(8, region, coef, wide, kept, l0, halo, work, rows)
     total = rows[0]
     for t in range(1, ITERS):
         total = total + rows[t]
@@ -402,23 +401,20 @@
 
 
 def border_scratch(tags, depth, lats):
-    return [
-        pltpu.VMEM((2, tags * EDGE, depth, lats), jnp.float32),
-        pltpu.VMEM((ITERS, 2, 2 * EDGE - 1, tags, depth, lats), jnp.float32),
-    ]
-
-
-def gradient(region, coef, wide, states, halos, rows):
+    return pltpu.VMEM((ITERS, 2, 2 * EDGE - 1, tags, depth, lats), jnp.float32)
+
+
+def gradient(region, coef, wide, halo, states, rows):
     cols, tags, levels, lats = states[1].shape
     vmem = pl.BlockSpec(memory_space=pltpu.VMEM)
-    operands = [region, coef, wide, *states, *halos, rows]
+    operands = [region, coef, wide, halo, *states, rows]
     return pl.pallas_call(
         low_kernel,
         in_specs=[vmem] * len(operands),
         out_specs=vmem,
         out_shape=pltpu.VMEM((cols, lats), jnp.float32),
         scratch_shapes=[
-            *border_scratch(tags, 8, lats),
+            border_scratch(tags, 8, lats),
             pltpu.VMEM((ITERS, cols, lats), jnp.float32),
         ],
         compiler_params=pltpu.CompilerParams(vmem_limit_bytes=32 << 20),
@@ -427,8 +423,8 @@
     )(*operands)
 
 
-def border_kernel(coef, wide, l0, l1, l2, l3, first, second, *refs):
-    final_in, out_in, final, out, halo, work, sides, sems = refs
+def border_kernel(coef, wide, halo, l0, l1, l2, l3, *refs):
+    final_in, out_in, final, out, work, sides, sems = refs
     cols, tags, levels, lats = l1.shape
     pitch = cols + 1
     store = storing_rows(final, tags, levels, pitch)
@@ -453,18 +449,16 @@
             )
             copies[-1].start()
 
-    border_steps(
-        levels, None, coef, wide, kept, l0, (first, second), halo, work, None, store, finish
-    )
+    border_steps(levels, None, coef, wide, kept, l0, halo, work, None, store, finish)
     for c in copies:
         c.wait()
 
 
-def border(coef, wide, states, halos, final, out):
+def border(coef, wide, halo, states, final, out):
     cols, tags, levels, lats = states[1].shape
     vmem = pl.BlockSpec(memory_space=pltpu.VMEM)
     hbm = pl.BlockSpec(memory_space=pltpu.HBM)
-    operands = [coef, wide, *states, *halos]
+    operands = [coef, wide, halo, *states]
     n = len(operands)
     return pl.pallas_call(
         border_kernel,
@@ -476,7 +470,7 @@
         ],
         input_output_aliases={n: 0, n + 1: 1},
         scratch_shapes=[
-            *border_scratch(tags, levels, lats),
+            border_scratch(tags, levels, lats),
             pltpu.VMEM((2, tags, levels, 8, lats), jnp.float32),
             pltpu.SemaphoreType.DMA((2 * tags,)),
         ],
@@ -534,23 +528,26 @@
     turn = lambda i: (((i - 1) % tiles ^ 1) + 1) % tiles
     coefs, first, second = pack(far[0], far[1:6], far[6])
 
+    senders = [i for i in range(tiles * groups) if i % 2]
+
     def partner(i):
         tile, rank = divmod(i, groups)
-        return (turn if rank % 2 else pairs)(tile) * groups + rank
-
-    coefs = swapped(coefs, ("dom", "grp"), partner)
+        return (turn if rank % 4 // 2 else pairs)(tile) * groups + rank
+
+    coefs = lax.ppermute(coefs, ("dom", "grp"), [(i, partner(i)) for i in senders])
     first = swapped(first, "dom", pairs)
     second = swapped(second, "dom", turn)
-    pieces = [coefs]
-    for by in range(1, BLOCK):
-        pieces.append(swapped(coefs, "grp", lambda i: i ^ by))
+    odd_ranks = range(1, groups, 2)
+    pieces = [coefs] + [
+        lax.ppermute(coefs, "grp", [(i, i ^ by) for i in odd_ranks]) for by in (1, 2, 3)
+    ]
     coef, *states, final, rows = inner(own[0], own[1:], top, region)
-    wide = outer_coefs(lam.shape[2], coef, pieces)
     out = write_inner(final, lam.shape)
-    wide, out = lax.optimization_barrier((wide, out))
-    grad = gradient(region, coef, wide, states, (first, second), rows)
+    coef, out = lax.optimization_barrier((coef, out))
+    wide, halo = outer_parts(first, second, coef, pieces)
+    grad = gradient(region, coef, wide, halo, states, rows)
     grad, wide = lax.optimization_barrier((grad, wide))
-    out = border(coef, wide, states, (first, second), final, out)
+    out = border(coef, wide, halo, states, final, out)
     share = grad
     for by in range(1, groups):
         grad = grad + swapped(share, "grp", lambda i: i ^ by)

time: 32.3 us -> 38.2 us (1.18)
  the two profiles are of different devices: /device:TPU:26 before, /device:TPU:0 now
where the time goes in v18:
time: 38.2 us; the launch traced here: 37.9 us
  starting transfers between devices  18.9 us (49%)
  Pallas kernels  11.8 us (31%)
  waiting for transfers between devices  4.99 us (13%)
  between operations  0.85 us (2%)
  local copies, waits for them, and re-layouts  0.78 us (2%)
  other arithmetic  0.63 us (2%)
    ppermute x5, starting transfers between devices, swapped(): lax.ppermute(value, axis, [(i, partner(i)) for i in range(lax.axis_size(a...  14.9 us
    pallas_call x1, Pallas kernels, inner(): pl.pallas_call(inner_kernel, in_specs=[vmem] * 8, out_specs=[vmem] * 7, o...  5.6 us
    ppermute x3, waiting for transfers between devices, local(): lax.ppermute(coefs, 'grp', [(i, i ^ by) for i in odd_ranks])  3.68 us
    ppermute x3, starting transfers between devices, local(): lax.ppermute(coefs, 'grp', [(i, i ^ by) for i in odd_ranks])  3.25 us
    pallas_call x1, Pallas kernels, border(): pl.pallas_call(border_kernel, in_specs=[vmem] * (n + 1) + [hbm], out_spec...  2.3 us
    pallas_call x1, Pallas kernels, pack(): pl.pallas_call(pack_kernel, in_specs=[hbm] * 7, out_specs=[pl.BlockSpec(m...  1.98 us
    ppermute x5, waiting for transfers between devices, swapped(): lax.ppermute(value, axis, [(i, partner(i)) for i in range(lax.axis_size(a...  1.31 us
    pallas_call x1, Pallas kernels, write_inner(): pl.pallas_call(write_kernel, in_specs=[pl.BlockSpec(memory_space=pltpu.VM...  1.14 us
  transfers between devices with their start and end apart: 9, of which 3 were waited for; matrix products, arithmetic and copies ran while one was open for 0% of the time, Pallas kernels for 24%

profile of v18, /device:TPU:0, one launch (start us, length us, event | category | flops | bytes accessed | tf_op | source)
XLA Modules:
  0.0 37.9 jit_solution(17377736420855157211)
XLA Ops:
  0.7 2.0 %pack_edges.1 = (f32[16,16,256]{2,1,0:T(8,128)S(1)}, f32[16,16,256]{2,1,0:T(8,128)S(1)}, f32[16,16,256]{2,1,0:T(8,128)S(1)}) custom-call(f32[4,16,32,256]{3,2,1,0:T(8,128)} %lam.3, f32[16,32,256]{2,1,0:T(8,128)} %ew.3, f32[16,32,256]{2,1,0:T(8,128)} %ed.3, f32[16,32,256]{2,1,0:T(8,128)} %nw.3, f32[16,32,256]{2,1,0:T(8,128)} %nd.3, f32[16,32,256]{2,1,0:T(8,128)} %mf.3, ...), custom_call_target="tpu_custom_call" | custom-call | flops 1000 | bytes 1000 | tf_op jit(solution)/shard_map/pack_edges/pallas_call | solution.py:153
  2.7 0.7 %collective-permute-start.2 = (f32[16,16,256]{2,1,0:T(8,128)S(1)}, f32[16,16,256]{2,1,0:T(8,128)S(1)}, u32[]{:S(2)}, u32[]{:S(2)}) collective-permute-start(f32[16,16,256]{2,1,0:T(8,128)S(1)} %get-tuple-element.24), channel_id=1, source_target_pairs={{1,5},{3,31},{5,1},{7,11},{9,13},{11,7},{13,9},{15,19},{17,21},{19... | collective-permute-start | bytes 786440 | tf_op jit(solution)/shard_map/ppermute | solution.py:537
  3.4 3.0 %collective-permute-start = (f32[16,16,256]{2,1,0:T(8,128)S(1)}, f32[16,16,256]{2,1,0:T(8,128)S(1)}, u32[]{:S(2)}, u32[]{:S(2)}) collective-permute-start(f32[16,16,256]{2,1,0:T(8,128)S(1)} %get-tuple-element.22), channel_id=1, source_target_pairs={{0,4},{4,0},{8,12},{12,8},{16,20},{20,16},{24,28},{28,24},{1,5},{5... | collective-permute-start | bytes 786440 | tf_op jit(solution)/shard_map/ppermute | solution.py:20
  6.4 3.6 %collective-permute-start.1 = (f32[16,16,256]{2,1,0:T(8,128)S(1)}, f32[16,16,256]{2,1,0:T(8,128)S(1)}, u32[]{:S(2)}, u32[]{:S(2)}) collective-permute-start(f32[16,16,256]{2,1,0:T(8,128)S(1)} %get-tuple-element.23), channel_id=1, source_target_pairs={{0,28},{4,8},{8,4},{12,16},{16,12},{20,24},{24,20},{28,0},{1,29},{... | collective-permute-start | bytes 786440 | tf_op jit(solution)/shard_map/ppermute | solution.py:20
  9.9 0.0 collective-permute-done.2.own
  10.0 1.3 %collective-permute-start.5 = (f32[16,16,256]{2,1,0:T(8,128)S(1)}, f32[16,16,256]{2,1,0:T(8,128)S(1)}, u32[]{:S(2)}, u32[]{:S(2)}) collective-permute-start(f32[16,16,256]{2,1,0:T(8,128)S(1)} %collective-permute-done.2.own), channel_id=1, source_target_pairs={{1,2},{3,0},{5,6},{7,4},{9,10},{11,8},{13,14},{15,12},{17,18},{19,... | collective-permute-start | bytes 786440 | tf_op jit(solution)/shard_map/ppermute | solution.py:542
  11.2 0.7 %collective-permute-start.4 = (f32[16,16,256]{2,1,0:T(8,128)S(1)}, f32[16,16,256]{2,1,0:T(8,128)S(1)}, u32[]{:S(2)}, u32[]{:S(2)}) collective-permute-start(f32[16,16,256]{2,1,0:T(8,128)S(1)} %collective-permute-done.2.own), channel_id=1, source_target_pairs={{1,3},{3,1},{5,7},{7,5},{9,11},{11,9},{13,15},{15,13},{17,19},{19,... | collective-permute-start | bytes 786440 | tf_op jit(solution)/shard_map/ppermute | solution.py:542
  11.9 1.3 %collective-permute-start.3 = (f32[16,16,256]{2,1,0:T(8,128)S(1)}, f32[16,16,256]{2,1,0:T(8,128)S(1)}, u32[]{:S(2)}, u32[]{:S(2)}) collective-permute-start(f32[16,16,256]{2,1,0:T(8,128)S(1)} %collective-permute-done.2.own), channel_id=1, source_target_pairs={{1,0},{3,2},{5,4},{7,6},{9,8},{11,10},{13,12},{15,14},{17,16},{19,... | collective-permute-start | bytes 786440 | tf_op jit(solution)/shard_map/ppermute | solution.py:542
  13.3 0.0 copy-start.7
  13.3 0.7 %copy-done.7 = s32[32,256]{1,0:T(8,128)S(1)} copy-done((s32[32,256]{1,0:T(8,128)S(1)}, s32[32,256]{1,0:T(8,128)}, u32[]{:S(2)}) %copy-start.7) | copy-done | bytes 32792
  14.1 5.6 %inner_steps.1 = (f32[33,6,16,256]{3,2,1,0:T(8,128)S(1)}, f32[4,4,16,256]{3,2,1,0:T(8,128)S(1)}, f32[32,4,16,256]{3,2,1,0:T(8,128)S(1)}, f32[32,4,16,256]{3,2,1,...) custom-call(f32[4,16,32,256]{3,2,1,0:T(8,128)S(1)} %copy-done, ...), custom_call_target="tpu_custom_call" | custom-call | flops 1000 | bytes 1000 | tf_op jit(solution)/shard_map/inner_steps/pallas_call | solution.py:272
  19.7 1.1 %write_inner.1.refs_1_ = f32[4,16,32,256]{3,2,1,0:T(8,128)} custom-call(f32[4264,128]{1,0:T(8,128)S(1)} %get-tuple-element.20.final.refs_0_), custom_call_target="tpu_custom_call" | custom-call | flops 1000 | bytes 1000 | tf_op jit(solution)/shard_map/write_inner/pallas_call | solution.py:507
  20.8 0.0 collective-permute-done.1.second
  20.8 1.4 %collective-permute-done.5.aslant = f32[16,16,256]{2,1,0:T(8,128)S(1)} collective-permute-done((f32[16,16,256]{2,1,0:T(8,128)S(1)}, f32[16,16,256]{2,1,0:T(8,128)S(1)}, u32[]{:S(2)}, u32[]{:S(2)}) %collective-permute-start.5) | collective-permute-done | bytes 262176 | tf_op jit(solution)/shard_map/ppermute | solution.py:542
  22.2 2.3 %collective-permute-done.3.mate = f32[16,16,256]{2,1,0:T(8,128)S(1)} collective-permute-done((f32[16,16,256]{2,1,0:T(8,128)S(1)}, f32[16,16,256]{2,1,0:T(8,128)S(1)}, u32[]{:S(2)}, u32[]{:S(2)}) %collective-permute-start.3) | collective-permute-done | bytes 262176 | tf_op jit(solution)/shard_map/ppermute | solution.py:542
  24.5 0.1 outer_parts.1
  24.6 0.7 %border_low_levels.1 = f32[32,256]{1,0:T(8,128)S(1)} custom-call(s32[32,256]{1,0:T(8,128)S(1)} %copy-done.7, f32[33,6,16,256]{3,2,1,0:T(8,128)S(1)} %get-tuple-element.21.coef, f32[2,7,6,16,256]{4,3,2,1,0:T(8,128)S(1)} %get-tuple-element.32.wide, f32[2,16,16,256]{3,2,1,0:T(8,128)S(1)} %get-tuple-element.26.halo, f32[4,4,16,256]{3,2,1,0:T(8,128)S(1)} %get-tuple-element.27.l0, ...), custom_call_target="tpu_custom_call" | custom-call | flops 1000 | bytes 1000 | tf_op jit(solution)/shard_map/border_low_levels/pallas_call | solution.py:411
  25.3 8.1 %collective-permute-start.8 = (f32[32,256]{1,0:T(8,128)S(1)}, f32[32,256]{1,0:T(8,128)S(1)}, u32[]{:S(2)}, u32[]{:S(2)}) collective-permute-start(f32[32,256]{1,0:T(8,128)S(1)} %border_low_levels.1), channel_id=1, source_target_pairs={{0,3},{1,2},{2,1},{3,0},{4,7},{5,6},{6,5},{7,4},{8,11},{9,10},{10,... | collective-permute-start | bytes 98312 | tf_op jit(solution)/shard_map/ppermute | solution.py:20
  33.4 0.3 collective-permute-start.7
  33.7 0.0 collective-permute-start.6
  33.7 2.3 %border_all_levels.1 = (f32[4264,128]{1,0:T(8,128)S(1)}, f32[4,16,32,256]{3,2,1,0:T(8,128)}) custom-call(f32[33,6,16,256]{3,2,1,0:T(8,128)S(1)} %get-tuple-element.21.coef, f32[2,7,6,16,256]{4,3,2,1,0:T(8,128)S(1)} %get-tuple-element.32.wide, f32[2,16,16,256]{3,2,1,0:T(8,128)S(1)} %get-tuple-element.26.halo, ...), custom_call_target="tpu_custom_call", output_to_operand_aliasing={{0}: (7, {}), {1}: (8, {})} | custom-call | flops 1000 | bytes 1000 | tf_op jit(solution)/shard_map/border_all_levels/pallas_call | solution.py:463
  36.0 0.0 collective-permute-done.8
  36.0 1.3 %collective-permute-done.7 = f32[32,256]{1,0:T(8,128)S(1)} collective-permute-done((f32[32,256]{1,0:T(8,128)S(1)}, f32[32,256]{1,0:T(8,128)S(1)}, u32[]{:S(2)}, u32[]{:S(2)}) %collective-permute-start.7) | collective-permute-done | bytes 32800 | tf_op jit(solution)/shard_map/ppermute | solution.py:20
  37.3 0.6 %add_add_fusion = f32[32,256]{1,0:T(8,128)} fusion(f32[32,256]{1,0:T(8,128)S(1)} %collective-permute-done.8, f32[32,256]{1,0:T(8,128)S(1)} %collective-permute-done.7, f32[32,256]{1,0:T(8,128)S(1)} %border_low_levels.1, f32[32,256]{1,0:T(8,128)S(1)} %collective-permute-done.6), kind=kLoop, calls=%fused_computation | loop fusion | flops 24576 | bytes 163840 | tf_op jit(solution)/shard_map/add | solution.py:553
  (17 shorter events, 0.0 us)
Async XLA Ops:
  0.6 12.6 %copy-start.6 = (s32[32,256]{1,0:T(8,128)S(1)}, s32[32,256]{1,0:T(8,128)}, u32[]{:S(2)}) copy-start(s32[32,256]{1,0:T(8,128)} %top.3) | copy-start | bytes 98308
  0.6 12.6 %copy-start.5 = (f32[16,32,256]{2,1,0:T(8,128)S(1)}, f32[16,32,256]{2,1,0:T(8,128)}, u32[]{:S(2)}) copy-start(f32[16,32,256]{2,1,0:T(8,128)} %mf.3) | copy-start | bytes 1572868
  0.7 12.6 %copy-start.4 = (f32[16,32,256]{2,1,0:T(8,128)S(1)}, f32[16,32,256]{2,1,0:T(8,128)}, u32[]{:S(2)}) copy-start(f32[16,32,256]{2,1,0:T(8,128)} %nd.3) | copy-start | bytes 1572868
  0.7 12.6 %copy-start.2 = (f32[16,32,256]{2,1,0:T(8,128)S(1)}, f32[16,32,256]{2,1,0:T(8,128)}, u32[]{:S(2)}) copy-start(f32[16,32,256]{2,1,0:T(8,128)} %ed.3) | copy-start | bytes 1572868
  0.7 12.6 %copy-start.3 = (f32[16,32,256]{2,1,0:T(8,128)S(1)}, f32[16,32,256]{2,1,0:T(8,128)}, u32[]{:S(2)}) copy-start(f32[16,32,256]{2,1,0:T(8,128)} %nw.3) | copy-start | bytes 1572868
  0.7 12.6 %copy-start.1 = (f32[16,32,256]{2,1,0:T(8,128)S(1)}, f32[16,32,256]{2,1,0:T(8,128)}, u32[]{:S(2)}) copy-start(f32[16,32,256]{2,1,0:T(8,128)} %ew.3) | copy-start | bytes 1572868
  0.7 12.6 %copy-start = (f32[4,16,32,256]{3,2,1,0:T(8,128)S(1)}, f32[4,16,32,256]{3,2,1,0:T(8,128)}, u32[]{:S(2)}) copy-start(f32[4,16,32,256]{3,2,1,0:T(8,128)} %lam.3) | copy-start | bytes 6291460
  2.7 7.3 %collective-permute-start.2 = (f32[16,16,256]{2,1,0:T(8,128)S(1)}, f32[16,16,256]{2,1,0:T(8,128)S(1)}, u32[]{:S(2)}, u32[]{:S(2)}) collective-permute-start(f32[16,16,256]{2,1,0:T(8,128)S(1)} %get-tuple-element.24), channel_id=1, source_target_pairs={{1,5},{3,31},{5,1},{7,11},{9,13},{11,7},{13,9},{15,19},{17,21},{19... | collective-permute-start | bytes 786440 | tf_op jit(solution)/shard_map/ppermute | solution.py:537
  3.4 17.4 %collective-permute-start = (f32[16,16,256]{2,1,0:T(8,128)S(1)}, f32[16,16,256]{2,1,0:T(8,128)S(1)}, u32[]{:S(2)}, u32[]{:S(2)}) collective-permute-start(f32[16,16,256]{2,1,0:T(8,128)S(1)} %get-tuple-element.22), channel_id=1, source_target_pairs={{0,4},{4,0},{8,12},{12,8},{16,20},{20,16},{24,28},{28,24},{1,5},{5... | collective-permute-start | bytes 786440 | tf_op jit(solution)/shard_map/ppermute | solution.py:20
  6.4 14.4 %collective-permute-start.1 = (f32[16,16,256]{2,1,0:T(8,128)S(1)}, f32[16,16,256]{2,1,0:T(8,128)S(1)}, u32[]{:S(2)}, u32[]{:S(2)}) collective-permute-start(f32[16,16,256]{2,1,0:T(8,128)S(1)} %get-tuple-element.23), channel_id=1, source_target_pairs={{0,28},{4,8},{8,4},{12,16},{16,12},{20,24},{24,20},{28,0},{1,29},{... | collective-permute-start | bytes 786440 | tf_op jit(solution)/shard_map/ppermute | solution.py:20
  10.0 12.3 %collective-permute-start.5 = (f32[16,16,256]{2,1,0:T(8,128)S(1)}, f32[16,16,256]{2,1,0:T(8,128)S(1)}, u32[]{:S(2)}, u32[]{:S(2)}) collective-permute-start(f32[16,16,256]{2,1,0:T(8,128)S(1)} %collective-permute-done.2.own), channel_id=1, source_target_pairs={{1,2},{3,0},{5,6},{7,4},{9,10},{11,8},{13,14},{15,12},{17,18},{19,... | collective-permute-start | bytes 786440 | tf_op jit(solution)/shard_map/ppermute | solution.py:542
  11.2 11.0 %collective-permute-start.4 = (f32[16,16,256]{2,1,0:T(8,128)S(1)}, f32[16,16,256]{2,1,0:T(8,128)S(1)}, u32[]{:S(2)}, u32[]{:S(2)}) collective-permute-start(f32[16,16,256]{2,1,0:T(8,128)S(1)} %collective-permute-done.2.own), channel_id=1, source_target_pairs={{1,3},{3,1},{5,7},{7,5},{9,11},{11,9},{13,15},{15,13},{17,19},{19,... | collective-permute-start | bytes 786440 | tf_op jit(solution)/shard_map/ppermute | solution.py:542
  11.9 12.6 %collective-permute-start.3 = (f32[16,16,256]{2,1,0:T(8,128)S(1)}, f32[16,16,256]{2,1,0:T(8,128)S(1)}, u32[]{:S(2)}, u32[]{:S(2)}) collective-permute-start(f32[16,16,256]{2,1,0:T(8,128)S(1)} %collective-permute-done.2.own), channel_id=1, source_target_pairs={{1,0},{3,2},{5,4},{7,6},{9,8},{11,10},{13,12},{15,14},{17,16},{19,... | collective-permute-start | bytes 786440 | tf_op jit(solution)/shard_map/ppermute | solution.py:542
  13.3 0.8 %copy-start.7 = (s32[32,256]{1,0:T(8,128)S(1)}, s32[32,256]{1,0:T(8,128)}, u32[]{:S(2)}) copy-start(s32[32,256]{1,0:T(8,128)} %region.3) | copy-start | bytes 98308
  25.3 10.7 %collective-permute-start.8 = (f32[32,256]{1,0:T(8,128)S(1)}, f32[32,256]{1,0:T(8,128)S(1)}, u32[]{:S(2)}, u32[]{:S(2)}) collective-permute-start(f32[32,256]{1,0:T(8,128)S(1)} %border_low_levels.1), channel_id=1, source_target_pairs={{0,3},{1,2},{2,1},{3,0},{4,7},{5,6},{6,5},{7,4},{8,11},{9,10},{10,... | collective-permute-start | bytes 98312 | tf_op jit(solution)/shard_map/ppermute | solution.py:20
  33.4 3.9 %collective-permute-start.7 = (f32[32,256]{1,0:T(8,128)S(1)}, f32[32,256]{1,0:T(8,128)S(1)}, u32[]{:S(2)}, u32[]{:S(2)}) collective-permute-start(f32[32,256]{1,0:T(8,128)S(1)} %border_low_levels.1), channel_id=1, source_target_pairs={{0,2},{1,3},{2,0},{3,1},{4,6},{5,7},{6,4},{7,5},{8,10},{9,11},{10,... | collective-permute-start | bytes 98312 | tf_op jit(solution)/shard_map/ppermute | solution.py:20
  33.7 3.6 %collective-permute-start.6 = (f32[32,256]{1,0:T(8,128)S(1)}, f32[32,256]{1,0:T(8,128)S(1)}, u32[]{:S(2)}, u32[]{:S(2)}) collective-permute-start(f32[32,256]{1,0:T(8,128)S(1)} %border_low_levels.1), channel_id=1, source_target_pairs={{0,1},{1,0},{2,3},{3,2},{4,5},{5,4},{6,7},{7,6},{8,9},{9,8},{10,11... | collective-permute-start | bytes 98312 | tf_op jit(solution)/shard_map/ppermute | solution.py:20

commit v19 on v16

--- a/solution.py
+++ b/solution.py
@@ -223,8 +223,7 @@
     return store
 
 
-def inner_kernel(lam, ew, ed, nw, nd, mf, top, region, *refs):
-    coef, l0, l1, l2, l3, final, rows, lam_p, field_p = refs
+def prepare_kernel(lam, ew, ed, nw, nd, mf, top, region, coef, l0, l1, l2, rows, lam_p, field_p):
     tags, levels, cols, lats = lam.shape
     pitch = cols + 1
     slab = levels * pitch
@@ -257,34 +256,32 @@
 
     west = lax.fori_loop(0, cols // 8, some, jnp.zeros((levels, lats), jnp.float32))
     coef[cols, 2] = west
+    for at, c in enumerate((0, 1, cols - 2, cols - 1)):
+        for tag in range(tags):
+            l0[at, tag] = column_at(lam_p, tag * slab + c, levels, pitch, tags * slab)
 
     def given(c, tag):
         return column_at(lam_p, tag * slab + c, levels, pitch, tags * slab)
 
-    for at, c in enumerate((0, 1, cols - 2, cols - 1)):
-        for tag in range(tags):
-            l0[at, tag] = given(c, tag)
-    last = storing_rows(final, tags, levels, pitch)
-    loads = (given, loading(l1), loading(l2), loading(l3))
-    stores = (storing(l1), storing(l2), storing(l3), last)
-    for t in range(ITERS):
-        sweep(t, lam.shape, lax.axis_index("grp") * tags, region, coef, loads[t], stores[t], rows)
-
-
-def inner(lam, fields, top, region):
+    first_tag = lax.axis_index("grp") * tags
+    sweep(0, lam.shape, first_tag, region, coef, given, storing(l1), rows)
+    sweep(1, lam.shape, first_tag, region, coef, loading(l1), storing(l2), rows)
+
+
+def prepare(lam, fields, top, region):
     tags, levels, cols, lats = lam.shape
     vmem = pl.BlockSpec(memory_space=pltpu.VMEM)
     state = pltpu.VMEM((cols, tags, levels, lats), jnp.float32)
     return pl.pallas_call(
-        inner_kernel,
+        prepare_kernel,
         in_specs=[vmem] * 8,
-        out_specs=[vmem] * 7,
+        out_specs=[vmem] * 5,
         out_shape=[
             pltpu.VMEM((cols + 1, 6, levels, lats), jnp.float32),
             pltpu.VMEM((4, tags, levels, lats), jnp.float32),
-            *[state] * 3,
-            pltpu.VMEM((pitched(2 * tags, levels, cols), LANES), jnp.float32),
-            pltpu.VMEM((ITERS, cols, lats), jnp.float32),
+            state,
+            state,
+            pltpu.VMEM((2, cols, lats), jnp.float32),
         ],
         scratch_shapes=[
             pltpu.VMEM((pitched(2 * tags, levels, cols), LANES), jnp.float32),
@@ -292,8 +289,36 @@
         ],
         compiler_params=pltpu.CompilerParams(vmem_limit_bytes=32 << 20),
         cost_estimate=SHORT,
+        name="first_steps",
+    )(lam, *fields, top, region)
+
+
+def inner_kernel(coef, l2, region, rows_in, l3, final, rows):
+    cols, tags, levels, lats = l2.shape
+    rows[0:2] = rows_in[...]
+    shape = (tags, levels, cols, lats)
+    first_tag = lax.axis_index("grp") * tags
+    last = storing_rows(final, tags, levels, cols + 1)
+    sweep(2, shape, first_tag, region, coef, loading(l2), storing(l3), rows)
+    sweep(3, shape, first_tag, region, coef, loading(l3), last, rows)
+
+
+def inner(coef, l2, region, rows):
+    cols, tags, levels, lats = l2.shape
+    vmem = pl.BlockSpec(memory_space=pltpu.VMEM)
+    return pl.pallas_call(
+        inner_kernel,
+        in_specs=[vmem] * 4,
+        out_specs=[vmem] * 3,
+        out_shape=[
+            pltpu.VMEM(l2.shape, jnp.float32),
+            pltpu.VMEM((pitched(2 * tags, levels, cols), LANES), jnp.float32),
+            pltpu.VMEM((ITERS, cols, lats), jnp.float32),
+        ],
+        compiler_params=pltpu.CompilerParams(vmem_limit_bytes=32 << 20),
+        cost_estimate=SHORT,
         name="inner_steps",
-    )(lam, *fields, top, region)
+    )(coef, l2, region, rows)
 
 
 def slot(c, cols):
@@ -539,12 +564,15 @@
         return (turn if rank % 2 else pairs)(tile) * groups + rank
 
     coefs = swapped(coefs, ("dom", "grp"), partner)
+    coef, l0, l1, l2, rows = prepare(own[0], own[1:], top, region)
+    second, coef = lax.optimization_barrier((second, coef))
     first = swapped(first, "dom", pairs)
     second = swapped(second, "dom", turn)
     pieces = [coefs]
     for by in range(1, BLOCK):
         pieces.append(swapped(coefs, "grp", lambda i: i ^ by))
-    coef, *states, final, rows = inner(own[0], own[1:], top, region)
+    l3, final, rows = inner(coef, l2, region, rows)
+    states = [l0, l1, l2, l3]
     wide = outer_coefs(lam.shape[2], coef, pieces)
     out = write_inner(final, lam.shape)
     wide, out = lax.optimization_barrier((wide, out))

time: 32.3 us -> 29.6 us (0.916)
  the two profiles are of different devices: /device:TPU:26 before, /device:TPU:0 now
where the time goes in v19:
time: 29.6 us; the launch traced here: 29.4 us
  starting transfers between devices  11.9 us (40%)
  Pallas kernels  11.7 us (40%)
  waiting for transfers between devices  3.55 us (12%)
  between operations  0.81 us (3%)
  local copies, waits for them, and re-layouts  0.78 us (3%)
  other arithmetic  0.63 us (2%)
    ppermute x9, starting transfers between devices, swapped(): lax.ppermute(value, axis, [(i, partner(i)) for i in range(lax.axis_size(a...  11.9 us
    ppermute x9, waiting for transfers between devices, swapped(): lax.ppermute(value, axis, [(i, partner(i)) for i in range(lax.axis_size(a...  3.55 us
    pallas_call x1, Pallas kernels, prepare(): pl.pallas_call(prepare_kernel, in_specs=[vmem] * 8, out_specs=[vmem] * 5,...  3.4 us
    pallas_call x1, Pallas kernels, border(): pl.pallas_call(border_kernel, in_specs=[vmem] * (n + 1) + [hbm], out_spec...  2.33 us
    pallas_call x1, Pallas kernels, inner(): pl.pallas_call(inner_kernel, in_specs=[vmem] * 4, out_specs=[vmem] * 3, o...  2.23 us
    pallas_call x1, Pallas kernels, pack(): pl.pallas_call(pack_kernel, in_specs=[hbm] * 7, out_specs=[pl.BlockSpec(m...  1.82 us
    pallas_call x1, Pallas kernels, write_inner(): pl.pallas_call(write_kernel, in_specs=[pl.BlockSpec(memory_space=pltpu.VM...  1.14 us
    unnamed x16, local copies, waits for them, and re-layouts  0.78 us
  transfers between devices with their start and end apart: 9, of which 3 were waited for; matrix products, arithmetic and copies ran while one was open for 0% of the time, Pallas kernels for 31%

profile of v19, /device:TPU:0, one launch (start us, length us, event | category | flops | bytes accessed | tf_op | source)
XLA Modules:
  0.0 29.4 jit_solution(4404479602599103440)
XLA Ops:
  0.7 1.8 %pack_edges.1 = (f32[16,8,256]{2,1,0:T(8,128)S(1)}, f32[16,16,256]{2,1,0:T(8,128)S(1)}, f32[16,16,256]{2,1,0:T(8,128)S(1)}) custom-call(f32[4,16,32,256]{3,2,1,0:T(8,128)} %lam.3, f32[16,32,256]{2,1,0:T(8,128)} %ew.3, f32[16,32,256]{2,1,0:T(8,128)} %ed.3, f32[16,32,256]{2,1,0:T(8,128)} %nw.3, f32[16,32,256]{2,1,0:T(8,128)} %nd.3, f32[16,32,256]{2,1,0:T(8,128)} %mf.3, ...), custom_call_target="tpu_custom_call" | custom-call | flops 1000 | bytes 1000 | tf_op jit(solution)/shard_map/pack_edges/pallas_call | solution.py:159
  2.5 3.0 %collective-permute-start = (f32[16,8,256]{2,1,0:T(8,128)S(1)}, f32[16,8,256]{2,1,0:T(8,128)S(1)}, u32[]{:S(2)}, u32[]{:S(2)}) collective-permute-start(f32[16,8,256]{2,1,0:T(8,128)S(1)} %get-tuple-element.23), channel_id=1, source_target_pairs={{0,4},{1,29},{2,6},{3,31},{4,0},{5,9},{6,2},{7,11},{8,12},{9,5},{1... | collective-permute-start | bytes 393224 | tf_op jit(solution)/shard_map/ppermute | solution.py:21
  5.5 0.1 collective-permute-start.4
  5.7 0.0 copy-start.7
  5.7 0.7 %copy-done.7 = s32[32,256]{1,0:T(8,128)S(1)} copy-done((s32[32,256]{1,0:T(8,128)S(1)}, s32[32,256]{1,0:T(8,128)}, u32[]{:S(2)}) %copy-start.7) | copy-done | bytes 32792
  6.4 3.4 %first_steps.1 = (f32[33,6,16,256]{3,2,1,0:T(8,128)S(1)}, f32[4,4,16,256]{3,2,1,0:T(8,128)S(1)}, f32[32,4,16,256]{3,2,1,0:T(8,128)S(1)}, f32[32,4,16,256]{3,2,1,0:T(8,128)S(1)}, f32[2,32,256]{2,1,0:T(8,128)S(1)}) custom-call(f32[4,16,32,256]{3,2,1,0:T(8,128)S(1)} %copy-done, f32[16,32,256]{2,1,0:T(8,128)S(1)} %copy-done.1, f32[16,32,256]{2,1,0:T(8,128)S(1)} %copy-done.2, ...), custom_call_target="tpu_custom_call" | custom-call | flops 1000 | bytes 1000 | tf_op jit(solution)/shard_map/first_steps/pallas_call | solution.py:275
  9.8 5.1 %collective-permute-start.5 = (f32[16,16,256]{2,1,0:T(8,128)S(1)}, f32[16,16,256]{2,1,0:T(8,128)S(1)}, u32[]{:S(2)}, u32[]{:S(2)}) collective-permute-start(f32[16,16,256]{2,1,0:T(8,128)S(1)} %get-tuple-element.32), channel_id=1, source_target_pairs={{0,28},{4,8},{8,4},{12,16},{16,12},{20,24},{24,20},{28,0},{1,29},{... | collective-permute-start | bytes 786440 | tf_op jit(solution)/shard_map/ppermute | solution.py:21
  14.9 0.0 collective-permute-done.refs_0_
  14.9 0.0 collective-permute-start.3
  14.9 1.5 %collective-permute-start.2 = (f32[16,8,256]{2,1,0:T(8,128)S(1)}, f32[16,8,256]{2,1,0:T(8,128)S(1)}, u32[]{:S(2)}, u32[]{:S(2)}) collective-permute-start(f32[16,8,256]{2,1,0:T(8,128)S(1)} %collective-permute-done.refs_0_), channel_id=1, source_target_pairs={{0,2},{1,3},{2,0},{3,1},{4,6},{5,7},{6,4},{7,5},{8,10},{9,11},{10,... | collective-permute-start | bytes 393224 | tf_op jit(solution)/shard_map/ppermute | solution.py:21
  16.4 0.3 %collective-permute-start.1 = (f32[16,8,256]{2,1,0:T(8,128)S(1)}, f32[16,8,256]{2,1,0:T(8,128)S(1)}, u32[]{:S(2)}, u32[]{:S(2)}) collective-permute-start(f32[16,8,256]{2,1,0:T(8,128)S(1)} %collective-permute-done.refs_0_), channel_id=1, source_target_pairs={{0,1},{1,0},{2,3},{3,2},{4,5},{5,4},{6,7},{7,6},{8,9},{9,8},{10,11... | collective-permute-start | bytes 393224 | tf_op jit(solution)/shard_map/ppermute | solution.py:21
  16.7 2.2 %inner_steps.1 = (f32[32,4,16,256]{3,2,1,0:T(8,128)S(1)}, f32[4264,128]{1,0:T(8,128)S(1)}, f32[4,32,256]{2,1,0:T(8,128)S(1)}) custom-call(f32[33,6,16,256]{3,2,1,0:T(8,128)S(1)} %get-tuple-element.22.coef, f32[32,4,16,256]{3,2,1,0:T(8,128)S(1)} %get-tuple-element.24.l2, s32[32,256]{1,0:T(8,128)S(1)} %copy-done.6, f32[2,32,256]{2,1,0:T(8,128)S(1)} %get-tuple-element.25.rows_in), custom_call_target="tpu_custom_call" | custom-call | flops 1000 | bytes 1000 | tf_op jit(solution)/shard_map/inner_steps/pallas_call | solution.py:309
  19.0 1.1 %write_inner.1.refs_1_ = f32[4,16,32,256]{3,2,1,0:T(8,128)} custom-call(f32[4264,128]{1,0:T(8,128)S(1)} %get-tuple-element.26.final.refs_0_), custom_call_target="tpu_custom_call" | custom-call | flops 1000 | bytes 1000 | tf_op jit(solution)/shard_map/write_inner/pallas_call | solution.py:538
  20.1 0.5 %collective-permute-done.3.refs_3_ = f32[16,8,256]{2,1,0:T(8,128)S(1)} collective-permute-done((f32[16,8,256]{2,1,0:T(8,128)S(1)}, f32[16,8,256]{2,1,0:T(8,128)S(1)}, u32[]{:S(2)}, u32[]{:S(2)}) %collective-permute-start.3) | collective-permute-done | bytes 131104 | tf_op jit(solution)/shard_map/ppermute | solution.py:21
  20.6 2.9 %collective-permute-done.2.refs_2_ = f32[16,8,256]{2,1,0:T(8,128)S(1)} collective-permute-done((f32[16,8,256]{2,1,0:T(8,128)S(1)}, f32[16,8,256]{2,1,0:T(8,128)S(1)}, u32[]{:S(2)}, u32[]{:S(2)}) %collective-permute-start.2) | collective-permute-done | bytes 131104 | tf_op jit(solution)/shard_map/ppermute | solution.py:21
  23.5 0.0 collective-permute-done.1.refs_1_
  23.5 0.1 outer_coefs.1.wide
  23.6 0.7 %border_low_levels.1 = f32[32,256]{1,0:T(8,128)S(1)} custom-call(s32[32,256]{1,0:T(8,128)S(1)} %copy-done.6, f32[33,6,16,256]{3,2,1,0:T(8,128)S(1)} %get-tuple-element.22.coef, f32[2,7,6,16,256]{4,3,2,1,0:T(8,128)S(1)} %outer_coefs.1.wide, f32[4,4,16,256]{3,2,1,0:T(8,128)S(1)} %get-tuple-element.28.l0, f32[32,4,16,256]{3,2,1,0:T(8,128)S(1)} %get-tuple-element.29.l1, ...), custom_call_target="tpu_custom_call" | custom-call | flops 1000 | bytes 1000 | tf_op jit(solution)/shard_map/border_low_levels/pallas_call | solution.py:440
  24.3 0.1 collective-permute-start.8
  24.4 1.7 %collective-permute-start.7 = (f32[32,256]{1,0:T(8,128)S(1)}, f32[32,256]{1,0:T(8,128)S(1)}, u32[]{:S(2)}, u32[]{:S(2)}) collective-permute-start(f32[32,256]{1,0:T(8,128)S(1)} %border_low_levels.1), channel_id=1, source_target_pairs={{0,2},{1,3},{2,0},{3,1},{4,6},{5,7},{6,4},{7,5},{8,10},{9,11},{10,... | collective-permute-start | bytes 98312 | tf_op jit(solution)/shard_map/ppermute | solution.py:21
  26.1 0.2 collective-permute-start.6
  26.3 2.3 %border_all_levels.1 = (f32[4264,128]{1,0:T(8,128)S(1)}, f32[4,16,32,256]{3,2,1,0:T(8,128)}) custom-call(f32[33,6,16,256]{3,2,1,0:T(8,128)S(1)} %get-tuple-element.22.coef, f32[2,7,6,16,256]{4,3,2,1,0:T(8,128)S(1)} %outer_coefs.1.wide, f32[4,4,16,256]{3,2,1,0:T(8,128)S(1)} %get-tuple-element.28.l0, ...), custom_call_target="tpu_custom_call", output_to_operand_aliasing={{0}: (8, {}), {1}: (9, {})} | custom-call | flops 1000 | bytes 1000 | tf_op jit(solution)/shard_map/border_all_levels/pallas_call | solution.py:494
  28.6 0.2 collective-permute-done.7
  28.8 0.6 %add_add_fusion = f32[32,256]{1,0:T(8,128)} fusion(f32[32,256]{1,0:T(8,128)S(1)} %collective-permute-done.8, f32[32,256]{1,0:T(8,128)S(1)} %collective-permute-done.7, f32[32,256]{1,0:T(8,128)S(1)} %border_low_levels.1, f32[32,256]{1,0:T(8,128)S(1)} %collective-permute-done.6), kind=kLoop, calls=%fused_computation | loop fusion | flops 24576 | bytes 163840 | tf_op jit(solution)/shard_map/add | solution.py:584
  (18 shorter events, 0.0 us)
Async XLA Ops:
  0.6 5.0 %copy-start.5 = (f32[16,32,256]{2,1,0:T(8,128)S(1)}, f32[16,32,256]{2,1,0:T(8,128)}, u32[]{:S(2)}) copy-start(f32[16,32,256]{2,1,0:T(8,128)} %mf.3) | copy-start | bytes 1572868
  0.6 5.0 %copy-start.4 = (f32[16,32,256]{2,1,0:T(8,128)S(1)}, f32[16,32,256]{2,1,0:T(8,128)}, u32[]{:S(2)}) copy-start(f32[16,32,256]{2,1,0:T(8,128)} %nd.3) | copy-start | bytes 1572868
  0.7 5.0 %copy-start.2 = (f32[16,32,256]{2,1,0:T(8,128)S(1)}, f32[16,32,256]{2,1,0:T(8,128)}, u32[]{:S(2)}) copy-start(f32[16,32,256]{2,1,0:T(8,128)} %ed.3) | copy-start | bytes 1572868
  0.7 5.0 %copy-start.3 = (f32[16,32,256]{2,1,0:T(8,128)S(1)}, f32[16,32,256]{2,1,0:T(8,128)}, u32[]{:S(2)}) copy-start(f32[16,32,256]{2,1,0:T(8,128)} %nw.3) | copy-start | bytes 1572868
  0.7 5.0 %copy-start.1 = (f32[16,32,256]{2,1,0:T(8,128)S(1)}, f32[16,32,256]{2,1,0:T(8,128)}, u32[]{:S(2)}) copy-start(f32[16,32,256]{2,1,0:T(8,128)} %ew.3) | copy-start | bytes 1572868
  0.7 5.0 %copy-start = (f32[4,16,32,256]{3,2,1,0:T(8,128)S(1)}, f32[4,16,32,256]{3,2,1,0:T(8,128)}, u32[]{:S(2)}) copy-start(f32[4,16,32,256]{3,2,1,0:T(8,128)} %lam.3) | copy-start | bytes 6291460
  0.7 5.0 %copy-start.6 = (s32[32,256]{1,0:T(8,128)S(1)}, s32[32,256]{1,0:T(8,128)}, u32[]{:S(2)}) copy-start(s32[32,256]{1,0:T(8,128)} %region.5) | copy-start | bytes 98308
  2.5 12.3 %collective-permute-start = (f32[16,8,256]{2,1,0:T(8,128)S(1)}, f32[16,8,256]{2,1,0:T(8,128)S(1)}, u32[]{:S(2)}, u32[]{:S(2)}) collective-permute-start(f32[16,8,256]{2,1,0:T(8,128)S(1)} %get-tuple-element.23), channel_id=1, source_target_pairs={{0,4},{1,29},{2,6},{3,31},{4,0},{5,9},{6,2},{7,11},{8,12},{9,5},{1... | collective-permute-start | bytes 393224 | tf_op jit(solution)/shard_map/ppermute | solution.py:21
  5.5 18.1 %collective-permute-start.4 = (f32[16,16,256]{2,1,0:T(8,128)S(1)}, f32[16,16,256]{2,1,0:T(8,128)S(1)}, u32[]{:S(2)}, u32[]{:S(2)}) collective-permute-start(f32[16,16,256]{2,1,0:T(8,128)S(1)} %get-tuple-element.31), channel_id=1, source_target_pairs={{0,4},{4,0},{8,12},{12,8},{16,20},{20,16},{24,28},{28,24},{1,5},{5... | collective-permute-start | bytes 786440 | tf_op jit(solution)/shard_map/ppermute | solution.py:21
  5.7 0.8 %copy-start.7 = (s32[32,256]{1,0:T(8,128)S(1)}, s32[32,256]{1,0:T(8,128)}, u32[]{:S(2)}) copy-start(s32[32,256]{1,0:T(8,128)} %top.3) | copy-start | bytes 98308
  9.8 13.8 %collective-permute-start.5 = (f32[16,16,256]{2,1,0:T(8,128)S(1)}, f32[16,16,256]{2,1,0:T(8,128)S(1)}, u32[]{:S(2)}, u32[]{:S(2)}) collective-permute-start(f32[16,16,256]{2,1,0:T(8,128)S(1)} %get-tuple-element.32), channel_id=1, source_target_pairs={{0,28},{4,8},{8,4},{12,16},{16,12},{20,24},{24,20},{28,0},{1,29},{... | collective-permute-start | bytes 786440 | tf_op jit(solution)/shard_map/ppermute | solution.py:21
  14.9 5.7 %collective-permute-start.3 = (f32[16,8,256]{2,1,0:T(8,128)S(1)}, f32[16,8,256]{2,1,0:T(8,128)S(1)}, u32[]{:S(2)}, u32[]{:S(2)}) collective-permute-start(f32[16,8,256]{2,1,0:T(8,128)S(1)} %collective-permute-done.refs_0_), channel_id=1, source_target_pairs={{0,3},{1,2},{2,1},{3,0},{4,7},{5,6},{6,5},{7,4},{8,11},{9,10},{10,... | collective-permute-start | bytes 393224 | tf_op jit(solution)/shard_map/ppermute | solution.py:21
  14.9 8.6 %collective-permute-start.2 = (f32[16,8,256]{2,1,0:T(8,128)S(1)}, f32[16,8,256]{2,1,0:T(8,128)S(1)}, u32[]{:S(2)}, u32[]{:S(2)}) collective-permute-start(f32[16,8,256]{2,1,0:T(8,128)S(1)} %collective-permute-done.refs_0_), channel_id=1, source_target_pairs={{0,2},{1,3},{2,0},{3,1},{4,6},{5,7},{6,4},{7,5},{8,10},{9,11},{10,... | collective-permute-start | bytes 393224 | tf_op jit(solution)/shard_map/ppermute | solution.py:21
  16.4 7.1 %collective-permute-start.1 = (f32[16,8,256]{2,1,0:T(8,128)S(1)}, f32[16,8,256]{2,1,0:T(8,128)S(1)}, u32[]{:S(2)}, u32[]{:S(2)}) collective-permute-start(f32[16,8,256]{2,1,0:T(8,128)S(1)} %collective-permute-done.refs_0_), channel_id=1, source_target_pairs={{0,1},{1,0},{2,3},{3,2},{4,5},{5,4},{6,7},{7,6},{8,9},{9,8},{10,11... | collective-permute-start | bytes 393224 | tf_op jit(solution)/shard_map/ppermute | solution.py:21
  24.3 4.3 %collective-permute-start.8 = (f32[32,256]{1,0:T(8,128)S(1)}, f32[32,256]{1,0:T(8,128)S(1)}, u32[]{:S(2)}, u32[]{:S(2)}) collective-permute-start(f32[32,256]{1,0:T(8,128)S(1)} %border_low_levels.1), channel_id=1, source_target_pairs={{0,3},{1,2},{2,1},{3,0},{4,7},{5,6},{6,5},{7,4},{8,11},{9,10},{10,... | collective-permute-start | bytes 98312 | tf_op jit(solution)/shard_map/ppermute | solution.py:21
  24.4 4.4 %collective-permute-start.7 = (f32[32,256]{1,0:T(8,128)S(1)}, f32[32,256]{1,0:T(8,128)S(1)}, u32[]{:S(2)}, u32[]{:S(2)}) collective-permute-start(f32[32,256]{1,0:T(8,128)S(1)} %border_low_levels.1), channel_id=1, source_target_pairs={{0,2},{1,3},{2,0},{3,1},{4,6},{5,7},{6,4},{7,5},{8,10},{9,11},{10,... | collective-permute-start | bytes 98312 | tf_op jit(solution)/shard_map/ppermute | solution.py:21
  26.1 2.7 %collective-permute-start.6 = (f32[32,256]{1,0:T(8,128)S(1)}, f32[32,256]{1,0:T(8,128)S(1)}, u32[]{:S(2)}, u32[]{:S(2)}) collective-permute-start(f32[32,256]{1,0:T(8,128)S(1)} %border_low_levels.1), channel_id=1, source_target_pairs={{0,1},{1,0},{2,3},{3,2},{4,5},{5,4},{6,7},{7,6},{8,9},{9,8},{10,11... | collective-permute-start | bytes 98312 | tf_op jit(solution)/shard_map/ppermute | solution.py:21

commit v20 on v19

--- a/solution.py
+++ b/solution.py
@@ -223,7 +223,7 @@
     return store
 
 
-def prepare_kernel(lam, ew, ed, nw, nd, mf, top, region, coef, l0, l1, l2, rows, lam_p, field_p):
+def prepare_kernel(lam, ew, ed, nw, nd, mf, top, region, coef, l0, l1, rows, lam_p, field_p):
     tags, levels, cols, lats = lam.shape
     pitch = cols + 1
     slab = levels * pitch
@@ -265,7 +265,6 @@
 
     first_tag = lax.axis_index("grp") * tags
     sweep(0, lam.shape, first_tag, region, coef, given, storing(l1), rows)
-    sweep(1, lam.shape, first_tag, region, coef, loading(l1), storing(l2), rows)
 
 
 def prepare(lam, fields, top, region):
@@ -275,13 +274,12 @@
     return pl.pallas_call(
         prepare_kernel,
         in_specs=[vmem] * 8,
-        out_specs=[vmem] * 5,
+        out_specs=[vmem] * 4,
         out_shape=[
             pltpu.VMEM((cols + 1, 6, levels, lats), jnp.float32),
             pltpu.VMEM((4, tags, levels, lats), jnp.float32),
             state,
-            state,
-            pltpu.VMEM((2, cols, lats), jnp.float32),
+            pltpu.VMEM((1, cols, lats), jnp.float32),
         ],
         scratch_shapes=[
             pltpu.VMEM((pitched(2 * tags, levels, cols), LANES), jnp.float32),
@@ -293,32 +291,34 @@
     )(lam, *fields, top, region)
 
 
-def inner_kernel(coef, l2, region, rows_in, l3, final, rows):
-    cols, tags, levels, lats = l2.shape
-    rows[0:2] = rows_in[...]
+def inner_kernel(coef, l1, region, rows_in, l2, l3, final, rows):
+    cols, tags, levels, lats = l1.shape
+    rows[0] = rows_in[0]
     shape = (tags, levels, cols, lats)
     first_tag = lax.axis_index("grp") * tags
     last = storing_rows(final, tags, levels, cols + 1)
+    sweep(1, shape, first_tag, region, coef, loading(l1), storing(l2), rows)
     sweep(2, shape, first_tag, region, coef, loading(l2), storing(l3), rows)
     sweep(3, shape, first_tag, region, coef, loading(l3), last, rows)
 
 
-def inner(coef, l2, region, rows):
-    cols, tags, levels, lats = l2.shape
+def inner(coef, l1, region, rows):
+    cols, tags, levels, lats = l1.shape
     vmem = pl.BlockSpec(memory_space=pltpu.VMEM)
     return pl.pallas_call(
         inner_kernel,
         in_specs=[vmem] * 4,
-        out_specs=[vmem] * 3,
+        out_specs=[vmem] * 4,
         out_shape=[
-            pltpu.VMEM(l2.shape, jnp.float32),
+            pltpu.VMEM(l1.shape, jnp.float32),
+            pltpu.VMEM(l1.shape, jnp.float32),
             pltpu.VMEM((pitched(2 * tags, levels, cols), LANES), jnp.float32),
             pltpu.VMEM((ITERS, cols, lats), jnp.float32),
         ],
         compiler_params=pltpu.CompilerParams(vmem_limit_bytes=32 << 20),
         cost_estimate=SHORT,
         name="inner_steps",
-    )(coef, l2, region, rows)
+    )(coef, l1, region, rows)
 
 
 def slot(c, cols):
@@ -564,14 +564,14 @@
         return (turn if rank % 2 else pairs)(tile) * groups + rank
 
     coefs = swapped(coefs, ("dom", "grp"), partner)
-    coef, l0, l1, l2, rows = prepare(own[0], own[1:], top, region)
+    coef, l0, l1, rows = prepare(own[0], own[1:], top, region)
     second, coef = lax.optimization_barrier((second, coef))
     first = swapped(first, "dom", pairs)
     second = swapped(second, "dom", turn)
     pieces = [coefs]
     for by in range(1, BLOCK):
         pieces.append(swapped(coefs, "grp", lambda i: i ^ by))
-    l3, final, rows = inner(coef, l2, region, rows)
+    l2, l3, final, rows = inner(coef, l1, region, rows)
     states = [l0, l1, l2, l3]
     wide = outer_coefs(lam.shape[2], coef, pieces)
     out = write_inner(final, lam.shape)

time: 29.6 us -> 28.4 us (0.959)
  waiting for transfers between devices: 3.55 us -> 2.35 us
    ppermute x9, waiting for transfers between devices: 3.55 us -> 2.35 us  [swapped(): lax.ppermute(value, axis, [(i, partner(i)) for i in range(lax.axis_size(a...]
  transfers between devices with their start and end apart: 9 -> 9, of which waited for: 3 -> 2; matrix products, arithmetic and copies ran while one was open for 0% -> 0% of each run, Pallas kernels for 31% -> 33%
where the time goes in v20:
time: 28.4 us; the launch traced here: 28.2 us
  starting transfers between devices  11.9 us (42%)
  Pallas kernels  11.7 us (41%)
  waiting for transfers between devices  2.35 us (8%)
  between operations  0.81 us (3%)
  local copies, waits for them, and re-layouts  0.78 us (3%)
  other arithmetic  0.63 us (2%)
    ppermute x9, starting transfers between devices, swapped(): lax.ppermute(value, axis, [(i, partner(i)) for i in range(lax.axis_size(a...  11.9 us
    pallas_call x1, Pallas kernels, inner(): pl.pallas_call(inner_kernel, in_specs=[vmem] * 4, out_specs=[vmem] * 4, o...  3.42 us
    pallas_call x1, Pallas kernels, border(): pl.pallas_call(border_kernel, in_specs=[vmem] * (n + 1) + [hbm], out_spec...  2.35 us
    ppermute x9, waiting for transfers between devices, swapped(): lax.ppermute(value, axis, [(i, partner(i)) for i in range(lax.axis_size(a...  2.35 us
    pallas_call x1, Pallas kernels, prepare(): pl.pallas_call(prepare_kernel, in_specs=[vmem] * 8, out_specs=[vmem] * 4,...  2.18 us
    pallas_call x1, Pallas kernels, pack(): pl.pallas_call(pack_kernel, in_specs=[hbm] * 7, out_specs=[pl.BlockSpec(m...  1.82 us
    pallas_call x1, Pallas kernels, write_inner(): pl.pallas_call(write_kernel, in_specs=[pl.BlockSpec(memory_space=pltpu.VM...  1.14 us
    unnamed x16, local copies, waits for them, and re-layouts  0.78 us
  transfers between devices with their start and end apart: 9, of which 2 were waited for; matrix products, arithmetic and copies ran while one was open for 0% of the time, Pallas kernels for 33%

profile of v20, /device:TPU:0, one launch (start us, length us, event | category | flops | bytes accessed | tf_op | source)
XLA Modules:
  0.0 28.2 jit_solution(4060130379026334794)
XLA Ops:
  0.7 1.8 %pack_edges.1 = (f32[16,8,256]{2,1,0:T(8,128)S(1)}, f32[16,16,256]{2,1,0:T(8,128)S(1)}, f32[16,16,256]{2,1,0:T(8,128)S(1)}) custom-call(f32[4,16,32,256]{3,2,1,0:T(8,128)} %lam.3, f32[16,32,256]{2,1,0:T(8,128)} %ew.3, f32[16,32,256]{2,1,0:T(8,128)} %ed.3, f32[16,32,256]{2,1,0:T(8,128)} %nw.3, f32[16,32,256]{2,1,0:T(8,128)} %nd.3, f32[16,32,256]{2,1,0:T(8,128)} %mf.3, ...), custom_call_target="tpu_custom_call" | custom-call | flops 1000 | bytes 1000 | tf_op jit(solution)/shard_map/pack_edges/pallas_call | solution.py:159
  2.5 3.0 %collective-permute-start = (f32[16,8,256]{2,1,0:T(8,128)S(1)}, f32[16,8,256]{2,1,0:T(8,128)S(1)}, u32[]{:S(2)}, u32[]{:S(2)}) collective-permute-start(f32[16,8,256]{2,1,0:T(8,128)S(1)} %get-tuple-element.23), channel_id=1, source_target_pairs={{0,4},{1,29},{2,6},{3,31},{4,0},{5,9},{6,2},{7,11},{8,12},{9,5},{1... | collective-permute-start | bytes 393224 | tf_op jit(solution)/shard_map/ppermute | solution.py:21
  5.5 0.1 collective-permute-start.4
  5.7 0.0 copy-start.7
  5.7 0.7 %copy-done.7 = s32[32,256]{1,0:T(8,128)S(1)} copy-done((s32[32,256]{1,0:T(8,128)S(1)}, s32[32,256]{1,0:T(8,128)}, u32[]{:S(2)}) %copy-start.7) | copy-done | bytes 32792
  6.4 2.2 %first_steps.1 = (f32[33,6,16,256]{3,2,1,0:T(8,128)S(1)}, f32[4,4,16,256]{3,2,1,0:T(8,128)S(1)}, f32[32,4,16,256]{3,2,1,0:T(8,128)S(1)}, f32[1,32,256]{2,1,0:T(8,128)S(1)}) custom-call(f32[4,16,32,256]{3,2,1,0:T(8,128)S(1)} %copy-done, f32[16,32,256]{2,1,0:T(8,128)S(1)} %copy-done.1, f32[16,32,256]{2,1,0:T(8,128)S(1)} %copy-done.2, ...), custom_call_target="tpu_custom_call" | custom-call | flops 1000 | bytes 1000 | tf_op jit(solution)/shard_map/first_steps/pallas_call | solution.py:274
  8.6 5.1 %collective-permute-start.5 = (f32[16,16,256]{2,1,0:T(8,128)S(1)}, f32[16,16,256]{2,1,0:T(8,128)S(1)}, u32[]{:S(2)}, u32[]{:S(2)}) collective-permute-start(f32[16,16,256]{2,1,0:T(8,128)S(1)} %get-tuple-element.32), channel_id=1, source_target_pairs={{0,28},{4,8},{8,4},{12,16},{16,12},{20,24},{24,20},{28,0},{1,29},{... | collective-permute-start | bytes 786440 | tf_op jit(solution)/shard_map/ppermute | solution.py:21
  13.7 0.0 collective-permute-start.3
  13.7 1.5 %collective-permute-start.2 = (f32[16,8,256]{2,1,0:T(8,128)S(1)}, f32[16,8,256]{2,1,0:T(8,128)S(1)}, u32[]{:S(2)}, u32[]{:S(2)}) collective-permute-start(f32[16,8,256]{2,1,0:T(8,128)S(1)} %collective-permute-done.refs_0_), channel_id=1, source_target_pairs={{0,2},{1,3},{2,0},{3,1},{4,6},{5,7},{6,4},{7,5},{8,10},{9,11},{10,... | collective-permute-start | bytes 393224 | tf_op jit(solution)/shard_map/ppermute | solution.py:21
  15.2 0.3 %collective-permute-start.1 = (f32[16,8,256]{2,1,0:T(8,128)S(1)}, f32[16,8,256]{2,1,0:T(8,128)S(1)}, u32[]{:S(2)}, u32[]{:S(2)}) collective-permute-start(f32[16,8,256]{2,1,0:T(8,128)S(1)} %collective-permute-done.refs_0_), channel_id=1, source_target_pairs={{0,1},{1,0},{2,3},{3,2},{4,5},{5,4},{6,7},{7,6},{8,9},{9,8},{10,11... | collective-permute-start | bytes 393224 | tf_op jit(solution)/shard_map/ppermute | solution.py:21
  15.5 3.4 %inner_steps.1 = (f32[32,4,16,256]{3,2,1,0:T(8,128)S(1)}, f32[32,4,16,256]{3,2,1,0:T(8,128)S(1)}, f32[4264,128]{1,0:T(8,128)S(1)}, f32[4,32,256]{2,1,0:T(8,128)S(1)}) custom-call(f32[33,6,16,256]{3,2,1,0:T(8,128)S(1)} %get-tuple-element.22.coef, f32[32,4,16,256]{3,2,1,0:T(8,128)S(1)} %get-tuple-element.24.l1, s32[32,256]{1,0:T(8,128)S(1)} %copy-done.6, ...), custom_call_target="tpu_custom_call" | custom-call | flops 1000 | bytes 1000 | tf_op jit(solution)/shard_map/inner_steps/pallas_call | solution.py:308
  18.9 1.1 %write_inner.1.refs_1_ = f32[4,16,32,256]{3,2,1,0:T(8,128)} custom-call(f32[4264,128]{1,0:T(8,128)S(1)} %get-tuple-element.26.final.refs_0_), custom_call_target="tpu_custom_call" | custom-call | flops 1000 | bytes 1000 | tf_op jit(solution)/shard_map/write_inner/pallas_call | solution.py:538
  20.1 0.0 collective-permute-done.3.refs_3_
  20.1 2.2 %collective-permute-done.2.refs_2_ = f32[16,8,256]{2,1,0:T(8,128)S(1)} collective-permute-done((f32[16,8,256]{2,1,0:T(8,128)S(1)}, f32[16,8,256]{2,1,0:T(8,128)S(1)}, u32[]{:S(2)}, u32[]{:S(2)}) %collective-permute-start.2) | collective-permute-done | bytes 131104 | tf_op jit(solution)/shard_map/ppermute | solution.py:21
  22.3 0.1 outer_coefs.1.wide
  22.4 0.0 collective-permute-done.4.first
  22.4 0.0 collective-permute-done.5.second
  22.4 0.7 %border_low_levels.1 = f32[32,256]{1,0:T(8,128)S(1)} custom-call(s32[32,256]{1,0:T(8,128)S(1)} %copy-done.6, f32[33,6,16,256]{3,2,1,0:T(8,128)S(1)} %get-tuple-element.22.coef, f32[2,7,6,16,256]{4,3,2,1,0:T(8,128)S(1)} %outer_coefs.1.wide, f32[4,4,16,256]{3,2,1,0:T(8,128)S(1)} %get-tuple-element.28.l0, f32[32,4,16,256]{3,2,1,0:T(8,128)S(1)} %get-tuple-element.24.l1, ...), custom_call_target="tpu_custom_call" | custom-call | flops 1000 | bytes 1000 | tf_op jit(solution)/shard_map/border_low_levels/pallas_call | solution.py:440
  23.1 0.4 %collective-permute-start.8 = (f32[32,256]{1,0:T(8,128)S(1)}, f32[32,256]{1,0:T(8,128)S(1)}, u32[]{:S(2)}, u32[]{:S(2)}) collective-permute-start(f32[32,256]{1,0:T(8,128)S(1)} %border_low_levels.1), channel_id=1, source_target_pairs={{0,3},{1,2},{2,1},{3,0},{4,7},{5,6},{6,5},{7,4},{8,11},{9,10},{10,... | collective-permute-start | bytes 98312 | tf_op jit(solution)/shard_map/ppermute | solution.py:21
  23.5 1.3 %collective-permute-start.7 = (f32[32,256]{1,0:T(8,128)S(1)}, f32[32,256]{1,0:T(8,128)S(1)}, u32[]{:S(2)}, u32[]{:S(2)}) collective-permute-start(f32[32,256]{1,0:T(8,128)S(1)} %border_low_levels.1), channel_id=1, source_target_pairs={{0,2},{1,3},{2,0},{3,1},{4,6},{5,7},{6,4},{7,5},{8,10},{9,11},{10,... | collective-permute-start | bytes 98312 | tf_op jit(solution)/shard_map/ppermute | solution.py:21
  24.8 0.2 collective-permute-start.6
  25.0 2.3 %border_all_levels.1 = (f32[4264,128]{1,0:T(8,128)S(1)}, f32[4,16,32,256]{3,2,1,0:T(8,128)}) custom-call(f32[33,6,16,256]{3,2,1,0:T(8,128)S(1)} %get-tuple-element.22.coef, f32[2,7,6,16,256]{4,3,2,1,0:T(8,128)S(1)} %outer_coefs.1.wide, f32[4,4,16,256]{3,2,1,0:T(8,128)S(1)} %get-tuple-element.28.l0, ...), custom_call_target="tpu_custom_call", output_to_operand_aliasing={{0}: (8, {}), {1}: (9, {})} | custom-call | flops 1000 | bytes 1000 | tf_op jit(solution)/shard_map/border_all_levels/pallas_call | solution.py:494
  27.4 0.2 collective-permute-done.7
  27.6 0.6 %add_add_fusion = f32[32,256]{1,0:T(8,128)} fusion(f32[32,256]{1,0:T(8,128)S(1)} %collective-permute-done.8, f32[32,256]{1,0:T(8,128)S(1)} %collective-permute-done.7, f32[32,256]{1,0:T(8,128)S(1)} %border_low_levels.1, f32[32,256]{1,0:T(8,128)S(1)} %collective-permute-done.6), kind=kLoop, calls=%fused_computation | loop fusion | flops 24576 | bytes 163840 | tf_op jit(solution)/shard_map/add | solution.py:584
  (18 shorter events, 0.0 us)
Async XLA Ops:
  0.6 5.0 %copy-start.5 = (f32[16,32,256]{2,1,0:T(8,128)S(1)}, f32[16,32,256]{2,1,0:T(8,128)}, u32[]{:S(2)}) copy-start(f32[16,32,256]{2,1,0:T(8,128)} %mf.3) | copy-start | bytes 1572868
  0.6 5.0 %copy-start.4 = (f32[16,32,256]{2,1,0:T(8,128)S(1)}, f32[16,32,256]{2,1,0:T(8,128)}, u32[]{:S(2)}) copy-start(f32[16,32,256]{2,1,0:T(8,128)} %nd.3) | copy-start | bytes 1572868
  0.7 5.0 %copy-start.2 = (f32[16,32,256]{2,1,0:T(8,128)S(1)}, f32[16,32,256]{2,1,0:T(8,128)}, u32[]{:S(2)}) copy-start(f32[16,32,256]{2,1,0:T(8,128)} %ed.3) | copy-start | bytes 1572868
  0.7 5.0 %copy-start.3 = (f32[16,32,256]{2,1,0:T(8,128)S(1)}, f32[16,32,256]{2,1,0:T(8,128)}, u32[]{:S(2)}) copy-start(f32[16,32,256]{2,1,0:T(8,128)} %nw.3) | copy-start | bytes 1572868
  0.7 5.0 %copy-start.1 = (f32[16,32,256]{2,1,0:T(8,128)S(1)}, f32[16,32,256]{2,1,0:T(8,128)}, u32[]{:S(2)}) copy-start(f32[16,32,256]{2,1,0:T(8,128)} %ew.3) | copy-start | bytes 1572868
  0.7 5.0 %copy-start = (f32[4,16,32,256]{3,2,1,0:T(8,128)S(1)}, f32[4,16,32,256]{3,2,1,0:T(8,128)}, u32[]{:S(2)}) copy-start(f32[4,16,32,256]{3,2,1,0:T(8,128)} %lam.3) | copy-start | bytes 6291460
  0.7 5.0 %copy-start.6 = (s32[32,256]{1,0:T(8,128)S(1)}, s32[32,256]{1,0:T(8,128)}, u32[]{:S(2)}) copy-start(s32[32,256]{1,0:T(8,128)} %region.5) | copy-start | bytes 98308
  2.5 11.1 %collective-permute-start = (f32[16,8,256]{2,1,0:T(8,128)S(1)}, f32[16,8,256]{2,1,0:T(8,128)S(1)}, u32[]{:S(2)}, u32[]{:S(2)}) collective-permute-start(f32[16,8,256]{2,1,0:T(8,128)S(1)} %get-tuple-element.23), channel_id=1, source_target_pairs={{0,4},{1,29},{2,6},{3,31},{4,0},{5,9},{6,2},{7,11},{8,12},{9,5},{1... | collective-permute-start | bytes 393224 | tf_op jit(solution)/shard_map/ppermute | solution.py:21
  5.5 16.8 %collective-permute-start.4 = (f32[16,16,256]{2,1,0:T(8,128)S(1)}, f32[16,16,256]{2,1,0:T(8,128)S(1)}, u32[]{:S(2)}, u32[]{:S(2)}) collective-permute-start(f32[16,16,256]{2,1,0:T(8,128)S(1)} %get-tuple-element.31), channel_id=1, source_target_pairs={{0,4},{4,0},{8,12},{12,8},{16,20},{20,16},{24,28},{28,24},{1,5},{5... | collective-permute-start | bytes 786440 | tf_op jit(solution)/shard_map/ppermute | solution.py:21
  5.7 0.8 %copy-start.7 = (s32[32,256]{1,0:T(8,128)S(1)}, s32[32,256]{1,0:T(8,128)}, u32[]{:S(2)}) copy-start(s32[32,256]{1,0:T(8,128)} %top.3) | copy-start | bytes 98308
  8.6 13.8 %collective-permute-start.5 = (f32[16,16,256]{2,1,0:T(8,128)S(1)}, f32[16,16,256]{2,1,0:T(8,128)S(1)}, u32[]{:S(2)}, u32[]{:S(2)}) collective-permute-start(f32[16,16,256]{2,1,0:T(8,128)S(1)} %get-tuple-element.32), channel_id=1, source_target_pairs={{0,28},{4,8},{8,4},{12,16},{16,12},{20,24},{24,20},{28,0},{1,29},{... | collective-permute-start | bytes 786440 | tf_op jit(solution)/shard_map/ppermute | solution.py:21
  13.7 6.4 %collective-permute-start.3 = (f32[16,8,256]{2,1,0:T(8,128)S(1)}, f32[16,8,256]{2,1,0:T(8,128)S(1)}, u32[]{:S(2)}, u32[]{:S(2)}) collective-permute-start(f32[16,8,256]{2,1,0:T(8,128)S(1)} %collective-permute-done.refs_0_), channel_id=1, source_target_pairs={{0,3},{1,2},{2,1},{3,0},{4,7},{5,6},{6,5},{7,4},{8,11},{9,10},{10,... | collective-permute-start | bytes 393224 | tf_op jit(solution)/shard_map/ppermute | solution.py:21
  13.7 8.6 %collective-permute-start.2 = (f32[16,8,256]{2,1,0:T(8,128)S(1)}, f32[16,8,256]{2,1,0:T(8,128)S(1)}, u32[]{:S(2)}, u32[]{:S(2)}) collective-permute-start(f32[16,8,256]{2,1,0:T(8,128)S(1)} %collective-permute-done.refs_0_), channel_id=1, source_target_pairs={{0,2},{1,3},{2,0},{3,1},{4,6},{5,7},{6,4},{7,5},{8,10},{9,11},{10,... | collective-permute-start | bytes 393224 | tf_op jit(solution)/shard_map/ppermute | solution.py:21
  15.2 7.1 %collective-permute-start.1 = (f32[16,8,256]{2,1,0:T(8,128)S(1)}, f32[16,8,256]{2,1,0:T(8,128)S(1)}, u32[]{:S(2)}, u32[]{:S(2)}) collective-permute-start(f32[16,8,256]{2,1,0:T(8,128)S(1)} %collective-permute-done.refs_0_), channel_id=1, source_target_pairs={{0,1},{1,0},{2,3},{3,2},{4,5},{5,4},{6,7},{7,6},{8,9},{9,8},{10,11... | collective-permute-start | bytes 393224 | tf_op jit(solution)/shard_map/ppermute | solution.py:21
  23.1 4.3 %collective-permute-start.8 = (f32[32,256]{1,0:T(8,128)S(1)}, f32[32,256]{1,0:T(8,128)S(1)}, u32[]{:S(2)}, u32[]{:S(2)}) collective-permute-start(f32[32,256]{1,0:T(8,128)S(1)} %border_low_levels.1), channel_id=1, source_target_pairs={{0,3},{1,2},{2,1},{3,0},{4,7},{5,6},{6,5},{7,4},{8,11},{9,10},{10,... | collective-permute-start | bytes 98312 | tf_op jit(solution)/shard_map/ppermute | solution.py:21
  23.5 4.1 %collective-permute-start.7 = (f32[32,256]{1,0:T(8,128)S(1)}, f32[32,256]{1,0:T(8,128)S(1)}, u32[]{:S(2)}, u32[]{:S(2)}) collective-permute-start(f32[32,256]{1,0:T(8,128)S(1)} %border_low_levels.1), channel_id=1, source_target_pairs={{0,2},{1,3},{2,0},{3,1},{4,6},{5,7},{6,4},{7,5},{8,10},{9,11},{10,... | collective-permute-start | bytes 98312 | tf_op jit(solution)/shard_map/ppermute | solution.py:21
  24.8 2.7 %collective-permute-start.6 = (f32[32,256]{1,0:T(8,128)S(1)}, f32[32,256]{1,0:T(8,128)S(1)}, u32[]{:S(2)}, u32[]{:S(2)}) collective-permute-start(f32[32,256]{1,0:T(8,128)S(1)} %border_low_levels.1), channel_id=1, source_target_pairs={{0,1},{1,0},{2,3},{3,2},{4,5},{5,4},{6,7},{7,6},{8,9},{9,8},{10,11... | collective-permute-start | bytes 98312 | tf_op jit(solution)/shard_map/ppermute | solution.py:21

commit v21 on v20

--- a/solution.py
+++ b/solution.py
@@ -81,8 +81,8 @@
 
 
 def pack_kernel(lam, ew, ed, nw, nd, mf, top, *refs):
-    coef_send, lam_first, lam_second = refs[:3]
-    field_s, top_s, lam_s, coef_p, lam_p, sems = refs[3:]
+    coef_send, lam_first, lam_second, top_v = refs[:4]
+    field_s, lam_s, coef_p, lam_p, sems = refs[4:]
     tags, levels, cols, lats = lam.shape
     per = levels // 2
     rank = lax.axis_index("grp")
@@ -97,7 +97,7 @@
 
     for f, field in enumerate((ew, ed, nw, nd, mf)):
         copy(field.at[pl.ds(base, per), edge], field_s.at[f])
-    copy(top.at[edge], top_s)
+    copy(top, top_v)
     for side, at in ((LOW, 0), (HIGH, cols - 8)):
         for tag in range(tags):
             copy(lam.at[tag, :, pl.ds(at, 8)], lam_s.at[side, tag])
@@ -112,7 +112,7 @@
             i = pair * 2 + half
             level = base + i
             ew, ed, nw, nd, mf = (field_s[f, i] for f in range(5))
-            lift = jnp.where((level < top_s[...]) & (level < levels - 1), mf, 0.0)
+            lift = jnp.where((level < top_v[edge]) & (level < levels - 1), mf, 0.0)
             for j, value in enumerate((*faces(ew, ed, nw, nd), lift)):
                 for k in range(2):
                     at = (j * 2 + k) * few + i * pitch
@@ -159,11 +159,10 @@
     return pl.pallas_call(
         pack_kernel,
         in_specs=[hbm] * 7,
-        out_specs=[pl.BlockSpec(memory_space=pltpu.VMEM)] * 3,
-        out_shape=[coef_send, lam_send, lam_send],
+        out_specs=[pl.BlockSpec(memory_space=pltpu.VMEM)] * 4,
+        out_shape=[coef_send, lam_send, lam_send, pltpu.VMEM((cols, lats), jnp.int32)],
         scratch_shapes=[
             pltpu.VMEM((5, per, 8, lats), jnp.float32),
-            pltpu.VMEM((8, lats), jnp.int32),
             pltpu.VMEM((2, tags, levels, 8, lats), jnp.float32),
             pltpu.VMEM((pitched(10, per, 8), LANES), jnp.float32),
             pltpu.VMEM((pitched(4 * tags, levels, 8), LANES), jnp.float32),
@@ -557,7 +556,7 @@
 
     pairs = lambda i: i ^ 1
     turn = lambda i: (((i - 1) % tiles ^ 1) + 1) % tiles
-    coefs, first, second = pack(far[0], far[1:6], far[6])
+    coefs, first, second, top = pack(far[0], far[1:6], far[6])
 
     def partner(i):
         tile, rank = divmod(i, groups)

time: 28.4 us -> 30.8 us (1.085)
  the two profiles are of different devices: /device:TPU:0 before, /device:TPU:25 now
where the time goes in v21:
time: 30.8 us; the launch traced here: 30.6 us
  starting transfers between devices  15.3 us (50%)
  Pallas kernels  11.7 us (38%)
  waiting for transfers between devices  2.09 us (7%)
  between operations  0.83 us (3%)
  other arithmetic  0.63 us (2%)
    ppermute x9, starting transfers between devices, swapped(): lax.ppermute(value, axis, [(i, partner(i)) for i in range(lax.axis_size(a...  15.3 us
    pallas_call x1, Pallas kernels, inner(): pl.pallas_call(inner_kernel, in_specs=[vmem] * 4, out_specs=[vmem] * 4, o...  3.42 us
    pallas_call x1, Pallas kernels, border(): pl.pallas_call(border_kernel, in_specs=[vmem] * (n + 1) + [hbm], out_spec...  2.35 us
    pallas_call x1, Pallas kernels, prepare(): pl.pallas_call(prepare_kernel, in_specs=[vmem] * 8, out_specs=[vmem] * 4,...  2.18 us
    ppermute x9, waiting for transfers between devices, swapped(): lax.ppermute(value, axis, [(i, partner(i)) for i in range(lax.axis_size(a...  2.09 us
    pallas_call x1, Pallas kernels, pack(): pl.pallas_call(pack_kernel, in_specs=[hbm] * 7, out_specs=[pl.BlockSpec(m...  1.83 us
    pallas_call x1, Pallas kernels, write_inner(): pl.pallas_call(write_kernel, in_specs=[pl.BlockSpec(memory_space=pltpu.VM...  1.14 us
    pallas_call x1, Pallas kernels, gradient(): pl.pallas_call(low_kernel, in_specs=[vmem] * len(operands), out_specs=vme...  0.72 us
  transfers between devices with their start and end apart: 9, of which 2 were waited for; matrix products, arithmetic and copies ran while one was open for 0% of the time, Pallas kernels for 30%

profile of v21, /device:TPU:25, one launch (start us, length us, event | category | flops | bytes accessed | tf_op | source)
XLA Modules:
  0.0 30.6 jit_solution(11208331577379912596)
XLA Ops:
  0.7 1.8 %pack_edges.1 = (f32[16,8,256]{2,1,0:T(8,128)S(1)}, f32[16,16,256]{2,1,0:T(8,128)S(1)}, f32[16,16,256]{2,1,0:T(8,128)S(1)}, s32[32,256]{1,0:T(8,128)S(1)}) custom-call(f32[4,16,32,256]{3,2,1,0:T(8,128)} %lam.3, f32[16,32,256]{2,1,0:T(8,128)} %ew.3, f32[16,32,256]{2,1,0:T(8,128)} %ed.3, f32[16,32,256]{2,1,0:T(8,128)} %nw.3, f32[16,32,256]{2,1,0:T(8,128)} %nd.3, ...), custom_call_target="tpu_custom_call" | custom-call | flops 1000 | bytes 1000 | tf_op jit(solution)/shard_map/pack_edges/pallas_call | solution.py:159
  2.5 1.2 %collective-permute-start = (f32[16,8,256]{2,1,0:T(8,128)S(1)}, f32[16,8,256]{2,1,0:T(8,128)S(1)}, u32[]{:S(2)}, u32[]{:S(2)}) collective-permute-start(f32[16,8,256]{2,1,0:T(8,128)S(1)} %get-tuple-element.25), channel_id=1, source_target_pairs={{0,4},{1,29},{2,6},{3,31},{4,0},{5,9},{6,2},{7,11},{8,12},{9,5},{1... | collective-permute-start | bytes 393224 | tf_op jit(solution)/shard_map/ppermute | solution.py:21
  3.7 0.2 collective-permute-start.4
  3.9 2.2 %first_steps.1 = (f32[33,6,16,256]{3,2,1,0:T(8,128)S(1)}, f32[4,4,16,256]{3,2,1,0:T(8,128)S(1)}, f32[32,4,16,256]{3,2,1,0:T(8,128)S(1)}, f32[1,32,256]{2,1,0:T(8,128)S(1)}) custom-call(f32[4,16,32,256]{3,2,1,0:T(8,128)S(1)} %copy-done, f32[16,32,256]{2,1,0:T(8,128)S(1)} %copy-done.1, f32[16,32,256]{2,1,0:T(8,128)S(1)} %copy-done.2, ...), custom_call_target="tpu_custom_call" | custom-call | flops 1000 | bytes 1000 | tf_op jit(solution)/shard_map/first_steps/pallas_call | solution.py:273
  6.1 1.2 %collective-permute-start.5 = (f32[16,16,256]{2,1,0:T(8,128)S(1)}, f32[16,16,256]{2,1,0:T(8,128)S(1)}, u32[]{:S(2)}, u32[]{:S(2)}) collective-permute-start(f32[16,16,256]{2,1,0:T(8,128)S(1)} %get-tuple-element.34), channel_id=1, source_target_pairs={{0,28},{4,8},{8,4},{12,16},{16,12},{20,24},{24,20},{28,0},{1,29},{... | collective-permute-start | bytes 786440 | tf_op jit(solution)/shard_map/ppermute | solution.py:21
  7.4 0.1 collective-permute-done.refs_0_
  7.4 10.1 %collective-permute-start.3 = (f32[16,8,256]{2,1,0:T(8,128)S(1)}, f32[16,8,256]{2,1,0:T(8,128)S(1)}, u32[]{:S(2)}, u32[]{:S(2)}) collective-permute-start(f32[16,8,256]{2,1,0:T(8,128)S(1)} %collective-permute-done.refs_0_), channel_id=1, source_target_pairs={{0,3},{1,2},{2,1},{3,0},{4,7},{5,6},{6,5},{7,4},{8,11},{9,10},{10,... | collective-permute-start | bytes 393224 | tf_op jit(solution)/shard_map/ppermute | solution.py:21
  17.6 0.2 collective-permute-start.2
  17.8 0.2 collective-permute-start.1
  18.0 3.4 %inner_steps.1 = (f32[32,4,16,256]{3,2,1,0:T(8,128)S(1)}, f32[32,4,16,256]{3,2,1,0:T(8,128)S(1)}, f32[4264,128]{1,0:T(8,128)S(1)}, f32[4,32,256]{2,1,0:T(8,128)S(1)}) custom-call(f32[33,6,16,256]{3,2,1,0:T(8,128)S(1)} %get-tuple-element.24.coef, f32[32,4,16,256]{3,2,1,0:T(8,128)S(1)} %get-tuple-element.26.l1, s32[32,256]{1,0:T(8,128)S(1)} %copy-done.6, ...), custom_call_target="tpu_custom_call" | custom-call | flops 1000 | bytes 1000 | tf_op jit(solution)/shard_map/inner_steps/pallas_call | solution.py:307
  21.4 1.1 %write_inner.1.refs_1_ = f32[4,16,32,256]{3,2,1,0:T(8,128)} custom-call(f32[4264,128]{1,0:T(8,128)S(1)} %get-tuple-element.28.final.refs_0_), custom_call_target="tpu_custom_call" | custom-call | flops 1000 | bytes 1000 | tf_op jit(solution)/shard_map/write_inner/pallas_call | solution.py:537
  22.6 0.0 collective-permute-done.3.refs_3_
  22.6 2.0 %collective-permute-done.2.refs_2_ = f32[16,8,256]{2,1,0:T(8,128)S(1)} collective-permute-done((f32[16,8,256]{2,1,0:T(8,128)S(1)}, f32[16,8,256]{2,1,0:T(8,128)S(1)}, u32[]{:S(2)}, u32[]{:S(2)}) %collective-permute-start.2) | collective-permute-done | bytes 131104 | tf_op jit(solution)/shard_map/ppermute | solution.py:21
  24.6 0.0 collective-permute-done.1.refs_1_
  24.6 0.1 outer_coefs.1.wide
  24.7 0.0 collective-permute-done.4.first
  24.7 0.0 collective-permute-done.5.second
  24.7 0.7 %border_low_levels.1 = f32[32,256]{1,0:T(8,128)S(1)} custom-call(s32[32,256]{1,0:T(8,128)S(1)} %copy-done.6, f32[33,6,16,256]{3,2,1,0:T(8,128)S(1)} %get-tuple-element.24.coef, f32[2,7,6,16,256]{4,3,2,1,0:T(8,128)S(1)} %outer_coefs.1.wide, f32[4,4,16,256]{3,2,1,0:T(8,128)S(1)} %get-tuple-element.30.l0, f32[32,4,16,256]{3,2,1,0:T(8,128)S(1)} %get-tuple-element.26.l1, ...), custom_call_target="tpu_custom_call" | custom-call | flops 1000 | bytes 1000 | tf_op jit(solution)/shard_map/border_low_levels/pallas_call | solution.py:439
  25.4 0.1 collective-permute-start.8
  25.5 1.8 %collective-permute-start.7 = (f32[32,256]{1,0:T(8,128)S(1)}, f32[32,256]{1,0:T(8,128)S(1)}, u32[]{:S(2)}, u32[]{:S(2)}) collective-permute-start(f32[32,256]{1,0:T(8,128)S(1)} %border_low_levels.1), channel_id=1, source_target_pairs={{0,2},{1,3},{2,0},{3,1},{4,6},{5,7},{6,4},{7,5},{8,10},{9,11},{10,... | collective-permute-start | bytes 98312 | tf_op jit(solution)/shard_map/ppermute | solution.py:21
  27.3 0.3 %collective-permute-start.6 = (f32[32,256]{1,0:T(8,128)S(1)}, f32[32,256]{1,0:T(8,128)S(1)}, u32[]{:S(2)}, u32[]{:S(2)}) collective-permute-start(f32[32,256]{1,0:T(8,128)S(1)} %border_low_levels.1), channel_id=1, source_target_pairs={{0,1},{1,0},{2,3},{3,2},{4,5},{5,4},{6,7},{7,6},{8,9},{9,8},{10,11... | collective-permute-start | bytes 98312 | tf_op jit(solution)/shard_map/ppermute | solution.py:21
  27.6 2.3 %border_all_levels.1 = (f32[4264,128]{1,0:T(8,128)S(1)}, f32[4,16,32,256]{3,2,1,0:T(8,128)}) custom-call(f32[33,6,16,256]{3,2,1,0:T(8,128)S(1)} %get-tuple-element.24.coef, f32[2,7,6,16,256]{4,3,2,1,0:T(8,128)S(1)} %outer_coefs.1.wide, f32[4,4,16,256]{3,2,1,0:T(8,128)S(1)} %get-tuple-element.30.l0, ...), custom_call_target="tpu_custom_call", output_to_operand_aliasing={{0}: (8, {}), {1}: (9, {})} | custom-call | flops 1000 | bytes 1000 | tf_op jit(solution)/shard_map/border_all_levels/pallas_call | solution.py:493
  30.0 0.0 collective-permute-done.6
  30.0 0.6 %add_add_fusion = f32[32,256]{1,0:T(8,128)} fusion(f32[32,256]{1,0:T(8,128)S(1)} %collective-permute-done.8, f32[32,256]{1,0:T(8,128)S(1)} %collective-permute-done.7, f32[32,256]{1,0:T(8,128)S(1)} %border_low_levels.1, f32[32,256]{1,0:T(8,128)S(1)} %collective-permute-done.6), kind=kLoop, calls=%fused_computation | loop fusion | flops 24576 | bytes 163840 | tf_op jit(solution)/shard_map/add | solution.py:583
  (16 shorter events, 0.0 us)
Async XLA Ops:
  0.6 3.3 %copy-start.5 = (f32[16,32,256]{2,1,0:T(8,128)S(1)}, f32[16,32,256]{2,1,0:T(8,128)}, u32[]{:S(2)}) copy-start(f32[16,32,256]{2,1,0:T(8,128)} %mf.3) | copy-start | bytes 1572868
  0.6 3.3 %copy-start.4 = (f32[16,32,256]{2,1,0:T(8,128)S(1)}, f32[16,32,256]{2,1,0:T(8,128)}, u32[]{:S(2)}) copy-start(f32[16,32,256]{2,1,0:T(8,128)} %nd.3) | copy-start | bytes 1572868
  0.7 3.3 %copy-start.2 = (f32[16,32,256]{2,1,0:T(8,128)S(1)}, f32[16,32,256]{2,1,0:T(8,128)}, u32[]{:S(2)}) copy-start(f32[16,32,256]{2,1,0:T(8,128)} %ed.3) | copy-start | bytes 1572868
  0.7 3.2 %copy-start.3 = (f32[16,32,256]{2,1,0:T(8,128)S(1)}, f32[16,32,256]{2,1,0:T(8,128)}, u32[]{:S(2)}) copy-start(f32[16,32,256]{2,1,0:T(8,128)} %nw.3) | copy-start | bytes 1572868
  0.7 3.2 %copy-start.1 = (f32[16,32,256]{2,1,0:T(8,128)S(1)}, f32[16,32,256]{2,1,0:T(8,128)}, u32[]{:S(2)}) copy-start(f32[16,32,256]{2,1,0:T(8,128)} %ew.3) | copy-start | bytes 1572868
  0.7 3.2 %copy-start = (f32[4,16,32,256]{3,2,1,0:T(8,128)S(1)}, f32[4,16,32,256]{3,2,1,0:T(8,128)}, u32[]{:S(2)}) copy-start(f32[4,16,32,256]{3,2,1,0:T(8,128)} %lam.3) | copy-start | bytes 6291460
  0.7 3.2 %copy-start.6 = (s32[32,256]{1,0:T(8,128)S(1)}, s32[32,256]{1,0:T(8,128)}, u32[]{:S(2)}) copy-start(s32[32,256]{1,0:T(8,128)} %region.5) | copy-start | bytes 98308
  2.5 4.9 %collective-permute-start = (f32[16,8,256]{2,1,0:T(8,128)S(1)}, f32[16,8,256]{2,1,0:T(8,128)S(1)}, u32[]{:S(2)}, u32[]{:S(2)}) collective-permute-start(f32[16,8,256]{2,1,0:T(8,128)S(1)} %get-tuple-element.25), channel_id=1, source_target_pairs={{0,4},{1,29},{2,6},{3,31},{4,0},{5,9},{6,2},{7,11},{8,12},{9,5},{1... | collective-permute-start | bytes 393224 | tf_op jit(solution)/shard_map/ppermute | solution.py:21
  3.7 21.0 %collective-permute-start.4 = (f32[16,16,256]{2,1,0:T(8,128)S(1)}, f32[16,16,256]{2,1,0:T(8,128)S(1)}, u32[]{:S(2)}, u32[]{:S(2)}) collective-permute-start(f32[16,16,256]{2,1,0:T(8,128)S(1)} %get-tuple-element.33), channel_id=1, source_target_pairs={{0,4},{4,0},{8,12},{12,8},{16,20},{20,16},{24,28},{28,24},{1,5},{5... | collective-permute-start | bytes 786440 | tf_op jit(solution)/shard_map/ppermute | solution.py:21
  6.1 18.6 %collective-permute-start.5 = (f32[16,16,256]{2,1,0:T(8,128)S(1)}, f32[16,16,256]{2,1,0:T(8,128)S(1)}, u32[]{:S(2)}, u32[]{:S(2)}) collective-permute-start(f32[16,16,256]{2,1,0:T(8,128)S(1)} %get-tuple-element.34), channel_id=1, source_target_pairs={{0,28},{4,8},{8,4},{12,16},{16,12},{20,24},{24,20},{28,0},{1,29},{... | collective-permute-start | bytes 786440 | tf_op jit(solution)/shard_map/ppermute | solution.py:21
  7.4 15.1 %collective-permute-start.3 = (f32[16,8,256]{2,1,0:T(8,128)S(1)}, f32[16,8,256]{2,1,0:T(8,128)S(1)}, u32[]{:S(2)}, u32[]{:S(2)}) collective-permute-start(f32[16,8,256]{2,1,0:T(8,128)S(1)} %collective-permute-done.refs_0_), channel_id=1, source_target_pairs={{0,3},{1,2},{2,1},{3,0},{4,7},{5,6},{6,5},{7,4},{8,11},{9,10},{10,... | collective-permute-start | bytes 393224 | tf_op jit(solution)/shard_map/ppermute | solution.py:21
  17.6 7.0 %collective-permute-start.2 = (f32[16,8,256]{2,1,0:T(8,128)S(1)}, f32[16,8,256]{2,1,0:T(8,128)S(1)}, u32[]{:S(2)}, u32[]{:S(2)}) collective-permute-start(f32[16,8,256]{2,1,0:T(8,128)S(1)} %collective-permute-done.refs_0_), channel_id=1, source_target_pairs={{0,2},{1,3},{2,0},{3,1},{4,6},{5,7},{6,4},{7,5},{8,10},{9,11},{10,... | collective-permute-start | bytes 393224 | tf_op jit(solution)/shard_map/ppermute | solution.py:21
  17.8 6.8 %collective-permute-start.1 = (f32[16,8,256]{2,1,0:T(8,128)S(1)}, f32[16,8,256]{2,1,0:T(8,128)S(1)}, u32[]{:S(2)}, u32[]{:S(2)}) collective-permute-start(f32[16,8,256]{2,1,0:T(8,128)S(1)} %collective-permute-done.refs_0_), channel_id=1, source_target_pairs={{0,1},{1,0},{2,3},{3,2},{4,5},{5,4},{6,7},{7,6},{8,9},{9,8},{10,11... | collective-permute-start | bytes 393224 | tf_op jit(solution)/shard_map/ppermute | solution.py:21
  25.4 4.6 %collective-permute-start.8 = (f32[32,256]{1,0:T(8,128)S(1)}, f32[32,256]{1,0:T(8,128)S(1)}, u32[]{:S(2)}, u32[]{:S(2)}) collective-permute-start(f32[32,256]{1,0:T(8,128)S(1)} %border_low_levels.1), channel_id=1, source_target_pairs={{0,3},{1,2},{2,1},{3,0},{4,7},{5,6},{6,5},{7,4},{8,11},{9,10},{10,... | collective-permute-start | bytes 98312 | tf_op jit(solution)/shard_map/ppermute | solution.py:21
  25.5 4.5 %collective-permute-start.7 = (f32[32,256]{1,0:T(8,128)S(1)}, f32[32,256]{1,0:T(8,128)S(1)}, u32[]{:S(2)}, u32[]{:S(2)}) collective-permute-start(f32[32,256]{1,0:T(8,128)S(1)} %border_low_levels.1), channel_id=1, source_target_pairs={{0,2},{1,3},{2,0},{3,1},{4,6},{5,7},{6,4},{7,5},{8,10},{9,11},{10,... | collective-permute-start | bytes 98312 | tf_op jit(solution)/shard_map/ppermute | solution.py:21
  27.3 2.7 %collective-permute-start.6 = (f32[32,256]{1,0:T(8,128)S(1)}, f32[32,256]{1,0:T(8,128)S(1)}, u32[]{:S(2)}, u32[]{:S(2)}) collective-permute-start(f32[32,256]{1,0:T(8,128)S(1)} %border_low_levels.1), channel_id=1, source_target_pairs={{0,1},{1,0},{2,3},{3,2},{4,5},{5,4},{6,7},{7,6},{8,9},{9,8},{10,11... | collective-permute-start | bytes 98312 | tf_op jit(solution)/shard_map/ppermute | solution.py:21

commit v22 on v19

--- a/solution.py
+++ b/solution.py
@@ -11,7 +11,7 @@
 EDGE = ITERS
 ENTRIES = 16
 BLOCK = 4
-CHUNKS = 2
+CHUNKS = 1
 LANES = 128
 HALVES = (slice(0, LANES), slice(LANES, 2 * LANES))
 SHORT = pl.CostEstimate(flops=1000, bytes_accessed=1000, transcendentals=0)
@@ -81,8 +81,8 @@
 
 
 def pack_kernel(lam, ew, ed, nw, nd, mf, top, *refs):
-    coef_send, lam_first, lam_second = refs[:3]
-    field_s, top_s, lam_s, coef_p, lam_p, sems = refs[3:]
+    coef_send, lam_first, lam_second, top_v = refs[:4]
+    field_s, lam_s, coef_p, lam_p, sems = refs[4:]
     tags, levels, cols, lats = lam.shape
     per = levels // 2
     rank = lax.axis_index("grp")
@@ -97,7 +97,7 @@
 
     for f, field in enumerate((ew, ed, nw, nd, mf)):
         copy(field.at[pl.ds(base, per), edge], field_s.at[f])
-    copy(top.at[edge], top_s)
+    copy(top, top_v)
     for side, at in ((LOW, 0), (HIGH, cols - 8)):
         for tag in range(tags):
             copy(lam.at[tag, :, pl.ds(at, 8)], lam_s.at[side, tag])
@@ -112,7 +112,7 @@
             i = pair * 2 + half
             level = base + i
             ew, ed, nw, nd, mf = (field_s[f, i] for f in range(5))
-            lift = jnp.where((level < top_s[...]) & (level < levels - 1), mf, 0.0)
+            lift = jnp.where((level < top_v[edge]) & (level < levels - 1), mf, 0.0)
             for j, value in enumerate((*faces(ew, ed, nw, nd), lift)):
                 for k in range(2):
                     at = (j * 2 + k) * few + i * pitch
@@ -159,11 +159,10 @@
     return pl.pallas_call(
         pack_kernel,
         in_specs=[hbm] * 7,
-        out_specs=[pl.BlockSpec(memory_space=pltpu.VMEM)] * 3,
-        out_shape=[coef_send, lam_send, lam_send],
+        out_specs=[pl.BlockSpec(memory_space=pltpu.VMEM)] * 4,
+        out_shape=[coef_send, lam_send, lam_send, pltpu.VMEM((cols, lats), jnp.int32)],
         scratch_shapes=[
             pltpu.VMEM((5, per, 8, lats), jnp.float32),
-            pltpu.VMEM((8, lats), jnp.int32),
             pltpu.VMEM((2, tags, levels, 8, lats), jnp.float32),
             pltpu.VMEM((pitched(10, per, 8), LANES), jnp.float32),
             pltpu.VMEM((pitched(4 * tags, levels, 8), LANES), jnp.float32),
@@ -557,7 +556,7 @@
 
     pairs = lambda i: i ^ 1
     turn = lambda i: (((i - 1) % tiles ^ 1) + 1) % tiles
-    coefs, first, second = pack(far[0], far[1:6], far[6])
+    coefs, first, second, top = pack(far[0], far[1:6], far[6])
 
     def partner(i):
         tile, rank = divmod(i, groups)

time: 29.6 us -> 28.5 us (0.963)
  local copies, waits for them, and re-layouts: 0.78 us -> 0.03 us
  Pallas kernels: 11.7 us -> 11.2 us
    unnamed x16 -> x14, local copies, waits for them, and re-layouts: 0.78 us -> 0.03 us
where the time goes in v22:
time: 28.5 us; the launch traced here: 28.4 us
  starting transfers between devices  11.9 us (42%)
  Pallas kernels  11.2 us (39%)
  waiting for transfers between devices  3.81 us (13%)
  between operations  0.79 us (3%)
  other arithmetic  0.63 us (2%)
    ppermute x9, starting transfers between devices, swapped(): lax.ppermute(value, axis, [(i, partner(i)) for i in range(lax.axis_size(a...  11.9 us
    ppermute x9, waiting for transfers between devices, swapped(): lax.ppermute(value, axis, [(i, partner(i)) for i in range(lax.axis_size(a...  3.81 us
    pallas_call x1, Pallas kernels, prepare(): pl.pallas_call(prepare_kernel, in_specs=[vmem] * 8, out_specs=[vmem] * 5,...  3.13 us
    pallas_call x1, Pallas kernels, border(): pl.pallas_call(border_kernel, in_specs=[vmem] * (n + 1) + [hbm], out_spec...  2.33 us
    pallas_call x1, Pallas kernels, inner(): pl.pallas_call(inner_kernel, in_specs=[vmem] * 4, out_specs=[vmem] * 3, o...  1.98 us
    pallas_call x1, Pallas kernels, pack(): pl.pallas_call(pack_kernel, in_specs=[hbm] * 7, out_specs=[pl.BlockSpec(m...  1.83 us
    pallas_call x1, Pallas kernels, write_inner(): pl.pallas_call(write_kernel, in_specs=[pl.BlockSpec(memory_space=pltpu.VM...  1.14 us
    pallas_call x1, Pallas kernels, gradient(): pl.pallas_call(low_kernel, in_specs=[vmem] * len(operands), out_specs=vme...  0.72 us
  transfers between devices with their start and end apart: 9, of which 3 were waited for; matrix products, arithmetic and copies ran while one was open for 0% of the time, Pallas kernels for 31%

profile of v22, /device:TPU:0, one launch (start us, length us, event | category | flops | bytes accessed | tf_op | source)
XLA Modules:
  0.0 28.4 jit_solution(13399809261309851952)
XLA Ops:
  0.7 1.8 %pack_edges.1 = (f32[16,8,256]{2,1,0:T(8,128)S(1)}, f32[16,16,256]{2,1,0:T(8,128)S(1)}, f32[16,16,256]{2,1,0:T(8,128)S(1)}, s32[32,256]{1,0:T(8,128)S(1)}) custom-call(f32[4,16,32,256]{3,2,1,0:T(8,128)} %lam.3, f32[16,32,256]{2,1,0:T(8,128)} %ew.3, f32[16,32,256]{2,1,0:T(8,128)} %ed.3, f32[16,32,256]{2,1,0:T(8,128)} %nw.3, f32[16,32,256]{2,1,0:T(8,128)} %nd.3, ...), custom_call_target="tpu_custom_call" | custom-call | flops 1000 | bytes 1000 | tf_op jit(solution)/shard_map/pack_edges/pallas_call | solution.py:159
  2.5 3.0 %collective-permute-start = (f32[16,8,256]{2,1,0:T(8,128)S(1)}, f32[16,8,256]{2,1,0:T(8,128)S(1)}, u32[]{:S(2)}, u32[]{:S(2)}) collective-permute-start(f32[16,8,256]{2,1,0:T(8,128)S(1)} %get-tuple-element.25), channel_id=1, source_target_pairs={{0,4},{1,29},{2,6},{3,31},{4,0},{5,9},{6,2},{7,11},{8,12},{9,5},{1... | collective-permute-start | bytes 393224 | tf_op jit(solution)/shard_map/ppermute | solution.py:21
  5.5 0.1 collective-permute-start.4
  5.7 3.1 %first_steps.1 = (f32[33,6,16,256]{3,2,1,0:T(8,128)S(1)}, f32[4,4,16,256]{3,2,1,0:T(8,128)S(1)}, f32[32,4,16,256]{3,2,1,0:T(8,128)S(1)}, f32[32,4,16,256]{3,2,1,0:T(8,128)S(1)}, f32[2,32,256]{2,1,0:T(8,128)S(1)}) custom-call(f32[4,16,32,256]{3,2,1,0:T(8,128)S(1)} %copy-done, f32[16,32,256]{2,1,0:T(8,128)S(1)} %copy-done.1, f32[16,32,256]{2,1,0:T(8,128)S(1)} %copy-done.2, ...), custom_call_target="tpu_custom_call" | custom-call | flops 1000 | bytes 1000 | tf_op jit(solution)/shard_map/first_steps/pallas_call | solution.py:274
  8.8 5.1 %collective-permute-start.5 = (f32[16,16,256]{2,1,0:T(8,128)S(1)}, f32[16,16,256]{2,1,0:T(8,128)S(1)}, u32[]{:S(2)}, u32[]{:S(2)}) collective-permute-start(f32[16,16,256]{2,1,0:T(8,128)S(1)} %get-tuple-element.34), channel_id=1, source_target_pairs={{0,28},{4,8},{8,4},{12,16},{16,12},{20,24},{24,20},{28,0},{1,29},{... | collective-permute-start | bytes 786440 | tf_op jit(solution)/shard_map/ppermute | solution.py:21
  13.9 0.0 collective-permute-done.refs_0_
  13.9 0.0 collective-permute-start.3
  13.9 1.5 %collective-permute-start.2 = (f32[16,8,256]{2,1,0:T(8,128)S(1)}, f32[16,8,256]{2,1,0:T(8,128)S(1)}, u32[]{:S(2)}, u32[]{:S(2)}) collective-permute-start(f32[16,8,256]{2,1,0:T(8,128)S(1)} %collective-permute-done.refs_0_), channel_id=1, source_target_pairs={{0,2},{1,3},{2,0},{3,1},{4,6},{5,7},{6,4},{7,5},{8,10},{9,11},{10,... | collective-permute-start | bytes 393224 | tf_op jit(solution)/shard_map/ppermute | solution.py:21
  15.4 0.3 %collective-permute-start.1 = (f32[16,8,256]{2,1,0:T(8,128)S(1)}, f32[16,8,256]{2,1,0:T(8,128)S(1)}, u32[]{:S(2)}, u32[]{:S(2)}) collective-permute-start(f32[16,8,256]{2,1,0:T(8,128)S(1)} %collective-permute-done.refs_0_), channel_id=1, source_target_pairs={{0,1},{1,0},{2,3},{3,2},{4,5},{5,4},{6,7},{7,6},{8,9},{9,8},{10,11... | collective-permute-start | bytes 393224 | tf_op jit(solution)/shard_map/ppermute | solution.py:21
  15.7 2.0 %inner_steps.1 = (f32[32,4,16,256]{3,2,1,0:T(8,128)S(1)}, f32[4264,128]{1,0:T(8,128)S(1)}, f32[4,32,256]{2,1,0:T(8,128)S(1)}) custom-call(f32[33,6,16,256]{3,2,1,0:T(8,128)S(1)} %get-tuple-element.24.coef, f32[32,4,16,256]{3,2,1,0:T(8,128)S(1)} %get-tuple-element.26.l2, s32[32,256]{1,0:T(8,128)S(1)} %copy-done.6, f32[2,32,256]{2,1,0:T(8,128)S(1)} %get-tuple-element.27.rows_in), custom_call_target="tpu_custom_call" | custom-call | flops 1000 | bytes 1000 | tf_op jit(solution)/shard_map/inner_steps/pallas_call | solution.py:308
  17.7 1.1 %write_inner.1.refs_1_ = f32[4,16,32,256]{3,2,1,0:T(8,128)} custom-call(f32[4264,128]{1,0:T(8,128)S(1)} %get-tuple-element.28.final.refs_0_), custom_call_target="tpu_custom_call" | custom-call | flops 1000 | bytes 1000 | tf_op jit(solution)/shard_map/write_inner/pallas_call | solution.py:537
  18.9 0.7 %collective-permute-done.3.refs_3_ = f32[16,8,256]{2,1,0:T(8,128)S(1)} collective-permute-done((f32[16,8,256]{2,1,0:T(8,128)S(1)}, f32[16,8,256]{2,1,0:T(8,128)S(1)}, u32[]{:S(2)}, u32[]{:S(2)}) %collective-permute-start.3) | collective-permute-done | bytes 131104 | tf_op jit(solution)/shard_map/ppermute | solution.py:21
  19.6 2.9 %collective-permute-done.2.refs_2_ = f32[16,8,256]{2,1,0:T(8,128)S(1)} collective-permute-done((f32[16,8,256]{2,1,0:T(8,128)S(1)}, f32[16,8,256]{2,1,0:T(8,128)S(1)}, u32[]{:S(2)}, u32[]{:S(2)}) %collective-permute-start.2) | collective-permute-done | bytes 131104 | tf_op jit(solution)/shard_map/ppermute | solution.py:21
  22.5 0.1 outer_coefs.1.wide
  22.6 0.0 collective-permute-done.4.first
  22.6 0.0 collective-permute-done.5.second
  22.6 0.7 %border_low_levels.1 = f32[32,256]{1,0:T(8,128)S(1)} custom-call(s32[32,256]{1,0:T(8,128)S(1)} %copy-done.6, f32[33,6,16,256]{3,2,1,0:T(8,128)S(1)} %get-tuple-element.24.coef, f32[2,7,6,16,256]{4,3,2,1,0:T(8,128)S(1)} %outer_coefs.1.wide, f32[4,4,16,256]{3,2,1,0:T(8,128)S(1)} %get-tuple-element.30.l0, f32[32,4,16,256]{3,2,1,0:T(8,128)S(1)} %get-tuple-element.31.l1, ...), custom_call_target="tpu_custom_call" | custom-call | flops 1000 | bytes 1000 | tf_op jit(solution)/shard_map/border_low_levels/pallas_call | solution.py:439
  23.3 0.3 %collective-permute-start.8 = (f32[32,256]{1,0:T(8,128)S(1)}, f32[32,256]{1,0:T(8,128)S(1)}, u32[]{:S(2)}, u32[]{:S(2)}) collective-permute-start(f32[32,256]{1,0:T(8,128)S(1)} %border_low_levels.1), channel_id=1, source_target_pairs={{0,3},{1,2},{2,1},{3,0},{4,7},{5,6},{6,5},{7,4},{8,11},{9,10},{10,... | collective-permute-start | bytes 98312 | tf_op jit(solution)/shard_map/ppermute | solution.py:21
  23.6 1.4 %collective-permute-start.7 = (f32[32,256]{1,0:T(8,128)S(1)}, f32[32,256]{1,0:T(8,128)S(1)}, u32[]{:S(2)}, u32[]{:S(2)}) collective-permute-start(f32[32,256]{1,0:T(8,128)S(1)} %border_low_levels.1), channel_id=1, source_target_pairs={{0,2},{1,3},{2,0},{3,1},{4,6},{5,7},{6,4},{7,5},{8,10},{9,11},{10,... | collective-permute-start | bytes 98312 | tf_op jit(solution)/shard_map/ppermute | solution.py:21
  25.0 0.2 collective-permute-start.6
  25.2 2.3 %border_all_levels.1 = (f32[4264,128]{1,0:T(8,128)S(1)}, f32[4,16,32,256]{3,2,1,0:T(8,128)}) custom-call(f32[33,6,16,256]{3,2,1,0:T(8,128)S(1)} %get-tuple-element.24.coef, f32[2,7,6,16,256]{4,3,2,1,0:T(8,128)S(1)} %outer_coefs.1.wide, f32[4,4,16,256]{3,2,1,0:T(8,128)S(1)} %get-tuple-element.30.l0, ...), custom_call_target="tpu_custom_call", output_to_operand_aliasing={{0}: (8, {}), {1}: (9, {})} | custom-call | flops 1000 | bytes 1000 | tf_op jit(solution)/shard_map/border_all_levels/pallas_call | solution.py:493
  27.6 0.0 collective-permute-done.8
  27.6 0.2 collective-permute-done.7
  27.8 0.6 %add_add_fusion = f32[32,256]{1,0:T(8,128)} fusion(f32[32,256]{1,0:T(8,128)S(1)} %collective-permute-done.8, f32[32,256]{1,0:T(8,128)S(1)} %collective-permute-done.7, f32[32,256]{1,0:T(8,128)S(1)} %border_low_levels.1, f32[32,256]{1,0:T(8,128)S(1)} %collective-permute-done.6), kind=kLoop, calls=%fused_computation | loop fusion | flops 24576 | bytes 163840 | tf_op jit(solution)/shard_map/add | solution.py:583
  (16 shorter events, 0.0 us)
Async XLA Ops:
  0.6 5.0 %copy-start.5 = (f32[16,32,256]{2,1,0:T(8,128)S(1)}, f32[16,32,256]{2,1,0:T(8,128)}, u32[]{:S(2)}) copy-start(f32[16,32,256]{2,1,0:T(8,128)} %mf.3) | copy-start | bytes 1572868
  0.6 5.0 %copy-start.4 = (f32[16,32,256]{2,1,0:T(8,128)S(1)}, f32[16,32,256]{2,1,0:T(8,128)}, u32[]{:S(2)}) copy-start(f32[16,32,256]{2,1,0:T(8,128)} %nd.3) | copy-start | bytes 1572868
  0.7 5.0 %copy-start.2 = (f32[16,32,256]{2,1,0:T(8,128)S(1)}, f32[16,32,256]{2,1,0:T(8,128)}, u32[]{:S(2)}) copy-start(f32[16,32,256]{2,1,0:T(8,128)} %ed.3) | copy-start | bytes 1572868
  0.7 5.0 %copy-start.3 = (f32[16,32,256]{2,1,0:T(8,128)S(1)}, f32[16,32,256]{2,1,0:T(8,128)}, u32[]{:S(2)}) copy-start(f32[16,32,256]{2,1,0:T(8,128)} %nw.3) | copy-start | bytes 1572868
  0.7 5.0 %copy-start.1 = (f32[16,32,256]{2,1,0:T(8,128)S(1)}, f32[16,32,256]{2,1,0:T(8,128)}, u32[]{:S(2)}) copy-start(f32[16,32,256]{2,1,0:T(8,128)} %ew.3) | copy-start | bytes 1572868
  0.7 5.0 %copy-start = (f32[4,16,32,256]{3,2,1,0:T(8,128)S(1)}, f32[4,16,32,256]{3,2,1,0:T(8,128)}, u32[]{:S(2)}) copy-start(f32[4,16,32,256]{3,2,1,0:T(8,128)} %lam.3) | copy-start | bytes 6291460
  0.7 5.0 %copy-start.6 = (s32[32,256]{1,0:T(8,128)S(1)}, s32[32,256]{1,0:T(8,128)}, u32[]{:S(2)}) copy-start(s32[32,256]{1,0:T(8,128)} %region.5) | copy-start | bytes 98308
  2.5 11.3 %collective-permute-start = (f32[16,8,256]{2,1,0:T(8,128)S(1)}, f32[16,8,256]{2,1,0:T(8,128)S(1)}, u32[]{:S(2)}, u32[]{:S(2)}) collective-permute-start(f32[16,8,256]{2,1,0:T(8,128)S(1)} %get-tuple-element.25), channel_id=1, source_target_pairs={{0,4},{1,29},{2,6},{3,31},{4,0},{5,9},{6,2},{7,11},{8,12},{9,5},{1... | collective-permute-start | bytes 393224 | tf_op jit(solution)/shard_map/ppermute | solution.py:21
  5.5 17.0 %collective-permute-start.4 = (f32[16,16,256]{2,1,0:T(8,128)S(1)}, f32[16,16,256]{2,1,0:T(8,128)S(1)}, u32[]{:S(2)}, u32[]{:S(2)}) collective-permute-start(f32[16,16,256]{2,1,0:T(8,128)S(1)} %get-tuple-element.33), channel_id=1, source_target_pairs={{0,4},{4,0},{8,12},{12,8},{16,20},{20,16},{24,28},{28,24},{1,5},{5... | collective-permute-start | bytes 786440 | tf_op jit(solution)/shard_map/ppermute | solution.py:21
  8.8 13.8 %collective-permute-start.5 = (f32[16,16,256]{2,1,0:T(8,128)S(1)}, f32[16,16,256]{2,1,0:T(8,128)S(1)}, u32[]{:S(2)}, u32[]{:S(2)}) collective-permute-start(f32[16,16,256]{2,1,0:T(8,128)S(1)} %get-tuple-element.34), channel_id=1, source_target_pairs={{0,28},{4,8},{8,4},{12,16},{16,12},{20,24},{24,20},{28,0},{1,29},{... | collective-permute-start | bytes 786440 | tf_op jit(solution)/shard_map/ppermute | solution.py:21
  13.9 5.7 %collective-permute-start.3 = (f32[16,8,256]{2,1,0:T(8,128)S(1)}, f32[16,8,256]{2,1,0:T(8,128)S(1)}, u32[]{:S(2)}, u32[]{:S(2)}) collective-permute-start(f32[16,8,256]{2,1,0:T(8,128)S(1)} %collective-permute-done.refs_0_), channel_id=1, source_target_pairs={{0,3},{1,2},{2,1},{3,0},{4,7},{5,6},{6,5},{7,4},{8,11},{9,10},{10,... | collective-permute-start | bytes 393224 | tf_op jit(solution)/shard_map/ppermute | solution.py:21
  13.9 8.6 %collective-permute-start.2 = (f32[16,8,256]{2,1,0:T(8,128)S(1)}, f32[16,8,256]{2,1,0:T(8,128)S(1)}, u32[]{:S(2)}, u32[]{:S(2)}) collective-permute-start(f32[16,8,256]{2,1,0:T(8,128)S(1)} %collective-permute-done.refs_0_), channel_id=1, source_target_pairs={{0,2},{1,3},{2,0},{3,1},{4,6},{5,7},{6,4},{7,5},{8,10},{9,11},{10,... | collective-permute-start | bytes 393224 | tf_op jit(solution)/shard_map/ppermute | solution.py:21
  15.4 7.1 %collective-permute-start.1 = (f32[16,8,256]{2,1,0:T(8,128)S(1)}, f32[16,8,256]{2,1,0:T(8,128)S(1)}, u32[]{:S(2)}, u32[]{:S(2)}) collective-permute-start(f32[16,8,256]{2,1,0:T(8,128)S(1)} %collective-permute-done.refs_0_), channel_id=1, source_target_pairs={{0,1},{1,0},{2,3},{3,2},{4,5},{5,4},{6,7},{7,6},{8,9},{9,8},{10,11... | collective-permute-start | bytes 393224 | tf_op jit(solution)/shard_map/ppermute | solution.py:21
  23.3 4.3 %collective-permute-start.8 = (f32[32,256]{1,0:T(8,128)S(1)}, f32[32,256]{1,0:T(8,128)S(1)}, u32[]{:S(2)}, u32[]{:S(2)}) collective-permute-start(f32[32,256]{1,0:T(8,128)S(1)} %border_low_levels.1), channel_id=1, source_target_pairs={{0,3},{1,2},{2,1},{3,0},{4,7},{5,6},{6,5},{7,4},{8,11},{9,10},{10,... | collective-permute-start | bytes 98312 | tf_op jit(solution)/shard_map/ppermute | solution.py:21
  23.6 4.1 %collective-permute-start.7 = (f32[32,256]{1,0:T(8,128)S(1)}, f32[32,256]{1,0:T(8,128)S(1)}, u32[]{:S(2)}, u32[]{:S(2)}) collective-permute-start(f32[32,256]{1,0:T(8,128)S(1)} %border_low_levels.1), channel_id=1, source_target_pairs={{0,2},{1,3},{2,0},{3,1},{4,6},{5,7},{6,4},{7,5},{8,10},{9,11},{10,... | collective-permute-start | bytes 98312 | tf_op jit(solution)/shard_map/ppermute | solution.py:21
  25.0 2.7 %collective-permute-start.6 = (f32[32,256]{1,0:T(8,128)S(1)}, f32[32,256]{1,0:T(8,128)S(1)}, u32[]{:S(2)}, u32[]{:S(2)}) collective-permute-start(f32[32,256]{1,0:T(8,128)S(1)} %border_low_levels.1), channel_id=1, source_target_pairs={{0,1},{1,0},{2,3},{3,2},{4,5},{5,4},{6,7},{7,6},{8,9},{9,8},{10,11... | collective-permute-start | bytes 98312 | tf_op jit(solution)/shard_map/ppermute | solution.py:21
